TPU v7x, 32 devices: a whole 2x2x4 slice. The times are simulated.
32 devices in a mesh: groups: 2 (over x), row: 16 (over z, y, core).
Axes of the slice: x: 2, y: 2, z: 4, core: 2. Of those that a mesh axis runs over, the one named last changes fastest.
Arguments:
- features: bfloat16 [64, 32, 4, 256], P('groups', 'row'), parts along dimension 0, may hold values from -6 to 6
- axial_taps: float32 [31, 256], replicated, may hold values from -1 to 1
- radial_taps: float32 [31, 256], replicated, may hold values from -1 to 1
- conv_bias: float32 [256], replicated, may hold values from -6 to 6
- ln_gain: float32 [256], replicated, may hold values from 0.5 to 1.5
- ln_bias: float32 [256], replicated, may hold values from -3 to 3
- w_in: bfloat16 [1024, 256], P('row'), may hold values from -0.375 to 0.375
- b_in: bfloat16 [1024], P('row'), may hold values from -3 to 3
- w_out: bfloat16 [1024, 256], P('row'), may hold values from -0.1875 to 0.1875
- b_out: float32 [256], replicated, may hold values from -1.75 to 1.75
- layer_scale: float32 [256], replicated, may hold values from 0.5 to 2
Outputs:
- block_out: bfloat16 [64, 32, 4, 256], P('groups', 'row'), parts along dimension 0
There are 2 independent parts, one for each index of `groups`. A program takes and returns all parts, laid end to end along the dimension named above; an argument that names none is the same for every part. Nothing has to cross between parts.
All inputs are finite; a program needn't handle non-finite values.
Results may differ from a plain program's by a relative error of at most 0.01.
Values may be sent and summed in bfloat16 or wider, within the bound.
No kernel may reach another device: no remote copies, remote signals or barrier semaphores. Data moves between devices by JAX's collectives and lax.ppermute only.
A program may use at most 64 MiB of HBM per device.

v0:
```python
from functools import partial

import jax
import jax.numpy as jnp
from jax import lax
from jax.sharding import PartitionSpec as P


def shifted_sum(source, tap_table, along_dim):
    half_span = tap_table.shape[0] // 2
    pad_widths = [(0, 0)] * source.ndim
    pad_widths[along_dim] = (half_span, half_span)
    padded = jnp.pad(source, pad_widths)
    extent = source.shape[along_dim]
    total_sum = jnp.zeros(source.shape, jnp.float32)
    for offset in range(tap_table.shape[0]):
        window = lax.slice_in_dim(padded, offset, offset + extent, axis=along_dim)
        total_sum = total_sum + window.astype(jnp.float32) * tap_table[offset]
    return total_sum


def block_mlp(params, row_block):
    w_in, b_in, w_out, ln_gain, ln_bias, b_out, layer_scale = params
    values = row_block.astype(jnp.float32)
    average = jnp.mean(values, axis=-1, keepdims=True)
    centred = values - average
    variance = jnp.mean(centred * centred, axis=-1, keepdims=True)
    normed = (centred * lax.rsqrt(variance + 1e-06) * ln_gain + ln_bias).astype(jnp.bfloat16)
    pre_act = lax.dot_general(
        normed, w_in, (((1,), (1,)), ((), ())), preferred_element_type=jnp.float32
    )
    pre_act = pre_act + b_in.astype(jnp.float32)
    hidden = jax.nn.gelu(pre_act, approximate=True).astype(jnp.bfloat16)
    projected = jnp.dot(hidden, w_out, preferred_element_type=jnp.float32) + b_out
    return (layer_scale * projected).astype(jnp.bfloat16)


def local(
    features,
    axial_taps,
    radial_taps,
    conv_bias,
    ln_gain,
    ln_bias,
    w_in,
    b_in,
    w_out,
    b_out,
    layer_scale,
):
    w_in_full, b_in_full, w_out_full = (
        lax.all_gather(w_in, "row", axis=0, tiled=True),
        lax.all_gather(b_in, "row", axis=0, tiled=True),
        lax.all_gather(w_out, "row", axis=0, tiled=True),
    )
    params = (w_in_full, b_in_full, w_out_full, ln_gain, ln_bias, b_out, layer_scale)
    channels = features.shape[-1]
    axial_mixed = shifted_sum(features, axial_taps, 0).astype(jnp.bfloat16)
    line_result = (
        shifted_sum(
            lax.all_to_all(axial_mixed, "row", split_axis=0, concat_axis=1, tiled=True),
            radial_taps,
            1,
        )
        + conv_bias
    ).astype(jnp.bfloat16)
    returned = lax.all_to_all(line_result, "row", split_axis=1, concat_axis=0, tiled=True)
    dims_out = returned.shape
    flat_rows = returned.reshape(-1, channels)
    row_count = flat_rows.shape[0]
    block_rows = 1024 if row_count % 1024 == 0 else row_count
    blocked = flat_rows.reshape(row_count // block_rows, block_rows, channels)
    result = lax.map(partial(block_mlp, params), blocked)
    branch = result.reshape(dims_out)
    return (features.astype(jnp.float32) + branch.astype(jnp.float32)).astype(jnp.bfloat16)


def solution(mesh):
    in_specs = (
        P("groups", "row", None, None),
        P(),
        P(),
        P(),
        P(),
        P(),
        P("row", None),
        P("row"),
        P("row", None),
        P(),
        P(),
    )
    out_specs = P("groups", "row", None, None)
    return jax.shard_map(local, mesh=mesh, in_specs=in_specs, out_specs=out_specs, check_vma=False)
```

profile of v0, /device:TPU:0, one launch (start us, length us, event | category | flops | bytes accessed | tf_op | source)
XLA Modules:
  0.0 100.2 jit_solution(3787928823563984789)
XLA Ops:
  0.0 1.0 fusion.45
  1.0 1.0 %fusion.44 = (f32[1,256]{1,0:T(1,128)S(1)}, f32[1,256]{1,0:T(1,128)S(1)}, f32[1,256]{1,0:T(1,128)S(1)}, f32[1,256]{1,0:T(1,128)S(1)}, f32[1,256]{1,0:T(1,128)S(1...) fusion(f32[31,256]{1,0:T(8,128)} %param.12), kind=kLoop, calls=%fused_computation.112 | loop fusion | bytes 38912 | tf_op jit(solution)/shard_map/slice | solution.py:18
  2.0 2.7 %add_convert_fusion.2 = bf16[32,2,4,256]{3,2,1,0:T(4,128)(2,1)} fusion(bf16[32,2,4,256]{3,2,1,0:T(4,128)(2,1)S(1)} %copy-done, f32[256]{0:T(256)S(1)} %bitcast.122, f32[256]{0:T(256)S(1)} %bitcast.123, f32[256]{0:T(256)S(1)} %bitcast.125, f32[256]{0:T(256)S(1)} %bitcast.126, f32[256]{0:T(256)S(1)} %bitcast.127, f32[256]{0:T(256)S(1)} %bitcast.128, ...), kind=kLoop, calls=%fused_computation.98 | loop fusion | flops 6094848 | bytes 293888 | tf_op jit(solution)/shard_map/convert_element_type | solution.py:58
  4.7 7.5 %all-to-all-start = ((bf16[32,2,4,256]{3,2,1,0:T(4,128)(2,1)}), bf16[32,2,4,256]{3,2,1,0:T(4,128)(2,1)S(1)}, u32[]{:S(2)}, u32[]{:S(2)}) async-start(bf16[32,2,4,256]{3,2,1,0:T(4,128)(2,1)} %add_convert_fusion.2), calls=%async_computation | async-start | bytes 262144 | tf_op jit(solution)/shard_map/all_to_all | solution.py:61
  12.3 0.0 copy-start.1
  12.3 0.0 copy-start.10
  12.3 0.6 copy-done.10
  13.0 0.6 dynamic-slice
  14.2 0.0 copy-start.9
  14.2 0.6 copy-done.9
  14.9 0.2 dynamic-update-slice
  15.0 33.9 %all-reduce.2 = bf16[1024]{0:T(1024)(128)(2,1)S(1)} all-reduce(bf16[1024]{0:T(1024)(128)(2,1)S(1)} %dynamic-update-slice), channel_id=1, replica_groups=mesh['groups'=2,'row'=16] {'row'}, use_global_device_ids=true, to_apply=%add.2 | all-reduce | flops 1024 | bytes 4096
  48.9 18.7 %all_gather.9 = bf16[1024,256]{1,0:T(8,128)(2,1)S(1)} all-gather(bf16[64,256]{1,0:T(8,128)(2,1)S(1)} %copy-done.1), channel_id=1, replica_groups=mesh['groups'=2,'row'=16] {'row'}, dimensions={0}, use_global_device_ids=true | all-gather | bytes 557056 | tf_op jit(solution)/shard_map/all_gather | solution.py:52
  67.7 0.0 copy-start.4
  67.7 0.7 copy-done.4
  68.4 1.0 add_convert_fusion.1
  69.3 0.8 copy.20
  70.1 3.9 %all-to-all-start.1 = ((bf16[2,32,4,256]{3,2,0,1:T(4,128)(2,1)}), bf16[2,32,4,256]{3,2,0,1:T(4,128)(2,1)S(1)}, u32[]{:S(2)}, u32[]{:S(2)}) async-start(bf16[2,32,4,256]{3,2,0,1:T(4,128)(2,1)} %copy.20), calls=%async_computation.1 | async-start | bytes 262144 | tf_op jit(solution)/shard_map/all_to_all | solution.py:67
  74.0 23.2 %all_gather.11 = bf16[1024,256]{1,0:T(8,128)(2,1)S(1)} all-gather(bf16[64,256]{1,0:T(8,128)(2,1)S(1)} %copy-done.2), channel_id=1, replica_groups=mesh['groups'=2,'row'=16] {'row'}, dimensions={0}, use_global_device_ids=true | all-gather | bytes 557056 | tf_op jit(solution)/shard_map/all_gather | solution.py:54
  97.2 0.2 fusion.41
  97.4 0.3 multiply_reduce_fusion
  97.7 0.1 div.11
  97.9 0.1 rsqrt.13
  98.0 0.0 copy-start.5
  98.0 0.1 reshape.112
  98.1 0.5 copy-done.5
  98.7 0.0 copy-done.6
  98.7 0.0 copy-done.7
  98.7 0.0 copy-done.8
  98.7 0.7 fusion.2
  99.4 0.1 reshape.113
  99.5 0.7 fusion.28
  (22 shorter events, 0.2 us)
Async XLA Ops:
  0.0 2.0 %copy-start = (bf16[32,2,4,256]{3,2,1,0:T(4,128)(2,1)S(1)}, bf16[32,2,4,256]{3,2,1,0:T(4,128)(2,1)}, u32[]{:S(2)}) copy-start(bf16[32,2,4,256]{3,2,1,0:T(4,128)(2,1)} %param.11) | copy-start | bytes 393220
  4.7 7.5 %copy-start.3 = (f32[31,256]{1,0:T(8,128)S(1)}, f32[31,256]{1,0:T(8,128)}, u32[]{:S(2)}) copy-start(f32[31,256]{1,0:T(8,128)} %param.13) | copy-start | bytes 95236
  4.7 62.9 %all-to-all-start = ((bf16[32,2,4,256]{3,2,1,0:T(4,128)(2,1)}), bf16[32,2,4,256]{3,2,1,0:T(4,128)(2,1)S(1)}, u32[]{:S(2)}, u32[]{:S(2)}) async-start(bf16[32,2,4,256]{3,2,1,0:T(4,128)(2,1)} %add_convert_fusion.2), calls=%async_computation | async-start | bytes 262144 | tf_op jit(solution)/shard_map/all_to_all | solution.py:61
  12.3 36.7 %copy-start.1 = (bf16[64,256]{1,0:T(8,128)(2,1)S(1)}, bf16[64,256]{1,0:T(8,128)(2,1)}, u32[]{:S(2)}) copy-start(bf16[64,256]{1,0:T(8,128)(2,1)} %param.17) | copy-start | bytes 98308
  12.3 0.7 copy-start.10
  14.2 0.7 copy-start.9
  67.7 0.7 copy-start.4
  70.1 3.9 %copy-start.2 = (bf16[64,256]{1,0:T(8,128)(2,1)S(1)}, bf16[64,256]{1,0:T(8,128)(2,1)}, u32[]{:S(2)}) copy-start(bf16[64,256]{1,0:T(8,128)(2,1)} %param.19) | copy-start | bytes 98308
  70.1 27.1 %all-to-all-start.1 = ((bf16[2,32,4,256]{3,2,0,1:T(4,128)(2,1)}), bf16[2,32,4,256]{3,2,0,1:T(4,128)(2,1)S(1)}, u32[]{:S(2)}, u32[]{:S(2)}) async-start(bf16[2,32,4,256]{3,2,0,1:T(4,128)(2,1)} %copy.20), calls=%async_computation.1 | async-start | bytes 262144 | tf_op jit(solution)/shard_map/all_to_all | solution.py:67
  98.0 0.7 copy-start.5
  98.0 0.7 copy-start.6
  98.0 0.7 copy-start.7
  98.0 0.7 copy-start.8
where the time goes:
time: 101 us; the launch traced here: 100 us
  blocking collectives  75.7 us (75%)
  starting transfers between devices  11.4 us (11%)
  local copies, waits for them, and re-layouts  6.6 us (7%)
  other arithmetic  4.9 us (5%)
    unnamed x1, blocking collectives  33.9 us
    all_gather x1, blocking collectives, local(): lax.all_gather(w_out, 'row', axis=0, tiled=True)  23.2 us
    all_gather x1, blocking collectives, local(): lax.all_gather(w_in, 'row', axis=0, tiled=True)  18.7 us
    all_to_all x1, starting transfers between devices, local(): lax.all_to_all(axial_mixed, 'row', split_axis=0, concat_axis=1, tiled=True)  7.52 us
    all_to_all x1, starting transfers between devices, local(): lax.all_to_all(line_result, 'row', split_axis=1, concat_axis=0, tiled=True)  3.93 us
    unnamed x25, local copies, waits for them, and re-layouts  3.36 us
    convert_element_type x1, other arithmetic, local(): axial_mixed = shifted_sum(features, axial_taps, 0).astype(jnp.bfloat16)  2.67 us
    slice x4, local copies, waits for them, and re-layouts, shifted_sum(): total_sum = total_sum + window.astype(jnp.float32) * tap_table[offset]  2.02 us
  transfers between devices with their start and end apart: 2, of which 0 were waited for; matrix products, arithmetic and copies ran while one was open for 1% of the time, Pallas kernels for 0%

commit v1 on v0

v1 whole, which is shorter than its diff:
```python
from functools import partial

import jax
import jax.numpy as jnp
from jax import lax
from jax.experimental import pallas as pl
from jax.experimental.pallas import tpu as pltpu
from jax.sharding import PartitionSpec as P

SLOT = 64
EXTRA = 16


def vmem():
    return pl.BlockSpec(memory_space=pltpu.VMEM)


def pack_kernel(w_in_ref, w_out_ref, b_ref, out_ref):
    out_ref[0:SLOT, :] = w_in_ref[...]
    out_ref[SLOT : 2 * SLOT, :] = w_out_ref[...]
    out_ref[2 * SLOT : 2 * SLOT + EXTRA, :] = jnp.broadcast_to(b_ref[...], (EXTRA, out_ref.shape[1]))


def radial_kernel(x_ref, taps_ref, out_ref, even, odd):
    n, a_loc, _, theta, c = x_ref.shape
    taps = taps_ref.shape[0]
    pad = (taps + 1) // 4
    zeros = jnp.zeros((pad, a_loc, 2 * theta, c), jnp.float32)
    even[0:pad] = zeros
    even[pad + n : 2 * pad + n] = zeros
    odd[0:pad] = zeros
    odd[pad + n - 1 : 2 * pad + n - 1] = zeros
    odd[2 * pad + n - 1 :] = zeros[:1]
    first = x_ref[:, :, 0].astype(jnp.float32)
    second = x_ref[:, :, 1].astype(jnp.float32)
    even[pad : pad + n, :, 0:theta] = first
    even[pad : pad + n, :, theta:] = second
    odd[pad : pad + n, :, 0:theta] = second
    odd[pad - 1 : pad + n - 1, :, theta:] = first

    def step(s, carry):
        total = jnp.zeros((a_loc, 2 * theta, c), jnp.float32)
        for k in range(taps):
            shift = k - taps // 2
            source = even if shift % 2 == 0 else odd
            total = total + source[s + (pad + shift // 2)] * taps_ref[k : k + 1, :]
        out_ref[s] = total.astype(out_ref.dtype)
        return carry

    lax.fori_loop(0, n, step, 0)


def mlp_kernel(z_ref, feat_ref, w_ref, taps_ref, conv_b_ref, gain_ref, lnb_ref, b_out_ref, scale_ref, out_ref, padded, branch):
    axial, rows, c = z_ref.shape
    theta = rows // 2
    taps = taps_ref.shape[0]
    half = taps // 2
    zeros = jnp.zeros((half, rows, c), jnp.float32)
    padded[0:half] = zeros
    padded[half + axial :] = zeros
    padded[half : half + axial] = z_ref[...].astype(jnp.float32)
    slots = w_ref.shape[0]
    per = c // SLOT
    lane_slot = lax.broadcasted_iota(jnp.int32, (1, c), 1) // SLOT
    block = 4
    token_block = 32

    def conv(i, carry):
        base = i * block
        total = jnp.zeros((block, rows, c), jnp.float32)
        for k in range(taps):
            total = total + padded[pl.ds(base + k, block)] * taps_ref[k : k + 1, :]
        branch[pl.ds(base, block)] = total + conv_b_ref[...]
        return carry

    lax.fori_loop(0, axial // block, conv, 0)

    def mlp(i, carry):
        base = i * token_block
        v = branch[pl.ds(base, token_block)].reshape(token_block * rows, c)
        v = v.astype(jnp.bfloat16).astype(jnp.float32)
        mean = jnp.mean(v, axis=-1, keepdims=True)
        centred = v - mean
        var = jnp.mean(centred * centred, axis=-1, keepdims=True)
        normed = (centred * lax.rsqrt(var + 1e-06) * gain_ref[...] + lnb_ref[...]).astype(jnp.bfloat16)
        total = jnp.zeros(v.shape, jnp.float32)
        for g in range(slots // per):
            own = slice(g * per, (g + 1) * per)
            w_in = w_ref[own, 0:SLOT, :].reshape(per * SLOT, c)
            w_out = w_ref[own, SLOT : 2 * SLOT, :].reshape(per * SLOT, c)
            bias = jnp.zeros((1, c), jnp.float32)
            for j in range(per):
                piece = w_ref[g * per + j, 2 * SLOT : 2 * SLOT + EXTRA, :].astype(jnp.float32)[0:1]
                bias = jnp.where(lane_slot == j, piece, bias)
            u = lax.dot_general(normed, w_in, (((1,), (1,)), ((), ())), preferred_element_type=jnp.float32)
            u = u + bias
            hidden = (0.5 * u * (1.0 + jnp.tanh(0.7978845608028654 * (u + 0.044715 * u * u * u)))).astype(jnp.bfloat16)
            total = total + jnp.dot(hidden, w_out, preferred_element_type=jnp.float32)
        result = (scale_ref[...] * (total + b_out_ref[...])).astype(jnp.bfloat16).astype(jnp.float32)
        branch[pl.ds(base, token_block)] = result.reshape(token_block, rows, c)
        return carry

    lax.fori_loop(0, axial // token_block, mlp, 0)
    for r in range(2):
        got = branch[:, r * theta : (r + 1) * theta, :]
        out_ref[:, r] = (feat_ref[:, r].astype(jnp.float32) + got).astype(out_ref.dtype)


def digits(n):
    chips = n // 2
    inner = 1
    while inner * inner * 4 <= chips:
        inner *= 2
    return chips // inner, inner, 2


def shifted(n, digit, by):
    sizes = digits(n)
    stride = [sizes[1] * sizes[2], sizes[2], 1][digit]
    pairs = []
    for i in range(n):
        at = (i // stride) % sizes[digit]
        to = (at + by) % sizes[digit]
        pairs.append((i, i + (to - at) * stride))
    return pairs


def gather_slots(slot, n):
    held = slot[None]
    for digit, size in enumerate(digits(n)):
        parts = [held]
        for by in range(1, size):
            parts.append(lax.ppermute(held, "row", shifted(n, digit, by)))
        held = jnp.concatenate(parts, axis=0)
    return held


def local(n, features, axial_taps, radial_taps, conv_bias, ln_gain, ln_bias, w_in, b_in, w_out, b_out, layer_scale):
    axial, r_loc, theta, c = features.shape
    hid_loc = w_in.shape[0]
    a_loc = axial // n
    if hid_loc == SLOT:
        packed = pl.pallas_call(
            pack_kernel,
            out_shape=jax.ShapeDtypeStruct((2 * SLOT + EXTRA, c), jnp.bfloat16),
            in_specs=[vmem()] * 3,
            out_specs=vmem(),
            name="pack",
        )(w_in, w_out, jnp.tile(b_in, c // SLOT)[None, :])
        slots = gather_slots(packed, n)
    else:
        w_all = lax.all_gather(w_in, "row", axis=0, tiled=True).reshape(-1, SLOT, c)
        o_all = lax.all_gather(w_out, "row", axis=0, tiled=True).reshape(-1, SLOT, c)
        b_all = lax.all_gather(b_in, "row", axis=0, tiled=True).reshape(-1, 1, SLOT)
        b_all = jnp.broadcast_to(jnp.tile(b_all, (1, 1, c // SLOT)), (w_all.shape[0], EXTRA, c))
        slots = jnp.concatenate([w_all, o_all, b_all], axis=1)

    got = lax.all_to_all(features, "row", split_axis=0, concat_axis=0, tiled=True)
    pad = (radial_taps.shape[0] + 1) // 4
    mixed = pl.pallas_call(
        radial_kernel,
        out_shape=jax.ShapeDtypeStruct((n, a_loc, r_loc * theta, c), jnp.bfloat16),
        in_specs=[vmem()] * 2,
        out_specs=vmem(),
        scratch_shapes=[pltpu.VMEM((n + 2 * pad, a_loc, r_loc * theta, c), jnp.float32)] * 2,
        compiler_params=pltpu.CompilerParams(vmem_limit_bytes=48 * 1024 * 1024),
        name="radial",
    )(got.reshape(n, a_loc, r_loc, theta, c), radial_taps)
    back = lax.all_to_all(mixed.reshape(axial, r_loc * theta, c), "row", split_axis=0, concat_axis=0, tiled=True)
    return pl.pallas_call(
        mlp_kernel,
        out_shape=jax.ShapeDtypeStruct(features.shape, jnp.bfloat16),
        in_specs=[vmem()] * 9,
        out_specs=vmem(),
        scratch_shapes=[
            pltpu.VMEM((axial + axial_taps.shape[0] - 1, r_loc * theta, c), jnp.float32),
            pltpu.VMEM((axial, r_loc * theta, c), jnp.float32),
        ],
        compiler_params=pltpu.CompilerParams(vmem_limit_bytes=48 * 1024 * 1024),
        name="mlp",
    )(back, features, slots, axial_taps, conv_bias[None, :], ln_gain[None, :], ln_bias[None, :], b_out[None, :], layer_scale[None, :])


def solution(mesh):
    in_specs = (
        P("groups", "row", None, None),
        P(),
        P(),
        P(),
        P(),
        P(),
        P("row", None),
        P("row"),
        P("row", None),
        P(),
        P(),
    )
    out_specs = P("groups", "row", None, None)
    return jax.shard_map(partial(local, mesh.shape["row"]), mesh=mesh, in_specs=in_specs, out_specs=out_specs, check_vma=False)
```

time: 101 us -> 51.6 us (0.51)
  blocking collectives: 75.7 us -> 12.1 us
  waiting for transfers between devices: 0.01 us -> 18 us
  Pallas kernels: 0 us -> 5.46 us
  local copies, waits for them, and re-layouts: 6.6 us -> 2.42 us
  other arithmetic: 4.9 us -> 0.92 us
    all_gather x2 -> x0, blocking collectives: 41.8 us -> none  [the longest x1 23.2 us: local(): lax.all_gather(w_out, 'row', axis=0, tiled=True)]
    unnamed x1 -> x0, blocking collectives: 33.9 us -> none
    all_to_all x0 -> x1, blocking collectives: none -> 12.1 us  [local(): lax.all_to_all(features, 'row', split_axis=0, concat_axis=0, tiled=True)]
    ppermute x0 -> x5, waiting for transfers between devices: none -> 10.1 us  [gather_slots(): parts.append(lax.ppermute(held, 'row', shifted(n, digit, by)))]
    ppermute x0 -> x5, starting transfers between devices: none -> 8.62 us  [gather_slots(): parts.append(lax.ppermute(held, 'row', shifted(n, digit, by)))]
    all_to_all x2 -> x1, starting transfers between devices: 11.4 us -> 3.51 us  [local(): lax.all_to_all(mixed.reshape(axial, r_loc * theta, c), 'row', split_axis=...]
    all_to_all x2 -> x1, waiting for transfers between devices: 0.01 us -> 7.84 us  [local(): lax.all_to_all(mixed.reshape(axial, r_loc * theta, c), 'row', split_axis=...]
    pallas_call x0 -> x3, Pallas kernels: none -> 5.46 us  [the longest x1 2.28 us: local(): pl.pallas_call(mlp_kernel, out_shape=jax.ShapeDtypeStruct(features.shape,...]
  transfers between devices with their start and end apart: 2 -> 6, of which waited for: 0 -> 5; matrix products, arithmetic and copies ran while one was open for 1% -> 2% of each run, Pallas kernels for 0% -> 3%
where the time goes in v1:
time: 51.6 us; the launch traced here: 51.2 us
  waiting for transfers between devices  18 us (35%)
  starting transfers between devices  12.1 us (23%)
  blocking collectives  12.1 us (23%)
  Pallas kernels  5.46 us (11%)
  local copies, waits for them, and re-layouts  2.42 us (5%)
  other arithmetic  0.92 us (2%)
    all_to_all x1, blocking collectives, local(): lax.all_to_all(features, 'row', split_axis=0, concat_axis=0, tiled=True)  12.1 us
    ppermute x5, waiting for transfers between devices, gather_slots(): parts.append(lax.ppermute(held, 'row', shifted(n, digit, by)))  10.1 us
    ppermute x5, starting transfers between devices, gather_slots(): parts.append(lax.ppermute(held, 'row', shifted(n, digit, by)))  8.62 us
    all_to_all x1, waiting for transfers between devices, local(): lax.all_to_all(mixed.reshape(axial, r_loc * theta, c), 'row', split_axis=...  7.84 us
    all_to_all x1, starting transfers between devices, local(): lax.all_to_all(mixed.reshape(axial, r_loc * theta, c), 'row', split_axis=...  3.51 us
    pallas_call x1, Pallas kernels, local(): pl.pallas_call(mlp_kernel, out_shape=jax.ShapeDtypeStruct(features.shape,...  2.28 us
    pallas_call x1, Pallas kernels, local(): pl.pallas_call(radial_kernel, out_shape=jax.ShapeDtypeStruct((n, a_loc, r...  1.77 us
    pallas_call x1, Pallas kernels, local(): pl.pallas_call(pack_kernel, out_shape=jax.ShapeDtypeStruct((2 * SLOT + EX...  1.42 us
  transfers between devices with their start and end apart: 6, of which 5 were waited for; matrix products, arithmetic and copies ran while one was open for 2% of the time, Pallas kernels for 3%

profile of v1, /device:TPU:0, one launch (start us, length us, event | category | flops | bytes accessed | tf_op | source)
XLA Modules:
  0.0 51.2 jit_solution(9206616724851608551)
XLA Ops:
  0.0 0.7 %tile.2 = bf16[4,64]{1,0:T(4,128)(2,1)S(1)} broadcast(bf16[64]{0:T(256)(128)(2,1)} %param.18), dimensions={1} | broadcast | bytes 640 | tf_op jit(solution)/shard_map/tile | solution.py:149
  0.7 0.7 %broadcast_in_dim_tile.3.b_ref = bf16[1,256]{1,0:T(2,128)(2,1)} reshape(bf16[4,64]{1,0:T(4,128)(2,1)S(1)} %tile.2) | data formatting | bytes 1024 | tf_op jit(solution)/shard_map/broadcast_in_dim;tile | solution.py:149
  1.3 1.4 %pack.1 = bf16[144,256]{1,0:T(8,128)(2,1)} custom-call(bf16[64,256]{1,0:T(8,128)(2,1)} %w_in_ref.1, bf16[64,256]{1,0:T(8,128)(2,1)} %w_out_ref.1, bf16[1,256]{1,0:T(2,128)(2,1)} %broadcast_in_dim_tile.3.b_ref), custom_call_target="tpu_custom_call" | custom-call | tf_op jit(solution)/shard_map/pack/pallas_call | solution.py:143
  2.8 3.0 %collective-permute-start = (bf16[1,144,256]{2,1,0:T(8,128)(2,1)}, bf16[1,144,256]{2,1,0:T(8,128)(2,1)S(1)}, u32[]{:S(2)}, u32[]{:S(2)}) collective-permute-start(bf16[1,144,256]{2,1,0:T(8,128)(2,1)} %bitcast.16), channel_id=1, source_target_pairs={{0,4},{1,5},{2,6},{3,7},{4,8},{5,9},{6,10},{7,11},{8,12},{9,13},{1... | collective-permute-start | bytes 221192 | tf_op jit(solution)/shard_map/ppermute | solution.py:133
  5.8 2.6 %collective-permute-start.1 = (bf16[1,144,256]{2,1,0:T(8,128)(2,1)}, bf16[1,144,256]{2,1,0:T(8,128)(2,1)S(1)}, u32[]{:S(2)}, u32[]{:S(2)}) collective-permute-start(bf16[1,144,256]{2,1,0:T(8,128)(2,1)} %bitcast.17), channel_id=1, source_target_pairs={{0,8},{1,9},{2,10},{3,11},{4,12},{5,13},{6,14},{7,15},{8,0},{9,1},... | collective-permute-start | bytes 221192 | tf_op jit(solution)/shard_map/ppermute | solution.py:133
  8.4 1.3 %collective-permute-start.2 = (bf16[1,144,256]{2,1,0:T(8,128)(2,1)}, bf16[1,144,256]{2,1,0:T(8,128)(2,1)S(1)}, u32[]{:S(2)}, u32[]{:S(2)}) collective-permute-start(bf16[1,144,256]{2,1,0:T(8,128)(2,1)} %bitcast.18), channel_id=1, source_target_pairs={{0,12},{1,13},{2,14},{3,15},{4,0},{5,1},{6,2},{7,3},{8,4},{9,5},{1... | collective-permute-start | bytes 221192 | tf_op jit(solution)/shard_map/ppermute | solution.py:133
  9.7 0.9 %constant_dynamic-update-slice_fusion.4 = (bf16[8,144,256]{2,1,0:T(8,128)(2,1)S(1)}, bf16[16,144,256]{2,1,0:T(8,128)(2,1)S(1)}) fusion(bf16[144,256]{1,0:T(8,128)(2,1)} %pack.1), kind=kLoop, calls=%fused_computation.5 | loop fusion | bytes 221184
  10.6 0.0 copy-start.1
  10.7 0.1 collective-permute-done
  10.7 2.8 %collective-permute-done.1 = bf16[1,144,256]{2,1,0:T(8,128)(2,1)S(1)} collective-permute-done((bf16[1,144,256]{2,1,0:T(8,128)(2,1)}, bf16[1,144,256]{2,1,0:T(8,128)(2,1)S(1)}, u32[]{:S(2)}, u32[]{:S(2)}) %collective-permute-start.1) | collective-permute-done | bytes 73760 | tf_op jit(solution)/shard_map/ppermute | solution.py:133
  13.5 0.2 collective-permute-done.2
  13.7 0.9 %pad_maximum_fusion = bf16[4,144,256]{2,1,0:T(8,128)(2,1)S(1)} fusion(bf16[1,144,256]{2,1,0:T(8,128)(2,1)S(1)} %collective-permute-done.2, bf16[1,144,256]{2,1,0:T(8,128)(2,1)S(1)} %collective-permute-done.1, bf16[1,144,256]{2,1,0:T(8,128)(2,1)S(1)} %collective-permute-done, bf16[1,144,256]{2,1,0:T(8,128)(2,1)} %bitcast.19), kind=kLoop, calls=%fused_computation | loop fusion | flops 442368 | bytes 589824 | tf_op jit(solution)/shard_map/concatenate | solution.py:134
  14.7 1.6 %collective-permute-start.3 = (bf16[4,144,256]{2,1,0:T(8,128)(2,1)S(1)}, bf16[4,144,256]{2,1,0:T(8,128)(2,1)S(1)}, u32[]{:S(2)}, u32[]{:S(2)}) collective-permute-start(bf16[4,144,256]{2,1,0:T(8,128)(2,1)S(1)} %pad_maximum_fusion), channel_id=1, source_target_pairs={{0,2},{1,3},{2,0},{3,1},{4,6},{5,7},{6,4},{7,5},{8,10},{9,11},{10,... | collective-permute-start | bytes 884744 | tf_op jit(solution)/shard_map/ppermute | solution.py:133
  16.3 7.0 %collective-permute-done.3 = bf16[4,144,256]{2,1,0:T(8,128)(2,1)S(1)} collective-permute-done((bf16[4,144,256]{2,1,0:T(8,128)(2,1)S(1)}, bf16[4,144,256]{2,1,0:T(8,128)(2,1)S(1)}, u32[]{:S(2)}, u32[]{:S(2)}) %collective-permute-start.3) | collective-permute-done | bytes 294944 | tf_op jit(solution)/shard_map/ppermute | solution.py:133
  23.4 0.0 copy-start.2
  23.4 0.0 copy-start.3
  23.4 0.0 copy-start.4
  23.4 0.0 copy-start.5
  23.5 0.0 copy-start.6
  23.5 0.0 copy-start.7
  23.5 0.1 collective-permute-start.4
  23.6 0.0 copy-done
  23.6 12.1 %all_to_all.10 = bf16[32,2,4,256]{3,2,1,0:T(4,128)(2,1)S(1)} all-to-all(bf16[32,2,4,256]{3,2,1,0:T(4,128)(2,1)S(1)} %copy-done), channel_id=1, replica_groups=mesh['groups'=2,'row'=16] {'row'}, dimensions={0} | all-to-all | bytes 262144 | tf_op jit(solution)/shard_map/all_to_all | solution.py:158
  35.7 0.0 copy-done.1
  35.7 1.8 %radial.1 = bf16[16,2,8,256]{3,2,1,0:T(8,128)(2,1)} custom-call(bf16[16,2,2,4,256]{4,3,2,1,0:T(4,128)(2,1)S(1)} %bitcast.10, f32[31,256]{1,0:T(8,128)S(1)} %copy-done.1), custom_call_target="tpu_custom_call" | custom-call | tf_op jit(solution)/shard_map/radial/pallas_call | solution.py:160
  37.4 3.5 %all-to-all-start.1 = ((bf16[32,8,256]{2,1,0:T(8,128)(2,1)}), bf16[32,8,256]{2,1,0:T(8,128)(2,1)S(1)}, u32[]{:S(2)}, u32[]{:S(2)}) async-start(bf16[32,8,256]{2,1,0:T(8,128)(2,1)} %bitcast.1), calls=%async_computation.1 | async-start | bytes 262144 | tf_op jit(solution)/shard_map/all_to_all | solution.py:169
  41.0 0.0 collective-permute-done.4
  41.0 7.8 %all-to-all-done.1.z_ref = bf16[32,8,256]{2,1,0:T(8,128)(2,1)S(1)} async-done(((bf16[32,8,256]{2,1,0:T(8,128)(2,1)}), bf16[32,8,256]{2,1,0:T(8,128)(2,1)S(1)}, u32[]{:S(2)}, u32[]{:S(2)}) %all-to-all-start.1) | async-done | bytes 131104 | tf_op jit(solution)/shard_map/all_to_all | solution.py:169
  48.9 0.0 copy-done.2
  48.9 0.0 copy-done.3
  48.9 0.0 copy-done.4
  48.9 2.3 %mlp.1 = bf16[32,2,4,256]{3,2,1,0:T(4,128)(2,1)} custom-call(bf16[32,8,256]{2,1,0:T(8,128)(2,1)S(1)} %all-to-all-done.1.z_ref, bf16[32,2,4,256]{3,2,1,0:T(4,128)(2,1)S(1)} %copy-done, bf16[16,144,256]{2,1,0:T(8,128)(2,1)S(1)} %constant_dynamic-update-slice_fusion.5.w_ref, f32[31,256]{1,0:T(8,128)S(1)} %copy-done.2, f32[1,256]{1,0:T(1,128)S(1)} %bitcast.11, ...), custom_call_target="tpu_custom_call" | custom-call | tf_op jit(solution)/shard_map/mlp/pallas_call | solution.py:170
  (9 shorter events, 0.1 us)
Async XLA Ops:
  2.7 20.8 %copy-start = (bf16[32,2,4,256]{3,2,1,0:T(4,128)(2,1)S(1)}, bf16[32,2,4,256]{3,2,1,0:T(4,128)(2,1)}, u32[]{:S(2)}) copy-start(bf16[32,2,4,256]{3,2,1,0:T(4,128)(2,1)} %feat_ref.1) | copy-start | bytes 393220
  2.8 8.0 %collective-permute-start = (bf16[1,144,256]{2,1,0:T(8,128)(2,1)}, bf16[1,144,256]{2,1,0:T(8,128)(2,1)S(1)}, u32[]{:S(2)}, u32[]{:S(2)}) collective-permute-start(bf16[1,144,256]{2,1,0:T(8,128)(2,1)} %bitcast.16), channel_id=1, source_target_pairs={{0,4},{1,5},{2,6},{3,7},{4,8},{5,9},{6,10},{7,11},{8,12},{9,13},{1... | collective-permute-start | bytes 221192 | tf_op jit(solution)/shard_map/ppermute | solution.py:133
  5.8 7.8 %collective-permute-start.1 = (bf16[1,144,256]{2,1,0:T(8,128)(2,1)}, bf16[1,144,256]{2,1,0:T(8,128)(2,1)S(1)}, u32[]{:S(2)}, u32[]{:S(2)}) collective-permute-start(bf16[1,144,256]{2,1,0:T(8,128)(2,1)} %bitcast.17), channel_id=1, source_target_pairs={{0,8},{1,9},{2,10},{3,11},{4,12},{5,13},{6,14},{7,15},{8,0},{9,1},... | collective-permute-start | bytes 221192 | tf_op jit(solution)/shard_map/ppermute | solution.py:133
  8.4 5.4 %collective-permute-start.2 = (bf16[1,144,256]{2,1,0:T(8,128)(2,1)}, bf16[1,144,256]{2,1,0:T(8,128)(2,1)S(1)}, u32[]{:S(2)}, u32[]{:S(2)}) collective-permute-start(bf16[1,144,256]{2,1,0:T(8,128)(2,1)} %bitcast.18), channel_id=1, source_target_pairs={{0,12},{1,13},{2,14},{3,15},{4,0},{5,1},{6,2},{7,3},{8,4},{9,5},{1... | collective-permute-start | bytes 221192 | tf_op jit(solution)/shard_map/ppermute | solution.py:133
  10.6 25.0 %copy-start.1 = (f32[31,256]{1,0:T(8,128)S(1)}, f32[31,256]{1,0:T(8,128)}, u32[]{:S(2)}) copy-start(f32[31,256]{1,0:T(8,128)} %taps_ref.2) | copy-start | bytes 95236
  14.7 8.7 %collective-permute-start.3 = (bf16[4,144,256]{2,1,0:T(8,128)(2,1)S(1)}, bf16[4,144,256]{2,1,0:T(8,128)(2,1)S(1)}, u32[]{:S(2)}, u32[]{:S(2)}) collective-permute-start(bf16[4,144,256]{2,1,0:T(8,128)(2,1)S(1)} %pad_maximum_fusion), channel_id=1, source_target_pairs={{0,2},{1,3},{2,0},{3,1},{4,6},{5,7},{6,4},{7,5},{8,10},{9,11},{10,... | collective-permute-start | bytes 884744 | tf_op jit(solution)/shard_map/ppermute | solution.py:133
  23.4 25.5 %copy-start.2 = (f32[31,256]{1,0:T(8,128)S(1)}, f32[31,256]{1,0:T(8,128)}, u32[]{:S(2)}) copy-start(f32[31,256]{1,0:T(8,128)} %taps_ref.3) | copy-start | bytes 95236
  23.4 25.5 %copy-start.3 = (f32[256]{0:T(256)S(1)}, f32[256]{0:T(256)}, u32[]{:S(2)}) copy-start(f32[256]{0:T(256)} %param.14) | copy-start | bytes 3076
  23.4 25.4 %copy-start.4 = (f32[256]{0:T(256)S(1)}, f32[256]{0:T(256)}, u32[]{:S(2)}) copy-start(f32[256]{0:T(256)} %param.15) | copy-start | bytes 3076
  23.4 25.4 %copy-start.5 = (f32[256]{0:T(256)S(1)}, f32[256]{0:T(256)}, u32[]{:S(2)}) copy-start(f32[256]{0:T(256)} %param.16) | copy-start | bytes 3076
  23.5 25.4 %copy-start.6 = (f32[256]{0:T(256)S(1)}, f32[256]{0:T(256)}, u32[]{:S(2)}) copy-start(f32[256]{0:T(256)} %param.20) | copy-start | bytes 3076
  23.5 25.4 %copy-start.7 = (f32[256]{0:T(256)S(1)}, f32[256]{0:T(256)}, u32[]{:S(2)}) copy-start(f32[256]{0:T(256)} %param.21) | copy-start | bytes 3076
  23.5 17.5 %collective-permute-start.4 = (bf16[8,144,256]{2,1,0:T(8,128)(2,1)S(1)}, bf16[8,144,256]{2,1,0:T(8,128)(2,1)S(1)}, u32[]{:S(2)}, u32[]{:S(2)}) collective-permute-start(bf16[8,144,256]{2,1,0:T(8,128)(2,1)S(1)} %get-tuple-element.5), channel_id=1, source_target_pairs={{0,1},{1,0},{2,3},{3,2},{4,5},{5,4},{6,7},{7,6},{8,9},{9,8},{10,11... | collective-permute-start | bytes 1769480 | tf_op jit(solution)/shard_map/ppermute | solution.py:133
  37.4 11.4 %all-to-all-start.1 = ((bf16[32,8,256]{2,1,0:T(8,128)(2,1)}), bf16[32,8,256]{2,1,0:T(8,128)(2,1)S(1)}, u32[]{:S(2)}, u32[]{:S(2)}) async-start(bf16[32,8,256]{2,1,0:T(8,128)(2,1)} %bitcast.1), calls=%async_computation.1 | async-start | bytes 262144 | tf_op jit(solution)/shard_map/all_to_all | solution.py:169

commit v2 on v1

--- a/solution.py
+++ b/solution.py
@@ -18,7 +18,9 @@
 def pack_kernel(w_in_ref, w_out_ref, b_ref, out_ref):
     out_ref[0:SLOT, :] = w_in_ref[...]
     out_ref[SLOT : 2 * SLOT, :] = w_out_ref[...]
-    out_ref[2 * SLOT : 2 * SLOT + EXTRA, :] = jnp.broadcast_to(b_ref[...], (EXTRA, out_ref.shape[1]))
+    bias = b_ref[...].astype(jnp.float32)[None, :]
+    wide = jnp.concatenate([bias] * (out_ref.shape[1] // SLOT), axis=1)
+    out_ref[2 * SLOT : 2 * SLOT + EXTRA, :] = jnp.broadcast_to(wide, (EXTRA, out_ref.shape[1])).astype(out_ref.dtype)
 
 
 def radial_kernel(x_ref, taps_ref, out_ref, even, odd):
@@ -50,7 +52,8 @@
     lax.fori_loop(0, n, step, 0)
 
 
-def mlp_kernel(z_ref, feat_ref, w_ref, taps_ref, conv_b_ref, gain_ref, lnb_ref, b_out_ref, scale_ref, out_ref, padded, branch):
+def mlp_kernel(z_ref, feat_ref, taps_ref, conv_b_ref, gain_ref, lnb_ref, b_out_ref, scale_ref, *rest):
+    *w_refs, out_ref, padded, branch = rest
     axial, rows, c = z_ref.shape
     theta = rows // 2
     taps = taps_ref.shape[0]
@@ -59,8 +62,8 @@
     padded[0:half] = zeros
     padded[half + axial :] = zeros
     padded[half : half + axial] = z_ref[...].astype(jnp.float32)
-    slots = w_ref.shape[0]
     per = c // SLOT
+    groups = [(w, g) for w in w_refs for g in range(w.shape[0] // per)]
     lane_slot = lax.broadcasted_iota(jnp.int32, (1, c), 1) // SLOT
     block = 4
     token_block = 32
@@ -84,7 +87,7 @@
         var = jnp.mean(centred * centred, axis=-1, keepdims=True)
         normed = (centred * lax.rsqrt(var + 1e-06) * gain_ref[...] + lnb_ref[...]).astype(jnp.bfloat16)
         total = jnp.zeros(v.shape, jnp.float32)
-        for g in range(slots // per):
+        for w_ref, g in groups:
             own = slice(g * per, (g + 1) * per)
             w_in = w_ref[own, 0:SLOT, :].reshape(per * SLOT, c)
             w_out = w_ref[own, SLOT : 2 * SLOT, :].reshape(per * SLOT, c)
@@ -125,14 +128,22 @@
     return pairs
 
 
-def gather_slots(slot, n):
-    held = slot[None]
-    for digit, size in enumerate(digits(n)):
-        parts = [held]
-        for by in range(1, size):
-            parts.append(lax.ppermute(held, "row", shifted(n, digit, by)))
-        held = jnp.concatenate(parts, axis=0)
-    return held
+def join_kernel(*refs):
+    out_ref = refs[-1]
+    for i, ref in enumerate(refs[:-1]):
+        out_ref[i] = ref[...]
+
+
+def line_slots(slot, n):
+    outer = digits(n)[0]
+    line = [slot] + [lax.ppermute(slot, "row", shifted(n, 0, by)) for by in range(1, outer)]
+    return pl.pallas_call(
+        join_kernel,
+        out_shape=jax.ShapeDtypeStruct((outer,) + slot.shape, slot.dtype),
+        in_specs=[vmem()] * outer,
+        out_specs=vmem(),
+        name="join",
+    )(*line)
 
 
 def local(n, features, axial_taps, radial_taps, conv_bias, ln_gain, ln_bias, w_in, b_in, w_out, b_out, layer_scale):
@@ -146,16 +157,19 @@
             in_specs=[vmem()] * 3,
             out_specs=vmem(),
             name="pack",
-        )(w_in, w_out, jnp.tile(b_in, c // SLOT)[None, :])
-        slots = gather_slots(packed, n)
+        )(w_in, w_out, b_in)
+        line = line_slots(packed, n)
     else:
         w_all = lax.all_gather(w_in, "row", axis=0, tiled=True).reshape(-1, SLOT, c)
         o_all = lax.all_gather(w_out, "row", axis=0, tiled=True).reshape(-1, SLOT, c)
         b_all = lax.all_gather(b_in, "row", axis=0, tiled=True).reshape(-1, 1, SLOT)
         b_all = jnp.broadcast_to(jnp.tile(b_all, (1, 1, c // SLOT)), (w_all.shape[0], EXTRA, c))
-        slots = jnp.concatenate([w_all, o_all, b_all], axis=1)
+        slots = [jnp.concatenate([w_all, o_all, b_all], axis=1)]
 
     got = lax.all_to_all(features, "row", split_axis=0, concat_axis=0, tiled=True)
+    if hid_loc == SLOT:
+        line, got = lax.optimization_barrier((line, got))
+        inner = [lax.ppermute(line, "row", shifted(n, 1, by)) for by in range(1, digits(n)[1])]
     pad = (radial_taps.shape[0] + 1) // 4
     mixed = pl.pallas_call(
         radial_kernel,
@@ -166,11 +180,15 @@
         compiler_params=pltpu.CompilerParams(vmem_limit_bytes=48 * 1024 * 1024),
         name="radial",
     )(got.reshape(n, a_loc, r_loc, theta, c), radial_taps)
+    if hid_loc == SLOT:
+        inner = [lax.optimization_barrier((h, mixed))[0] for h in inner]
+        slots = [line] + inner
+        slots = slots + [lax.ppermute(h, "row", shifted(n, 2, 1)) for h in slots]
     back = lax.all_to_all(mixed.reshape(axial, r_loc * theta, c), "row", split_axis=0, concat_axis=0, tiled=True)
     return pl.pallas_call(
         mlp_kernel,
         out_shape=jax.ShapeDtypeStruct(features.shape, jnp.bfloat16),
-        in_specs=[vmem()] * 9,
+        in_specs=[vmem()] * (8 + len(slots)),
         out_specs=vmem(),
         scratch_shapes=[
             pltpu.VMEM((axial + axial_taps.shape[0] - 1, r_loc * theta, c), jnp.float32),
@@ -178,7 +196,7 @@
         ],
         compiler_params=pltpu.CompilerParams(vmem_limit_bytes=48 * 1024 * 1024),
         name="mlp",
-    )(back, features, slots, axial_taps, conv_bias[None, :], ln_gain[None, :], ln_bias[None, :], b_out[None, :], layer_scale[None, :])
+    )(back, features, axial_taps, conv_bias[None, :], ln_gain[None, :], ln_bias[None, :], b_out[None, :], layer_scale[None, :], *slots)
 
 
 def solution(mesh):

time: 51.6 us -> 46.8 us (0.907)
  waiting for transfers between devices: 18 us -> 13.3 us
  starting transfers between devices: 12.1 us -> 13.7 us
  blocking collectives: 12.1 us -> 10.8 us
  Pallas kernels: 5.46 us -> 6.59 us
  other arithmetic: 0.92 us -> 0 us
  local copies, waits for them, and re-layouts: 2.42 us -> 1.89 us
    all_to_all x1, waiting for transfers between devices: 7.84 us -> 0.01 us  [local(): lax.all_to_all(features, 'row', split_axis=0, concat_axis=0, tiled=True)]
    all_to_all x1, starting transfers between devices: 3.51 us -> 7.39 us  [local(): lax.all_to_all(features, 'row', split_axis=0, concat_axis=0, tiled=True)]
    ppermute x5 -> x6, waiting for transfers between devices: 10.1 us -> 13.3 us  [the longest x3 6.87 us: line_slots(): lax.ppermute(slot, 'row', shifted(n, 0, by))]
    ppermute x5 -> x6, starting transfers between devices: 8.62 us -> 6.32 us  [the longest x3 4.85 us: line_slots(): lax.ppermute(slot, 'row', shifted(n, 0, by))]
    pallas_call x0 -> x1, Pallas kernels: none -> 1.72 us  [line_slots(): pl.pallas_call(join_kernel, out_shape=jax.ShapeDtypeStruct((outer,) + slo...]
    another operation x2 -> x0, local copies, waits for them, and re-layouts: 1.33 us -> none  [local(): jnp.tile(b_in, c // SLOT)[None, :]]
    all_to_all x1, blocking collectives: 12.1 us -> 10.8 us  [local(): lax.all_to_all(mixed.reshape(axial, r_loc * theta, c), 'row', split_axis=...]
    concatenate x1 -> x0, other arithmetic: 0.92 us -> none  [gather_slots(): held = jnp.concatenate(parts, axis=0)]
  transfers between devices with their start and end apart: 6 -> 7, of which waited for: 5 -> 3; matrix products, arithmetic and copies ran while one was open for 2% -> 0% of each run, Pallas kernels for 3% -> 9%
where the time goes in v2:
time: 46.8 us; the launch traced here: 46.4 us
  starting transfers between devices  13.7 us (29%)
  waiting for transfers between devices  13.3 us (28%)
  blocking collectives  10.8 us (23%)
  Pallas kernels  6.59 us (14%)
  local copies, waits for them, and re-layouts  1.89 us (4%)
    all_to_all x1, blocking collectives, local(): lax.all_to_all(mixed.reshape(axial, r_loc * theta, c), 'row', split_axis=...  10.8 us
    all_to_all x1, starting transfers between devices, local(): lax.all_to_all(features, 'row', split_axis=0, concat_axis=0, tiled=True)  7.39 us
    ppermute x3, waiting for transfers between devices, line_slots(): lax.ppermute(slot, 'row', shifted(n, 0, by))  6.87 us
    ppermute x1, waiting for transfers between devices, local(): lax.ppermute(line, 'row', shifted(n, 1, by))  6.4 us
    ppermute x3, starting transfers between devices, line_slots(): lax.ppermute(slot, 'row', shifted(n, 0, by))  4.85 us
    pallas_call x1, Pallas kernels, local(): pl.pallas_call(mlp_kernel, out_shape=jax.ShapeDtypeStruct(features.shape,...  2.27 us
    unnamed x24, local copies, waits for them, and re-layouts  1.89 us
    pallas_call x1, Pallas kernels, line_slots(): pl.pallas_call(join_kernel, out_shape=jax.ShapeDtypeStruct((outer,) + slo...  1.72 us
  transfers between devices with their start and end apart: 7, of which 3 were waited for; matrix products, arithmetic and copies ran while one was open for 0% of the time, Pallas kernels for 9%

profile of v2, /device:TPU:0, one launch (start us, length us, event | category | flops | bytes accessed | tf_op | source)
XLA Modules:
  0.0 46.4 jit_solution(17993356152561198946)
XLA Ops:
  0.0 7.4 %all-to-all-start = ((bf16[32,2,4,256]{3,2,1,0:T(4,128)(2,1)}), bf16[32,2,4,256]{3,2,1,0:T(4,128)(2,1)S(1)}, u32[]{:S(2)}, u32[]{:S(2)}) async-start(bf16[32,2,4,256]{3,2,1,0:T(4,128)(2,1)} %feat_ref.1), calls=%async_computation | async-start | bytes 262144 | tf_op jit(solution)/shard_map/all_to_all | solution.py:169
  7.4 1.5 %pack.1.refs_0_ = bf16[144,256]{1,0:T(8,128)(2,1)} custom-call(bf16[64,256]{1,0:T(8,128)(2,1)} %w_in_ref.1, bf16[64,256]{1,0:T(8,128)(2,1)} %w_out_ref.1, bf16[64]{0:T(256)(128)(2,1)} %b_ref.1), custom_call_target="tpu_custom_call" | custom-call | tf_op jit(solution)/shard_map/pack/pallas_call | solution.py:154
  8.9 3.7 %collective-permute-start.2 = (bf16[144,256]{1,0:T(8,128)(2,1)}, bf16[144,256]{1,0:T(8,128)(2,1)S(1)}, u32[]{:S(2)}, u32[]{:S(2)}) collective-permute-start(bf16[144,256]{1,0:T(8,128)(2,1)} %pack.1.refs_0_), channel_id=1, source_target_pairs={{0,12},{1,13},{2,14},{3,15},{4,0},{5,1},{6,2},{7,3},{8,4},{9,5},{1... | collective-permute-start | bytes 221192 | tf_op jit(solution)/shard_map/ppermute | solution.py:139
  12.6 0.0 collective-permute-start.1
  12.6 1.1 %collective-permute-start = (bf16[144,256]{1,0:T(8,128)(2,1)}, bf16[144,256]{1,0:T(8,128)(2,1)S(1)}, u32[]{:S(2)}, u32[]{:S(2)}) collective-permute-start(bf16[144,256]{1,0:T(8,128)(2,1)} %pack.1.refs_0_), channel_id=1, source_target_pairs={{0,4},{1,5},{2,6},{3,7},{4,8},{5,9},{6,10},{7,11},{8,12},{9,13},{1... | collective-permute-start | bytes 221192 | tf_op jit(solution)/shard_map/ppermute | solution.py:139
  13.7 1.9 %collective-permute-done.2.refs_3_ = bf16[144,256]{1,0:T(8,128)(2,1)S(1)} collective-permute-done((bf16[144,256]{1,0:T(8,128)(2,1)}, bf16[144,256]{1,0:T(8,128)(2,1)S(1)}, u32[]{:S(2)}, u32[]{:S(2)}) %collective-permute-start.2) | collective-permute-done | bytes 73760 | tf_op jit(solution)/shard_map/ppermute | solution.py:139
  15.6 5.0 %collective-permute-done.1.refs_2_ = bf16[144,256]{1,0:T(8,128)(2,1)S(1)} collective-permute-done((bf16[144,256]{1,0:T(8,128)(2,1)}, bf16[144,256]{1,0:T(8,128)(2,1)S(1)}, u32[]{:S(2)}, u32[]{:S(2)}) %collective-permute-start.1) | collective-permute-done | bytes 73760 | tf_op jit(solution)/shard_map/ppermute | solution.py:139
  20.6 0.0 collective-permute-done.refs_1_
  20.6 0.0 copy-done.9
  20.6 0.6 %copy-done.10 = bf16[144,256]{1,0:T(8,128)(2,1)} copy-done((bf16[144,256]{1,0:T(8,128)(2,1)}, bf16[144,256]{1,0:T(8,128)(2,1)S(1)}, u32[]{:S(2)}) %copy-start.10) | copy-done | bytes 73752
  21.2 0.6 %copy-done.11 = bf16[144,256]{1,0:T(8,128)(2,1)} copy-done((bf16[144,256]{1,0:T(8,128)(2,1)}, bf16[144,256]{1,0:T(8,128)(2,1)S(1)}, u32[]{:S(2)}) %copy-start.11) | copy-done | bytes 73752
  21.9 1.7 %join.1.rest_0_ = bf16[4,144,256]{2,1,0:T(8,128)(2,1)} custom-call(bf16[144,256]{1,0:T(8,128)(2,1)} %pack.1.refs_0_, bf16[144,256]{1,0:T(8,128)(2,1)} %copy-done.11, bf16[144,256]{1,0:T(8,128)(2,1)} %copy-done.10, bf16[144,256]{1,0:T(8,128)(2,1)} %copy-done.9), custom_call_target="tpu_custom_call" | custom-call | tf_op jit(solution)/shard_map/join/pallas_call | solution.py:140
  23.6 0.0 all-to-all-done
  23.6 1.5 %collective-permute-start.3 = (bf16[4,144,256]{2,1,0:T(8,128)(2,1)}, bf16[4,144,256]{2,1,0:T(8,128)(2,1)S(1)}, u32[]{:S(2)}, u32[]{:S(2)}) collective-permute-start(bf16[4,144,256]{2,1,0:T(8,128)(2,1)} %join.1.rest_0_), channel_id=1, source_target_pairs={{0,2},{1,3},{2,0},{3,1},{4,6},{5,7},{6,4},{7,5},{8,10},{9,11},{10,... | collective-permute-start | bytes 884744 | tf_op jit(solution)/shard_map/ppermute | solution.py:172
  25.0 0.0 collective-permute-start.4
  25.0 0.0 copy-done.2
  25.1 1.1 %radial.1 = bf16[16,2,8,256]{3,2,1,0:T(8,128)(2,1)S(1)} custom-call(bf16[16,2,2,4,256]{4,3,2,1,0:T(4,128)(2,1)S(1)} %bitcast.7, f32[31,256]{1,0:T(8,128)S(1)} %copy-done.2), custom_call_target="tpu_custom_call" | custom-call | tf_op jit(solution)/shard_map/radial/pallas_call | solution.py:174
  26.2 6.4 %collective-permute-done.3.rest_1_ = bf16[4,144,256]{2,1,0:T(8,128)(2,1)S(1)} collective-permute-done((bf16[4,144,256]{2,1,0:T(8,128)(2,1)}, bf16[4,144,256]{2,1,0:T(8,128)(2,1)S(1)}, u32[]{:S(2)}, u32[]{:S(2)}) %collective-permute-start.3) | collective-permute-done | bytes 294944 | tf_op jit(solution)/shard_map/ppermute | solution.py:172
  32.6 0.0 collective-permute-start.5
  32.6 0.0 copy-start.6
  32.6 0.0 copy-start.7
  32.6 0.0 copy-start.8
  32.6 10.8 %all_to_all.10.z_ref = bf16[32,8,256]{2,1,0:T(8,128)(2,1)S(1)} all-to-all(bf16[32,8,256]{2,1,0:T(8,128)(2,1)S(1)} %bitcast.8), channel_id=1, replica_groups=mesh['groups'=2,'row'=16] {'row'}, dimensions={0} | all-to-all | bytes 262144 | tf_op jit(solution)/shard_map/all_to_all | solution.py:187
  43.4 0.0 collective-permute-done.4.rest_2_
  43.4 0.0 collective-permute-done.5.rest_3_
  43.4 0.0 copy-done
  43.5 0.0 copy-done.1
  43.5 0.0 copy-done.3
  43.5 0.0 copy-done.5
  43.5 0.0 copy-done.6
  43.5 0.6 %copy-done.4 = f32[256]{0:T(256)S(1)} copy-done((f32[256]{0:T(256)S(1)}, f32[256]{0:T(256)}, u32[]{:S(2)}) %copy-start.4) | copy-done | bytes 1048
  44.1 2.3 %mlp.1 = bf16[32,2,4,256]{3,2,1,0:T(4,128)(2,1)} custom-call(bf16[32,8,256]{2,1,0:T(8,128)(2,1)S(1)} %all_to_all.10.z_ref, bf16[32,2,4,256]{3,2,1,0:T(4,128)(2,1)S(1)} %copy-done.1, f32[31,256]{1,0:T(8,128)S(1)} %copy-done.3, f32[1,256]{1,0:T(1,128)S(1)} %bitcast.9, f32[1,256]{1,0:T(1,128)S(1)} %bitcast.10, f32[1,256]{1,0:T(1,128)S(1)} %bitcast.11, ...), custom_call_target="tpu_custom_call" | custom-call | tf_op jit(solution)/shard_map/mlp/pallas_call | solution.py:188
  (11 shorter events, 0.0 us)
Async XLA Ops:
  0.0 23.6 %all-to-all-start = ((bf16[32,2,4,256]{3,2,1,0:T(4,128)(2,1)}), bf16[32,2,4,256]{3,2,1,0:T(4,128)(2,1)S(1)}, u32[]{:S(2)}, u32[]{:S(2)}) async-start(bf16[32,2,4,256]{3,2,1,0:T(4,128)(2,1)} %feat_ref.1), calls=%async_computation | async-start | bytes 262144 | tf_op jit(solution)/shard_map/all_to_all | solution.py:169
  8.9 16.2 %copy-start.2 = (f32[31,256]{1,0:T(8,128)S(1)}, f32[31,256]{1,0:T(8,128)}, u32[]{:S(2)}) copy-start(f32[31,256]{1,0:T(8,128)} %taps_ref.2) | copy-start | bytes 95236
  8.9 6.7 %collective-permute-start.2 = (bf16[144,256]{1,0:T(8,128)(2,1)}, bf16[144,256]{1,0:T(8,128)(2,1)S(1)}, u32[]{:S(2)}, u32[]{:S(2)}) collective-permute-start(bf16[144,256]{1,0:T(8,128)(2,1)} %pack.1.refs_0_), channel_id=1, source_target_pairs={{0,12},{1,13},{2,14},{3,15},{4,0},{5,1},{6,2},{7,3},{8,4},{9,5},{1... | collective-permute-start | bytes 221192 | tf_op jit(solution)/shard_map/ppermute | solution.py:139
  12.6 8.0 %collective-permute-start.1 = (bf16[144,256]{1,0:T(8,128)(2,1)}, bf16[144,256]{1,0:T(8,128)(2,1)S(1)}, u32[]{:S(2)}, u32[]{:S(2)}) collective-permute-start(bf16[144,256]{1,0:T(8,128)(2,1)} %pack.1.refs_0_), channel_id=1, source_target_pairs={{0,8},{1,9},{2,10},{3,11},{4,12},{5,13},{6,14},{7,15},{8,0},{9,1},... | collective-permute-start | bytes 221192 | tf_op jit(solution)/shard_map/ppermute | solution.py:139
  12.6 8.0 %collective-permute-start = (bf16[144,256]{1,0:T(8,128)(2,1)}, bf16[144,256]{1,0:T(8,128)(2,1)S(1)}, u32[]{:S(2)}, u32[]{:S(2)}) collective-permute-start(bf16[144,256]{1,0:T(8,128)(2,1)} %pack.1.refs_0_), channel_id=1, source_target_pairs={{0,4},{1,5},{2,6},{3,7},{4,8},{5,9},{6,10},{7,11},{8,12},{9,13},{1... | collective-permute-start | bytes 221192 | tf_op jit(solution)/shard_map/ppermute | solution.py:139
  15.6 5.0 %copy-start.9 = (bf16[144,256]{1,0:T(8,128)(2,1)}, bf16[144,256]{1,0:T(8,128)(2,1)S(1)}, u32[]{:S(2)}) copy-start(bf16[144,256]{1,0:T(8,128)(2,1)S(1)} %collective-permute-done.2.refs_3_) | copy-start | bytes 221188
  20.6 0.6 %copy-start.10 = (bf16[144,256]{1,0:T(8,128)(2,1)}, bf16[144,256]{1,0:T(8,128)(2,1)S(1)}, u32[]{:S(2)}) copy-start(bf16[144,256]{1,0:T(8,128)(2,1)S(1)} %collective-permute-done.1.refs_2_) | copy-start | bytes 221188
  21.2 0.6 %copy-start.11 = (bf16[144,256]{1,0:T(8,128)(2,1)}, bf16[144,256]{1,0:T(8,128)(2,1)S(1)}, u32[]{:S(2)}) copy-start(bf16[144,256]{1,0:T(8,128)(2,1)S(1)} %collective-permute-done.refs_1_) | copy-start | bytes 221188
  23.6 19.9 %copy-start = (bf16[4,144,256]{2,1,0:T(8,128)(2,1)S(1)}, bf16[4,144,256]{2,1,0:T(8,128)(2,1)}, u32[]{:S(2)}) copy-start(bf16[4,144,256]{2,1,0:T(8,128)(2,1)} %join.1.rest_0_) | copy-start | bytes 884740
  23.6 9.0 %collective-permute-start.3 = (bf16[4,144,256]{2,1,0:T(8,128)(2,1)}, bf16[4,144,256]{2,1,0:T(8,128)(2,1)S(1)}, u32[]{:S(2)}, u32[]{:S(2)}) collective-permute-start(bf16[4,144,256]{2,1,0:T(8,128)(2,1)} %join.1.rest_0_), channel_id=1, source_target_pairs={{0,2},{1,3},{2,0},{3,1},{4,6},{5,7},{6,4},{7,5},{8,10},{9,11},{10,... | collective-permute-start | bytes 884744 | tf_op jit(solution)/shard_map/ppermute | solution.py:172
  25.0 18.4 %collective-permute-start.4 = (bf16[4,144,256]{2,1,0:T(8,128)(2,1)}, bf16[4,144,256]{2,1,0:T(8,128)(2,1)S(1)}, u32[]{:S(2)}, u32[]{:S(2)}) collective-permute-start(bf16[4,144,256]{2,1,0:T(8,128)(2,1)} %join.1.rest_0_), channel_id=1, source_target_pairs={{0,1},{1,0},{2,3},{3,2},{4,5},{5,4},{6,7},{7,6},{8,9},{9,8},{10,11... | collective-permute-start | bytes 884744 | tf_op jit(solution)/shard_map/ppermute | solution.py:186
  32.6 10.9 %collective-permute-start.5 = (bf16[4,144,256]{2,1,0:T(8,128)(2,1)S(1)}, bf16[4,144,256]{2,1,0:T(8,128)(2,1)S(1)}, u32[]{:S(2)}, u32[]{:S(2)}) collective-permute-start(bf16[4,144,256]{2,1,0:T(8,128)(2,1)S(1)} %collective-permute-done.3.rest_1_), channel_id=1, source_target_pairs={{0,1},{1,0},{2,3},{3,2},{4,5},{5,4},{6,7},{7,6},{8,9},{9,8},{10,11... | collective-permute-start | bytes 884744 | tf_op jit(solution)/shard_map/ppermute | solution.py:186
  32.6 10.9 %copy-start.1 = (bf16[32,2,4,256]{3,2,1,0:T(4,128)(2,1)S(1)}, bf16[32,2,4,256]{3,2,1,0:T(4,128)(2,1)}, u32[]{:S(2)}) copy-start(bf16[32,2,4,256]{3,2,1,0:T(4,128)(2,1)} %feat_ref.1) | copy-start | bytes 393220
  32.6 10.9 %copy-start.3 = (f32[31,256]{1,0:T(8,128)S(1)}, f32[31,256]{1,0:T(8,128)}, u32[]{:S(2)}) copy-start(f32[31,256]{1,0:T(8,128)} %taps_ref.3) | copy-start | bytes 95236
  32.6 10.9 %copy-start.5 = (f32[256]{0:T(256)S(1)}, f32[256]{0:T(256)}, u32[]{:S(2)}) copy-start(f32[256]{0:T(256)} %param.15) | copy-start | bytes 3076
  32.6 10.9 %copy-start.6 = (f32[256]{0:T(256)S(1)}, f32[256]{0:T(256)}, u32[]{:S(2)}) copy-start(f32[256]{0:T(256)} %param.16) | copy-start | bytes 3076
  32.6 10.9 %copy-start.7 = (f32[256]{0:T(256)S(1)}, f32[256]{0:T(256)}, u32[]{:S(2)}) copy-start(f32[256]{0:T(256)} %param.20) | copy-start | bytes 3076
  32.6 10.9 %copy-start.8 = (f32[256]{0:T(256)S(1)}, f32[256]{0:T(256)}, u32[]{:S(2)}) copy-start(f32[256]{0:T(256)} %param.21) | copy-start | bytes 3076
  43.4 0.7 %copy-start.4 = (f32[256]{0:T(256)S(1)}, f32[256]{0:T(256)}, u32[]{:S(2)}) copy-start(f32[256]{0:T(256)} %param.14) | copy-start | bytes 3076

commit v3 on v1

v3 whole, which is shorter than its diff:
```python
from functools import partial

import jax
import jax.numpy as jnp
from jax import lax
from jax.experimental import pallas as pl
from jax.experimental.pallas import tpu as pltpu
from jax.sharding import PartitionSpec as P

SLOT = 64
EXTRA = 16


def vmem():
    return pl.BlockSpec(memory_space=pltpu.VMEM)


def pack_kernel(w_in_ref, w_out_ref, b_ref, out_ref):
    out_ref[0, 0:SLOT, :] = w_in_ref[...]
    out_ref[0, SLOT : 2 * SLOT, :] = w_out_ref[...]
    bias = b_ref[...].astype(jnp.float32)[None, :]
    c = out_ref.shape[2]
    wide = jnp.concatenate([bias] * (c // SLOT), axis=1)
    out_ref[0, 2 * SLOT : 2 * SLOT + EXTRA, :] = jnp.broadcast_to(wide, (EXTRA, c)).astype(out_ref.dtype)


def radial_kernel(pieces, x_ref, taps_ref, *rest):
    if pieces:
        joined_ref, even, odd, sems = rest[pieces + 1 :]
        copies = [pltpu.make_async_copy(rest[i], joined_ref.at[i : i + 1], sems.at[i]) for i in range(pieces)]
    else:
        even, odd = rest[1:]
        copies = []
    out_ref = rest[pieces]
    for copy in copies:
        copy.start()
    n, a_loc, _, theta, c = x_ref.shape
    taps = taps_ref.shape[0]
    pad = (taps + 1) // 4
    zeros = jnp.zeros((pad, a_loc, 2 * theta, c), jnp.float32)
    even[0:pad] = zeros
    even[pad + n : 2 * pad + n] = zeros
    odd[0:pad] = zeros
    odd[pad + n - 1 : 2 * pad + n - 1] = zeros
    odd[2 * pad + n - 1 :] = zeros[:1]
    first = x_ref[:, :, 0].astype(jnp.float32)
    second = x_ref[:, :, 1].astype(jnp.float32)
    even[pad : pad + n, :, 0:theta] = first
    even[pad : pad + n, :, theta:] = second
    odd[pad : pad + n, :, 0:theta] = second
    odd[pad - 1 : pad + n - 1, :, theta:] = first

    def step(s, carry):
        total = jnp.zeros((a_loc, 2 * theta, c), jnp.float32)
        for k in range(taps):
            shift = k - taps // 2
            source = even if shift % 2 == 0 else odd
            total = total + source[s + (pad + shift // 2)] * taps_ref[k : k + 1, :]
        out_ref[s] = total.astype(out_ref.dtype)
        return carry

    lax.fori_loop(0, n, step, 0)
    for copy in copies:
        copy.wait()


def axial_kernel(z_ref, taps_ref, conv_b_ref, gain_ref, lnb_ref, out_ref, padded):
    axial, rows, c = z_ref.shape
    taps = taps_ref.shape[0]
    half = taps // 2
    zeros = jnp.zeros((half, rows, c), jnp.float32)
    padded[0:half] = zeros
    padded[half + axial :] = zeros
    padded[half : half + axial] = z_ref[...].astype(jnp.float32)
    block = 4

    def conv(i, carry):
        base = i * block
        total = jnp.zeros((block, rows, c), jnp.float32)
        for k in range(taps):
            total = total + padded[pl.ds(base + k, block)] * taps_ref[k : k + 1, :]
        v = (total + conv_b_ref[...]).reshape(block * rows, c)
        v = v.astype(jnp.bfloat16).astype(jnp.float32)
        mean = jnp.mean(v, axis=-1, keepdims=True)
        centred = v - mean
        var = jnp.mean(centred * centred, axis=-1, keepdims=True)
        normed = centred * lax.rsqrt(var + 1e-06) * gain_ref[...] + lnb_ref[...]
        at = pl.multiple_of(base * rows, block * rows)
        out_ref[pl.ds(at, block * rows), :] = normed.astype(out_ref.dtype)
        return carry

    lax.fori_loop(0, axial // block, conv, 0)


def mlp_kernel(normed_ref, feat_ref, b_out_ref, scale_ref, *rest):
    *w_refs, out_ref, slots, branch, sems = rest
    axial, _, theta, c = feat_ref.shape
    rows = 2 * theta
    per = c // SLOT
    lane_slot = lax.broadcasted_iota(jnp.int32, (1, c), 1) // SLOT
    token_block = 32 * rows
    copies, at = [], 0
    for i, w_ref in enumerate(w_refs):
        copies.append(pltpu.make_async_copy(w_ref, slots.at[at : at + w_ref.shape[0]], sems.at[i]))
        at += w_ref.shape[0]
    for copy in copies:
        copy.start()
    for copy in copies:
        copy.wait()

    def mlp(i, carry):
        base = pl.multiple_of(i * token_block, token_block)
        normed = normed_ref[pl.ds(base, token_block), :]
        total = jnp.zeros((token_block, c), jnp.float32)
        for g in range(slots.shape[0] // per):
            own = slice(g * per, (g + 1) * per)
            w_in = slots[own, 0:SLOT, :].reshape(per * SLOT, c)
            w_out = slots[own, SLOT : 2 * SLOT, :].reshape(per * SLOT, c)
            bias = jnp.zeros((1, c), jnp.float32)
            for j in range(per):
                piece = slots[g * per + j, 2 * SLOT : 2 * SLOT + EXTRA, :].astype(jnp.float32)[0:1]
                bias = jnp.where(lane_slot == j, piece, bias)
            u = lax.dot_general(normed, w_in, (((1,), (1,)), ((), ())), preferred_element_type=jnp.float32)
            u = u + bias
            hidden = (0.5 * u * (1.0 + jnp.tanh(0.7978845608028654 * (u + 0.044715 * u * u * u)))).astype(jnp.bfloat16)
            total = total + jnp.dot(hidden, w_out, preferred_element_type=jnp.float32)
        result = (scale_ref[...] * (total + b_out_ref[...])).astype(jnp.bfloat16).astype(jnp.float32)
        branch[pl.ds(i * 32, 32)] = result.reshape(32, rows, c)
        return carry

    lax.fori_loop(0, axial // 32, mlp, 0)
    for r in range(2):
        got = branch[:, r * theta : (r + 1) * theta, :]
        out_ref[:, r] = (feat_ref[:, r].astype(jnp.float32) + got).astype(out_ref.dtype)


def digits(n):
    chips = n // 2
    inner = 1
    while inner * inner * 4 <= chips:
        inner *= 2
    return chips // inner, inner, 2


def shifted(n, digit, by):
    sizes = digits(n)
    stride = [sizes[1] * sizes[2], sizes[2], 1][digit]
    pairs = []
    for i in range(n):
        at = (i // stride) % sizes[digit]
        to = (at + by) % sizes[digit]
        pairs.append((i, i + (to - at) * stride))
    return pairs


def local(n, features, axial_taps, radial_taps, conv_bias, ln_gain, ln_bias, w_in, b_in, w_out, b_out, layer_scale):
    axial, r_loc, theta, c = features.shape
    rows = r_loc * theta
    hid_loc = w_in.shape[0]
    a_loc = axial // n
    spread = hid_loc == SLOT
    params = pltpu.CompilerParams(vmem_limit_bytes=48 * 1024 * 1024)

    def move(piece, digit, by=1):
        return lax.ppermute(piece, "row", shifted(n, digit, by))

    outer, inner, _ = digits(n)
    if spread:
        own = pl.pallas_call(
            pack_kernel,
            out_shape=jax.ShapeDtypeStruct((1, 2 * SLOT + EXTRA, c), jnp.bfloat16),
            in_specs=[vmem()] * 3,
            out_specs=vmem(),
            name="pack",
        )(w_in, w_out, b_in)
        line = [own] + [move(own, 0, by) for by in range(1, outer)]
    else:
        line = []
        w_all = lax.all_gather(w_in, "row", axis=0, tiled=True).reshape(-1, SLOT, c)
        o_all = lax.all_gather(w_out, "row", axis=0, tiled=True).reshape(-1, SLOT, c)
        b_all = lax.all_gather(b_in, "row", axis=0, tiled=True).reshape(-1, 1, SLOT)
        b_all = jnp.broadcast_to(jnp.tile(b_all, (1, 1, c // SLOT)), (w_all.shape[0], EXTRA, c))
        slots = [jnp.concatenate([w_all, o_all, b_all], axis=1)]

    got = lax.all_to_all(features, "row", split_axis=0, concat_axis=0, tiled=True)
    pad = (radial_taps.shape[0] + 1) // 4
    anywhere = pl.BlockSpec(memory_space=pl.ANY)
    pieces = len(line)
    slot_shape = (2 * SLOT + EXTRA, c)
    out_shape = [jax.ShapeDtypeStruct((n, a_loc, rows, c), jnp.bfloat16)]
    scratch = [pltpu.VMEM((n + 2 * pad, a_loc, rows, c), jnp.float32)] * 2
    if spread:
        out_shape.append(jax.ShapeDtypeStruct((pieces,) + slot_shape, jnp.bfloat16))
        scratch.append(pltpu.SemaphoreType.DMA((pieces,)))
    mixed, *joined = pl.pallas_call(
        partial(radial_kernel, pieces),
        out_shape=out_shape,
        in_specs=[vmem()] * 2 + [anywhere] * pieces,
        out_specs=[vmem()] + [anywhere] * (len(out_shape) - 1),
        scratch_shapes=scratch,
        compiler_params=params,
        name="radial",
    )(got.reshape(n, a_loc, r_loc, theta, c), radial_taps, *line)
    if spread:
        across = [move(h, 1, by) for by in range(1, inner) for h in joined]
        twin = [move(h, 2) for h in joined]
    back = lax.all_to_all(mixed.reshape(axial, rows, c), "row", split_axis=0, concat_axis=0, tiled=True)
    if spread:
        across, back = lax.optimization_barrier((across, back))
        slots = joined + across + twin + [move(h, 2) for h in across]
    normed = pl.pallas_call(
        axial_kernel,
        out_shape=jax.ShapeDtypeStruct((axial * rows, c), jnp.bfloat16),
        in_specs=[vmem()] * 5,
        out_specs=vmem(),
        scratch_shapes=[pltpu.VMEM((axial + axial_taps.shape[0] - 1, rows, c), jnp.float32)],
        compiler_params=params,
        name="axial",
    )(back, axial_taps, conv_bias[None, :], ln_gain[None, :], ln_bias[None, :])
    count = sum(h.shape[0] for h in slots)
    return pl.pallas_call(
        mlp_kernel,
        out_shape=jax.ShapeDtypeStruct(features.shape, jnp.bfloat16),
        in_specs=[vmem()] * 4 + [anywhere] * len(slots),
        out_specs=vmem(),
        scratch_shapes=[
            pltpu.VMEM((count,) + slot_shape, jnp.bfloat16),
            pltpu.VMEM((axial, rows, c), jnp.float32),
            pltpu.SemaphoreType.DMA((len(slots),)),
        ],
        compiler_params=params,
        name="mlp",
    )(normed, features, b_out[None, :], layer_scale[None, :], *slots)


def solution(mesh):
    in_specs = (
        P("groups", "row", None, None),
        P(),
        P(),
        P(),
        P(),
        P(),
        P("row", None),
        P("row"),
        P("row", None),
        P(),
        P(),
    )
    out_specs = P("groups", "row", None, None)
    return jax.shard_map(partial(local, mesh.shape["row"]), mesh=mesh, in_specs=in_specs, out_specs=out_specs, check_vma=False)
```

time: 51.6 us -> 42.5 us (0.82)
  blocking collectives: 12.1 us -> 0 us
  starting transfers between devices: 12.1 us -> 17.7 us
  waiting for transfers between devices: 18 us -> 14.5 us
  Pallas kernels: 5.46 us -> 7.51 us
  other arithmetic: 0.92 us -> 0 us
    all_to_all x1 -> x0, blocking collectives: 12.1 us -> none  [local(): lax.all_to_all(features, 'row', split_axis=0, concat_axis=0, tiled=True)]
    all_to_all x1 -> x2, starting transfers between devices: 3.51 us -> 11 us  [the longest x1 7.39 us: local(): lax.all_to_all(features, 'row', split_axis=0, concat_axis=0, tiled=True)]
    ppermute x5 -> x6, waiting for transfers between devices: 10.1 us -> 6.87 us  [move(): return lax.ppermute(piece, 'row', shifted(n, digit, by))]
    pallas_call x2 -> x3, Pallas kernels: 3.19 us -> 5.85 us  [the longest x1 2.36 us: local(): pl.pallas_call(partial(radial_kernel, pieces), out_shape=out_shape, in_sp...]
    ppermute x5 -> x6, starting transfers between devices: 8.62 us -> 6.67 us  [move(): return lax.ppermute(piece, 'row', shifted(n, digit, by))]
    another operation x2 -> x0, local copies, waits for them, and re-layouts: 1.33 us -> none  [local(): jnp.tile(b_in, c // SLOT)[None, :]]
    unnamed x20 -> x18, local copies, waits for them, and re-layouts: 1.01 us -> 2.2 us
    concatenate x1 -> x0, other arithmetic: 0.92 us -> none  [gather_slots(): held = jnp.concatenate(parts, axis=0)]
  transfers between devices with their start and end apart: 6 -> 8, of which waited for: 5 -> 3; matrix products, arithmetic and copies ran while one was open for 2% -> 0% of each run, Pallas kernels for 3% -> 8%
where the time goes in v3:
time: 42.5 us; the launch traced here: 42 us
  starting transfers between devices  17.7 us (42%)
  waiting for transfers between devices  14.5 us (34%)
  Pallas kernels  7.51 us (18%)
  local copies, waits for them, and re-layouts  2.2 us (5%)
    all_to_all x1, waiting for transfers between devices, local(): lax.all_to_all(mixed.reshape(axial, rows, c), 'row', split_axis=0, concat...  7.61 us
    all_to_all x1, starting transfers between devices, local(): lax.all_to_all(features, 'row', split_axis=0, concat_axis=0, tiled=True)  7.39 us
    ppermute x6, waiting for transfers between devices, move(): return lax.ppermute(piece, 'row', shifted(n, digit, by))  6.87 us
    ppermute x6, starting transfers between devices, move(): return lax.ppermute(piece, 'row', shifted(n, digit, by))  6.67 us
    all_to_all x1, starting transfers between devices, local(): lax.all_to_all(mixed.reshape(axial, rows, c), 'row', split_axis=0, concat...  3.64 us
    pallas_call x1, Pallas kernels, local(): pl.pallas_call(partial(radial_kernel, pieces), out_shape=out_shape, in_sp...  2.36 us
    unnamed x18, local copies, waits for them, and re-layouts  2.2 us
    pallas_call x1, Pallas kernels, local(): pl.pallas_call(axial_kernel, out_shape=jax.ShapeDtypeStruct((axial * rows...  2 us
  transfers between devices with their start and end apart: 8, of which 3 were waited for; matrix products, arithmetic and copies ran while one was open for 0% of the time, Pallas kernels for 8%

profile of v3, /device:TPU:0, one launch (start us, length us, event | category | flops | bytes accessed | tf_op | source)
XLA Modules:
  0.0 42.0 jit_solution(433923338830264460)
XLA Ops:
  0.0 7.4 %all-to-all-start = ((bf16[32,2,4,256]{3,2,1,0:T(4,128)(2,1)}), bf16[32,2,4,256]{3,2,1,0:T(4,128)(2,1)S(1)}, u32[]{:S(2)}, u32[]{:S(2)}) async-start(bf16[32,2,4,256]{3,2,1,0:T(4,128)(2,1)} %feat_ref.1), calls=%async_computation | async-start | bytes 262144 | tf_op jit(solution)/shard_map/all_to_all | solution.py:185
  7.4 0.0 copy-start.2
  7.4 1.5 %pack.1.rest_0_ = bf16[1,144,256]{2,1,0:T(8,128)(2,1)} custom-call(bf16[64,256]{1,0:T(8,128)(2,1)} %w_in_ref.1, bf16[64,256]{1,0:T(8,128)(2,1)} %w_out_ref.1, bf16[64]{0:T(256)(128)(2,1)} %b_ref.1), custom_call_target="tpu_custom_call" | custom-call | tf_op jit(solution)/shard_map/pack/pallas_call | solution.py:169
  8.9 3.7 %collective-permute-start.2 = (bf16[1,144,256]{2,1,0:T(8,128)(2,1)}, bf16[1,144,256]{2,1,0:T(8,128)(2,1)S(1)}, u32[]{:S(2)}, u32[]{:S(2)}) collective-permute-start(bf16[1,144,256]{2,1,0:T(8,128)(2,1)} %pack.1.rest_0_), channel_id=1, source_target_pairs={{0,12},{1,13},{2,14},{3,15},{4,0},{5,1},{6,2},{7,3},{8,4},{9,5},{1... | collective-permute-start | bytes 221192 | tf_op jit(solution)/shard_map/ppermute | solution.py:165
  12.6 0.0 collective-permute-start.1
  12.6 1.1 %collective-permute-start = (bf16[1,144,256]{2,1,0:T(8,128)(2,1)}, bf16[1,144,256]{2,1,0:T(8,128)(2,1)S(1)}, u32[]{:S(2)}, u32[]{:S(2)}) collective-permute-start(bf16[1,144,256]{2,1,0:T(8,128)(2,1)} %pack.1.rest_0_), channel_id=1, source_target_pairs={{0,4},{1,5},{2,6},{3,7},{4,8},{5,9},{6,10},{7,11},{8,12},{9,13},{1... | collective-permute-start | bytes 221192 | tf_op jit(solution)/shard_map/ppermute | solution.py:165
  13.7 1.9 %collective-permute-done.2.rest_3_ = bf16[1,144,256]{2,1,0:T(8,128)(2,1)S(1)} collective-permute-done((bf16[1,144,256]{2,1,0:T(8,128)(2,1)}, bf16[1,144,256]{2,1,0:T(8,128)(2,1)S(1)}, u32[]{:S(2)}, u32[]{:S(2)}) %collective-permute-start.2) | collective-permute-done | bytes 73760 | tf_op jit(solution)/shard_map/ppermute | solution.py:165
  15.6 5.0 %collective-permute-done.1.rest_2_ = bf16[1,144,256]{2,1,0:T(8,128)(2,1)S(1)} collective-permute-done((bf16[1,144,256]{2,1,0:T(8,128)(2,1)}, bf16[1,144,256]{2,1,0:T(8,128)(2,1)S(1)}, u32[]{:S(2)}, u32[]{:S(2)}) %collective-permute-start.1) | collective-permute-done | bytes 73760 | tf_op jit(solution)/shard_map/ppermute | solution.py:165
  20.6 0.0 collective-permute-done.rest_1_
  20.6 0.0 all-to-all-done
  20.6 0.0 copy-done.2
  20.6 0.0 copy-start.1
  20.6 0.9 %copy-done.1 = bf16[1,144,256]{2,1,0:T(8,128)(2,1)S(1)} copy-done((bf16[1,144,256]{2,1,0:T(8,128)(2,1)S(1)}, bf16[1,144,256]{2,1,0:T(8,128)(2,1)}, u32[]{:S(2)}) %copy-start.1) | copy-done | bytes 73752
  21.5 2.4 %radial.1 = (bf16[16,2,8,256]{3,2,1,0:T(8,128)(2,1)}, bf16[4,144,256]{2,1,0:T(8,128)(2,1)S(1)}) custom-call(bf16[16,2,2,4,256]{4,3,2,1,0:T(4,128)(2,1)S(1)} %bitcast.7, f32[31,256]{1,0:T(8,128)S(1)} %copy-done.2, bf16[1,144,256]{2,1,0:T(8,128)(2,1)S(1)} %copy-done.1, bf16[1,144,256]{2,1,0:T(8,128)(2,1)S(1)} %collective-permute-done.rest_1_, ...), custom_call_target="tpu_custom_call" | custom-call | tf_op jit(solution)/shard_map/radial/pallas_call | solution.py:195
  23.9 1.5 %collective-permute-start.3 = (bf16[4,144,256]{2,1,0:T(8,128)(2,1)S(1)}, bf16[4,144,256]{2,1,0:T(8,128)(2,1)S(1)}, u32[]{:S(2)}, u32[]{:S(2)}) collective-permute-start(bf16[4,144,256]{2,1,0:T(8,128)(2,1)S(1)} %get-tuple-element.9.rest_0_), channel_id=1, source_target_pairs={{0,2},{1,3},{2,0},{3,1},{4,6},{5,7},{6,4},{7,5},{8,10},{9,11},{10,... | collective-permute-start | bytes 884744 | tf_op jit(solution)/shard_map/ppermute | solution.py:165
  25.4 3.6 %all-to-all-start.1 = ((bf16[32,8,256]{2,1,0:T(8,128)(2,1)}), bf16[32,8,256]{2,1,0:T(8,128)(2,1)S(1)}, u32[]{:S(2)}, u32[]{:S(2)}) async-start(bf16[32,8,256]{2,1,0:T(8,128)(2,1)} %bitcast.1), calls=%async_computation.1 | async-start | bytes 262144 | tf_op jit(solution)/shard_map/all_to_all | solution.py:207
  29.1 0.3 collective-permute-start.4
  29.4 7.6 %all-to-all-done.1.z_ref = bf16[32,8,256]{2,1,0:T(8,128)(2,1)S(1)} async-done(((bf16[32,8,256]{2,1,0:T(8,128)(2,1)}), bf16[32,8,256]{2,1,0:T(8,128)(2,1)S(1)}, u32[]{:S(2)}, u32[]{:S(2)}) %all-to-all-start.1) | async-done | bytes 131104 | tf_op jit(solution)/shard_map/all_to_all | solution.py:207
  37.0 0.0 collective-permute-done.3.rest_1_
  37.0 0.0 collective-permute-start.5
  37.0 0.0 copy-done.3
  37.0 0.0 copy-done.5
  37.0 0.0 copy-done.6
  37.0 0.6 %copy-done.4 = f32[256]{0:T(256)S(1)} copy-done((f32[256]{0:T(256)S(1)}, f32[256]{0:T(256)}, u32[]{:S(2)}) %copy-start.4) | copy-done | bytes 1048
  37.7 2.0 %axial.1.normed_ref = bf16[256,256]{1,0:T(8,128)(2,1)S(1)} custom-call(bf16[32,8,256]{2,1,0:T(8,128)(2,1)S(1)} %all-to-all-done.1.z_ref, f32[31,256]{1,0:T(8,128)S(1)} %copy-done.3, f32[1,256]{1,0:T(1,128)S(1)} %bitcast.8, f32[1,256]{1,0:T(1,128)S(1)} %bitcast.9, f32[1,256]{1,0:T(1,128)S(1)} %bitcast.10), custom_call_target="tpu_custom_call" | custom-call | tf_op jit(solution)/shard_map/axial/pallas_call | solution.py:211
  39.7 0.0 collective-permute-done.4.rest_2_
  39.7 0.0 collective-permute-done.5.rest_3_
  39.7 0.0 copy-start.7
  39.7 0.0 copy-done
  39.7 0.0 copy-done.8
  39.7 0.7 %copy-done.7 = f32[256]{0:T(256)S(1)} copy-done((f32[256]{0:T(256)S(1)}, f32[256]{0:T(256)}, u32[]{:S(2)}) %copy-start.7) | copy-done | bytes 1048
  40.4 1.7 %mlp.1 = bf16[32,2,4,256]{3,2,1,0:T(4,128)(2,1)} custom-call(bf16[256,256]{1,0:T(8,128)(2,1)S(1)} %axial.1.normed_ref, bf16[32,2,4,256]{3,2,1,0:T(4,128)(2,1)S(1)} %copy-done, f32[1,256]{1,0:T(1,128)S(1)} %bitcast.11, f32[1,256]{1,0:T(1,128)S(1)} %bitcast.12, bf16[4,144,256]{2,1,0:T(8,128)(2,1)S(1)} %get-tuple-element.9.rest_0_, ...), custom_call_target="tpu_custom_call" | custom-call | tf_op jit(solution)/shard_map/mlp/pallas_call | solution.py:221
  (6 shorter events, 0.0 us)
Async XLA Ops:
  0.0 20.6 %all-to-all-start = ((bf16[32,2,4,256]{3,2,1,0:T(4,128)(2,1)}), bf16[32,2,4,256]{3,2,1,0:T(4,128)(2,1)S(1)}, u32[]{:S(2)}, u32[]{:S(2)}) async-start(bf16[32,2,4,256]{3,2,1,0:T(4,128)(2,1)} %feat_ref.1), calls=%async_computation | async-start | bytes 262144 | tf_op jit(solution)/shard_map/all_to_all | solution.py:185
  7.4 13.2 %copy-start.2 = (f32[31,256]{1,0:T(8,128)S(1)}, f32[31,256]{1,0:T(8,128)}, u32[]{:S(2)}) copy-start(f32[31,256]{1,0:T(8,128)} %taps_ref.2) | copy-start | bytes 95236
  8.9 6.7 %collective-permute-start.2 = (bf16[1,144,256]{2,1,0:T(8,128)(2,1)}, bf16[1,144,256]{2,1,0:T(8,128)(2,1)S(1)}, u32[]{:S(2)}, u32[]{:S(2)}) collective-permute-start(bf16[1,144,256]{2,1,0:T(8,128)(2,1)} %pack.1.rest_0_), channel_id=1, source_target_pairs={{0,12},{1,13},{2,14},{3,15},{4,0},{5,1},{6,2},{7,3},{8,4},{9,5},{1... | collective-permute-start | bytes 221192 | tf_op jit(solution)/shard_map/ppermute | solution.py:165
  12.6 8.0 %collective-permute-start.1 = (bf16[1,144,256]{2,1,0:T(8,128)(2,1)}, bf16[1,144,256]{2,1,0:T(8,128)(2,1)S(1)}, u32[]{:S(2)}, u32[]{:S(2)}) collective-permute-start(bf16[1,144,256]{2,1,0:T(8,128)(2,1)} %pack.1.rest_0_), channel_id=1, source_target_pairs={{0,8},{1,9},{2,10},{3,11},{4,12},{5,13},{6,14},{7,15},{8,0},{9,1},... | collective-permute-start | bytes 221192 | tf_op jit(solution)/shard_map/ppermute | solution.py:165
  12.6 8.0 %collective-permute-start = (bf16[1,144,256]{2,1,0:T(8,128)(2,1)}, bf16[1,144,256]{2,1,0:T(8,128)(2,1)S(1)}, u32[]{:S(2)}, u32[]{:S(2)}) collective-permute-start(bf16[1,144,256]{2,1,0:T(8,128)(2,1)} %pack.1.rest_0_), channel_id=1, source_target_pairs={{0,4},{1,5},{2,6},{3,7},{4,8},{5,9},{6,10},{7,11},{8,12},{9,13},{1... | collective-permute-start | bytes 221192 | tf_op jit(solution)/shard_map/ppermute | solution.py:165
  20.6 0.9 %copy-start.1 = (bf16[1,144,256]{2,1,0:T(8,128)(2,1)S(1)}, bf16[1,144,256]{2,1,0:T(8,128)(2,1)}, u32[]{:S(2)}) copy-start(bf16[1,144,256]{2,1,0:T(8,128)(2,1)} %pack.1.rest_0_) | copy-start | bytes 221188
  23.9 13.1 %collective-permute-start.3 = (bf16[4,144,256]{2,1,0:T(8,128)(2,1)S(1)}, bf16[4,144,256]{2,1,0:T(8,128)(2,1)S(1)}, u32[]{:S(2)}, u32[]{:S(2)}) collective-permute-start(bf16[4,144,256]{2,1,0:T(8,128)(2,1)S(1)} %get-tuple-element.9.rest_0_), channel_id=1, source_target_pairs={{0,2},{1,3},{2,0},{3,1},{4,6},{5,7},{6,4},{7,5},{8,10},{9,11},{10,... | collective-permute-start | bytes 884744 | tf_op jit(solution)/shard_map/ppermute | solution.py:165
  25.4 11.6 %copy-start.3 = (f32[31,256]{1,0:T(8,128)S(1)}, f32[31,256]{1,0:T(8,128)}, u32[]{:S(2)}) copy-start(f32[31,256]{1,0:T(8,128)} %taps_ref.3) | copy-start | bytes 95236
  25.4 11.6 %copy-start.5 = (f32[256]{0:T(256)S(1)}, f32[256]{0:T(256)}, u32[]{:S(2)}) copy-start(f32[256]{0:T(256)} %param.15) | copy-start | bytes 3076
  25.4 11.6 %copy-start.6 = (f32[256]{0:T(256)S(1)}, f32[256]{0:T(256)}, u32[]{:S(2)}) copy-start(f32[256]{0:T(256)} %param.16) | copy-start | bytes 3076
  25.4 11.6 %all-to-all-start.1 = ((bf16[32,8,256]{2,1,0:T(8,128)(2,1)}), bf16[32,8,256]{2,1,0:T(8,128)(2,1)S(1)}, u32[]{:S(2)}, u32[]{:S(2)}) async-start(bf16[32,8,256]{2,1,0:T(8,128)(2,1)} %bitcast.1), calls=%async_computation.1 | async-start | bytes 262144 | tf_op jit(solution)/shard_map/all_to_all | solution.py:207
  29.1 10.6 %collective-permute-start.4 = (bf16[4,144,256]{2,1,0:T(8,128)(2,1)S(1)}, bf16[4,144,256]{2,1,0:T(8,128)(2,1)S(1)}, u32[]{:S(2)}, u32[]{:S(2)}) collective-permute-start(bf16[4,144,256]{2,1,0:T(8,128)(2,1)S(1)} %get-tuple-element.9.rest_0_), channel_id=1, source_target_pairs={{0,1},{1,0},{2,3},{3,2},{4,5},{5,4},{6,7},{7,6},{8,9},{9,8},{10,11... | collective-permute-start | bytes 884744 | tf_op jit(solution)/shard_map/ppermute | solution.py:165
  37.0 2.7 %collective-permute-start.5 = (bf16[4,144,256]{2,1,0:T(8,128)(2,1)S(1)}, bf16[4,144,256]{2,1,0:T(8,128)(2,1)S(1)}, u32[]{:S(2)}, u32[]{:S(2)}) collective-permute-start(bf16[4,144,256]{2,1,0:T(8,128)(2,1)S(1)} %collective-permute-done.3.rest_1_), channel_id=1, source_target_pairs={{0,1},{1,0},{2,3},{3,2},{4,5},{5,4},{6,7},{7,6},{8,9},{9,8},{10,11... | collective-permute-start | bytes 884744 | tf_op jit(solution)/shard_map/ppermute | solution.py:165
  37.0 0.7 %copy-start.4 = (f32[256]{0:T(256)S(1)}, f32[256]{0:T(256)}, u32[]{:S(2)}) copy-start(f32[256]{0:T(256)} %param.14) | copy-start | bytes 3076
  37.6 2.0 %copy-start = (bf16[32,2,4,256]{3,2,1,0:T(4,128)(2,1)S(1)}, bf16[32,2,4,256]{3,2,1,0:T(4,128)(2,1)}, u32[]{:S(2)}) copy-start(bf16[32,2,4,256]{3,2,1,0:T(4,128)(2,1)} %feat_ref.1) | copy-start | bytes 393220
  37.7 2.1 %copy-start.8 = (f32[256]{0:T(256)S(1)}, f32[256]{0:T(256)}, u32[]{:S(2)}) copy-start(f32[256]{0:T(256)} %param.21) | copy-start | bytes 3076
  39.7 0.7 %copy-start.7 = (f32[256]{0:T(256)S(1)}, f32[256]{0:T(256)}, u32[]{:S(2)}) copy-start(f32[256]{0:T(256)} %param.20) | copy-start | bytes 3076

commit v4 on v3

v4 whole, which is shorter than its diff:
```python
from functools import partial

import jax
import jax.numpy as jnp
from jax import lax
from jax.experimental import pallas as pl
from jax.experimental.pallas import tpu as pltpu
from jax.sharding import PartitionSpec as P

SLOT = 64
EXTRA = 16


def vmem():
    return pl.BlockSpec(memory_space=pltpu.VMEM)


def pack_kernel(b_ref, w_in_ref, w_out_ref, taps_ref, *rest):
    vectors = rest[:5]
    slot_ref, taps_out, consts_out, staged, sems = rest[5:]
    copies = [
        pltpu.make_async_copy(w_in_ref, slot_ref.at[0, 0:SLOT], sems.at[0]),
        pltpu.make_async_copy(w_out_ref, slot_ref.at[0, SLOT : 2 * SLOT], sems.at[1]),
        pltpu.make_async_copy(taps_ref, taps_out, sems.at[2]),
    ]
    for i, vector in enumerate(vectors):
        copies.append(pltpu.make_async_copy(vector, staged.at[i], sems.at[3 + i]))
    for copy in copies:
        copy.start()
    bias = b_ref[...].astype(jnp.float32)[None, :]
    c = slot_ref.shape[2]
    wide = jnp.concatenate([bias] * (c // SLOT), axis=1)
    slot_ref[0, 2 * SLOT : 2 * SLOT + EXTRA, :] = jnp.broadcast_to(wide, (EXTRA, c)).astype(slot_ref.dtype)
    for copy in copies:
        copy.wait()
    for i in range(5):
        consts_out[i : i + 1, :] = staged[i]


def radial_kernel(x_ref, taps_ref, out_ref, even, odd):
    n, a_loc, _, theta, c = x_ref.shape
    taps = taps_ref.shape[0]
    pad = (taps + 1) // 4
    zeros = jnp.zeros((pad, a_loc, 2 * theta, c), jnp.float32)
    even[0:pad] = zeros
    even[pad + n : 2 * pad + n] = zeros
    odd[0:pad] = zeros
    odd[pad + n - 1 : 2 * pad + n - 1] = zeros
    odd[2 * pad + n - 1 :] = zeros[:1]
    first = x_ref[:, :, 0].astype(jnp.float32)
    second = x_ref[:, :, 1].astype(jnp.float32)
    even[pad : pad + n, :, 0:theta] = first
    even[pad : pad + n, :, theta:] = second
    odd[pad : pad + n, :, 0:theta] = second
    odd[pad - 1 : pad + n - 1, :, theta:] = first

    def step(s, carry):
        total = jnp.zeros((a_loc, 2 * theta, c), jnp.float32)
        for k in range(taps):
            shift = k - taps // 2
            source = even if shift % 2 == 0 else odd
            total = total + source[s + (pad + shift // 2)] * taps_ref[k : k + 1, :]
        out_ref[s] = total.astype(out_ref.dtype)
        return carry

    lax.fori_loop(0, n, step, 0)


def join_kernel(pieces, *refs):
    out_ref, sems = refs[pieces + 1 :]
    copies = [pltpu.make_async_copy(refs[i], out_ref.at[i : i + 1], sems.at[i]) for i in range(pieces)]
    for copy in copies:
        copy.start()
    for copy in copies:
        copy.wait()


def axial_kernel(z_ref, taps_ref, consts_ref, out_ref, padded, summed):
    axial, rows, c = z_ref.shape
    taps = taps_ref.shape[0]
    half = taps // 2
    zeros = jnp.zeros((half, rows, c), jnp.float32)
    padded[0:half] = zeros
    padded[half + axial :] = zeros
    padded[half : half + axial] = z_ref[...].astype(jnp.float32)
    block = 4

    def conv(i, carry):
        base = i * block
        total = jnp.zeros((block, rows, c), jnp.float32)
        for k in range(taps):
            total = total + padded[pl.ds(base + k, block)] * taps_ref[k : k + 1, :]
        summed[pl.ds(base, block)] = total
        return carry

    lax.fori_loop(0, axial // block, conv, 0)

    def norm(i, carry):
        v = (summed[pl.ds(i * 32, 32)] + consts_ref[0:1, :]).reshape(32 * rows, c)
        v = v.astype(jnp.bfloat16).astype(jnp.float32)
        mean = jnp.mean(v, axis=-1, keepdims=True)
        centred = v - mean
        var = jnp.mean(centred * centred, axis=-1, keepdims=True)
        normed = centred * lax.rsqrt(var + 1e-06) * consts_ref[1:2, :] + consts_ref[2:3, :]
        at = pl.multiple_of(i * 32 * rows, 32 * rows)
        out_ref[pl.ds(at, 32 * rows), :] = normed.astype(out_ref.dtype)
        return carry

    lax.fori_loop(0, axial // 32, norm, 0)


def mlp_kernel(normed_ref, feat_ref, consts_ref, *rest):
    *w_refs, out_ref, slots, branch, sems = rest
    axial, _, theta, c = feat_ref.shape
    rows = 2 * theta
    per = c // SLOT
    lane_slot = lax.broadcasted_iota(jnp.int32, (1, c), 1) // SLOT
    token_block = 32 * rows
    copies, begins = [], []
    for i, w_ref in enumerate(w_refs):
        begins.append(sum(w.shape[0] for w in w_refs[:i]))
        copies.append(pltpu.make_async_copy(w_ref, slots.at[begins[i] : begins[i] + w_ref.shape[0]], sems.at[i]))
    for copy in copies:
        copy.start()
    single = axial == 32
    if not single:
        for copy in copies:
            copy.wait()

    def mlp(i, carry):
        base = pl.multiple_of(i * token_block, token_block)
        normed = normed_ref[pl.ds(base, token_block), :]
        total = jnp.zeros((token_block, c), jnp.float32)
        for g in range(slots.shape[0] // per):
            own = slice(g * per, (g + 1) * per)
            for at, copy in zip(begins, copies):
                if single and own.start <= at < own.stop:
                    copy.wait()
            w_in = slots[own, 0:SLOT, :].reshape(per * SLOT, c)
            w_out = slots[own, SLOT : 2 * SLOT, :].reshape(per * SLOT, c)
            bias = jnp.zeros((1, c), jnp.float32)
            for j in range(per):
                piece = slots[g * per + j, 2 * SLOT : 2 * SLOT + EXTRA, :].astype(jnp.float32)[0:1]
                bias = jnp.where(lane_slot == j, piece, bias)
            u = lax.dot_general(normed, w_in, (((1,), (1,)), ((), ())), preferred_element_type=jnp.float32)
            u = u + bias
            hidden = (0.5 * u * (1.0 + jnp.tanh(0.7978845608028654 * (u + 0.044715 * u * u * u)))).astype(jnp.bfloat16)
            total = total + jnp.dot(hidden, w_out, preferred_element_type=jnp.float32)
        result = (consts_ref[4:5, :] * (total + consts_ref[3:4, :])).astype(jnp.bfloat16).astype(jnp.float32)
        branch[pl.ds(i * 32, 32)] = result.reshape(32, rows, c)
        return carry

    if single:
        mlp(0, 0)
    else:
        lax.fori_loop(0, axial // 32, mlp, 0)
    for r in range(2):
        got = branch[:, r * theta : (r + 1) * theta, :]
        out_ref[:, r] = (feat_ref[:, r].astype(jnp.float32) + got).astype(out_ref.dtype)


def digits(n):
    chips = n // 2
    inner = 1
    while inner * inner * 4 <= chips:
        inner *= 2
    return chips // inner, inner, 2


def shifted(n, digit, by):
    sizes = digits(n)
    stride = [sizes[1] * sizes[2], sizes[2], 1][digit]
    pairs = []
    for i in range(n):
        at = (i // stride) % sizes[digit]
        to = (at + by) % sizes[digit]
        pairs.append((i, i + (to - at) * stride))
    return pairs


def local(n, features, axial_taps, radial_taps, conv_bias, ln_gain, ln_bias, w_in, b_in, w_out, b_out, layer_scale):
    axial, r_loc, theta, c = features.shape
    rows = r_loc * theta
    hid_loc = w_in.shape[0]
    a_loc = axial // n
    spread = hid_loc == SLOT
    params = pltpu.CompilerParams(vmem_limit_bytes=48 * 1024 * 1024)

    def move(piece, digit, by=1):
        return lax.ppermute(piece, "row", shifted(n, digit, by))

    outer, inner, _ = digits(n)
    anywhere = pl.BlockSpec(memory_space=pl.ANY)
    vectors = [v[None, :] for v in (conv_bias, ln_gain, ln_bias, b_out, layer_scale)]
    slot_shape = (2 * SLOT + EXTRA, c)
    if spread:
        own, axial_taps, consts = pl.pallas_call(
            pack_kernel,
            out_shape=[
                jax.ShapeDtypeStruct((1,) + slot_shape, jnp.bfloat16),
                jax.ShapeDtypeStruct(axial_taps.shape, jnp.float32),
                jax.ShapeDtypeStruct((8, c), jnp.float32),
            ],
            in_specs=[vmem()] + [anywhere] * 8,
            out_specs=[vmem()] * 3,
            scratch_shapes=[pltpu.VMEM((5, 1, c), jnp.float32), pltpu.SemaphoreType.DMA((8,))],
            name="pack",
        )(b_in, w_in, w_out, axial_taps, *vectors)
        line = [own] + [move(own, 0, by) for by in range(1, outer)]
    else:
        consts = jnp.concatenate(vectors + [jnp.zeros((3, c), jnp.float32)], axis=0)
        w_all = lax.all_gather(w_in, "row", axis=0, tiled=True).reshape(-1, SLOT, c)
        o_all = lax.all_gather(w_out, "row", axis=0, tiled=True).reshape(-1, SLOT, c)
        b_all = lax.all_gather(b_in, "row", axis=0, tiled=True).reshape(-1, 1, SLOT)
        b_all = jnp.broadcast_to(jnp.tile(b_all, (1, 1, c // SLOT)), (w_all.shape[0], EXTRA, c))
        slots = [jnp.concatenate([w_all, o_all, b_all], axis=1)]

    got = lax.all_to_all(features, "row", split_axis=0, concat_axis=0, tiled=True)
    pad = (radial_taps.shape[0] + 1) // 4
    mixed = pl.pallas_call(
        radial_kernel,
        out_shape=jax.ShapeDtypeStruct((n, a_loc, rows, c), jnp.bfloat16),
        in_specs=[vmem()] * 2,
        out_specs=vmem(),
        scratch_shapes=[pltpu.VMEM((n + 2 * pad, a_loc, rows, c), jnp.float32)] * 2,
        compiler_params=params,
        name="radial",
    )(got.reshape(n, a_loc, r_loc, theta, c), radial_taps)
    if spread:
        joined = pl.pallas_call(
            partial(join_kernel, outer),
            out_shape=jax.ShapeDtypeStruct((outer,) + slot_shape, jnp.bfloat16),
            in_specs=[anywhere] * (outer + 1),
            out_specs=vmem(),
            scratch_shapes=[pltpu.SemaphoreType.DMA((outer,))],
            name="join",
        )(*line, mixed)
        across = [move(joined, 1, by) for by in range(1, inner)]
        twin = [move(joined, 2)]
    back = lax.all_to_all(mixed.reshape(axial, rows, c), "row", split_axis=0, concat_axis=0, tiled=True)
    if spread:
        across, back = lax.optimization_barrier((across, back))
        slots = [joined] + across + twin + [move(h, 2) for h in across]
    normed = pl.pallas_call(
        axial_kernel,
        out_shape=jax.ShapeDtypeStruct((axial * rows, c), jnp.bfloat16),
        in_specs=[vmem()] * 3,
        out_specs=vmem(),
        scratch_shapes=[
            pltpu.VMEM((axial + axial_taps.shape[0] - 1, rows, c), jnp.float32),
            pltpu.VMEM((axial, rows, c), jnp.float32),
        ],
        compiler_params=params,
        name="axial",
    )(back, axial_taps, consts)
    count = sum(h.shape[0] for h in slots)
    return pl.pallas_call(
        mlp_kernel,
        out_shape=jax.ShapeDtypeStruct(features.shape, jnp.bfloat16),
        in_specs=[vmem()] * 3 + [anywhere] * len(slots),
        out_specs=vmem(),
        scratch_shapes=[
            pltpu.VMEM((count,) + slot_shape, jnp.bfloat16),
            pltpu.VMEM((axial, rows, c), jnp.float32),
            pltpu.SemaphoreType.DMA((len(slots),)),
        ],
        compiler_params=params,
        name="mlp",
    )(normed, features, consts, *slots)


def solution(mesh):
    in_specs = (
        P("groups", "row", None, None),
        P(),
        P(),
        P(),
        P(),
        P(),
        P("row", None),
        P("row"),
        P("row", None),
        P(),
        P(),
    )
    out_specs = P("groups", "row", None, None)
    return jax.shard_map(partial(local, mesh.shape["row"]), mesh=mesh, in_specs=in_specs, out_specs=out_specs, check_vma=False)
```

time: 42.5 us -> 41.3 us (0.972)
  waiting for transfers between devices: 14.5 us -> 12.9 us
  Pallas kernels: 7.51 us -> 9 us
  local copies, waits for them, and re-layouts: 2.2 us -> 1.26 us
    ppermute x6, waiting for transfers between devices: 6.87 us -> 4.48 us  [move(): return lax.ppermute(piece, 'row', shifted(n, digit, by))]
    pallas_call x2 -> x3, Pallas kernels: 3.85 us -> 5.7 us  [the longest x1 2.18 us: local(): pl.pallas_call(pack_kernel, out_shape=[jax.ShapeDtypeStruct((1,) + slot_s...]
    pallas_call x1, Pallas kernels: 2 us -> 0.99 us  [local(): pl.pallas_call(axial_kernel, out_shape=jax.ShapeDtypeStruct((axial * rows...]
    unnamed x18 -> x16, local copies, waits for them, and re-layouts: 2.2 us -> 1.26 us
    all_to_all x1, waiting for transfers between devices: 0.01 us -> 0.84 us  [local(): lax.all_to_all(features, 'row', split_axis=0, concat_axis=0, tiled=True)]
    pallas_call x1, Pallas kernels: 1.66 us -> 2.3 us  [local(): pl.pallas_call(mlp_kernel, out_shape=jax.ShapeDtypeStruct(features.shape,...]
  transfers between devices with their start and end apart: 8 -> 8, of which waited for: 3 -> 4; matrix products, arithmetic and copies ran while one was open for 0% -> 0% of each run, Pallas kernels for 8% -> 12%
where the time goes in v4:
time: 41.3 us; the launch traced here: 40.9 us
  starting transfers between devices  17.6 us (43%)
  waiting for transfers between devices  12.9 us (31%)
  Pallas kernels  9 us (22%)
  local copies, waits for them, and re-layouts  1.26 us (3%)
    all_to_all x1, waiting for transfers between devices, local(): lax.all_to_all(mixed.reshape(axial, rows, c), 'row', split_axis=0, concat...  7.61 us
    all_to_all x1, starting transfers between devices, local(): lax.all_to_all(features, 'row', split_axis=0, concat_axis=0, tiled=True)  7.38 us
    ppermute x6, starting transfers between devices, move(): return lax.ppermute(piece, 'row', shifted(n, digit, by))  6.72 us
    ppermute x6, waiting for transfers between devices, move(): return lax.ppermute(piece, 'row', shifted(n, digit, by))  4.48 us
    all_to_all x1, starting transfers between devices, local(): lax.all_to_all(mixed.reshape(axial, rows, c), 'row', split_axis=0, concat...  3.51 us
    pallas_call x1, Pallas kernels, local(): pl.pallas_call(mlp_kernel, out_shape=jax.ShapeDtypeStruct(features.shape,...  2.3 us
    pallas_call x1, Pallas kernels, local(): pl.pallas_call(pack_kernel, out_shape=[jax.ShapeDtypeStruct((1,) + slot_s...  2.18 us
    pallas_call x1, Pallas kernels, local(): pl.pallas_call(radial_kernel, out_shape=jax.ShapeDtypeStruct((n, a_loc, r...  1.77 us
  transfers between devices with their start and end apart: 8, of which 4 were waited for; matrix products, arithmetic and copies ran while one was open for 0% of the time, Pallas kernels for 12%

profile of v4, /device:TPU:0, one launch (start us, length us, event | category | flops | bytes accessed | tf_op | source)
XLA Modules:
  0.0 40.9 jit_solution(3740548599381246509)
XLA Ops:
  0.0 7.4 %all-to-all-start = ((bf16[32,2,4,256]{3,2,1,0:T(4,128)(2,1)}), bf16[32,2,4,256]{3,2,1,0:T(4,128)(2,1)S(1)}, u32[]{:S(2)}, u32[]{:S(2)}) async-start(bf16[32,2,4,256]{3,2,1,0:T(4,128)(2,1)} %feat_ref.1), calls=%async_computation | async-start | bytes 262144 | tf_op jit(solution)/shard_map/all_to_all | solution.py:218
  7.4 0.0 copy-start.3
  7.4 2.2 %pack.1 = (bf16[1,144,256]{2,1,0:T(8,128)(2,1)}, f32[31,256]{1,0:T(8,128)}, f32[8,256]{1,0:T(8,128)}) custom-call(bf16[64]{0:T(256)(128)(2,1)} %b_ref.1, bf16[64,256]{1,0:T(8,128)(2,1)} %w_in_ref.1, bf16[64,256]{1,0:T(8,128)(2,1)} %w_out_ref.1, f32[31,256]{1,0:T(8,128)} %taps_ref.2, f32[1,256]{1,0:T(1,128)} %bitcast.8, f32[1,256]{1,0:T(1,128)} %bitcast.9, ...), custom_call_target="tpu_custom_call" | custom-call | tf_op jit(solution)/shard_map/pack/pallas_call | solution.py:197
  9.6 3.8 %collective-permute-start.2 = (bf16[1,144,256]{2,1,0:T(8,128)(2,1)}, bf16[1,144,256]{2,1,0:T(8,128)(2,1)S(1)}, u32[]{:S(2)}, u32[]{:S(2)}) collective-permute-start(bf16[1,144,256]{2,1,0:T(8,128)(2,1)} %get-tuple-element.10.refs_0_), channel_id=1, source_target_pairs={{0,12},{1,13},{2,14},{3,15},{4,0},{5,1},{6,2},{7,3},{8,4},{9,5},{1... | collective-permute-start | bytes 221192 | tf_op jit(solution)/shard_map/ppermute | solution.py:190
  13.4 0.0 collective-permute-start.1
  13.4 1.1 %collective-permute-start = (bf16[1,144,256]{2,1,0:T(8,128)(2,1)}, bf16[1,144,256]{2,1,0:T(8,128)(2,1)S(1)}, u32[]{:S(2)}, u32[]{:S(2)}) collective-permute-start(bf16[1,144,256]{2,1,0:T(8,128)(2,1)} %get-tuple-element.10.refs_0_), channel_id=1, source_target_pairs={{0,4},{1,5},{2,6},{3,7},{4,8},{5,9},{6,10},{7,11},{8,12},{9,13},{1... | collective-permute-start | bytes 221192 | tf_op jit(solution)/shard_map/ppermute | solution.py:190
  14.5 0.8 %all-to-all-done = bf16[32,2,4,256]{3,2,1,0:T(4,128)(2,1)S(1)} async-done(((bf16[32,2,4,256]{3,2,1,0:T(4,128)(2,1)}), bf16[32,2,4,256]{3,2,1,0:T(4,128)(2,1)S(1)}, u32[]{:S(2)}, u32[]{:S(2)}) %all-to-all-start) | async-done | bytes 131104 | tf_op jit(solution)/shard_map/all_to_all | solution.py:218
  15.3 0.0 copy-done.3
  15.3 1.8 %radial.1.refs_4_ = bf16[16,2,8,256]{3,2,1,0:T(8,128)(2,1)} custom-call(bf16[16,2,2,4,256]{4,3,2,1,0:T(4,128)(2,1)S(1)} %bitcast.7, f32[31,256]{1,0:T(8,128)S(1)} %copy-done.3), custom_call_target="tpu_custom_call" | custom-call | tf_op jit(solution)/shard_map/radial/pallas_call | solution.py:220
  17.1 0.0 collective-permute-done.2.refs_3_
  17.1 3.9 %collective-permute-done.1.refs_2_ = bf16[1,144,256]{2,1,0:T(8,128)(2,1)S(1)} collective-permute-done((bf16[1,144,256]{2,1,0:T(8,128)(2,1)}, bf16[1,144,256]{2,1,0:T(8,128)(2,1)S(1)}, u32[]{:S(2)}, u32[]{:S(2)}) %collective-permute-start.1) | collective-permute-done | bytes 73760 | tf_op jit(solution)/shard_map/ppermute | solution.py:190
  21.0 0.0 collective-permute-done.refs_1_
  21.0 0.0 copy-done.5
  21.0 0.6 %copy-done.6 = bf16[1,144,256]{2,1,0:T(8,128)(2,1)} copy-done((bf16[1,144,256]{2,1,0:T(8,128)(2,1)}, bf16[1,144,256]{2,1,0:T(8,128)(2,1)S(1)}, u32[]{:S(2)}) %copy-start.6) | copy-done | bytes 73752
  21.7 0.6 %copy-done.7 = bf16[1,144,256]{2,1,0:T(8,128)(2,1)} copy-done((bf16[1,144,256]{2,1,0:T(8,128)(2,1)}, bf16[1,144,256]{2,1,0:T(8,128)(2,1)S(1)}, u32[]{:S(2)}) %copy-start.7) | copy-done | bytes 73752
  22.3 1.8 %join.1.rest_0_ = bf16[4,144,256]{2,1,0:T(8,128)(2,1)} custom-call(bf16[1,144,256]{2,1,0:T(8,128)(2,1)} %get-tuple-element.10.refs_0_, bf16[1,144,256]{2,1,0:T(8,128)(2,1)} %copy-done.7, bf16[1,144,256]{2,1,0:T(8,128)(2,1)} %copy-done.6, bf16[1,144,256]{2,1,0:T(8,128)(2,1)} %copy-done.5, bf16[16,2,8,256]{3,2,1,0:T(8,128)(2,1)} %radial.1.refs_4_), custom_call_target="tpu_custom_call" | custom-call | tf_op jit(solution)/shard_map/join/pallas_call | solution.py:230
  24.0 0.0 copy-start
  24.1 1.5 %collective-permute-start.3 = (bf16[4,144,256]{2,1,0:T(8,128)(2,1)}, bf16[4,144,256]{2,1,0:T(8,128)(2,1)S(1)}, u32[]{:S(2)}, u32[]{:S(2)}) collective-permute-start(bf16[4,144,256]{2,1,0:T(8,128)(2,1)} %join.1.rest_0_), channel_id=1, source_target_pairs={{0,2},{1,3},{2,0},{3,1},{4,6},{5,7},{6,4},{7,5},{8,10},{9,11},{10,... | collective-permute-start | bytes 884744 | tf_op jit(solution)/shard_map/ppermute | solution.py:190
  25.6 3.5 %all-to-all-start.1 = ((bf16[32,8,256]{2,1,0:T(8,128)(2,1)}), bf16[32,8,256]{2,1,0:T(8,128)(2,1)S(1)}, u32[]{:S(2)}, u32[]{:S(2)}) async-start(bf16[32,8,256]{2,1,0:T(8,128)(2,1)} %bitcast.6), calls=%async_computation.1 | async-start | bytes 262144 | tf_op jit(solution)/shard_map/all_to_all | solution.py:240
  29.1 0.3 collective-permute-start.4
  29.4 7.6 %all-to-all-done.1.z_ref = bf16[32,8,256]{2,1,0:T(8,128)(2,1)S(1)} async-done(((bf16[32,8,256]{2,1,0:T(8,128)(2,1)}), bf16[32,8,256]{2,1,0:T(8,128)(2,1)S(1)}, u32[]{:S(2)}, u32[]{:S(2)}) %all-to-all-start.1) | async-done | bytes 131104 | tf_op jit(solution)/shard_map/all_to_all | solution.py:240
  37.0 0.0 collective-permute-done.3.rest_1_
  37.0 0.0 collective-permute-start.5
  37.0 0.0 copy-done.2
  37.0 0.0 copy-done.4
  37.0 0.0 copy-start.1
  37.0 1.0 %axial.1.normed_ref = bf16[256,256]{1,0:T(8,128)(2,1)S(1)} custom-call(bf16[32,8,256]{2,1,0:T(8,128)(2,1)S(1)} %all-to-all-done.1.z_ref, f32[31,256]{1,0:T(8,128)S(1)} %copy-done.4, f32[8,256]{1,0:T(8,128)S(1)} %copy-done.2), custom_call_target="tpu_custom_call" | custom-call | tf_op jit(solution)/shard_map/axial/pallas_call | solution.py:244
  38.0 0.0 collective-permute-done.4.rest_2_
  38.0 0.5 %collective-permute-done.5.rest_3_ = bf16[4,144,256]{2,1,0:T(8,128)(2,1)S(1)} collective-permute-done((bf16[4,144,256]{2,1,0:T(8,128)(2,1)S(1)}, bf16[4,144,256]{2,1,0:T(8,128)(2,1)S(1)}, u32[]{:S(2)}, u32[]{:S(2)}) %collective-permute-start.5) | collective-permute-done | bytes 294944 | tf_op jit(solution)/shard_map/ppermute | solution.py:190
  38.6 0.0 copy-done
  38.6 0.0 copy-done.1
  38.6 2.3 %mlp.1 = bf16[32,2,4,256]{3,2,1,0:T(4,128)(2,1)} custom-call(bf16[256,256]{1,0:T(8,128)(2,1)S(1)} %axial.1.normed_ref, bf16[32,2,4,256]{3,2,1,0:T(4,128)(2,1)S(1)} %copy-done.1, f32[8,256]{1,0:T(8,128)S(1)} %copy-done.2, bf16[4,144,256]{2,1,0:T(8,128)(2,1)S(1)} %copy-done, bf16[4,144,256]{2,1,0:T(8,128)(2,1)S(1)} %collective-permute-done.3.rest_1_, ...), custom_call_target="tpu_custom_call" | custom-call | tf_op jit(solution)/shard_map/mlp/pallas_call | solution.py:257
  (5 shorter events, 0.0 us)
Async XLA Ops:
  0.0 15.3 %all-to-all-start = ((bf16[32,2,4,256]{3,2,1,0:T(4,128)(2,1)}), bf16[32,2,4,256]{3,2,1,0:T(4,128)(2,1)S(1)}, u32[]{:S(2)}, u32[]{:S(2)}) async-start(bf16[32,2,4,256]{3,2,1,0:T(4,128)(2,1)} %feat_ref.1), calls=%async_computation | async-start | bytes 262144 | tf_op jit(solution)/shard_map/all_to_all | solution.py:218
  7.4 7.9 %copy-start.3 = (f32[31,256]{1,0:T(8,128)S(1)}, f32[31,256]{1,0:T(8,128)}, u32[]{:S(2)}) copy-start(f32[31,256]{1,0:T(8,128)} %taps_ref.3) | copy-start | bytes 95236
  9.6 7.5 %collective-permute-start.2 = (bf16[1,144,256]{2,1,0:T(8,128)(2,1)}, bf16[1,144,256]{2,1,0:T(8,128)(2,1)S(1)}, u32[]{:S(2)}, u32[]{:S(2)}) collective-permute-start(bf16[1,144,256]{2,1,0:T(8,128)(2,1)} %get-tuple-element.10.refs_0_), channel_id=1, source_target_pairs={{0,12},{1,13},{2,14},{3,15},{4,0},{5,1},{6,2},{7,3},{8,4},{9,5},{1... | collective-permute-start | bytes 221192 | tf_op jit(solution)/shard_map/ppermute | solution.py:190
  13.4 7.7 %collective-permute-start.1 = (bf16[1,144,256]{2,1,0:T(8,128)(2,1)}, bf16[1,144,256]{2,1,0:T(8,128)(2,1)S(1)}, u32[]{:S(2)}, u32[]{:S(2)}) collective-permute-start(bf16[1,144,256]{2,1,0:T(8,128)(2,1)} %get-tuple-element.10.refs_0_), channel_id=1, source_target_pairs={{0,8},{1,9},{2,10},{3,11},{4,12},{5,13},{6,14},{7,15},{8,0},{9,1},... | collective-permute-start | bytes 221192 | tf_op jit(solution)/shard_map/ppermute | solution.py:190
  13.4 7.7 %collective-permute-start = (bf16[1,144,256]{2,1,0:T(8,128)(2,1)}, bf16[1,144,256]{2,1,0:T(8,128)(2,1)S(1)}, u32[]{:S(2)}, u32[]{:S(2)}) collective-permute-start(bf16[1,144,256]{2,1,0:T(8,128)(2,1)} %get-tuple-element.10.refs_0_), channel_id=1, source_target_pairs={{0,4},{1,5},{2,6},{3,7},{4,8},{5,9},{6,10},{7,11},{8,12},{9,13},{1... | collective-permute-start | bytes 221192 | tf_op jit(solution)/shard_map/ppermute | solution.py:190
  17.1 3.9 %copy-start.5 = (bf16[1,144,256]{2,1,0:T(8,128)(2,1)}, bf16[1,144,256]{2,1,0:T(8,128)(2,1)S(1)}, u32[]{:S(2)}) copy-start(bf16[1,144,256]{2,1,0:T(8,128)(2,1)S(1)} %collective-permute-done.2.refs_3_) | copy-start | bytes 221188
  21.0 0.6 %copy-start.6 = (bf16[1,144,256]{2,1,0:T(8,128)(2,1)}, bf16[1,144,256]{2,1,0:T(8,128)(2,1)S(1)}, u32[]{:S(2)}) copy-start(bf16[1,144,256]{2,1,0:T(8,128)(2,1)S(1)} %collective-permute-done.1.refs_2_) | copy-start | bytes 221188
  21.7 0.6 %copy-start.7 = (bf16[1,144,256]{2,1,0:T(8,128)(2,1)}, bf16[1,144,256]{2,1,0:T(8,128)(2,1)S(1)}, u32[]{:S(2)}) copy-start(bf16[1,144,256]{2,1,0:T(8,128)(2,1)S(1)} %collective-permute-done.refs_1_) | copy-start | bytes 221188
  22.3 14.7 %copy-start.2 = (f32[8,256]{1,0:T(8,128)S(1)}, f32[8,256]{1,0:T(8,128)}, u32[]{:S(2)}) copy-start(f32[8,256]{1,0:T(8,128)} %get-tuple-element.13.consts_ref) | copy-start | bytes 24580
  22.3 14.7 %copy-start.4 = (f32[31,256]{1,0:T(8,128)S(1)}, f32[31,256]{1,0:T(8,128)}, u32[]{:S(2)}) copy-start(f32[31,256]{1,0:T(8,128)} %get-tuple-element.12.taps_ref) | copy-start | bytes 95236
  24.0 14.5 %copy-start = (bf16[4,144,256]{2,1,0:T(8,128)(2,1)S(1)}, bf16[4,144,256]{2,1,0:T(8,128)(2,1)}, u32[]{:S(2)}) copy-start(bf16[4,144,256]{2,1,0:T(8,128)(2,1)} %join.1.rest_0_) | copy-start | bytes 884740
  24.1 13.0 %collective-permute-start.3 = (bf16[4,144,256]{2,1,0:T(8,128)(2,1)}, bf16[4,144,256]{2,1,0:T(8,128)(2,1)S(1)}, u32[]{:S(2)}, u32[]{:S(2)}) collective-permute-start(bf16[4,144,256]{2,1,0:T(8,128)(2,1)} %join.1.rest_0_), channel_id=1, source_target_pairs={{0,2},{1,3},{2,0},{3,1},{4,6},{5,7},{6,4},{7,5},{8,10},{9,11},{10,... | collective-permute-start | bytes 884744 | tf_op jit(solution)/shard_map/ppermute | solution.py:190
  25.6 11.4 %all-to-all-start.1 = ((bf16[32,8,256]{2,1,0:T(8,128)(2,1)}), bf16[32,8,256]{2,1,0:T(8,128)(2,1)S(1)}, u32[]{:S(2)}, u32[]{:S(2)}) async-start(bf16[32,8,256]{2,1,0:T(8,128)(2,1)} %bitcast.6), calls=%async_computation.1 | async-start | bytes 262144 | tf_op jit(solution)/shard_map/all_to_all | solution.py:240
  29.1 8.9 %collective-permute-start.4 = (bf16[4,144,256]{2,1,0:T(8,128)(2,1)}, bf16[4,144,256]{2,1,0:T(8,128)(2,1)S(1)}, u32[]{:S(2)}, u32[]{:S(2)}) collective-permute-start(bf16[4,144,256]{2,1,0:T(8,128)(2,1)} %join.1.rest_0_), channel_id=1, source_target_pairs={{0,1},{1,0},{2,3},{3,2},{4,5},{5,4},{6,7},{7,6},{8,9},{9,8},{10,11... | collective-permute-start | bytes 884744 | tf_op jit(solution)/shard_map/ppermute | solution.py:190
  37.0 1.6 %collective-permute-start.5 = (bf16[4,144,256]{2,1,0:T(8,128)(2,1)S(1)}, bf16[4,144,256]{2,1,0:T(8,128)(2,1)S(1)}, u32[]{:S(2)}, u32[]{:S(2)}) collective-permute-start(bf16[4,144,256]{2,1,0:T(8,128)(2,1)S(1)} %collective-permute-done.3.rest_1_), channel_id=1, source_target_pairs={{0,1},{1,0},{2,3},{3,2},{4,5},{5,4},{6,7},{7,6},{8,9},{9,8},{10,11... | collective-permute-start | bytes 884744 | tf_op jit(solution)/shard_map/ppermute | solution.py:190
  37.0 1.6 %copy-start.1 = (bf16[32,2,4,256]{3,2,1,0:T(4,128)(2,1)S(1)}, bf16[32,2,4,256]{3,2,1,0:T(4,128)(2,1)}, u32[]{:S(2)}) copy-start(bf16[32,2,4,256]{3,2,1,0:T(4,128)(2,1)} %feat_ref.1) | copy-start | bytes 393220

commit v5 on v4

--- a/solution.py
+++ b/solution.py
@@ -66,15 +66,6 @@
     lax.fori_loop(0, n, step, 0)
 
 
-def join_kernel(pieces, *refs):
-    out_ref, sems = refs[pieces + 1 :]
-    copies = [pltpu.make_async_copy(refs[i], out_ref.at[i : i + 1], sems.at[i]) for i in range(pieces)]
-    for copy in copies:
-        copy.start()
-    for copy in copies:
-        copy.wait()
-
-
 def axial_kernel(z_ref, taps_ref, consts_ref, out_ref, padded, summed):
     axial, rows, c = z_ref.shape
     taps = taps_ref.shape[0]
@@ -116,16 +107,14 @@
     per = c // SLOT
     lane_slot = lax.broadcasted_iota(jnp.int32, (1, c), 1) // SLOT
     token_block = 32 * rows
-    copies, begins = [], []
+    copies, at = [], 0
     for i, w_ref in enumerate(w_refs):
-        begins.append(sum(w.shape[0] for w in w_refs[:i]))
-        copies.append(pltpu.make_async_copy(w_ref, slots.at[begins[i] : begins[i] + w_ref.shape[0]], sems.at[i]))
+        copies.append(pltpu.make_async_copy(w_ref, slots.at[at : at + w_ref.shape[0]], sems.at[i]))
+        at += w_ref.shape[0]
     for copy in copies:
         copy.start()
-    single = axial == 32
-    if not single:
-        for copy in copies:
-            copy.wait()
+    for copy in copies:
+        copy.wait()
 
     def mlp(i, carry):
         base = pl.multiple_of(i * token_block, token_block)
@@ -133,9 +122,6 @@
         total = jnp.zeros((token_block, c), jnp.float32)
         for g in range(slots.shape[0] // per):
             own = slice(g * per, (g + 1) * per)
-            for at, copy in zip(begins, copies):
-                if single and own.start <= at < own.stop:
-                    copy.wait()
             w_in = slots[own, 0:SLOT, :].reshape(per * SLOT, c)
             w_out = slots[own, SLOT : 2 * SLOT, :].reshape(per * SLOT, c)
             bias = jnp.zeros((1, c), jnp.float32)
@@ -150,7 +136,7 @@
         branch[pl.ds(i * 32, 32)] = result.reshape(32, rows, c)
         return carry
 
-    if single:
+    if axial == 32:
         mlp(0, 0)
     else:
         lax.fori_loop(0, axial // 32, mlp, 0)
@@ -206,7 +192,8 @@
             scratch_shapes=[pltpu.VMEM((5, 1, c), jnp.float32), pltpu.SemaphoreType.DMA((8,))],
             name="pack",
         )(b_in, w_in, w_out, axial_taps, *vectors)
-        line = [own] + [move(own, 0, by) for by in range(1, outer)]
+        line = [move(own, 0, by) for by in range(1, outer)]
+        side = [move(own, 1, by) for by in range(1, inner)]
     else:
         consts = jnp.concatenate(vectors + [jnp.zeros((3, c), jnp.float32)], axis=0)
         w_all = lax.all_gather(w_in, "row", axis=0, tiled=True).reshape(-1, SLOT, c)
@@ -227,20 +214,13 @@
         name="radial",
     )(got.reshape(n, a_loc, r_loc, theta, c), radial_taps)
     if spread:
-        joined = pl.pallas_call(
-            partial(join_kernel, outer),
-            out_shape=jax.ShapeDtypeStruct((outer,) + slot_shape, jnp.bfloat16),
-            in_specs=[anywhere] * (outer + 1),
-            out_specs=vmem(),
-            scratch_shapes=[pltpu.SemaphoreType.DMA((outer,))],
-            name="join",
-        )(*line, mixed)
-        across = [move(joined, 1, by) for by in range(1, inner)]
-        twin = [move(joined, 2)]
+        line = [lax.optimization_barrier((h, mixed))[0] for h in line]
+        across = side + [move(h, 1, by) for by in range(1, inner) for h in line]
+        twin = [move(h, 2) for h in [own] + line]
     back = lax.all_to_all(mixed.reshape(axial, rows, c), "row", split_axis=0, concat_axis=0, tiled=True)
     if spread:
         across, back = lax.optimization_barrier((across, back))
-        slots = [joined] + across + twin + [move(h, 2) for h in across]
+        slots = [own] + line + across + twin + [move(h, 2) for h in across]
     normed = pl.pallas_call(
         axial_kernel,
         out_shape=jax.ShapeDtypeStruct((axial * rows, c), jnp.bfloat16),

time: 41.3 us -> 47.4 us (1.15)
  blocking collectives: 0 us -> 15.5 us
  waiting for transfers between devices: 12.9 us -> 6.94 us
  starting transfers between devices: 17.6 us -> 14.9 us
  Pallas kernels: 9 us -> 7.99 us
    all_to_all x0 -> x1, blocking collectives: none -> 15.5 us  [local(): lax.all_to_all(features, 'row', split_axis=0, concat_axis=0, tiled=True)]
    all_to_all x1, waiting for transfers between devices: 7.61 us -> 0.01 us  [local(): lax.all_to_all(mixed.reshape(axial, rows, c), 'row', split_axis=0, concat...]
    all_to_all x1 -> x0, starting transfers between devices: 7.38 us -> none  [local(): lax.all_to_all(features, 'row', split_axis=0, concat_axis=0, tiled=True)]
    ppermute x6 -> x15, starting transfers between devices: 6.72 us -> 11.4 us  [move(): return lax.ppermute(piece, 'row', shifted(n, digit, by))]
    ppermute x6 -> x15, waiting for transfers between devices: 4.48 us -> 6.94 us  [move(): return lax.ppermute(piece, 'row', shifted(n, digit, by))]
    pallas_call x1 -> x0, Pallas kernels: 1.75 us -> none  [local(): pl.pallas_call(partial(join_kernel, outer), out_shape=jax.ShapeDtypeStruc...]
    all_to_all x1 -> x0, waiting for transfers between devices: 0.84 us -> none  [local(): lax.all_to_all(features, 'row', split_axis=0, concat_axis=0, tiled=True)]
    pallas_call x1, Pallas kernels: 2.3 us -> 3.1 us  [local(): pl.pallas_call(mlp_kernel, out_shape=jax.ShapeDtypeStruct(features.shape,...]
  transfers between devices with their start and end apart: 8 -> 16, of which waited for: 4 -> 4; matrix products, arithmetic and copies ran while one was open for 0% -> 0% of each run, Pallas kernels for 12% -> 7%
where the time goes in v5:
time: 47.4 us; the launch traced here: 46.9 us
  blocking collectives  15.5 us (33%)
  starting transfers between devices  14.9 us (31%)
  Pallas kernels  7.99 us (17%)
  waiting for transfers between devices  6.94 us (15%)
  local copies, waits for them, and re-layouts  1.46 us (3%)
    all_to_all x1, blocking collectives, local(): lax.all_to_all(features, 'row', split_axis=0, concat_axis=0, tiled=True)  15.5 us
    ppermute x15, starting transfers between devices, move(): return lax.ppermute(piece, 'row', shifted(n, digit, by))  11.4 us
    ppermute x15, waiting for transfers between devices, move(): return lax.ppermute(piece, 'row', shifted(n, digit, by))  6.94 us
    all_to_all x1, starting transfers between devices, local(): lax.all_to_all(mixed.reshape(axial, rows, c), 'row', split_axis=0, concat...  3.51 us
    pallas_call x1, Pallas kernels, local(): pl.pallas_call(mlp_kernel, out_shape=jax.ShapeDtypeStruct(features.shape,...  3.1 us
    pallas_call x1, Pallas kernels, local(): pl.pallas_call(pack_kernel, out_shape=[jax.ShapeDtypeStruct((1,) + slot_s...  2.18 us
    pallas_call x1, Pallas kernels, local(): pl.pallas_call(radial_kernel, out_shape=jax.ShapeDtypeStruct((n, a_loc, r...  1.77 us
    unnamed x10, local copies, waits for them, and re-layouts  1.46 us
  transfers between devices with their start and end apart: 16, of which 4 were waited for; matrix products, arithmetic and copies ran while one was open for 0% of the time, Pallas kernels for 7%

profile of v5, /device:TPU:0, one launch (start us, length us, event | category | flops | bytes accessed | tf_op | source)
XLA Modules:
  0.0 46.9 jit_solution(977869681369814401)
XLA Ops:
  0.0 15.5 %all_to_all.10 = bf16[32,2,4,256]{3,2,1,0:T(4,128)(2,1)S(1)} all-to-all(bf16[32,2,4,256]{3,2,1,0:T(4,128)(2,1)} %feat_ref.1), channel_id=1, replica_groups=mesh['groups'=2,'row'=16] {'row'}, dimensions={0} | all-to-all | bytes 262144 | tf_op jit(solution)/shard_map/all_to_all | solution.py:205
  15.5 1.8 %radial.1 = bf16[16,2,8,256]{3,2,1,0:T(8,128)(2,1)} custom-call(bf16[16,2,2,4,256]{4,3,2,1,0:T(4,128)(2,1)S(1)} %bitcast.7, f32[31,256]{1,0:T(8,128)S(1)} %copy-done.3), custom_call_target="tpu_custom_call" | custom-call | tf_op jit(solution)/shard_map/radial/pallas_call | solution.py:207
  17.2 3.5 %all-to-all-start.1 = ((bf16[32,8,256]{2,1,0:T(8,128)(2,1)}), bf16[32,8,256]{2,1,0:T(8,128)(2,1)S(1)}, u32[]{:S(2)}, u32[]{:S(2)}) async-start(bf16[32,8,256]{2,1,0:T(8,128)(2,1)} %bitcast.6), calls=%async_computation.1 | async-start | bytes 262144 | tf_op jit(solution)/shard_map/all_to_all | solution.py:220
  20.7 2.2 %pack.1 = (bf16[1,144,256]{2,1,0:T(8,128)(2,1)}, f32[31,256]{1,0:T(8,128)}, f32[8,256]{1,0:T(8,128)}) custom-call(bf16[64]{0:T(256)(128)(2,1)} %b_ref.1, bf16[64,256]{1,0:T(8,128)(2,1)} %w_in_ref.1, bf16[64,256]{1,0:T(8,128)(2,1)} %w_out_ref.1, f32[31,256]{1,0:T(8,128)} %taps_ref.2, f32[1,256]{1,0:T(1,128)} %bitcast.8, f32[1,256]{1,0:T(1,128)} %bitcast.9, ...), custom_call_target="tpu_custom_call" | custom-call | tf_op jit(solution)/shard_map/pack/pallas_call | solution.py:183
  22.9 3.7 %collective-permute-start.5 = (bf16[1,144,256]{2,1,0:T(8,128)(2,1)}, bf16[1,144,256]{2,1,0:T(8,128)(2,1)S(1)}, u32[]{:S(2)}, u32[]{:S(2)}) collective-permute-start(bf16[1,144,256]{2,1,0:T(8,128)(2,1)} %get-tuple-element.16.rest_0_), channel_id=1, source_target_pairs={{0,12},{1,13},{2,14},{3,15},{4,0},{5,1},{6,2},{7,3},{8,4},{9,5},{1... | collective-permute-start | bytes 221192 | tf_op jit(solution)/shard_map/ppermute | solution.py:176
  26.7 0.0 collective-permute-start.3
  26.7 1.1 %collective-permute-start.1 = (bf16[1,144,256]{2,1,0:T(8,128)(2,1)}, bf16[1,144,256]{2,1,0:T(8,128)(2,1)S(1)}, u32[]{:S(2)}, u32[]{:S(2)}) collective-permute-start(bf16[1,144,256]{2,1,0:T(8,128)(2,1)} %get-tuple-element.16.rest_0_), channel_id=1, source_target_pairs={{0,4},{1,5},{2,6},{3,7},{4,8},{5,9},{6,10},{7,11},{8,12},{9,13},{1... | collective-permute-start | bytes 221192 | tf_op jit(solution)/shard_map/ppermute | solution.py:176
  27.8 1.5 %collective-permute-start = (bf16[1,144,256]{2,1,0:T(8,128)(2,1)}, bf16[1,144,256]{2,1,0:T(8,128)(2,1)S(1)}, u32[]{:S(2)}, u32[]{:S(2)}) collective-permute-start(bf16[1,144,256]{2,1,0:T(8,128)(2,1)} %get-tuple-element.16.rest_0_), channel_id=1, source_target_pairs={{0,2},{1,3},{2,0},{3,1},{4,6},{5,7},{6,4},{7,5},{8,10},{9,11},{10,... | collective-permute-start | bytes 221192 | tf_op jit(solution)/shard_map/ppermute | solution.py:176
  29.2 0.4 collective-permute-done.5.rest_3_
  29.7 1.5 %collective-permute-start.6 = (bf16[1,144,256]{2,1,0:T(8,128)(2,1)S(1)}, bf16[1,144,256]{2,1,0:T(8,128)(2,1)S(1)}, u32[]{:S(2)}, u32[]{:S(2)}) collective-permute-start(bf16[1,144,256]{2,1,0:T(8,128)(2,1)S(1)} %collective-permute-done.5.rest_3_), channel_id=1, source_target_pairs={{0,2},{1,3},{2,0},{3,1},{4,6},{5,7},{6,4},{7,5},{8,10},{9,11},{10,... | collective-permute-start | bytes 221192 | tf_op jit(solution)/shard_map/ppermute | solution.py:176
  31.1 3.2 %collective-permute-done.3.rest_2_ = bf16[1,144,256]{2,1,0:T(8,128)(2,1)S(1)} collective-permute-done((bf16[1,144,256]{2,1,0:T(8,128)(2,1)}, bf16[1,144,256]{2,1,0:T(8,128)(2,1)S(1)}, u32[]{:S(2)}, u32[]{:S(2)}) %collective-permute-start.3) | collective-permute-done | bytes 73760 | tf_op jit(solution)/shard_map/ppermute | solution.py:176
  34.3 1.5 %collective-permute-start.4 = (bf16[1,144,256]{2,1,0:T(8,128)(2,1)S(1)}, bf16[1,144,256]{2,1,0:T(8,128)(2,1)S(1)}, u32[]{:S(2)}, u32[]{:S(2)}) collective-permute-start(bf16[1,144,256]{2,1,0:T(8,128)(2,1)S(1)} %collective-permute-done.3.rest_2_), channel_id=1, source_target_pairs={{0,2},{1,3},{2,0},{3,1},{4,6},{5,7},{6,4},{7,5},{8,10},{9,11},{10,... | collective-permute-start | bytes 221192 | tf_op jit(solution)/shard_map/ppermute | solution.py:176
  35.8 0.0 collective-permute-done.1.rest_1_
  35.8 0.6 %collective-permute-start.2 = (bf16[1,144,256]{2,1,0:T(8,128)(2,1)S(1)}, bf16[1,144,256]{2,1,0:T(8,128)(2,1)S(1)}, u32[]{:S(2)}, u32[]{:S(2)}) collective-permute-start(bf16[1,144,256]{2,1,0:T(8,128)(2,1)S(1)} %collective-permute-done.1.rest_1_), channel_id=1, source_target_pairs={{0,2},{1,3},{2,0},{3,1},{4,6},{5,7},{6,4},{7,5},{8,10},{9,11},{10,... | collective-permute-start | bytes 221192 | tf_op jit(solution)/shard_map/ppermute | solution.py:176
  36.3 0.0 collective-permute-start.7
  36.3 0.0 collective-permute-done.rest_4_
  36.4 0.5 %collective-permute-start.10 = (bf16[1,144,256]{2,1,0:T(8,128)(2,1)S(1)}, bf16[1,144,256]{2,1,0:T(8,128)(2,1)S(1)}, u32[]{:S(2)}, u32[]{:S(2)}) collective-permute-start(bf16[1,144,256]{2,1,0:T(8,128)(2,1)S(1)} %collective-permute-done.5.rest_3_), channel_id=1, source_target_pairs={{0,1},{1,0},{2,3},{3,2},{4,5},{5,4},{6,7},{7,6},{8,9},{9,8},{10,11... | collective-permute-start | bytes 221192 | tf_op jit(solution)/shard_map/ppermute | solution.py:176
  36.9 0.0 collective-permute-done.6.rest_7_
  36.9 0.1 collective-permute-start.9
  36.9 2.3 %collective-permute-done.4.rest_6_ = bf16[1,144,256]{2,1,0:T(8,128)(2,1)S(1)} collective-permute-done((bf16[1,144,256]{2,1,0:T(8,128)(2,1)S(1)}, bf16[1,144,256]{2,1,0:T(8,128)(2,1)S(1)}, u32[]{:S(2)}, u32[]{:S(2)}) %collective-permute-start.4) | collective-permute-done | bytes 73760 | tf_op jit(solution)/shard_map/ppermute | solution.py:176
  39.2 0.0 collective-permute-start.8
  39.2 1.0 %collective-permute-done.2.rest_5_ = bf16[1,144,256]{2,1,0:T(8,128)(2,1)S(1)} collective-permute-done((bf16[1,144,256]{2,1,0:T(8,128)(2,1)S(1)}, bf16[1,144,256]{2,1,0:T(8,128)(2,1)S(1)}, u32[]{:S(2)}, u32[]{:S(2)}) %collective-permute-start.2) | collective-permute-done | bytes 73760 | tf_op jit(solution)/shard_map/ppermute | solution.py:176
  40.3 0.5 %collective-permute-start.12 = (bf16[1,144,256]{2,1,0:T(8,128)(2,1)S(1)}, bf16[1,144,256]{2,1,0:T(8,128)(2,1)S(1)}, u32[]{:S(2)}, u32[]{:S(2)}) collective-permute-start(bf16[1,144,256]{2,1,0:T(8,128)(2,1)S(1)} %collective-permute-done.2.rest_5_), channel_id=1, source_target_pairs={{0,1},{1,0},{2,3},{3,2},{4,5},{5,4},{6,7},{7,6},{8,9},{9,8},{10,11... | collective-permute-start | bytes 221192 | tf_op jit(solution)/shard_map/ppermute | solution.py:176
  40.8 0.0 collective-permute-done.10.rest_11_
  40.8 0.1 collective-permute-start.13
  40.8 0.0 collective-permute-done.9.rest_10_
  40.8 0.4 collective-permute-start.14
  41.3 0.7 %copy-done.2 = f32[8,256]{1,0:T(8,128)S(1)} copy-done((f32[8,256]{1,0:T(8,128)S(1)}, f32[8,256]{1,0:T(8,128)}, u32[]{:S(2)}) %copy-start.2) | copy-done | bytes 8216
  42.0 0.8 %copy-done.4 = f32[31,256]{1,0:T(8,128)S(1)} copy-done((f32[31,256]{1,0:T(8,128)S(1)}, f32[31,256]{1,0:T(8,128)}, u32[]{:S(2)}) %copy-start.4) | copy-done | bytes 31768
  42.7 0.9 %axial.1.normed_ref = bf16[256,256]{1,0:T(8,128)(2,1)S(1)} custom-call(bf16[32,8,256]{2,1,0:T(8,128)(2,1)S(1)} %all-to-all-done.1.z_ref, f32[31,256]{1,0:T(8,128)S(1)} %copy-done.4, f32[8,256]{1,0:T(8,128)S(1)} %copy-done.2), custom_call_target="tpu_custom_call" | custom-call | tf_op jit(solution)/shard_map/axial/pallas_call | solution.py:224
  43.7 0.0 collective-permute-done.12.rest_13_
  43.8 3.1 %mlp.1 = bf16[32,2,4,256]{3,2,1,0:T(4,128)(2,1)} custom-call(bf16[256,256]{1,0:T(8,128)(2,1)S(1)} %axial.1.normed_ref, bf16[32,2,4,256]{3,2,1,0:T(4,128)(2,1)S(1)} %copy-done, f32[8,256]{1,0:T(8,128)S(1)} %copy-done.2, bf16[1,144,256]{2,1,0:T(8,128)(2,1)S(1)} %copy-done.1, bf16[1,144,256]{2,1,0:T(8,128)(2,1)S(1)} %collective-permute-done.1.rest_1_, ...), custom_call_target="tpu_custom_call" | custom-call | tf_op jit(solution)/shard_map/mlp/pallas_call | solution.py:237
  (15 shorter events, 0.0 us)
Async XLA Ops:
  0.0 15.5 %copy-start.3 = (f32[31,256]{1,0:T(8,128)S(1)}, f32[31,256]{1,0:T(8,128)}, u32[]{:S(2)}) copy-start(f32[31,256]{1,0:T(8,128)} %taps_ref.3) | copy-start | bytes 95236
  17.2 23.0 %all-to-all-start.1 = ((bf16[32,8,256]{2,1,0:T(8,128)(2,1)}), bf16[32,8,256]{2,1,0:T(8,128)(2,1)S(1)}, u32[]{:S(2)}, u32[]{:S(2)}) async-start(bf16[32,8,256]{2,1,0:T(8,128)(2,1)} %bitcast.6), calls=%async_computation.1 | async-start | bytes 262144 | tf_op jit(solution)/shard_map/all_to_all | solution.py:220
  22.9 6.7 %collective-permute-start.5 = (bf16[1,144,256]{2,1,0:T(8,128)(2,1)}, bf16[1,144,256]{2,1,0:T(8,128)(2,1)S(1)}, u32[]{:S(2)}, u32[]{:S(2)}) collective-permute-start(bf16[1,144,256]{2,1,0:T(8,128)(2,1)} %get-tuple-element.16.rest_0_), channel_id=1, source_target_pairs={{0,12},{1,13},{2,14},{3,15},{4,0},{5,1},{6,2},{7,3},{8,4},{9,5},{1... | collective-permute-start | bytes 221192 | tf_op jit(solution)/shard_map/ppermute | solution.py:176
  26.7 7.7 %collective-permute-start.3 = (bf16[1,144,256]{2,1,0:T(8,128)(2,1)}, bf16[1,144,256]{2,1,0:T(8,128)(2,1)S(1)}, u32[]{:S(2)}, u32[]{:S(2)}) collective-permute-start(bf16[1,144,256]{2,1,0:T(8,128)(2,1)} %get-tuple-element.16.rest_0_), channel_id=1, source_target_pairs={{0,8},{1,9},{2,10},{3,11},{4,12},{5,13},{6,14},{7,15},{8,0},{9,1},... | collective-permute-start | bytes 221192 | tf_op jit(solution)/shard_map/ppermute | solution.py:176
  26.7 9.1 %collective-permute-start.1 = (bf16[1,144,256]{2,1,0:T(8,128)(2,1)}, bf16[1,144,256]{2,1,0:T(8,128)(2,1)S(1)}, u32[]{:S(2)}, u32[]{:S(2)}) collective-permute-start(bf16[1,144,256]{2,1,0:T(8,128)(2,1)} %get-tuple-element.16.rest_0_), channel_id=1, source_target_pairs={{0,4},{1,5},{2,6},{3,7},{4,8},{5,9},{6,10},{7,11},{8,12},{9,13},{1... | collective-permute-start | bytes 221192 | tf_op jit(solution)/shard_map/ppermute | solution.py:176
  27.8 8.6 %collective-permute-start = (bf16[1,144,256]{2,1,0:T(8,128)(2,1)}, bf16[1,144,256]{2,1,0:T(8,128)(2,1)S(1)}, u32[]{:S(2)}, u32[]{:S(2)}) collective-permute-start(bf16[1,144,256]{2,1,0:T(8,128)(2,1)} %get-tuple-element.16.rest_0_), channel_id=1, source_target_pairs={{0,2},{1,3},{2,0},{3,1},{4,6},{5,7},{6,4},{7,5},{8,10},{9,11},{10,... | collective-permute-start | bytes 221192 | tf_op jit(solution)/shard_map/ppermute | solution.py:176
  29.7 7.2 %collective-permute-start.6 = (bf16[1,144,256]{2,1,0:T(8,128)(2,1)S(1)}, bf16[1,144,256]{2,1,0:T(8,128)(2,1)S(1)}, u32[]{:S(2)}, u32[]{:S(2)}) collective-permute-start(bf16[1,144,256]{2,1,0:T(8,128)(2,1)S(1)} %collective-permute-done.5.rest_3_), channel_id=1, source_target_pairs={{0,2},{1,3},{2,0},{3,1},{4,6},{5,7},{6,4},{7,5},{8,10},{9,11},{10,... | collective-permute-start | bytes 221192 | tf_op jit(solution)/shard_map/ppermute | solution.py:176
  34.3 4.9 %collective-permute-start.4 = (bf16[1,144,256]{2,1,0:T(8,128)(2,1)S(1)}, bf16[1,144,256]{2,1,0:T(8,128)(2,1)S(1)}, u32[]{:S(2)}, u32[]{:S(2)}) collective-permute-start(bf16[1,144,256]{2,1,0:T(8,128)(2,1)S(1)} %collective-permute-done.3.rest_2_), channel_id=1, source_target_pairs={{0,2},{1,3},{2,0},{3,1},{4,6},{5,7},{6,4},{7,5},{8,10},{9,11},{10,... | collective-permute-start | bytes 221192 | tf_op jit(solution)/shard_map/ppermute | solution.py:176
  35.8 4.5 %collective-permute-start.2 = (bf16[1,144,256]{2,1,0:T(8,128)(2,1)S(1)}, bf16[1,144,256]{2,1,0:T(8,128)(2,1)S(1)}, u32[]{:S(2)}, u32[]{:S(2)}) collective-permute-start(bf16[1,144,256]{2,1,0:T(8,128)(2,1)S(1)} %collective-permute-done.1.rest_1_), channel_id=1, source_target_pairs={{0,2},{1,3},{2,0},{3,1},{4,6},{5,7},{6,4},{7,5},{8,10},{9,11},{10,... | collective-permute-start | bytes 221192 | tf_op jit(solution)/shard_map/ppermute | solution.py:176
  36.3 3.9 %collective-permute-start.7 = (bf16[1,144,256]{2,1,0:T(8,128)(2,1)}, bf16[1,144,256]{2,1,0:T(8,128)(2,1)S(1)}, u32[]{:S(2)}, u32[]{:S(2)}) collective-permute-start(bf16[1,144,256]{2,1,0:T(8,128)(2,1)} %get-tuple-element.16.rest_0_), channel_id=1, source_target_pairs={{0,1},{1,0},{2,3},{3,2},{4,5},{5,4},{6,7},{7,6},{8,9},{9,8},{10,11... | collective-permute-start | bytes 221192 | tf_op jit(solution)/shard_map/ppermute | solution.py:176
  36.4 4.4 %collective-permute-start.10 = (bf16[1,144,256]{2,1,0:T(8,128)(2,1)S(1)}, bf16[1,144,256]{2,1,0:T(8,128)(2,1)S(1)}, u32[]{:S(2)}, u32[]{:S(2)}) collective-permute-start(bf16[1,144,256]{2,1,0:T(8,128)(2,1)S(1)} %collective-permute-done.5.rest_3_), channel_id=1, source_target_pairs={{0,1},{1,0},{2,3},{3,2},{4,5},{5,4},{6,7},{7,6},{8,9},{9,8},{10,11... | collective-permute-start | bytes 221192 | tf_op jit(solution)/shard_map/ppermute | solution.py:176
  36.9 4.0 %collective-permute-start.9 = (bf16[1,144,256]{2,1,0:T(8,128)(2,1)S(1)}, bf16[1,144,256]{2,1,0:T(8,128)(2,1)S(1)}, u32[]{:S(2)}, u32[]{:S(2)}) collective-permute-start(bf16[1,144,256]{2,1,0:T(8,128)(2,1)S(1)} %collective-permute-done.3.rest_2_), channel_id=1, source_target_pairs={{0,1},{1,0},{2,3},{3,2},{4,5},{5,4},{6,7},{7,6},{8,9},{9,8},{10,11... | collective-permute-start | bytes 221192 | tf_op jit(solution)/shard_map/ppermute | solution.py:176
  39.2 4.5 %collective-permute-start.8 = (bf16[1,144,256]{2,1,0:T(8,128)(2,1)S(1)}, bf16[1,144,256]{2,1,0:T(8,128)(2,1)S(1)}, u32[]{:S(2)}, u32[]{:S(2)}) collective-permute-start(bf16[1,144,256]{2,1,0:T(8,128)(2,1)S(1)} %collective-permute-done.1.rest_1_), channel_id=1, source_target_pairs={{0,1},{1,0},{2,3},{3,2},{4,5},{5,4},{6,7},{7,6},{8,9},{9,8},{10,11... | collective-permute-start | bytes 221192 | tf_op jit(solution)/shard_map/ppermute | solution.py:176
  40.2 3.5 %collective-permute-start.11 = (bf16[1,144,256]{2,1,0:T(8,128)(2,1)S(1)}, bf16[1,144,256]{2,1,0:T(8,128)(2,1)S(1)}, u32[]{:S(2)}, u32[]{:S(2)}) collective-permute-start(bf16[1,144,256]{2,1,0:T(8,128)(2,1)S(1)} %collective-permute-done.rest_4_), channel_id=1, source_target_pairs={{0,1},{1,0},{2,3},{3,2},{4,5},{5,4},{6,7},{7,6},{8,9},{9,8},{10,11... | collective-permute-start | bytes 221192 | tf_op jit(solution)/shard_map/ppermute | solution.py:176
  40.3 3.5 %collective-permute-start.12 = (bf16[1,144,256]{2,1,0:T(8,128)(2,1)S(1)}, bf16[1,144,256]{2,1,0:T(8,128)(2,1)S(1)}, u32[]{:S(2)}, u32[]{:S(2)}) collective-permute-start(bf16[1,144,256]{2,1,0:T(8,128)(2,1)S(1)} %collective-permute-done.2.rest_5_), channel_id=1, source_target_pairs={{0,1},{1,0},{2,3},{3,2},{4,5},{5,4},{6,7},{7,6},{8,9},{9,8},{10,11... | collective-permute-start | bytes 221192 | tf_op jit(solution)/shard_map/ppermute | solution.py:176
  40.8 3.0 %collective-permute-start.13 = (bf16[1,144,256]{2,1,0:T(8,128)(2,1)S(1)}, bf16[1,144,256]{2,1,0:T(8,128)(2,1)S(1)}, u32[]{:S(2)}, u32[]{:S(2)}) collective-permute-start(bf16[1,144,256]{2,1,0:T(8,128)(2,1)S(1)} %collective-permute-done.4.rest_6_), channel_id=1, source_target_pairs={{0,1},{1,0},{2,3},{3,2},{4,5},{5,4},{6,7},{7,6},{8,9},{9,8},{10,11... | collective-permute-start | bytes 221192 | tf_op jit(solution)/shard_map/ppermute | solution.py:176
  40.8 2.9 %collective-permute-start.14 = (bf16[1,144,256]{2,1,0:T(8,128)(2,1)S(1)}, bf16[1,144,256]{2,1,0:T(8,128)(2,1)S(1)}, u32[]{:S(2)}, u32[]{:S(2)}) collective-permute-start(bf16[1,144,256]{2,1,0:T(8,128)(2,1)S(1)} %collective-permute-done.6.rest_7_), channel_id=1, source_target_pairs={{0,1},{1,0},{2,3},{3,2},{4,5},{5,4},{6,7},{7,6},{8,9},{9,8},{10,11... | collective-permute-start | bytes 221192 | tf_op jit(solution)/shard_map/ppermute | solution.py:176
  41.3 0.7 %copy-start.2 = (f32[8,256]{1,0:T(8,128)S(1)}, f32[8,256]{1,0:T(8,128)}, u32[]{:S(2)}) copy-start(f32[8,256]{1,0:T(8,128)} %get-tuple-element.22.consts_ref) | copy-start | bytes 24580
  42.0 0.8 %copy-start.4 = (f32[31,256]{1,0:T(8,128)S(1)}, f32[31,256]{1,0:T(8,128)}, u32[]{:S(2)}) copy-start(f32[31,256]{1,0:T(8,128)} %get-tuple-element.21.taps_ref) | copy-start | bytes 95236
  42.7 1.0 %copy-start = (bf16[32,2,4,256]{3,2,1,0:T(4,128)(2,1)S(1)}, bf16[32,2,4,256]{3,2,1,0:T(4,128)(2,1)}, u32[]{:S(2)}) copy-start(bf16[32,2,4,256]{3,2,1,0:T(4,128)(2,1)} %feat_ref.1) | copy-start | bytes 393220
  42.7 1.0 %copy-start.1 = (bf16[1,144,256]{2,1,0:T(8,128)(2,1)S(1)}, bf16[1,144,256]{2,1,0:T(8,128)(2,1)}, u32[]{:S(2)}) copy-start(bf16[1,144,256]{2,1,0:T(8,128)(2,1)} %get-tuple-element.16.rest_0_) | copy-start | bytes 221188

commit v6 on v5

--- a/solution.py
+++ b/solution.py
@@ -7,7 +7,7 @@
 from jax.experimental.pallas import tpu as pltpu
 from jax.sharding import PartitionSpec as P
 
-SLOT = 64
+SLOT = 32
 EXTRA = 16
 
 
@@ -15,29 +15,48 @@
     return pl.BlockSpec(memory_space=pltpu.VMEM)
 
 
-def pack_kernel(b_ref, w_in_ref, w_out_ref, taps_ref, *rest):
-    vectors = rest[:5]
-    slot_ref, taps_out, consts_out, staged, sems = rest[5:]
+def pack_kernel(b_ref, w_in_ref, w_out_ref, slot_ref, sems):
+    half = lax.axis_index("groups")
+    at = pl.multiple_of(half * SLOT, SLOT)
     copies = [
-        pltpu.make_async_copy(w_in_ref, slot_ref.at[0, 0:SLOT], sems.at[0]),
-        pltpu.make_async_copy(w_out_ref, slot_ref.at[0, SLOT : 2 * SLOT], sems.at[1]),
-        pltpu.make_async_copy(taps_ref, taps_out, sems.at[2]),
+        pltpu.make_async_copy(w_in_ref.at[pl.ds(at, SLOT)], slot_ref.at[0, 0:SLOT], sems.at[0]),
+        pltpu.make_async_copy(w_out_ref.at[pl.ds(at, SLOT)], slot_ref.at[0, SLOT : 2 * SLOT], sems.at[1]),
     ]
-    for i, vector in enumerate(vectors):
-        copies.append(pltpu.make_async_copy(vector, staged.at[i], sems.at[3 + i]))
     for copy in copies:
         copy.start()
     bias = b_ref[...].astype(jnp.float32)[None, :]
     c = slot_ref.shape[2]
-    wide = jnp.concatenate([bias] * (c // SLOT), axis=1)
+    low, high = bias[:, :SLOT], bias[:, SLOT:]
+    wide = jnp.where(half == 0, jnp.concatenate([low] * (c // SLOT), axis=1), jnp.concatenate([high] * (c // SLOT), axis=1))
     slot_ref[0, 2 * SLOT : 2 * SLOT + EXTRA, :] = jnp.broadcast_to(wide, (EXTRA, c)).astype(slot_ref.dtype)
+    for copy in copies:
+        copy.wait()
+
+
+def stage_kernel(order_ref, taps_ref, *rest):
+    vectors = rest[:5]
+    taps_out, consts_out, staged, sems = rest[5:]
+    copies = [pltpu.make_async_copy(taps_ref, taps_out, sems.at[5])]
+    for i, vector in enumerate(vectors):
+        copies.append(pltpu.make_async_copy(vector, staged.at[i], sems.at[i]))
+    for copy in copies:
+        copy.start()
     for copy in copies:
         copy.wait()
     for i in range(5):
         consts_out[i : i + 1, :] = staged[i]
 
 
-def radial_kernel(x_ref, taps_ref, out_ref, even, odd):
+def radial_kernel(pieces, x_ref, taps_ref, *rest):
+    out_ref = rest[pieces]
+    copies = []
+    if pieces:
+        joined_ref, even, odd, sems = rest[pieces + 1 :]
+        copies = [pltpu.make_async_copy(rest[i], joined_ref.at[i : i + 1], sems.at[i]) for i in range(pieces)]
+    else:
+        even, odd = rest[1:]
+    for copy in copies:
+        copy.start()
     n, a_loc, _, theta, c = x_ref.shape
     taps = taps_ref.shape[0]
     pad = (taps + 1) // 4
@@ -64,6 +83,8 @@
         return carry
 
     lax.fori_loop(0, n, step, 0)
+    for copy in copies:
+        copy.wait()
 
 
 def axial_kernel(z_ref, taps_ref, consts_ref, out_ref, padded, summed):
@@ -156,46 +177,43 @@
 def shifted(n, digit, by):
     sizes = digits(n)
     stride = [sizes[1] * sizes[2], sizes[2], 1][digit]
-    pairs = []
+    targets = []
     for i in range(n):
         at = (i // stride) % sizes[digit]
-        to = (at + by) % sizes[digit]
-        pairs.append((i, i + (to - at) * stride))
-    return pairs
-
-
-def local(n, features, axial_taps, radial_taps, conv_bias, ln_gain, ln_bias, w_in, b_in, w_out, b_out, layer_scale):
+        targets.append(i + ((at + by) % sizes[digit] - at) * stride)
+    return targets
+
+
+def local(parts, n, features, axial_taps, radial_taps, conv_bias, ln_gain, ln_bias, w_in, b_in, w_out, b_out, layer_scale):
     axial, r_loc, theta, c = features.shape
     rows = r_loc * theta
     hid_loc = w_in.shape[0]
     a_loc = axial // n
-    spread = hid_loc == SLOT
+    outer, inner, _ = digits(n)
+    spread = hid_loc == parts * SLOT and parts == 2 and inner == 2
     params = pltpu.CompilerParams(vmem_limit_bytes=48 * 1024 * 1024)
-
-    def move(piece, digit, by=1):
-        return lax.ppermute(piece, "row", shifted(n, digit, by))
-
-    outer, inner, _ = digits(n)
     anywhere = pl.BlockSpec(memory_space=pl.ANY)
-    vectors = [v[None, :] for v in (conv_bias, ln_gain, ln_bias, b_out, layer_scale)]
+
+    def move(piece, digit, by, swap=False):
+        targets = shifted(n, digit, by)
+        if not swap:
+            return lax.ppermute(piece, "row", list(enumerate(targets)))
+        pairs = [(g * n + i, (1 - g) * n + t) for g in range(2) for i, t in enumerate(targets)]
+        return lax.ppermute(piece, ("groups", "row"), pairs)
+
     slot_shape = (2 * SLOT + EXTRA, c)
+    line = []
     if spread:
-        own, axial_taps, consts = pl.pallas_call(
+        own = pl.pallas_call(
             pack_kernel,
-            out_shape=[
-                jax.ShapeDtypeStruct((1,) + slot_shape, jnp.bfloat16),
-                jax.ShapeDtypeStruct(axial_taps.shape, jnp.float32),
-                jax.ShapeDtypeStruct((8, c), jnp.float32),
-            ],
-            in_specs=[vmem()] + [anywhere] * 8,
-            out_specs=[vmem()] * 3,
-            scratch_shapes=[pltpu.VMEM((5, 1, c), jnp.float32), pltpu.SemaphoreType.DMA((8,))],
+            out_shape=jax.ShapeDtypeStruct((1,) + slot_shape, jnp.bfloat16),
+            in_specs=[vmem()] + [anywhere] * 2,
+            out_specs=vmem(),
+            scratch_shapes=[pltpu.SemaphoreType.DMA((2,))],
             name="pack",
-        )(b_in, w_in, w_out, axial_taps, *vectors)
-        line = [move(own, 0, by) for by in range(1, outer)]
-        side = [move(own, 1, by) for by in range(1, inner)]
+        )(b_in, w_in, w_out)
+        line = [own] + [move(own, 0, by) for by in range(1, outer)]
     else:
-        consts = jnp.concatenate(vectors + [jnp.zeros((3, c), jnp.float32)], axis=0)
         w_all = lax.all_gather(w_in, "row", axis=0, tiled=True).reshape(-1, SLOT, c)
         o_all = lax.all_gather(w_out, "row", axis=0, tiled=True).reshape(-1, SLOT, c)
         b_all = lax.all_gather(b_in, "row", axis=0, tiled=True).reshape(-1, 1, SLOT)
@@ -204,23 +222,37 @@
 
     got = lax.all_to_all(features, "row", split_axis=0, concat_axis=0, tiled=True)
     pad = (radial_taps.shape[0] + 1) // 4
-    mixed = pl.pallas_call(
-        radial_kernel,
-        out_shape=jax.ShapeDtypeStruct((n, a_loc, rows, c), jnp.bfloat16),
-        in_specs=[vmem()] * 2,
-        out_specs=vmem(),
-        scratch_shapes=[pltpu.VMEM((n + 2 * pad, a_loc, rows, c), jnp.float32)] * 2,
+    pieces = len(line)
+    out_shape = [jax.ShapeDtypeStruct((n, a_loc, rows, c), jnp.bfloat16)]
+    scratch = [pltpu.VMEM((n + 2 * pad, a_loc, rows, c), jnp.float32)] * 2
+    if spread:
+        out_shape.append(jax.ShapeDtypeStruct((pieces,) + slot_shape, jnp.bfloat16))
+        scratch.append(pltpu.SemaphoreType.DMA((pieces,)))
+    mixed, *joined = pl.pallas_call(
+        partial(radial_kernel, pieces),
+        out_shape=out_shape,
+        in_specs=[vmem()] * 2 + [anywhere] * pieces,
+        out_specs=[vmem()] * len(out_shape),
+        scratch_shapes=scratch,
         compiler_params=params,
         name="radial",
-    )(got.reshape(n, a_loc, r_loc, theta, c), radial_taps)
+    )(got.reshape(n, a_loc, r_loc, theta, c), radial_taps, *line)
+    back = lax.all_to_all(mixed.reshape(axial, rows, c), "row", split_axis=0, concat_axis=0, tiled=True)
+    vectors = [v[None, :] for v in (conv_bias, ln_gain, ln_bias, b_out, layer_scale)]
+    axial_taps, consts = pl.pallas_call(
+        stage_kernel,
+        out_shape=[jax.ShapeDtypeStruct(axial_taps.shape, jnp.float32), jax.ShapeDtypeStruct((8, c), jnp.float32)],
+        in_specs=[anywhere] * 7,
+        out_specs=[vmem()] * 2,
+        scratch_shapes=[pltpu.VMEM((5, 1, c), jnp.float32), pltpu.SemaphoreType.DMA((6,))],
+        name="stage",
+    )(mixed, axial_taps, *vectors)
     if spread:
-        line = [lax.optimization_barrier((h, mixed))[0] for h in line]
-        across = side + [move(h, 1, by) for by in range(1, inner) for h in line]
-        twin = [move(h, 2) for h in [own] + line]
-    back = lax.all_to_all(mixed.reshape(axial, rows, c), "row", split_axis=0, concat_axis=0, tiled=True)
-    if spread:
-        across, back = lax.optimization_barrier((across, back))
-        slots = [own] + line + across + twin + [move(h, 2) for h in across]
+        (block,) = joined
+        others = [move(block, 1, 0, swap=True), move(block, 1, 1), move(block, 1, 1, swap=True)]
+        twin = [move(block, 2, 1)]
+        others, back, axial_taps, consts = lax.optimization_barrier((others, back, axial_taps, consts))
+        slots = [block] + others + twin + [move(h, 2, 1) for h in others]
     normed = pl.pallas_call(
         axial_kernel,
         out_shape=jax.ShapeDtypeStruct((axial * rows, c), jnp.bfloat16),
@@ -264,4 +296,4 @@
         P(),
     )
     out_specs = P("groups", "row", None, None)
-    return jax.shard_map(partial(local, mesh.shape["row"]), mesh=mesh, in_specs=in_specs, out_specs=out_specs, check_vma=False)
+    return jax.shard_map(partial(local, mesh.shape["groups"], mesh.shape["row"]), mesh=mesh, in_specs=in_specs, out_specs=out_specs, check_vma=False)

time: 47.4 us -> 44.5 us (0.939)
  blocking collectives: 15.5 us -> 0 us
  starting transfers between devices: 14.9 us -> 20 us
  waiting for transfers between devices: 6.94 us -> 11.8 us
  Pallas kernels: 7.99 us -> 9.76 us
  local copies, waits for them, and re-layouts: 1.46 us -> 2.24 us
    all_to_all x1 -> x0, blocking collectives: 15.5 us -> none  [local(): lax.all_to_all(features, 'row', split_axis=0, concat_axis=0, tiled=True)]
    all_to_all x0 -> x1, starting transfers between devices: none -> 7.39 us  [local(): lax.all_to_all(features, 'row', split_axis=0, concat_axis=0, tiled=True)]
    ppermute x15 -> x10, waiting for transfers between devices: 6.94 us -> 11.8 us  [the longest x8 8.11 us: move(): return lax.ppermute(piece, 'row', list(enumerate(targets)))]
    ppermute x15 -> x10, starting transfers between devices: 11.4 us -> 9.11 us  [the longest x8 5.83 us: move(): return lax.ppermute(piece, 'row', list(enumerate(targets)))]
    pallas_call x2 -> x3, Pallas kernels: 3.95 us -> 5.66 us  [the longest x1 2.2 us: local(): pl.pallas_call(partial(radial_kernel, pieces), out_shape=out_shape, in_sp...]
    unnamed x10, local copies, waits for them, and re-layouts: 1.46 us -> 2.24 us
  transfers between devices with their start and end apart: 16 -> 12, of which waited for: 4 -> 5; matrix products, arithmetic and copies ran while one was open for 0% -> 0% of each run, Pallas kernels for 7% -> 10%
where the time goes in v6:
time: 44.5 us; the launch traced here: 43.9 us
  starting transfers between devices  20 us (45%)
  waiting for transfers between devices  11.8 us (27%)
  Pallas kernels  9.76 us (22%)
  local copies, waits for them, and re-layouts  2.24 us (5%)
    ppermute x8, waiting for transfers between devices, move(): return lax.ppermute(piece, 'row', list(enumerate(targets)))  8.11 us
    all_to_all x1, starting transfers between devices, local(): lax.all_to_all(features, 'row', split_axis=0, concat_axis=0, tiled=True)  7.39 us
    ppermute x8, starting transfers between devices, move(): return lax.ppermute(piece, 'row', list(enumerate(targets)))  5.83 us
    ppermute x2, waiting for transfers between devices, move(): return lax.ppermute(piece, ('groups', 'row'), pairs)  3.66 us
    all_to_all x1, starting transfers between devices, local(): lax.all_to_all(mixed.reshape(axial, rows, c), 'row', split_axis=0, concat...  3.52 us
    ppermute x2, starting transfers between devices, move(): return lax.ppermute(piece, ('groups', 'row'), pairs)  3.28 us
    pallas_call x1, Pallas kernels, local(): pl.pallas_call(mlp_kernel, out_shape=jax.ShapeDtypeStruct(features.shape,...  3.15 us
    unnamed x10, local copies, waits for them, and re-layouts  2.24 us
  transfers between devices with their start and end apart: 12, of which 5 were waited for; matrix products, arithmetic and copies ran while one was open for 0% of the time, Pallas kernels for 10%

profile of v6, /device:TPU:0, one launch (start us, length us, event | category | flops | bytes accessed | tf_op | source)
XLA Modules:
  0.0 43.9 jit_solution(9343782970548792214)
XLA Ops:
  0.0 7.4 %all-to-all-start = ((bf16[32,2,4,256]{3,2,1,0:T(4,128)(2,1)}), bf16[32,2,4,256]{3,2,1,0:T(4,128)(2,1)S(1)}, u32[]{:S(2)}, u32[]{:S(2)}) async-start(bf16[32,2,4,256]{3,2,1,0:T(4,128)(2,1)} %feat_ref.1), calls=%async_computation | async-start | bytes 262144 | tf_op jit(solution)/shard_map/all_to_all | solution.py:223
  7.4 0.0 copy-start.3
  7.4 2.0 %pack.1.rest_0_ = bf16[1,80,256]{2,1,0:T(8,128)(2,1)} custom-call(bf16[64]{0:T(256)(128)(2,1)} %b_ref.1, bf16[64,256]{1,0:T(8,128)(2,1)} %w_in_ref.1, bf16[64,256]{1,0:T(8,128)(2,1)} %w_out_ref.1), custom_call_target="tpu_custom_call" | custom-call | tf_op jit(solution)/shard_map/pack/pallas_call | solution.py:207
  9.4 3.8 %collective-permute-start.2 = (bf16[1,80,256]{2,1,0:T(8,128)(2,1)}, bf16[1,80,256]{2,1,0:T(8,128)(2,1)S(1)}, u32[]{:S(2)}, u32[]{:S(2)}) collective-permute-start(bf16[1,80,256]{2,1,0:T(8,128)(2,1)} %pack.1.rest_0_), channel_id=1, source_target_pairs={{0,12},{1,13},{2,14},{3,15},{4,0},{5,1},{6,2},{7,3},{8,4},{9,5},{1... | collective-permute-start | bytes 122888 | tf_op jit(solution)/shard_map/ppermute | solution.py:200
  13.2 0.0 collective-permute-start.1
  13.2 1.1 %collective-permute-start = (bf16[1,80,256]{2,1,0:T(8,128)(2,1)}, bf16[1,80,256]{2,1,0:T(8,128)(2,1)S(1)}, u32[]{:S(2)}, u32[]{:S(2)}) collective-permute-start(bf16[1,80,256]{2,1,0:T(8,128)(2,1)} %pack.1.rest_0_), channel_id=1, source_target_pairs={{0,4},{1,5},{2,6},{3,7},{4,8},{5,9},{6,10},{7,11},{8,12},{9,13},{1... | collective-permute-start | bytes 122888 | tf_op jit(solution)/shard_map/ppermute | solution.py:200
  14.4 1.1 %collective-permute-done.2.rest_3_ = bf16[1,80,256]{2,1,0:T(8,128)(2,1)S(1)} collective-permute-done((bf16[1,80,256]{2,1,0:T(8,128)(2,1)}, bf16[1,80,256]{2,1,0:T(8,128)(2,1)S(1)}, u32[]{:S(2)}, u32[]{:S(2)}) %collective-permute-start.2) | collective-permute-done | bytes 40992 | tf_op jit(solution)/shard_map/ppermute | solution.py:200
  15.5 3.1 %collective-permute-done.1.rest_2_ = bf16[1,80,256]{2,1,0:T(8,128)(2,1)S(1)} collective-permute-done((bf16[1,80,256]{2,1,0:T(8,128)(2,1)}, bf16[1,80,256]{2,1,0:T(8,128)(2,1)S(1)}, u32[]{:S(2)}, u32[]{:S(2)}) %collective-permute-start.1) | collective-permute-done | bytes 40992 | tf_op jit(solution)/shard_map/ppermute | solution.py:200
  18.6 0.7 %collective-permute-done.rest_1_ = bf16[1,80,256]{2,1,0:T(8,128)(2,1)S(1)} collective-permute-done((bf16[1,80,256]{2,1,0:T(8,128)(2,1)}, bf16[1,80,256]{2,1,0:T(8,128)(2,1)S(1)}, u32[]{:S(2)}, u32[]{:S(2)}) %collective-permute-start) | collective-permute-done | bytes 40992 | tf_op jit(solution)/shard_map/ppermute | solution.py:200
  19.2 0.0 all-to-all-done
  19.3 0.8 %copy-done.1 = bf16[1,80,256]{2,1,0:T(8,128)(2,1)S(1)} copy-done((bf16[1,80,256]{2,1,0:T(8,128)(2,1)S(1)}, bf16[1,80,256]{2,1,0:T(8,128)(2,1)}, u32[]{:S(2)}) %copy-start.1) | copy-done | bytes 40984
  20.0 2.2 %radial.1 = (bf16[16,2,8,256]{3,2,1,0:T(8,128)(2,1)}, bf16[4,80,256]{2,1,0:T(8,128)(2,1)S(1)}) custom-call(bf16[16,2,2,4,256]{4,3,2,1,0:T(4,128)(2,1)S(1)} %bitcast.7, f32[31,256]{1,0:T(8,128)S(1)} %copy-done.3, bf16[1,80,256]{2,1,0:T(8,128)(2,1)S(1)} %copy-done.1, bf16[1,80,256]{2,1,0:T(8,128)(2,1)S(1)} %collective-permute-done.rest_1_, ...), custom_call_target="tpu_custom_call" | custom-call | tf_op jit(solution)/shard_map/radial/pallas_call | solution.py:231
  22.2 3.5 %all-to-all-start.1 = ((bf16[32,8,256]{2,1,0:T(8,128)(2,1)}), bf16[32,8,256]{2,1,0:T(8,128)(2,1)S(1)}, u32[]{:S(2)}, u32[]{:S(2)}) async-start(bf16[32,8,256]{2,1,0:T(8,128)(2,1)} %bitcast.1), calls=%async_computation.1 | async-start | bytes 262144 | tf_op jit(solution)/shard_map/all_to_all | solution.py:240
  25.8 2.7 %collective-permute-start.5 = (bf16[4,80,256]{2,1,0:T(8,128)(2,1)S(1)}, bf16[4,80,256]{2,1,0:T(8,128)(2,1)S(1)}, u32[]{:S(2)}, u32[]{:S(2)}) collective-permute-start(bf16[4,80,256]{2,1,0:T(8,128)(2,1)S(1)} %get-tuple-element.15.rest_0_), channel_id=1, source_target_pairs={{0,18},{1,19},{2,16},{3,17},{4,22},{5,23},{6,20},{7,21},{8,26},{9,... | collective-permute-start | bytes 491528 | tf_op jit(solution)/shard_map/ppermute | solution.py:202
  28.5 0.3 collective-permute-start.4
  28.8 0.5 %collective-permute-start.3 = (bf16[4,80,256]{2,1,0:T(8,128)(2,1)S(1)}, bf16[4,80,256]{2,1,0:T(8,128)(2,1)S(1)}, u32[]{:S(2)}, u32[]{:S(2)}) collective-permute-start(bf16[4,80,256]{2,1,0:T(8,128)(2,1)S(1)} %get-tuple-element.15.rest_0_), channel_id=1, source_target_pairs={{0,16},{1,17},{2,18},{3,19},{4,20},{5,21},{6,22},{7,23},{8,24},{9,... | collective-permute-start | bytes 491528 | tf_op jit(solution)/shard_map/ppermute | solution.py:202
  29.3 0.0 collective-permute-start.6
  29.3 1.4 %stage.1 = (f32[31,256]{1,0:T(8,128)}, f32[8,256]{1,0:T(8,128)}) custom-call(bf16[16,2,8,256]{3,2,1,0:T(8,128)(2,1)} %get-tuple-element.16.order_ref, f32[31,256]{1,0:T(8,128)} %taps_ref.3, f32[1,256]{1,0:T(1,128)} %bitcast.8, f32[1,256]{1,0:T(1,128)} %bitcast.9, f32[1,256]{1,0:T(1,128)} %bitcast.10, f32[1,256]{1,0:T(1,128)} %bitcast.11, f32[1,256]{1,0:T(1,128)} %bitcast.12), custom_call_target="tpu_custom_call" | custom-call | tf_op jit(solution)/shard_map/stage/pallas_call | solution.py:242
  30.8 3.7 %collective-permute-done.5.rest_3_ = bf16[4,80,256]{2,1,0:T(8,128)(2,1)S(1)} collective-permute-done((bf16[4,80,256]{2,1,0:T(8,128)(2,1)S(1)}, bf16[4,80,256]{2,1,0:T(8,128)(2,1)S(1)}, u32[]{:S(2)}, u32[]{:S(2)}) %collective-permute-start.5) | collective-permute-done | bytes 163872 | tf_op jit(solution)/shard_map/ppermute | solution.py:202
  34.4 3.2 %collective-permute-done.4.rest_2_ = bf16[4,80,256]{2,1,0:T(8,128)(2,1)S(1)} collective-permute-done((bf16[4,80,256]{2,1,0:T(8,128)(2,1)S(1)}, bf16[4,80,256]{2,1,0:T(8,128)(2,1)S(1)}, u32[]{:S(2)}, u32[]{:S(2)}) %collective-permute-start.4) | collective-permute-done | bytes 163872 | tf_op jit(solution)/shard_map/ppermute | solution.py:200
  37.6 0.0 collective-permute-done.3.rest_1_
  37.6 0.0 all-to-all-done.1.z_ref
  37.6 0.1 collective-permute-start.7
  37.7 0.5 %collective-permute-start.8 = (bf16[4,80,256]{2,1,0:T(8,128)(2,1)S(1)}, bf16[4,80,256]{2,1,0:T(8,128)(2,1)S(1)}, u32[]{:S(2)}, u32[]{:S(2)}) collective-permute-start(bf16[4,80,256]{2,1,0:T(8,128)(2,1)S(1)} %collective-permute-done.4.rest_2_), channel_id=1, source_target_pairs={{0,1},{1,0},{2,3},{3,2},{4,5},{5,4},{6,7},{7,6},{8,9},{9,8},{10,11... | collective-permute-start | bytes 491528 | tf_op jit(solution)/shard_map/ppermute | solution.py:200
  38.2 0.1 collective-permute-start.9
  38.3 0.7 %copy-done.2 = f32[8,256]{1,0:T(8,128)S(1)} copy-done((f32[8,256]{1,0:T(8,128)S(1)}, f32[8,256]{1,0:T(8,128)}, u32[]{:S(2)}) %copy-start.2) | copy-done | bytes 8216
  39.0 0.8 %copy-done.4 = f32[31,256]{1,0:T(8,128)S(1)} copy-done((f32[31,256]{1,0:T(8,128)S(1)}, f32[31,256]{1,0:T(8,128)}, u32[]{:S(2)}) %copy-start.4) | copy-done | bytes 31768
  39.8 0.9 %axial.1.normed_ref = bf16[256,256]{1,0:T(8,128)(2,1)S(1)} custom-call(bf16[32,8,256]{2,1,0:T(8,128)(2,1)S(1)} %all-to-all-done.1.z_ref, f32[31,256]{1,0:T(8,128)S(1)} %copy-done.4, f32[8,256]{1,0:T(8,128)S(1)} %copy-done.2), custom_call_target="tpu_custom_call" | custom-call | tf_op jit(solution)/shard_map/axial/pallas_call | solution.py:256
  40.7 0.0 collective-permute-done.6.rest_4_
  40.7 0.0 collective-permute-done.8.rest_6_
  40.7 0.0 collective-permute-done.9.rest_7_
  40.8 3.2 %mlp.1 = bf16[32,2,4,256]{3,2,1,0:T(4,128)(2,1)} custom-call(bf16[256,256]{1,0:T(8,128)(2,1)S(1)} %axial.1.normed_ref, bf16[32,2,4,256]{3,2,1,0:T(4,128)(2,1)S(1)} %copy-done, f32[8,256]{1,0:T(8,128)S(1)} %copy-done.2, bf16[4,80,256]{2,1,0:T(8,128)(2,1)S(1)} %get-tuple-element.15.rest_0_, bf16[4,80,256]{2,1,0:T(8,128)(2,1)S(1)} %collective-permute-done.3.rest_1_, ...), custom_call_target="tpu_custom_call" | custom-call | tf_op jit(solution)/shard_map/mlp/pallas_call | solution.py:269
  (7 shorter events, 0.0 us)
Async XLA Ops:
  0.0 19.2 %all-to-all-start = ((bf16[32,2,4,256]{3,2,1,0:T(4,128)(2,1)}), bf16[32,2,4,256]{3,2,1,0:T(4,128)(2,1)S(1)}, u32[]{:S(2)}, u32[]{:S(2)}) async-start(bf16[32,2,4,256]{3,2,1,0:T(4,128)(2,1)} %feat_ref.1), calls=%async_computation | async-start | bytes 262144 | tf_op jit(solution)/shard_map/all_to_all | solution.py:223
  7.4 11.9 %copy-start.3 = (f32[31,256]{1,0:T(8,128)S(1)}, f32[31,256]{1,0:T(8,128)}, u32[]{:S(2)}) copy-start(f32[31,256]{1,0:T(8,128)} %taps_ref.2) | copy-start | bytes 95236
  9.4 6.0 %collective-permute-start.2 = (bf16[1,80,256]{2,1,0:T(8,128)(2,1)}, bf16[1,80,256]{2,1,0:T(8,128)(2,1)S(1)}, u32[]{:S(2)}, u32[]{:S(2)}) collective-permute-start(bf16[1,80,256]{2,1,0:T(8,128)(2,1)} %pack.1.rest_0_), channel_id=1, source_target_pairs={{0,12},{1,13},{2,14},{3,15},{4,0},{5,1},{6,2},{7,3},{8,4},{9,5},{1... | collective-permute-start | bytes 122888 | tf_op jit(solution)/shard_map/ppermute | solution.py:200
  13.2 5.4 %collective-permute-start.1 = (bf16[1,80,256]{2,1,0:T(8,128)(2,1)}, bf16[1,80,256]{2,1,0:T(8,128)(2,1)S(1)}, u32[]{:S(2)}, u32[]{:S(2)}) collective-permute-start(bf16[1,80,256]{2,1,0:T(8,128)(2,1)} %pack.1.rest_0_), channel_id=1, source_target_pairs={{0,8},{1,9},{2,10},{3,11},{4,12},{5,13},{6,14},{7,15},{8,0},{9,1},... | collective-permute-start | bytes 122888 | tf_op jit(solution)/shard_map/ppermute | solution.py:200
  13.2 6.0 %collective-permute-start = (bf16[1,80,256]{2,1,0:T(8,128)(2,1)}, bf16[1,80,256]{2,1,0:T(8,128)(2,1)S(1)}, u32[]{:S(2)}, u32[]{:S(2)}) collective-permute-start(bf16[1,80,256]{2,1,0:T(8,128)(2,1)} %pack.1.rest_0_), channel_id=1, source_target_pairs={{0,4},{1,5},{2,6},{3,7},{4,8},{5,9},{6,10},{7,11},{8,12},{9,13},{1... | collective-permute-start | bytes 122888 | tf_op jit(solution)/shard_map/ppermute | solution.py:200
  19.2 0.8 %copy-start.1 = (bf16[1,80,256]{2,1,0:T(8,128)(2,1)S(1)}, bf16[1,80,256]{2,1,0:T(8,128)(2,1)}, u32[]{:S(2)}) copy-start(bf16[1,80,256]{2,1,0:T(8,128)(2,1)} %pack.1.rest_0_) | copy-start | bytes 122884
  22.2 15.4 %all-to-all-start.1 = ((bf16[32,8,256]{2,1,0:T(8,128)(2,1)}), bf16[32,8,256]{2,1,0:T(8,128)(2,1)S(1)}, u32[]{:S(2)}, u32[]{:S(2)}) async-start(bf16[32,8,256]{2,1,0:T(8,128)(2,1)} %bitcast.1), calls=%async_computation.1 | async-start | bytes 262144 | tf_op jit(solution)/shard_map/all_to_all | solution.py:240
  25.8 8.7 %collective-permute-start.5 = (bf16[4,80,256]{2,1,0:T(8,128)(2,1)S(1)}, bf16[4,80,256]{2,1,0:T(8,128)(2,1)S(1)}, u32[]{:S(2)}, u32[]{:S(2)}) collective-permute-start(bf16[4,80,256]{2,1,0:T(8,128)(2,1)S(1)} %get-tuple-element.15.rest_0_), channel_id=1, source_target_pairs={{0,18},{1,19},{2,16},{3,17},{4,22},{5,23},{6,20},{7,21},{8,26},{9,... | collective-permute-start | bytes 491528 | tf_op jit(solution)/shard_map/ppermute | solution.py:202
  28.5 9.1 %collective-permute-start.4 = (bf16[4,80,256]{2,1,0:T(8,128)(2,1)S(1)}, bf16[4,80,256]{2,1,0:T(8,128)(2,1)S(1)}, u32[]{:S(2)}, u32[]{:S(2)}) collective-permute-start(bf16[4,80,256]{2,1,0:T(8,128)(2,1)S(1)} %get-tuple-element.15.rest_0_), channel_id=1, source_target_pairs={{0,2},{1,3},{2,0},{3,1},{4,6},{5,7},{6,4},{7,5},{8,10},{9,11},{10,... | collective-permute-start | bytes 491528 | tf_op jit(solution)/shard_map/ppermute | solution.py:200
  28.8 8.9 %collective-permute-start.3 = (bf16[4,80,256]{2,1,0:T(8,128)(2,1)S(1)}, bf16[4,80,256]{2,1,0:T(8,128)(2,1)S(1)}, u32[]{:S(2)}, u32[]{:S(2)}) collective-permute-start(bf16[4,80,256]{2,1,0:T(8,128)(2,1)S(1)} %get-tuple-element.15.rest_0_), channel_id=1, source_target_pairs={{0,16},{1,17},{2,18},{3,19},{4,20},{5,21},{6,22},{7,23},{8,24},{9,... | collective-permute-start | bytes 491528 | tf_op jit(solution)/shard_map/ppermute | solution.py:202
  29.3 11.4 %collective-permute-start.6 = (bf16[4,80,256]{2,1,0:T(8,128)(2,1)S(1)}, bf16[4,80,256]{2,1,0:T(8,128)(2,1)S(1)}, u32[]{:S(2)}, u32[]{:S(2)}) collective-permute-start(bf16[4,80,256]{2,1,0:T(8,128)(2,1)S(1)} %get-tuple-element.15.rest_0_), channel_id=1, source_target_pairs={{0,1},{1,0},{2,3},{3,2},{4,5},{5,4},{6,7},{7,6},{8,9},{9,8},{10,11... | collective-permute-start | bytes 491528 | tf_op jit(solution)/shard_map/ppermute | solution.py:200
  37.6 3.1 %copy-start = (bf16[32,2,4,256]{3,2,1,0:T(4,128)(2,1)S(1)}, bf16[32,2,4,256]{3,2,1,0:T(4,128)(2,1)}, u32[]{:S(2)}) copy-start(bf16[32,2,4,256]{3,2,1,0:T(4,128)(2,1)} %feat_ref.1) | copy-start | bytes 393220
  37.6 3.1 %collective-permute-start.7 = (bf16[4,80,256]{2,1,0:T(8,128)(2,1)S(1)}, bf16[4,80,256]{2,1,0:T(8,128)(2,1)S(1)}, u32[]{:S(2)}, u32[]{:S(2)}) collective-permute-start(bf16[4,80,256]{2,1,0:T(8,128)(2,1)S(1)} %collective-permute-done.3.rest_1_), channel_id=1, source_target_pairs={{0,1},{1,0},{2,3},{3,2},{4,5},{5,4},{6,7},{7,6},{8,9},{9,8},{10,11... | collective-permute-start | bytes 491528 | tf_op jit(solution)/shard_map/ppermute | solution.py:200
  37.7 3.0 %collective-permute-start.8 = (bf16[4,80,256]{2,1,0:T(8,128)(2,1)S(1)}, bf16[4,80,256]{2,1,0:T(8,128)(2,1)S(1)}, u32[]{:S(2)}, u32[]{:S(2)}) collective-permute-start(bf16[4,80,256]{2,1,0:T(8,128)(2,1)S(1)} %collective-permute-done.4.rest_2_), channel_id=1, source_target_pairs={{0,1},{1,0},{2,3},{3,2},{4,5},{5,4},{6,7},{7,6},{8,9},{9,8},{10,11... | collective-permute-start | bytes 491528 | tf_op jit(solution)/shard_map/ppermute | solution.py:200
  38.2 2.5 %collective-permute-start.9 = (bf16[4,80,256]{2,1,0:T(8,128)(2,1)S(1)}, bf16[4,80,256]{2,1,0:T(8,128)(2,1)S(1)}, u32[]{:S(2)}, u32[]{:S(2)}) collective-permute-start(bf16[4,80,256]{2,1,0:T(8,128)(2,1)S(1)} %collective-permute-done.5.rest_3_), channel_id=1, source_target_pairs={{0,1},{1,0},{2,3},{3,2},{4,5},{5,4},{6,7},{7,6},{8,9},{9,8},{10,11... | collective-permute-start | bytes 491528 | tf_op jit(solution)/shard_map/ppermute | solution.py:200
  38.3 0.7 %copy-start.2 = (f32[8,256]{1,0:T(8,128)S(1)}, f32[8,256]{1,0:T(8,128)}, u32[]{:S(2)}) copy-start(f32[8,256]{1,0:T(8,128)} %get-tuple-element.21.consts_ref) | copy-start | bytes 24580
  39.0 0.8 %copy-start.4 = (f32[31,256]{1,0:T(8,128)S(1)}, f32[31,256]{1,0:T(8,128)}, u32[]{:S(2)}) copy-start(f32[31,256]{1,0:T(8,128)} %get-tuple-element.20.taps_ref) | copy-start | bytes 95236

commit v7 on v5

--- a/solution.py
+++ b/solution.py
@@ -66,8 +66,11 @@
     lax.fori_loop(0, n, step, 0)
 
 
-def axial_kernel(z_ref, taps_ref, consts_ref, out_ref, padded, summed):
+def tail_kernel(z_ref, feat_ref, taps_ref, consts_ref, w_ref, out_ref, padded, branch, slots, sem):
+    fetch = pltpu.make_async_copy(w_ref, slots, sem)
+    fetch.start()
     axial, rows, c = z_ref.shape
+    theta = rows // 2
     taps = taps_ref.shape[0]
     half = taps // 2
     zeros = jnp.zeros((half, rows, c), jnp.float32)
@@ -81,45 +84,23 @@
         total = jnp.zeros((block, rows, c), jnp.float32)
         for k in range(taps):
             total = total + padded[pl.ds(base + k, block)] * taps_ref[k : k + 1, :]
-        summed[pl.ds(base, block)] = total
+        branch[pl.ds(base, block)] = total
         return carry
 
     lax.fori_loop(0, axial // block, conv, 0)
-
-    def norm(i, carry):
-        v = (summed[pl.ds(i * 32, 32)] + consts_ref[0:1, :]).reshape(32 * rows, c)
+    fetch.wait()
+    per = c // SLOT
+    lane_slot = lax.broadcasted_iota(jnp.int32, (1, c), 1) // SLOT
+    planes = 32
+
+    def mlp(i, carry):
+        v = (branch[pl.ds(i * planes, planes)] + consts_ref[0:1, :]).reshape(planes * rows, c)
         v = v.astype(jnp.bfloat16).astype(jnp.float32)
         mean = jnp.mean(v, axis=-1, keepdims=True)
         centred = v - mean
         var = jnp.mean(centred * centred, axis=-1, keepdims=True)
-        normed = centred * lax.rsqrt(var + 1e-06) * consts_ref[1:2, :] + consts_ref[2:3, :]
-        at = pl.multiple_of(i * 32 * rows, 32 * rows)
-        out_ref[pl.ds(at, 32 * rows), :] = normed.astype(out_ref.dtype)
-        return carry
-
-    lax.fori_loop(0, axial // 32, norm, 0)
-
-
-def mlp_kernel(normed_ref, feat_ref, consts_ref, *rest):
-    *w_refs, out_ref, slots, branch, sems = rest
-    axial, _, theta, c = feat_ref.shape
-    rows = 2 * theta
-    per = c // SLOT
-    lane_slot = lax.broadcasted_iota(jnp.int32, (1, c), 1) // SLOT
-    token_block = 32 * rows
-    copies, at = [], 0
-    for i, w_ref in enumerate(w_refs):
-        copies.append(pltpu.make_async_copy(w_ref, slots.at[at : at + w_ref.shape[0]], sems.at[i]))
-        at += w_ref.shape[0]
-    for copy in copies:
-        copy.start()
-    for copy in copies:
-        copy.wait()
-
-    def mlp(i, carry):
-        base = pl.multiple_of(i * token_block, token_block)
-        normed = normed_ref[pl.ds(base, token_block), :]
-        total = jnp.zeros((token_block, c), jnp.float32)
+        normed = (centred * lax.rsqrt(var + 1e-06) * consts_ref[1:2, :] + consts_ref[2:3, :]).astype(jnp.bfloat16)
+        total = jnp.zeros((planes * rows, c), jnp.float32)
         for g in range(slots.shape[0] // per):
             own = slice(g * per, (g + 1) * per)
             w_in = slots[own, 0:SLOT, :].reshape(per * SLOT, c)
@@ -133,35 +114,16 @@
             hidden = (0.5 * u * (1.0 + jnp.tanh(0.7978845608028654 * (u + 0.044715 * u * u * u)))).astype(jnp.bfloat16)
             total = total + jnp.dot(hidden, w_out, preferred_element_type=jnp.float32)
         result = (consts_ref[4:5, :] * (total + consts_ref[3:4, :])).astype(jnp.bfloat16).astype(jnp.float32)
-        branch[pl.ds(i * 32, 32)] = result.reshape(32, rows, c)
+        branch[pl.ds(i * planes, planes)] = result.reshape(planes, rows, c)
         return carry
 
-    if axial == 32:
+    if axial == planes:
         mlp(0, 0)
     else:
-        lax.fori_loop(0, axial // 32, mlp, 0)
+        lax.fori_loop(0, axial // planes, mlp, 0)
     for r in range(2):
         got = branch[:, r * theta : (r + 1) * theta, :]
         out_ref[:, r] = (feat_ref[:, r].astype(jnp.float32) + got).astype(out_ref.dtype)
-
-
-def digits(n):
-    chips = n // 2
-    inner = 1
-    while inner * inner * 4 <= chips:
-        inner *= 2
-    return chips // inner, inner, 2
-
-
-def shifted(n, digit, by):
-    sizes = digits(n)
-    stride = [sizes[1] * sizes[2], sizes[2], 1][digit]
-    pairs = []
-    for i in range(n):
-        at = (i // stride) % sizes[digit]
-        to = (at + by) % sizes[digit]
-        pairs.append((i, i + (to - at) * stride))
-    return pairs
 
 
 def local(n, features, axial_taps, radial_taps, conv_bias, ln_gain, ln_bias, w_in, b_in, w_out, b_out, layer_scale):
@@ -172,10 +134,6 @@
     spread = hid_loc == SLOT
     params = pltpu.CompilerParams(vmem_limit_bytes=48 * 1024 * 1024)
 
-    def move(piece, digit, by=1):
-        return lax.ppermute(piece, "row", shifted(n, digit, by))
-
-    outer, inner, _ = digits(n)
     anywhere = pl.BlockSpec(memory_space=pl.ANY)
     vectors = [v[None, :] for v in (conv_bias, ln_gain, ln_bias, b_out, layer_scale)]
     slot_shape = (2 * SLOT + EXTRA, c)
@@ -192,15 +150,14 @@
             scratch_shapes=[pltpu.VMEM((5, 1, c), jnp.float32), pltpu.SemaphoreType.DMA((8,))],
             name="pack",
         )(b_in, w_in, w_out, axial_taps, *vectors)
-        line = [move(own, 0, by) for by in range(1, outer)]
-        side = [move(own, 1, by) for by in range(1, inner)]
+        slots = lax.all_gather(own, "row", axis=0, tiled=True)
     else:
         consts = jnp.concatenate(vectors + [jnp.zeros((3, c), jnp.float32)], axis=0)
         w_all = lax.all_gather(w_in, "row", axis=0, tiled=True).reshape(-1, SLOT, c)
         o_all = lax.all_gather(w_out, "row", axis=0, tiled=True).reshape(-1, SLOT, c)
         b_all = lax.all_gather(b_in, "row", axis=0, tiled=True).reshape(-1, 1, SLOT)
         b_all = jnp.broadcast_to(jnp.tile(b_all, (1, 1, c // SLOT)), (w_all.shape[0], EXTRA, c))
-        slots = [jnp.concatenate([w_all, o_all, b_all], axis=1)]
+        slots = jnp.concatenate([w_all, o_all, b_all], axis=1)
 
     got = lax.all_to_all(features, "row", split_axis=0, concat_axis=0, tiled=True)
     pad = (radial_taps.shape[0] + 1) // 4
@@ -213,40 +170,21 @@
         compiler_params=params,
         name="radial",
     )(got.reshape(n, a_loc, r_loc, theta, c), radial_taps)
-    if spread:
-        line = [lax.optimization_barrier((h, mixed))[0] for h in line]
-        across = side + [move(h, 1, by) for by in range(1, inner) for h in line]
-        twin = [move(h, 2) for h in [own] + line]
     back = lax.all_to_all(mixed.reshape(axial, rows, c), "row", split_axis=0, concat_axis=0, tiled=True)
-    if spread:
-        across, back = lax.optimization_barrier((across, back))
-        slots = [own] + line + across + twin + [move(h, 2) for h in across]
-    normed = pl.pallas_call(
-        axial_kernel,
-        out_shape=jax.ShapeDtypeStruct((axial * rows, c), jnp.bfloat16),
-        in_specs=[vmem()] * 3,
+    return pl.pallas_call(
+        tail_kernel,
+        out_shape=jax.ShapeDtypeStruct(features.shape, jnp.bfloat16),
+        in_specs=[vmem()] * 4 + [anywhere],
         out_specs=vmem(),
         scratch_shapes=[
             pltpu.VMEM((axial + axial_taps.shape[0] - 1, rows, c), jnp.float32),
             pltpu.VMEM((axial, rows, c), jnp.float32),
+            pltpu.VMEM(slots.shape, jnp.bfloat16),
+            pltpu.SemaphoreType.DMA(()),
         ],
         compiler_params=params,
-        name="axial",
-    )(back, axial_taps, consts)
-    count = sum(h.shape[0] for h in slots)
-    return pl.pallas_call(
-        mlp_kernel,
-        out_shape=jax.ShapeDtypeStruct(features.shape, jnp.bfloat16),
-        in_specs=[vmem()] * 3 + [anywhere] * len(slots),
-        out_specs=vmem(),
-        scratch_shapes=[
-            pltpu.VMEM((count,) + slot_shape, jnp.bfloat16),
-            pltpu.VMEM((axial, rows, c), jnp.float32),
-            pltpu.SemaphoreType.DMA((len(slots),)),
-        ],
-        compiler_params=params,
-        name="mlp",
-    )(normed, features, consts, *slots)
+        name="tail",
+    )(back, features, axial_taps, consts, slots)
 
 
 def solution(mesh):

time: 47.4 us -> 64.2 us (1.35)
  starting transfers between devices: 14.9 us -> 0.01 us
  between operations: 0.1 us -> 13.4 us
  blocking collectives: 15.5 us -> 25.9 us
  waiting for transfers between devices: 6.94 us -> 14.2 us
  local copies, waits for them, and re-layouts: 1.46 us -> 4.39 us
  Pallas kernels: 7.99 us -> 5.79 us
    all_gather x0 -> x1, waiting for transfers between devices: none -> 14.2 us  [local(): slots = lax.all_gather(own, 'row', axis=0, tiled=True)]
    ppermute x15 -> x0, starting transfers between devices: 11.4 us -> none  [move(): return lax.ppermute(piece, 'row', shifted(n, digit, by))]
    all_to_all x0 -> x1, blocking collectives: none -> 10.5 us  [local(): lax.all_to_all(mixed.reshape(axial, rows, c), 'row', split_axis=0, concat...]
    ppermute x15 -> x0, waiting for transfers between devices: 6.94 us -> none  [move(): return lax.ppermute(piece, 'row', shifted(n, digit, by))]
    all_to_all x1 -> x0, starting transfers between devices: 3.51 us -> none  [local(): lax.all_to_all(mixed.reshape(axial, rows, c), 'row', split_axis=0, concat...]
    unnamed x10, local copies, waits for them, and re-layouts: 1.46 us -> 4.39 us
    pallas_call x2 -> x1, Pallas kernels: 4.04 us -> 2.51 us  [local(): pl.pallas_call(tail_kernel, out_shape=jax.ShapeDtypeStruct(features.shape...]
    pallas_call x1, Pallas kernels: 1.77 us -> 1.12 us  [local(): pl.pallas_call(radial_kernel, out_shape=jax.ShapeDtypeStruct((n, a_loc, r...]
  transfers between devices with their start and end apart: 16 -> 1, of which waited for: 4 -> 1; matrix products, arithmetic and copies ran while one was open for 0% -> 0% of each run, Pallas kernels for 7% -> 2%
where the time goes in v7:
time: 64.2 us; the launch traced here: 63.7 us
  blocking collectives  25.9 us (40%)
  waiting for transfers between devices  14.2 us (22%)
  between operations  13.4 us (21%)
  Pallas kernels  5.79 us (9%)
  local copies, waits for them, and re-layouts  4.39 us (7%)
    all_to_all x1, blocking collectives, local(): lax.all_to_all(features, 'row', split_axis=0, concat_axis=0, tiled=True)  15.3 us
    all_gather x1, waiting for transfers between devices, local(): slots = lax.all_gather(own, 'row', axis=0, tiled=True)  14.2 us
    all_to_all x1, blocking collectives, local(): lax.all_to_all(mixed.reshape(axial, rows, c), 'row', split_axis=0, concat...  10.5 us
    unnamed x10, local copies, waits for them, and re-layouts  4.39 us
    pallas_call x1, Pallas kernels, local(): pl.pallas_call(tail_kernel, out_shape=jax.ShapeDtypeStruct(features.shape...  2.51 us
    pallas_call x1, Pallas kernels, local(): pl.pallas_call(pack_kernel, out_shape=[jax.ShapeDtypeStruct((1,) + slot_s...  2.17 us
  transfers between devices with their start and end apart: 1, of which 1 were waited for; matrix products, arithmetic and copies ran while one was open for 0% of the time, Pallas kernels for 2%

profile of v7, /device:TPU:0, one launch (start us, length us, event | category | flops | bytes accessed | tf_op | source)
XLA Modules:
  0.0 63.7 jit_solution(14172732320984676639)
XLA Ops:
  6.5 0.0 all-gather.2.cloned.1.call-start
  6.5 2.2 %pack.1 = (bf16[1,144,256]{2,1,0:T(8,128)(2,1)}, f32[31,256]{1,0:T(8,128)}, f32[8,256]{1,0:T(8,128)}) custom-call(bf16[64]{0:T(256)(128)(2,1)} %b_ref.1, bf16[64,256]{1,0:T(8,128)(2,1)} %w_in_ref.1, bf16[64,256]{1,0:T(8,128)(2,1)} %w_out_ref.1, f32[31,256]{1,0:T(8,128)} %taps_ref.3, f32[1,256]{1,0:T(1,128)} %bitcast.9, f32[1,256]{1,0:T(1,128)} %bitcast.10, ...), custom_call_target="tpu_custom_call" | custom-call | tf_op jit(solution)/shard_map/pack/pallas_call | solution.py:141
  8.7 0.0 all-gather.2.cloned.1.call-update
  8.7 15.3 %all_to_all.10 = bf16[32,2,4,256]{3,2,1,0:T(4,128)(2,1)S(1)} all-to-all(bf16[32,2,4,256]{3,2,1,0:T(4,128)(2,1)} %feat_ref.1), channel_id=1, replica_groups=mesh['groups'=2,'row'=16] {'row'}, dimensions={0} | all-to-all | bytes 262144 | tf_op jit(solution)/shard_map/all_to_all | solution.py:162
  24.1 0.0 copy-start.2
  24.1 0.8 %copy-done.2 = f32[31,256]{1,0:T(8,128)S(1)} copy-done((f32[31,256]{1,0:T(8,128)S(1)}, f32[31,256]{1,0:T(8,128)}, u32[]{:S(2)}) %copy-start.2) | copy-done | bytes 31768
  24.8 1.1 %radial.1 = bf16[16,2,8,256]{3,2,1,0:T(8,128)(2,1)S(1)} custom-call(bf16[16,2,2,4,256]{4,3,2,1,0:T(4,128)(2,1)S(1)} %bitcast.8, f32[31,256]{1,0:T(8,128)S(1)} %copy-done.2), custom_call_target="tpu_custom_call" | custom-call | tf_op jit(solution)/shard_map/radial/pallas_call | solution.py:164
  26.0 10.5 %all_to_all.11.z_ref = bf16[32,8,256]{2,1,0:T(8,128)(2,1)S(1)} all-to-all(bf16[32,8,256]{2,1,0:T(8,128)(2,1)S(1)} %bitcast.7), channel_id=1, replica_groups=mesh['groups'=2,'row'=16] {'row'}, dimensions={0} | all-to-all | bytes 262144 | tf_op jit(solution)/shard_map/all_to_all | solution.py:173
  36.5 14.2 %all-gather.2.cloned.1.call-done.w_ref = bf16[16,144,256]{2,1,0:T(8,128)(2,1)} async-done(((bf16[1,144,256]{2,1,0:T(8,128)(2,1)}), bf16[16,144,256]{2,1,0:T(8,128)(2,1)}) %all-gather.2.cloned.1.call-update) | async-done | bytes 1179664 | tf_op jit(solution)/shard_map/all_gather | solution.py:153
  50.7 0.0 copy-start
  50.7 1.3 %copy-done = bf16[16,144,256]{2,1,0:T(8,128)(2,1)S(1)} copy-done((bf16[16,144,256]{2,1,0:T(8,128)(2,1)S(1)}, bf16[16,144,256]{2,1,0:T(8,128)(2,1)}, u32[]{:S(2)}) %copy-start) | copy-done | bytes 1179672
  52.0 0.0 copy-start.1
  52.0 0.9 %copy-done.1 = bf16[32,2,4,256]{3,2,1,0:T(4,128)(2,1)S(1)} copy-done((bf16[32,2,4,256]{3,2,1,0:T(4,128)(2,1)S(1)}, bf16[32,2,4,256]{3,2,1,0:T(4,128)(2,1)}, u32[]{:S(2)}) %copy-start.1) | copy-done | bytes 131096
  52.9 0.0 copy-start.3
  52.9 0.8 %copy-done.3 = f32[31,256]{1,0:T(8,128)S(1)} copy-done((f32[31,256]{1,0:T(8,128)S(1)}, f32[31,256]{1,0:T(8,128)}, u32[]{:S(2)}) %copy-start.3) | copy-done | bytes 31768
  53.6 0.0 copy-start.4
  53.6 0.7 %copy-done.4 = f32[8,256]{1,0:T(8,128)S(1)} copy-done((f32[8,256]{1,0:T(8,128)S(1)}, f32[8,256]{1,0:T(8,128)}, u32[]{:S(2)}) %copy-start.4) | copy-done | bytes 8216
  54.3 2.5 %tail.1 = bf16[32,2,4,256]{3,2,1,0:T(4,128)(2,1)} custom-call(bf16[32,8,256]{2,1,0:T(8,128)(2,1)S(1)} %all_to_all.11.z_ref, bf16[32,2,4,256]{3,2,1,0:T(4,128)(2,1)S(1)} %copy-done.1, f32[31,256]{1,0:T(8,128)S(1)} %copy-done.3, f32[8,256]{1,0:T(8,128)S(1)} %copy-done.4, bf16[16,144,256]{2,1,0:T(8,128)(2,1)S(1)} %copy-done), custom_call_target="tpu_custom_call" | custom-call | tf_op jit(solution)/shard_map/tail/pallas_call | solution.py:174
Async XLA Ops:
  6.5 44.2 %all-gather.2.cloned.1.call-start = ((), (), s32[]{:S(2)}) async-start(), calls=%async_computation.2 | async-start | bytes 1253376 | tf_op jit(solution)/shard_map/all_gather | solution.py:153
  24.1 0.8 %copy-start.2 = (f32[31,256]{1,0:T(8,128)S(1)}, f32[31,256]{1,0:T(8,128)}, u32[]{:S(2)}) copy-start(f32[31,256]{1,0:T(8,128)} %taps_ref.2) | copy-start | bytes 95236
  50.7 1.3 %copy-start = (bf16[16,144,256]{2,1,0:T(8,128)(2,1)S(1)}, bf16[16,144,256]{2,1,0:T(8,128)(2,1)}, u32[]{:S(2)}) copy-start(bf16[16,144,256]{2,1,0:T(8,128)(2,1)} %all-gather.2.cloned.1.call-done.w_ref) | copy-start | bytes 3538948
  52.0 0.9 %copy-start.1 = (bf16[32,2,4,256]{3,2,1,0:T(4,128)(2,1)S(1)}, bf16[32,2,4,256]{3,2,1,0:T(4,128)(2,1)}, u32[]{:S(2)}) copy-start(bf16[32,2,4,256]{3,2,1,0:T(4,128)(2,1)} %feat_ref.1) | copy-start | bytes 393220
  52.9 0.8 %copy-start.3 = (f32[31,256]{1,0:T(8,128)S(1)}, f32[31,256]{1,0:T(8,128)}, u32[]{:S(2)}) copy-start(f32[31,256]{1,0:T(8,128)} %get-tuple-element.8.taps_ref) | copy-start | bytes 95236
  53.6 0.7 %copy-start.4 = (f32[8,256]{1,0:T(8,128)S(1)}, f32[8,256]{1,0:T(8,128)}, u32[]{:S(2)}) copy-start(f32[8,256]{1,0:T(8,128)} %get-tuple-element.9.consts_ref) | copy-start | bytes 24580
Sparse Core Ops, SparseCore 0:
  9.6 41.0 all-gather.1

commit v8 on v7

v8 whole, which is shorter than its diff:
```python
import math
from functools import partial

import jax
import jax.numpy as jnp
from jax import lax
from jax.experimental import pallas as pl
from jax.experimental.pallas import tpu as pltpu
from jax.sharding import PartitionSpec as P

SLOT = 64
EXTRA = 16


def vmem():
    return pl.BlockSpec(memory_space=pltpu.VMEM)


def pack_kernel(b_ref, w_in_ref, w_out_ref, slot_ref, sems):
    copies = [
        pltpu.make_async_copy(w_in_ref, slot_ref.at[0, 0:SLOT], sems.at[0]),
        pltpu.make_async_copy(w_out_ref, slot_ref.at[0, SLOT : 2 * SLOT], sems.at[1]),
    ]
    for copy in copies:
        copy.start()
    bias = b_ref[...].astype(jnp.float32)[None, :]
    c = slot_ref.shape[2]
    wide = jnp.concatenate([bias] * (c // SLOT), axis=1)
    slot_ref[0, 2 * SLOT : 2 * SLOT + EXTRA, :] = jnp.broadcast_to(wide, (EXTRA, c)).astype(slot_ref.dtype)
    for copy in copies:
        copy.wait()


def gate_kernel(*refs):
    refs[-1][...] = jnp.zeros_like(refs[-1])


def radial_kernel(x_ref, taps_ref, out_ref, even, odd):
    n, a_loc, _, theta, c = x_ref.shape
    taps = taps_ref.shape[0]
    pad = (taps + 1) // 4
    zeros = jnp.zeros((pad, a_loc, 2 * theta, c), jnp.float32)
    even[0:pad] = zeros
    even[pad + n : 2 * pad + n] = zeros
    odd[0:pad] = zeros
    odd[pad + n - 1 : 2 * pad + n - 1] = zeros
    odd[2 * pad + n - 1 :] = zeros[:1]
    first = x_ref[:, :, 0].astype(jnp.float32)
    second = x_ref[:, :, 1].astype(jnp.float32)
    even[pad : pad + n, :, 0:theta] = first
    even[pad : pad + n, :, theta:] = second
    odd[pad : pad + n, :, 0:theta] = second
    odd[pad - 1 : pad + n - 1, :, theta:] = first

    def step(s, carry):
        total = jnp.zeros((a_loc, 2 * theta, c), jnp.float32)
        for k in range(taps):
            shift = k - taps // 2
            source = even if shift % 2 == 0 else odd
            total = total + source[s + (pad + shift // 2)] * taps_ref[k : k + 1, :]
        out_ref[s] = total.astype(out_ref.dtype)
        return carry

    lax.fori_loop(0, n, step, 0)


def tail_kernel(n_slots, z_ref, taps_ref, feat_ref, *rest):
    vectors, w_refs = rest[:5], rest[5 : 5 + n_slots]
    out_ref, padded, branch, field, consts, sems = rest[-6:]
    fetches = [pltpu.make_async_copy(feat_ref, field, sems.at[5])]
    for i, vector in enumerate(vectors):
        fetches.append(pltpu.make_async_copy(vector, consts.at[i], sems.at[i]))
    for fetch in fetches:
        fetch.start()
    axial, rows, c = z_ref.shape
    theta = rows // 2
    taps = taps_ref.shape[0]
    half = taps // 2
    zeros = jnp.zeros((half, rows, c), jnp.float32)
    padded[0:half] = zeros
    padded[half + axial :] = zeros
    padded[half : half + axial] = z_ref[...].astype(jnp.float32)
    block = 4

    def conv(i, carry):
        base = i * block
        total = jnp.zeros((block, rows, c), jnp.float32)
        for k in range(taps):
            total = total + padded[pl.ds(base + k, block)] * taps_ref[k : k + 1, :]
        branch[pl.ds(base, block)] = total
        return carry

    lax.fori_loop(0, axial // block, conv, 0)
    for fetch in fetches:
        fetch.wait()
    slots = [(w_ref, i) for w_ref in w_refs for i in range(w_ref.shape[0])]
    per = c // SLOT
    lane_slot = lax.broadcasted_iota(jnp.int32, (1, c), 1) // SLOT
    planes = 32

    def mlp(i, carry):
        v = (branch[pl.ds(i * planes, planes)] + consts[0]).reshape(planes * rows, c)
        v = v.astype(jnp.bfloat16).astype(jnp.float32)
        mean = jnp.mean(v, axis=-1, keepdims=True)
        centred = v - mean
        var = jnp.mean(centred * centred, axis=-1, keepdims=True)
        normed = (centred * lax.rsqrt(var + 1e-06) * consts[1] + consts[2]).astype(jnp.bfloat16)
        total = jnp.zeros((planes * rows, c), jnp.float32)
        for g in range(len(slots) // per):
            own = slots[g * per : (g + 1) * per]
            w_in = jnp.concatenate([w[j, 0:SLOT, :] for w, j in own], axis=0)
            w_out = jnp.concatenate([w[j, SLOT : 2 * SLOT, :] for w, j in own], axis=0)
            bias = jnp.zeros((1, c), jnp.float32)
            for at, (w, j) in enumerate(own):
                piece = w[j, 2 * SLOT : 2 * SLOT + EXTRA, :].astype(jnp.float32)[0:1]
                bias = jnp.where(lane_slot == at, piece, bias)
            u = lax.dot_general(normed, w_in, (((1,), (1,)), ((), ())), preferred_element_type=jnp.float32)
            u = u + bias
            hidden = (0.5 * u * (1.0 + jnp.tanh(0.7978845608028654 * (u + 0.044715 * u * u * u)))).astype(jnp.bfloat16)
            total = total + jnp.dot(hidden, w_out, preferred_element_type=jnp.float32)
        result = (consts[4] * (total + consts[3])).astype(jnp.bfloat16).astype(jnp.float32)
        branch[pl.ds(i * planes, planes)] = result.reshape(planes, rows, c)
        return carry

    if axial == planes:
        mlp(0, 0)
    else:
        lax.fori_loop(0, axial // planes, mlp, 0)
    for r in range(2):
        got = branch[:, r * theta : (r + 1) * theta, :]
        out_ref[:, r] = (field[:, r].astype(jnp.float32) + got).astype(out_ref.dtype)


def digits(n):
    chips = n // 2
    inner = 1
    while inner * inner * 4 <= chips:
        inner *= 2
    return chips // inner, inner, 2


def local(n, features, axial_taps, radial_taps, conv_bias, ln_gain, ln_bias, w_in, b_in, w_out, b_out, layer_scale):
    axial, r_loc, theta, c = features.shape
    rows = r_loc * theta
    hid_loc = w_in.shape[0]
    a_loc = axial // n
    outer, inner, _ = digits(n)
    spread = hid_loc == SLOT and n == 4 * outer
    params = pltpu.CompilerParams(vmem_limit_bytes=24 * 1024 * 1024)
    anywhere = pl.BlockSpec(memory_space=pl.ANY)

    def move(piece, digit, by):
        stride = math.prod(digits(n)[digit + 1 :])
        return lax.ppermute(piece, "row", [(i, i ^ (by * stride)) for i in range(n)])

    if spread:
        own = pl.pallas_call(
            pack_kernel,
            out_shape=jax.ShapeDtypeStruct((1, 2 * SLOT + EXTRA, c), jnp.bfloat16),
            in_specs=[vmem()] + [anywhere] * 2,
            out_specs=vmem(),
            scratch_shapes=[pltpu.SemaphoreType.DMA((2,))],
            name="pack",
        )(b_in, w_in, w_out)
        line = [move(own, 0, by) for by in range(1, outer)]
        across = [move(own, 1, 1)]
        twin = [move(own, 2, 1)]
    else:
        w_all = lax.all_gather(w_in, "row", axis=0, tiled=True).reshape(-1, SLOT, c)
        o_all = lax.all_gather(w_out, "row", axis=0, tiled=True).reshape(-1, SLOT, c)
        b_all = lax.all_gather(b_in, "row", axis=0, tiled=True).reshape(-1, 1, SLOT)
        b_all = jnp.broadcast_to(jnp.tile(b_all, (1, 1, c // SLOT)), (w_all.shape[0], EXTRA, c))
        slots, order = [jnp.concatenate([w_all, o_all, b_all], axis=1)], []

    got = lax.all_to_all(features, "row", split_axis=0, concat_axis=0, tiled=True)
    pad = (radial_taps.shape[0] + 1) // 4
    mixed = pl.pallas_call(
        radial_kernel,
        out_shape=jax.ShapeDtypeStruct((n, a_loc, rows, c), jnp.bfloat16),
        in_specs=[vmem()] * 2,
        out_specs=vmem(),
        scratch_shapes=[pltpu.VMEM((n + 2 * pad, a_loc, rows, c), jnp.float32)] * 2,
        compiler_params=params,
        name="radial",
    )(got.reshape(n, a_loc, r_loc, theta, c), radial_taps)
    if spread:
        gate = pl.pallas_call(
            gate_kernel,
            out_shape=jax.ShapeDtypeStruct((8, 128), jnp.float32),
            in_specs=[anywhere] * outer,
            out_specs=vmem(),
            cost_estimate=pl.CostEstimate(flops=10**10, bytes_accessed=2 * 10**7, transcendentals=0),
            name="gate",
        )(mixed, *line)
        line, *order = lax.optimization_barrier((line, gate))
        across = across + [move(h, 1, 1) for h in line]
        twin = twin + [move(h, 2, 1) for h in line]
    back = lax.all_to_all(mixed.reshape(axial, rows, c), "row", split_axis=0, concat_axis=0, tiled=True)
    if spread:
        across, back = lax.optimization_barrier((across, back))
        slots = [own] + line + across + twin + [move(h, 2, 1) for h in across]
    vectors = [v[None, :] for v in (conv_bias, ln_gain, ln_bias, b_out, layer_scale)]
    return pl.pallas_call(
        partial(tail_kernel, len(slots)),
        out_shape=jax.ShapeDtypeStruct(features.shape, jnp.bfloat16),
        in_specs=[vmem()] * 2 + [anywhere] * 6 + [vmem()] * len(slots) + [anywhere] * len(order),
        out_specs=vmem(),
        scratch_shapes=[
            pltpu.VMEM((axial + axial_taps.shape[0] - 1, rows, c), jnp.float32),
            pltpu.VMEM((axial, rows, c), jnp.float32),
            pltpu.VMEM(features.shape, jnp.bfloat16),
            pltpu.VMEM((5, 1, c), jnp.float32),
            pltpu.SemaphoreType.DMA((6,)),
        ],
        compiler_params=params,
        name="tail",
    )(back, axial_taps, features, *vectors, *slots, *order)


def solution(mesh):
    in_specs = (
        P("groups", "row", None, None),
        P(),
        P(),
        P(),
        P(),
        P(),
        P("row", None),
        P("row"),
        P("row", None),
        P(),
        P(),
    )
    out_specs = P("groups", "row", None, None)
    return jax.shard_map(partial(local, mesh.shape["row"]), mesh=mesh, in_specs=in_specs, out_specs=out_specs, check_vma=False)
```

time: 64.2 us -> 41.5 us (0.65)
  blocking collectives: 25.9 us -> 0 us
  starting transfers between devices: 0.01 us -> 23.9 us
  between operations: 13.4 us -> 0.17 us
  waiting for transfers between devices: 14.2 us -> 5.05 us
  Pallas kernels: 5.79 us -> 7.31 us
    all_to_all x2 -> x0, blocking collectives: 25.9 us -> none  [the longest x1 15.3 us: local(): lax.all_to_all(features, 'row', split_axis=0, concat_axis=0, tiled=True)]
    all_gather x1 -> x0, waiting for transfers between devices: 14.2 us -> none  [local(): slots = lax.all_gather(own, 'row', axis=0, tiled=True)]
    all_to_all x0 -> x2, starting transfers between devices: none -> 12 us  [the longest x1 7.39 us: local(): lax.all_to_all(features, 'row', split_axis=0, concat_axis=0, tiled=True)]
    ppermute x0 -> x15, starting transfers between devices: none -> 11.9 us  [move(): return lax.ppermute(piece, 'row', [(i, i ^ by * stride) for i in range(n)])]
    ppermute x0 -> x15, waiting for transfers between devices: none -> 5.04 us  [move(): return lax.ppermute(piece, 'row', [(i, i ^ by * stride) for i in range(n)])]
    pallas_call x1, Pallas kernels: 1.12 us -> 2.04 us  [local(): pl.pallas_call(radial_kernel, out_shape=jax.ShapeDtypeStruct((n, a_loc, r...]
    pallas_call x2 -> x3, Pallas kernels: 4.67 us -> 5.27 us  [the longest x1 2.59 us: local(): pl.pallas_call(partial(tail_kernel, len(slots)), out_shape=jax.ShapeDtype...]
    unnamed x10 -> x32, local copies, waits for them, and re-layouts: 4.39 us -> 4.56 us
  transfers between devices with their start and end apart: 1 -> 17, of which waited for: 1 -> 7; matrix products, arithmetic and copies ran while one was open for 0% -> 0% of each run, Pallas kernels for 2% -> 12%
where the time goes in v8:
time: 41.5 us; the launch traced here: 41 us
  starting transfers between devices  23.9 us (58%)
  Pallas kernels  7.31 us (18%)
  waiting for transfers between devices  5.05 us (12%)
  local copies, waits for them, and re-layouts  4.56 us (11%)
    ppermute x15, starting transfers between devices, move(): return lax.ppermute(piece, 'row', [(i, i ^ by * stride) for i in range(n)])  11.9 us
    all_to_all x1, starting transfers between devices, local(): lax.all_to_all(features, 'row', split_axis=0, concat_axis=0, tiled=True)  7.39 us
    ppermute x15, waiting for transfers between devices, move(): return lax.ppermute(piece, 'row', [(i, i ^ by * stride) for i in range(n)])  5.04 us
    all_to_all x1, starting transfers between devices, local(): lax.all_to_all(mixed.reshape(axial, rows, c), 'row', split_axis=0, concat...  4.65 us
    unnamed x32, local copies, waits for them, and re-layouts  4.56 us
    pallas_call x1, Pallas kernels, local(): pl.pallas_call(partial(tail_kernel, len(slots)), out_shape=jax.ShapeDtype...  2.59 us
    pallas_call x1, Pallas kernels, local(): pl.pallas_call(pack_kernel, out_shape=jax.ShapeDtypeStruct((1, 2 * SLOT +...  2.09 us
    pallas_call x1, Pallas kernels, local(): pl.pallas_call(radial_kernel, out_shape=jax.ShapeDtypeStruct((n, a_loc, r...  2.04 us
  transfers between devices with their start and end apart: 17, of which 7 were waited for; matrix products, arithmetic and copies ran while one was open for 0% of the time, Pallas kernels for 12%

profile of v8, /device:TPU:0, one launch (start us, length us, event | category | flops | bytes accessed | tf_op | source)
XLA Modules:
  0.0 41.0 jit_solution(2760876123747586764)
XLA Ops:
  0.0 7.4 %all-to-all-start = ((bf16[32,2,4,256]{3,2,1,0:T(4,128)(2,1)}), bf16[32,2,4,256]{3,2,1,0:T(4,128)(2,1)S(1)}, u32[]{:S(2)}, u32[]{:S(2)}) async-start(bf16[32,2,4,256]{3,2,1,0:T(4,128)(2,1)} %feat_ref.1), calls=%async_computation | async-start | bytes 262144 | tf_op jit(solution)/shard_map/all_to_all | solution.py:175
  7.4 0.0 copy-start.8
  7.4 2.1 %pack.1.rest_5_ = bf16[1,144,256]{2,1,0:T(8,128)(2,1)} custom-call(bf16[64]{0:T(256)(128)(2,1)} %b_ref.1, bf16[64,256]{1,0:T(8,128)(2,1)} %w_in_ref.1, bf16[64,256]{1,0:T(8,128)(2,1)} %w_out_ref.1), custom_call_target="tpu_custom_call" | custom-call | tf_op jit(solution)/shard_map/pack/pallas_call | solution.py:157
  9.5 3.8 %collective-permute-start.3 = (bf16[1,144,256]{2,1,0:T(8,128)(2,1)}, bf16[1,144,256]{2,1,0:T(8,128)(2,1)S(1)}, u32[]{:S(2)}, u32[]{:S(2)}) collective-permute-start(bf16[1,144,256]{2,1,0:T(8,128)(2,1)} %pack.1.rest_5_), channel_id=1, source_target_pairs={{0,12},{1,13},{2,14},{3,15},{4,8},{5,9},{6,10},{7,11},{8,4},{9,5},... | collective-permute-start | bytes 221192 | tf_op jit(solution)/shard_map/ppermute | solution.py:154
  13.3 0.7 %collective-permute-start.1 = (bf16[1,144,256]{2,1,0:T(8,128)(2,1)}, bf16[1,144,256]{2,1,0:T(8,128)(2,1)S(1)}, u32[]{:S(2)}, u32[]{:S(2)}) collective-permute-start(bf16[1,144,256]{2,1,0:T(8,128)(2,1)} %pack.1.rest_5_), channel_id=1, source_target_pairs={{0,4},{1,5},{2,6},{3,7},{4,0},{5,1},{6,2},{7,3},{8,12},{9,13},{10,... | collective-permute-start | bytes 221192 | tf_op jit(solution)/shard_map/ppermute | solution.py:154
  14.0 1.9 %collective-permute-start = (bf16[1,144,256]{2,1,0:T(8,128)(2,1)}, bf16[1,144,256]{2,1,0:T(8,128)(2,1)S(1)}, u32[]{:S(2)}, u32[]{:S(2)}) collective-permute-start(bf16[1,144,256]{2,1,0:T(8,128)(2,1)} %pack.1.rest_5_), channel_id=1, source_target_pairs={{0,2},{1,3},{2,0},{3,1},{4,6},{5,7},{6,4},{7,5},{8,10},{9,11},{10,... | collective-permute-start | bytes 221192 | tf_op jit(solution)/shard_map/ppermute | solution.py:154
  15.9 2.0 %radial.1.refs_0_ = bf16[16,2,8,256]{3,2,1,0:T(8,128)(2,1)} custom-call(bf16[16,2,2,4,256]{4,3,2,1,0:T(4,128)(2,1)S(1)} %bitcast.7, f32[31,256]{1,0:T(8,128)S(1)} %copy-done.8), custom_call_target="tpu_custom_call" | custom-call | tf_op jit(solution)/shard_map/radial/pallas_call | solution.py:177
  17.9 4.6 %all-to-all-start.1 = ((bf16[32,8,256]{2,1,0:T(8,128)(2,1)}), bf16[32,8,256]{2,1,0:T(8,128)(2,1)S(1)}, u32[]{:S(2)}, u32[]{:S(2)}) async-start(bf16[32,8,256]{2,1,0:T(8,128)(2,1)} %bitcast.1), calls=%async_computation.1 | async-start | bytes 262144 | tf_op jit(solution)/shard_map/all_to_all | solution.py:198
  22.7 0.6 %copy-done.2 = bf16[1,144,256]{2,1,0:T(8,128)(2,1)} copy-done((bf16[1,144,256]{2,1,0:T(8,128)(2,1)}, bf16[1,144,256]{2,1,0:T(8,128)(2,1)S(1)}, u32[]{:S(2)}) %copy-start.2) | copy-done | bytes 73752
  23.3 0.0 copy-done.4
  23.3 0.6 %copy-done.6 = bf16[1,144,256]{2,1,0:T(8,128)(2,1)} copy-done((bf16[1,144,256]{2,1,0:T(8,128)(2,1)}, bf16[1,144,256]{2,1,0:T(8,128)(2,1)S(1)}, u32[]{:S(2)}) %copy-start.6) | copy-done | bytes 73752
  23.9 0.6 %gate.1.rest_21_ = f32[8,128]{1,0:T(8,128)} custom-call(bf16[16,2,8,256]{3,2,1,0:T(8,128)(2,1)} %radial.1.refs_0_, bf16[1,144,256]{2,1,0:T(8,128)(2,1)} %copy-done.6, bf16[1,144,256]{2,1,0:T(8,128)(2,1)} %copy-done.4, bf16[1,144,256]{2,1,0:T(8,128)(2,1)} %copy-done.2), custom_call_target="tpu_custom_call" | custom-call | flops 10000000000 | bytes 20000000 | tf_op jit(solution)/shard_map/gate/pallas_call | solution.py:187
  24.5 1.9 %collective-permute-start.4 = (bf16[1,144,256]{2,1,0:T(8,128)(2,1)}, bf16[1,144,256]{2,1,0:T(8,128)(2,1)S(1)}, u32[]{:S(2)}, u32[]{:S(2)}) collective-permute-start(bf16[1,144,256]{2,1,0:T(8,128)(2,1)} %copy-done.6), channel_id=1, source_target_pairs={{0,2},{1,3},{2,0},{3,1},{4,6},{5,7},{6,4},{7,5},{8,10},{9,11},{10,... | collective-permute-start | bytes 221192 | tf_op jit(solution)/shard_map/ppermute | solution.py:154
  26.4 0.1 collective-permute-start.5
  26.5 1.9 %collective-permute-start.6 = (bf16[1,144,256]{2,1,0:T(8,128)(2,1)}, bf16[1,144,256]{2,1,0:T(8,128)(2,1)S(1)}, u32[]{:S(2)}, u32[]{:S(2)}) collective-permute-start(bf16[1,144,256]{2,1,0:T(8,128)(2,1)} %copy-done.2), channel_id=1, source_target_pairs={{0,2},{1,3},{2,0},{3,1},{4,6},{5,7},{6,4},{7,5},{8,10},{9,11},{10,... | collective-permute-start | bytes 221192 | tf_op jit(solution)/shard_map/ppermute | solution.py:154
  28.5 0.5 %collective-permute-start.8 = (bf16[1,144,256]{2,1,0:T(8,128)(2,1)}, bf16[1,144,256]{2,1,0:T(8,128)(2,1)S(1)}, u32[]{:S(2)}, u32[]{:S(2)}) collective-permute-start(bf16[1,144,256]{2,1,0:T(8,128)(2,1)} %copy-done.6), channel_id=1, source_target_pairs={{0,1},{1,0},{2,3},{3,2},{4,5},{5,4},{6,7},{7,6},{8,9},{9,8},{10,11... | collective-permute-start | bytes 221192 | tf_op jit(solution)/shard_map/ppermute | solution.py:154
  29.0 1.2 %collective-permute-done.4.rest_10_ = bf16[1,144,256]{2,1,0:T(8,128)(2,1)S(1)} collective-permute-done((bf16[1,144,256]{2,1,0:T(8,128)(2,1)}, bf16[1,144,256]{2,1,0:T(8,128)(2,1)S(1)}, u32[]{:S(2)}, u32[]{:S(2)}) %collective-permute-start.4) | collective-permute-done | bytes 73760 | tf_op jit(solution)/shard_map/ppermute | solution.py:154
  30.1 1.8 %collective-permute-done.5.rest_11_ = bf16[1,144,256]{2,1,0:T(8,128)(2,1)S(1)} collective-permute-done((bf16[1,144,256]{2,1,0:T(8,128)(2,1)}, bf16[1,144,256]{2,1,0:T(8,128)(2,1)S(1)}, u32[]{:S(2)}, u32[]{:S(2)}) %collective-permute-start.5) | collective-permute-done | bytes 73760 | tf_op jit(solution)/shard_map/ppermute | solution.py:154
  31.9 1.2 %collective-permute-done.6.rest_12_ = bf16[1,144,256]{2,1,0:T(8,128)(2,1)S(1)} collective-permute-done((bf16[1,144,256]{2,1,0:T(8,128)(2,1)}, bf16[1,144,256]{2,1,0:T(8,128)(2,1)S(1)}, u32[]{:S(2)}, u32[]{:S(2)}) %collective-permute-start.6) | collective-permute-done | bytes 73760 | tf_op jit(solution)/shard_map/ppermute | solution.py:154
  33.1 0.5 %collective-permute-start.12 = (bf16[1,144,256]{2,1,0:T(8,128)(2,1)S(1)}, bf16[1,144,256]{2,1,0:T(8,128)(2,1)S(1)}, u32[]{:S(2)}, u32[]{:S(2)}) collective-permute-start(bf16[1,144,256]{2,1,0:T(8,128)(2,1)S(1)} %collective-permute-done.4.rest_10_), channel_id=1, source_target_pairs={{0,1},{1,0},{2,3},{3,2},{4,5},{5,4},{6,7},{7,6},{8,9},{9,8},{10,11... | collective-permute-start | bytes 221192 | tf_op jit(solution)/shard_map/ppermute | solution.py:154
  33.6 0.1 collective-permute-start.13
  33.7 0.4 %collective-permute-start.14 = (bf16[1,144,256]{2,1,0:T(8,128)(2,1)S(1)}, bf16[1,144,256]{2,1,0:T(8,128)(2,1)S(1)}, u32[]{:S(2)}, u32[]{:S(2)}) collective-permute-start(bf16[1,144,256]{2,1,0:T(8,128)(2,1)S(1)} %collective-permute-done.6.rest_12_), channel_id=1, source_target_pairs={{0,1},{1,0},{2,3},{3,2},{4,5},{5,4},{6,7},{7,6},{8,9},{9,8},{10,11... | collective-permute-start | bytes 221192 | tf_op jit(solution)/shard_map/ppermute | solution.py:154
  34.1 0.2 collective-permute-done.11.rest_17_
  34.4 0.2 collective-permute-done.12.rest_18_
  34.5 0.4 collective-permute-done.13.rest_19_
  34.9 0.2 collective-permute-done.14.rest_20_
  35.1 0.6 %copy-done.10 = f32[8,128]{1,0:T(8,128)S(1)} copy-done((f32[8,128]{1,0:T(8,128)S(1)}, f32[8,128]{1,0:T(8,128)}, u32[]{:S(2)}) %copy-start.10) | copy-done | bytes 4120
  35.7 0.0 copy-done.11
  35.7 0.9 %copy-done.3 = bf16[1,144,256]{2,1,0:T(8,128)(2,1)S(1)} copy-done((bf16[1,144,256]{2,1,0:T(8,128)(2,1)S(1)}, bf16[1,144,256]{2,1,0:T(8,128)(2,1)}, u32[]{:S(2)}) %copy-start.3) | copy-done | bytes 73752
  36.6 0.9 %copy-done.5 = bf16[1,144,256]{2,1,0:T(8,128)(2,1)S(1)} copy-done((bf16[1,144,256]{2,1,0:T(8,128)(2,1)S(1)}, bf16[1,144,256]{2,1,0:T(8,128)(2,1)}, u32[]{:S(2)}) %copy-start.5) | copy-done | bytes 73752
  37.5 0.9 %copy-done.7 = bf16[1,144,256]{2,1,0:T(8,128)(2,1)S(1)} copy-done((bf16[1,144,256]{2,1,0:T(8,128)(2,1)S(1)}, bf16[1,144,256]{2,1,0:T(8,128)(2,1)}, u32[]{:S(2)}) %copy-start.7) | copy-done | bytes 73752
  38.4 2.6 %tail.1 = bf16[32,2,4,256]{3,2,1,0:T(4,128)(2,1)} custom-call(bf16[32,8,256]{2,1,0:T(8,128)(2,1)S(1)} %all-to-all-done.1.z_ref, f32[31,256]{1,0:T(8,128)S(1)} %copy-done.9, bf16[32,2,4,256]{3,2,1,0:T(4,128)(2,1)S(1)} %copy-done, f32[1,256]{1,0:T(1,128)S(1)} %bitcast.8, f32[1,256]{1,0:T(1,128)S(1)} %bitcast.9, f32[1,256]{1,0:T(1,128)S(1)} %bitcast.10, ...), custom_call_target="tpu_custom_call" | custom-call | tf_op jit(solution)/shard_map/tail/pallas_call | solution.py:203
  (38 shorter events, 0.1 us)
Async XLA Ops:
  0.0 15.9 %all-to-all-start = ((bf16[32,2,4,256]{3,2,1,0:T(4,128)(2,1)}), bf16[32,2,4,256]{3,2,1,0:T(4,128)(2,1)S(1)}, u32[]{:S(2)}, u32[]{:S(2)}) async-start(bf16[32,2,4,256]{3,2,1,0:T(4,128)(2,1)} %feat_ref.1), calls=%async_computation | async-start | bytes 262144 | tf_op jit(solution)/shard_map/all_to_all | solution.py:175
  7.4 8.5 %copy-start.8 = (f32[31,256]{1,0:T(8,128)S(1)}, f32[31,256]{1,0:T(8,128)}, u32[]{:S(2)}) copy-start(f32[31,256]{1,0:T(8,128)} %taps_ref.2) | copy-start | bytes 95236
  9.5 13.1 %collective-permute-start.3 = (bf16[1,144,256]{2,1,0:T(8,128)(2,1)}, bf16[1,144,256]{2,1,0:T(8,128)(2,1)S(1)}, u32[]{:S(2)}, u32[]{:S(2)}) collective-permute-start(bf16[1,144,256]{2,1,0:T(8,128)(2,1)} %pack.1.rest_5_), channel_id=1, source_target_pairs={{0,12},{1,13},{2,14},{3,15},{4,8},{5,9},{6,10},{7,11},{8,4},{9,5},... | collective-permute-start | bytes 221192 | tf_op jit(solution)/shard_map/ppermute | solution.py:154
  13.3 9.3 %collective-permute-start.2 = (bf16[1,144,256]{2,1,0:T(8,128)(2,1)}, bf16[1,144,256]{2,1,0:T(8,128)(2,1)S(1)}, u32[]{:S(2)}, u32[]{:S(2)}) collective-permute-start(bf16[1,144,256]{2,1,0:T(8,128)(2,1)} %pack.1.rest_5_), channel_id=1, source_target_pairs={{0,8},{1,9},{2,10},{3,11},{4,12},{5,13},{6,14},{7,15},{8,0},{9,1},... | collective-permute-start | bytes 221192 | tf_op jit(solution)/shard_map/ppermute | solution.py:154
  13.3 9.4 %collective-permute-start.1 = (bf16[1,144,256]{2,1,0:T(8,128)(2,1)}, bf16[1,144,256]{2,1,0:T(8,128)(2,1)S(1)}, u32[]{:S(2)}, u32[]{:S(2)}) collective-permute-start(bf16[1,144,256]{2,1,0:T(8,128)(2,1)} %pack.1.rest_5_), channel_id=1, source_target_pairs={{0,4},{1,5},{2,6},{3,7},{4,0},{5,1},{6,2},{7,3},{8,12},{9,13},{10,... | collective-permute-start | bytes 221192 | tf_op jit(solution)/shard_map/ppermute | solution.py:154
  14.0 14.5 %collective-permute-start = (bf16[1,144,256]{2,1,0:T(8,128)(2,1)}, bf16[1,144,256]{2,1,0:T(8,128)(2,1)S(1)}, u32[]{:S(2)}, u32[]{:S(2)}) collective-permute-start(bf16[1,144,256]{2,1,0:T(8,128)(2,1)} %pack.1.rest_5_), channel_id=1, source_target_pairs={{0,2},{1,3},{2,0},{3,1},{4,6},{5,7},{6,4},{7,5},{8,10},{9,11},{10,... | collective-permute-start | bytes 221192 | tf_op jit(solution)/shard_map/ppermute | solution.py:154
  17.9 15.2 %all-to-all-start.1 = ((bf16[32,8,256]{2,1,0:T(8,128)(2,1)}), bf16[32,8,256]{2,1,0:T(8,128)(2,1)S(1)}, u32[]{:S(2)}, u32[]{:S(2)}) async-start(bf16[32,8,256]{2,1,0:T(8,128)(2,1)} %bitcast.1), calls=%async_computation.1 | async-start | bytes 262144 | tf_op jit(solution)/shard_map/all_to_all | solution.py:198
  22.6 5.9 %copy-start.1 = (bf16[1,144,256]{2,1,0:T(8,128)(2,1)S(1)}, bf16[1,144,256]{2,1,0:T(8,128)(2,1)}, u32[]{:S(2)}) copy-start(bf16[1,144,256]{2,1,0:T(8,128)(2,1)} %pack.1.rest_5_) | copy-start | bytes 221188
  22.6 12.5 %copy-start = (bf16[32,2,4,256]{3,2,1,0:T(4,128)(2,1)S(1)}, bf16[32,2,4,256]{3,2,1,0:T(4,128)(2,1)}, u32[]{:S(2)}) copy-start(bf16[32,2,4,256]{3,2,1,0:T(4,128)(2,1)} %feat_ref.1) | copy-start | bytes 393220
  22.6 12.4 %copy-start.9 = (f32[31,256]{1,0:T(8,128)S(1)}, f32[31,256]{1,0:T(8,128)}, u32[]{:S(2)}) copy-start(f32[31,256]{1,0:T(8,128)} %taps_ref.3) | copy-start | bytes 95236
  22.6 0.6 %copy-start.2 = (bf16[1,144,256]{2,1,0:T(8,128)(2,1)}, bf16[1,144,256]{2,1,0:T(8,128)(2,1)S(1)}, u32[]{:S(2)}) copy-start(bf16[1,144,256]{2,1,0:T(8,128)(2,1)S(1)} %collective-permute-done.3.refs_3_.rest_8_) | copy-start | bytes 221188
  22.6 0.6 %copy-start.4 = (bf16[1,144,256]{2,1,0:T(8,128)(2,1)}, bf16[1,144,256]{2,1,0:T(8,128)(2,1)S(1)}, u32[]{:S(2)}) copy-start(bf16[1,144,256]{2,1,0:T(8,128)(2,1)S(1)} %collective-permute-done.2.refs_2_.rest_7_) | copy-start | bytes 221188
  23.9 11.2 %copy-start.12 = (f32[256]{0:T(256)S(1)}, f32[256]{0:T(256)}, u32[]{:S(2)}) copy-start(f32[256]{0:T(256)} %param.15) | copy-start | bytes 3076
  23.9 11.2 %copy-start.13 = (f32[256]{0:T(256)S(1)}, f32[256]{0:T(256)}, u32[]{:S(2)}) copy-start(f32[256]{0:T(256)} %param.16) | copy-start | bytes 3076
  23.9 11.2 %copy-start.14 = (f32[256]{0:T(256)S(1)}, f32[256]{0:T(256)}, u32[]{:S(2)}) copy-start(f32[256]{0:T(256)} %param.20) | copy-start | bytes 3076
  23.9 11.2 %copy-start.15 = (f32[256]{0:T(256)S(1)}, f32[256]{0:T(256)}, u32[]{:S(2)}) copy-start(f32[256]{0:T(256)} %param.21) | copy-start | bytes 3076
  24.5 5.6 %collective-permute-start.4 = (bf16[1,144,256]{2,1,0:T(8,128)(2,1)}, bf16[1,144,256]{2,1,0:T(8,128)(2,1)S(1)}, u32[]{:S(2)}, u32[]{:S(2)}) collective-permute-start(bf16[1,144,256]{2,1,0:T(8,128)(2,1)} %copy-done.6), channel_id=1, source_target_pairs={{0,2},{1,3},{2,0},{3,1},{4,6},{5,7},{6,4},{7,5},{8,10},{9,11},{10,... | collective-permute-start | bytes 221192 | tf_op jit(solution)/shard_map/ppermute | solution.py:154
  26.4 5.5 %collective-permute-start.5 = (bf16[1,144,256]{2,1,0:T(8,128)(2,1)}, bf16[1,144,256]{2,1,0:T(8,128)(2,1)S(1)}, u32[]{:S(2)}, u32[]{:S(2)}) collective-permute-start(bf16[1,144,256]{2,1,0:T(8,128)(2,1)} %copy-done.4), channel_id=1, source_target_pairs={{0,2},{1,3},{2,0},{3,1},{4,6},{5,7},{6,4},{7,5},{8,10},{9,11},{10,... | collective-permute-start | bytes 221192 | tf_op jit(solution)/shard_map/ppermute | solution.py:154
  26.5 6.6 %collective-permute-start.6 = (bf16[1,144,256]{2,1,0:T(8,128)(2,1)}, bf16[1,144,256]{2,1,0:T(8,128)(2,1)S(1)}, u32[]{:S(2)}, u32[]{:S(2)}) collective-permute-start(bf16[1,144,256]{2,1,0:T(8,128)(2,1)} %copy-done.2), channel_id=1, source_target_pairs={{0,2},{1,3},{2,0},{3,1},{4,6},{5,7},{6,4},{7,5},{8,10},{9,11},{10,... | collective-permute-start | bytes 221192 | tf_op jit(solution)/shard_map/ppermute | solution.py:154
  28.5 4.6 %collective-permute-start.7 = (bf16[1,144,256]{2,1,0:T(8,128)(2,1)S(1)}, bf16[1,144,256]{2,1,0:T(8,128)(2,1)S(1)}, u32[]{:S(2)}, u32[]{:S(2)}) collective-permute-start(bf16[1,144,256]{2,1,0:T(8,128)(2,1)S(1)} %copy-done.1), channel_id=1, source_target_pairs={{0,1},{1,0},{2,3},{3,2},{4,5},{5,4},{6,7},{7,6},{8,9},{9,8},{10,11... | collective-permute-start | bytes 221192 | tf_op jit(solution)/shard_map/ppermute | solution.py:154
  28.5 5.1 %collective-permute-start.8 = (bf16[1,144,256]{2,1,0:T(8,128)(2,1)}, bf16[1,144,256]{2,1,0:T(8,128)(2,1)S(1)}, u32[]{:S(2)}, u32[]{:S(2)}) collective-permute-start(bf16[1,144,256]{2,1,0:T(8,128)(2,1)} %copy-done.6), channel_id=1, source_target_pairs={{0,1},{1,0},{2,3},{3,2},{4,5},{5,4},{6,7},{7,6},{8,9},{9,8},{10,11... | collective-permute-start | bytes 221192 | tf_op jit(solution)/shard_map/ppermute | solution.py:154
  30.1 3.5 %collective-permute-start.9 = (bf16[1,144,256]{2,1,0:T(8,128)(2,1)}, bf16[1,144,256]{2,1,0:T(8,128)(2,1)S(1)}, u32[]{:S(2)}, u32[]{:S(2)}) collective-permute-start(bf16[1,144,256]{2,1,0:T(8,128)(2,1)} %copy-done.4), channel_id=1, source_target_pairs={{0,1},{1,0},{2,3},{3,2},{4,5},{5,4},{6,7},{7,6},{8,9},{9,8},{10,11... | collective-permute-start | bytes 221192 | tf_op jit(solution)/shard_map/ppermute | solution.py:154
  31.9 2.2 %collective-permute-start.10 = (bf16[1,144,256]{2,1,0:T(8,128)(2,1)}, bf16[1,144,256]{2,1,0:T(8,128)(2,1)S(1)}, u32[]{:S(2)}, u32[]{:S(2)}) collective-permute-start(bf16[1,144,256]{2,1,0:T(8,128)(2,1)} %copy-done.2), channel_id=1, source_target_pairs={{0,1},{1,0},{2,3},{3,2},{4,5},{5,4},{6,7},{7,6},{8,9},{9,8},{10,11... | collective-permute-start | bytes 221192 | tf_op jit(solution)/shard_map/ppermute | solution.py:154
  33.1 1.3 %collective-permute-start.11 = (bf16[1,144,256]{2,1,0:T(8,128)(2,1)S(1)}, bf16[1,144,256]{2,1,0:T(8,128)(2,1)S(1)}, u32[]{:S(2)}, u32[]{:S(2)}) collective-permute-start(bf16[1,144,256]{2,1,0:T(8,128)(2,1)S(1)} %collective-permute-done.rest_9_), channel_id=1, source_target_pairs={{0,1},{1,0},{2,3},{3,2},{4,5},{5,4},{6,7},{7,6},{8,9},{9,8},{10,11... | collective-permute-start | bytes 221192 | tf_op jit(solution)/shard_map/ppermute | solution.py:154
  33.1 1.4 %collective-permute-start.12 = (bf16[1,144,256]{2,1,0:T(8,128)(2,1)S(1)}, bf16[1,144,256]{2,1,0:T(8,128)(2,1)S(1)}, u32[]{:S(2)}, u32[]{:S(2)}) collective-permute-start(bf16[1,144,256]{2,1,0:T(8,128)(2,1)S(1)} %collective-permute-done.4.rest_10_), channel_id=1, source_target_pairs={{0,1},{1,0},{2,3},{3,2},{4,5},{5,4},{6,7},{7,6},{8,9},{9,8},{10,11... | collective-permute-start | bytes 221192 | tf_op jit(solution)/shard_map/ppermute | solution.py:154
  33.6 1.3 %collective-permute-start.13 = (bf16[1,144,256]{2,1,0:T(8,128)(2,1)S(1)}, bf16[1,144,256]{2,1,0:T(8,128)(2,1)S(1)}, u32[]{:S(2)}, u32[]{:S(2)}) collective-permute-start(bf16[1,144,256]{2,1,0:T(8,128)(2,1)S(1)} %collective-permute-done.5.rest_11_), channel_id=1, source_target_pairs={{0,1},{1,0},{2,3},{3,2},{4,5},{5,4},{6,7},{7,6},{8,9},{9,8},{10,11... | collective-permute-start | bytes 221192 | tf_op jit(solution)/shard_map/ppermute | solution.py:154
  33.7 1.4 %collective-permute-start.14 = (bf16[1,144,256]{2,1,0:T(8,128)(2,1)S(1)}, bf16[1,144,256]{2,1,0:T(8,128)(2,1)S(1)}, u32[]{:S(2)}, u32[]{:S(2)}) collective-permute-start(bf16[1,144,256]{2,1,0:T(8,128)(2,1)S(1)} %collective-permute-done.6.rest_12_), channel_id=1, source_target_pairs={{0,1},{1,0},{2,3},{3,2},{4,5},{5,4},{6,7},{7,6},{8,9},{9,8},{10,11... | collective-permute-start | bytes 221192 | tf_op jit(solution)/shard_map/ppermute | solution.py:154
  35.0 0.7 %copy-start.10 = (f32[8,128]{1,0:T(8,128)S(1)}, f32[8,128]{1,0:T(8,128)}, u32[]{:S(2)}) copy-start(f32[8,128]{1,0:T(8,128)} %gate.1.rest_21_) | copy-start | bytes 12292
  35.0 0.7 %copy-start.11 = (f32[256]{0:T(256)S(1)}, f32[256]{0:T(256)}, u32[]{:S(2)}) copy-start(f32[256]{0:T(256)} %param.14) | copy-start | bytes 3076
  35.7 0.9 %copy-start.3 = (bf16[1,144,256]{2,1,0:T(8,128)(2,1)S(1)}, bf16[1,144,256]{2,1,0:T(8,128)(2,1)}, u32[]{:S(2)}) copy-start(bf16[1,144,256]{2,1,0:T(8,128)(2,1)} %copy-done.2) | copy-start | bytes 221188
  36.6 0.9 %copy-start.5 = (bf16[1,144,256]{2,1,0:T(8,128)(2,1)S(1)}, bf16[1,144,256]{2,1,0:T(8,128)(2,1)}, u32[]{:S(2)}) copy-start(bf16[1,144,256]{2,1,0:T(8,128)(2,1)} %copy-done.4) | copy-start | bytes 221188
  37.5 0.9 %copy-start.7 = (bf16[1,144,256]{2,1,0:T(8,128)(2,1)S(1)}, bf16[1,144,256]{2,1,0:T(8,128)(2,1)}, u32[]{:S(2)}) copy-start(bf16[1,144,256]{2,1,0:T(8,128)(2,1)} %copy-done.6) | copy-start | bytes 221188
  (1 other events, 0.6 us)

commit v9 on v8

--- a/solution.py
+++ b/solution.py
@@ -16,23 +16,27 @@
     return pl.BlockSpec(memory_space=pltpu.VMEM)
 
 
-def pack_kernel(b_ref, w_in_ref, w_out_ref, slot_ref, sems):
+def pack_kernel(b_ref, w_in_ref, w_out_ref, slot_ref, bias_ref, sems):
     copies = [
         pltpu.make_async_copy(w_in_ref, slot_ref.at[0, 0:SLOT], sems.at[0]),
         pltpu.make_async_copy(w_out_ref, slot_ref.at[0, SLOT : 2 * SLOT], sems.at[1]),
+        pltpu.make_async_copy(b_ref, bias_ref, sems.at[2]),
     ]
     for copy in copies:
         copy.start()
-    bias = b_ref[...].astype(jnp.float32)[None, :]
+    for copy in copies:
+        copy.wait()
+    bias = bias_ref[...].astype(jnp.float32)[None, :]
     c = slot_ref.shape[2]
     wide = jnp.concatenate([bias] * (c // SLOT), axis=1)
     slot_ref[0, 2 * SLOT : 2 * SLOT + EXTRA, :] = jnp.broadcast_to(wide, (EXTRA, c)).astype(slot_ref.dtype)
-    for copy in copies:
-        copy.wait()
-
-
-def gate_kernel(*refs):
-    refs[-1][...] = jnp.zeros_like(refs[-1])
+
+
+def join_kernel(order_ref, *refs):
+    *slots, early_ref, late_ref = refs
+    for i, slot in enumerate(slots):
+        out_ref, at = (early_ref, i) if i < early_ref.shape[0] else (late_ref, i - early_ref.shape[0])
+        out_ref[at] = slot[0]
 
 
 def radial_kernel(x_ref, taps_ref, out_ref, even, odd):
@@ -145,8 +149,8 @@
     hid_loc = w_in.shape[0]
     a_loc = axial // n
     outer, inner, _ = digits(n)
-    spread = hid_loc == SLOT and n == 4 * outer
-    params = pltpu.CompilerParams(vmem_limit_bytes=24 * 1024 * 1024)
+    spread = hid_loc == SLOT and n == 4 * outer and outer > 2
+    small, middle, large = (pltpu.CompilerParams(vmem_limit_bytes=mib * 1024 * 1024) for mib in (2, 12, 24))
     anywhere = pl.BlockSpec(memory_space=pl.ANY)
 
     def move(piece, digit, by):
@@ -157,9 +161,10 @@
         own = pl.pallas_call(
             pack_kernel,
             out_shape=jax.ShapeDtypeStruct((1, 2 * SLOT + EXTRA, c), jnp.bfloat16),
-            in_specs=[vmem()] + [anywhere] * 2,
+            in_specs=[anywhere] * 3,
             out_specs=vmem(),
-            scratch_shapes=[pltpu.SemaphoreType.DMA((2,))],
+            scratch_shapes=[pltpu.VMEM(b_in.shape, jnp.bfloat16), pltpu.SemaphoreType.DMA((3,))],
+            compiler_params=small,
             name="pack",
         )(b_in, w_in, w_out)
         line = [move(own, 0, by) for by in range(1, outer)]
@@ -170,7 +175,7 @@
         o_all = lax.all_gather(w_out, "row", axis=0, tiled=True).reshape(-1, SLOT, c)
         b_all = lax.all_gather(b_in, "row", axis=0, tiled=True).reshape(-1, 1, SLOT)
         b_all = jnp.broadcast_to(jnp.tile(b_all, (1, 1, c // SLOT)), (w_all.shape[0], EXTRA, c))
-        slots, order = [jnp.concatenate([w_all, o_all, b_all], axis=1)], []
+        slots = [jnp.concatenate([w_all, o_all, b_all], axis=1)]
 
     got = lax.all_to_all(features, "row", split_axis=0, concat_axis=0, tiled=True)
     pad = (radial_taps.shape[0] + 1) // 4
@@ -180,19 +185,22 @@
         in_specs=[vmem()] * 2,
         out_specs=vmem(),
         scratch_shapes=[pltpu.VMEM((n + 2 * pad, a_loc, rows, c), jnp.float32)] * 2,
-        compiler_params=params,
+        compiler_params=middle,
         name="radial",
     )(got.reshape(n, a_loc, r_loc, theta, c), radial_taps)
     if spread:
-        gate = pl.pallas_call(
-            gate_kernel,
-            out_shape=jax.ShapeDtypeStruct((8, 128), jnp.float32),
-            in_specs=[anywhere] * outer,
-            out_specs=vmem(),
+        early = (outer - 1) // 2
+        sizes = (outer - 1 - early, early)
+        line = pl.pallas_call(
+            join_kernel,
+            out_shape=[jax.ShapeDtypeStruct((size,) + own.shape[1:], own.dtype) for size in sizes],
+            in_specs=[anywhere] + [vmem()] * (outer - 1),
+            out_specs=[vmem()] * 2,
+            compiler_params=small,
             cost_estimate=pl.CostEstimate(flops=10**10, bytes_accessed=2 * 10**7, transcendentals=0),
-            name="gate",
+            name="join",
         )(mixed, *line)
-        line, *order = lax.optimization_barrier((line, gate))
+        line = list(line)
         across = across + [move(h, 1, 1) for h in line]
         twin = twin + [move(h, 2, 1) for h in line]
     back = lax.all_to_all(mixed.reshape(axial, rows, c), "row", split_axis=0, concat_axis=0, tiled=True)
@@ -203,7 +211,7 @@
     return pl.pallas_call(
         partial(tail_kernel, len(slots)),
         out_shape=jax.ShapeDtypeStruct(features.shape, jnp.bfloat16),
-        in_specs=[vmem()] * 2 + [anywhere] * 6 + [vmem()] * len(slots) + [anywhere] * len(order),
+        in_specs=[vmem()] * 2 + [anywhere] * 6 + [vmem()] * len(slots),
         out_specs=vmem(),
         scratch_shapes=[
             pltpu.VMEM((axial + axial_taps.shape[0] - 1, rows, c), jnp.float32),
@@ -212,9 +220,9 @@
             pltpu.VMEM((5, 1, c), jnp.float32),
             pltpu.SemaphoreType.DMA((6,)),
         ],
-        compiler_params=params,
+        compiler_params=large,
         name="tail",
-    )(back, axial_taps, features, *vectors, *slots, *order)
+    )(back, axial_taps, features, *vectors, *slots)
 
 
 def solution(mesh):

time: 41.5 us -> 38.5 us (0.928)
  waiting for transfers between devices: 5.05 us -> 10.9 us
  local copies, waits for them, and re-layouts: 4.56 us -> 0.69 us
  Pallas kernels: 7.31 us -> 4.53 us
  starting transfers between devices: 23.9 us -> 21.9 us
    unnamed x32 -> x22, local copies, waits for them, and re-layouts: 4.56 us -> 0.69 us
    all_to_all x1, waiting for transfers between devices: 0.01 us -> 3.73 us  [local(): lax.all_to_all(features, 'row', split_axis=0, concat_axis=0, tiled=True)]
    ppermute x15 -> x12, waiting for transfers between devices: 5.04 us -> 7.12 us  [move(): return lax.ppermute(piece, 'row', [(i, i ^ by * stride) for i in range(n)])]
    pallas_call x1, Pallas kernels: 2.09 us -> 0.19 us  [local(): pl.pallas_call(pack_kernel, out_shape=jax.ShapeDtypeStruct((1, 2 * SLOT +...]
    ppermute x15 -> x12, starting transfers between devices: 11.9 us -> 9.99 us  [move(): return lax.ppermute(piece, 'row', [(i, i ^ by * stride) for i in range(n)])]
    pallas_call x1, Pallas kernels: 0.59 us -> 0.02 us  [local(): pl.pallas_call(join_kernel, out_shape=[jax.ShapeDtypeStruct((size,) + own...]
  transfers between devices with their start and end apart: 17 -> 14, of which waited for: 7 -> 6; matrix products, arithmetic and copies ran while one was open for 0% -> 0% of each run, Pallas kernels for 12% -> 5%
where the time goes in v9:
time: 38.5 us; the launch traced here: 38.2 us
  starting transfers between devices  21.9 us (57%)
  waiting for transfers between devices  10.9 us (28%)
  Pallas kernels  4.53 us (12%)
  local copies, waits for them, and re-layouts  0.69 us (2%)
    ppermute x12, starting transfers between devices, move(): return lax.ppermute(piece, 'row', [(i, i ^ by * stride) for i in range(n)])  9.99 us
    all_to_all x1, starting transfers between devices, local(): lax.all_to_all(features, 'row', split_axis=0, concat_axis=0, tiled=True)  7.53 us
    ppermute x12, waiting for transfers between devices, move(): return lax.ppermute(piece, 'row', [(i, i ^ by * stride) for i in range(n)])  7.12 us
    all_to_all x1, starting transfers between devices, local(): lax.all_to_all(mixed.reshape(axial, rows, c), 'row', split_axis=0, concat...  4.4 us
    all_to_all x1, waiting for transfers between devices, local(): lax.all_to_all(features, 'row', split_axis=0, concat_axis=0, tiled=True)  3.73 us
    pallas_call x1, Pallas kernels, local(): pl.pallas_call(partial(tail_kernel, len(slots)), out_shape=jax.ShapeDtype...  2.55 us
    pallas_call x1, Pallas kernels, local(): pl.pallas_call(radial_kernel, out_shape=jax.ShapeDtypeStruct((n, a_loc, r...  1.77 us
  transfers between devices with their start and end apart: 14, of which 6 were waited for; matrix products, arithmetic and copies ran while one was open for 0% of the time, Pallas kernels for 5%

profile of v9, /device:TPU:0, one launch (start us, length us, event | category | flops | bytes accessed | tf_op | source)
XLA Modules:
  0.0 38.2 jit_solution(8173167632190548334)
XLA Ops:
  0.0 7.5 %all-to-all-start = ((bf16[32,2,4,256]{3,2,1,0:T(4,128)(2,1)}), bf16[32,2,4,256]{3,2,1,0:T(4,128)(2,1)S(1)}, u32[]{:S(2)}, u32[]{:S(2)}) async-start(bf16[32,2,4,256]{3,2,1,0:T(4,128)(2,1)} %feat_ref.1), calls=%async_computation | async-start | bytes 262144 | tf_op jit(solution)/shard_map/all_to_all | solution.py:180
  7.6 0.0 copy-start.3
  7.6 0.2 pack.1.rest_5_
  7.8 3.8 %collective-permute-start.3 = (bf16[1,144,256]{2,1,0:T(8,128)(2,1)S(1)}, bf16[1,144,256]{2,1,0:T(8,128)(2,1)S(1)}, u32[]{:S(2)}, u32[]{:S(2)}) collective-permute-start(bf16[1,144,256]{2,1,0:T(8,128)(2,1)S(1)} %pack.1.rest_5_), channel_id=1, source_target_pairs={{0,12},{1,13},{2,14},{3,15},{4,8},{5,9},{6,10},{7,11},{8,4},{9,5},... | collective-permute-start | bytes 221192 | tf_op jit(solution)/shard_map/ppermute | solution.py:158
  11.6 0.7 %collective-permute-start.1 = (bf16[1,144,256]{2,1,0:T(8,128)(2,1)S(1)}, bf16[1,144,256]{2,1,0:T(8,128)(2,1)S(1)}, u32[]{:S(2)}, u32[]{:S(2)}) collective-permute-start(bf16[1,144,256]{2,1,0:T(8,128)(2,1)S(1)} %pack.1.rest_5_), channel_id=1, source_target_pairs={{0,4},{1,5},{2,6},{3,7},{4,0},{5,1},{6,2},{7,3},{8,12},{9,13},{10,... | collective-permute-start | bytes 221192 | tf_op jit(solution)/shard_map/ppermute | solution.py:158
  12.2 3.7 %all-to-all-done = bf16[32,2,4,256]{3,2,1,0:T(4,128)(2,1)S(1)} async-done(((bf16[32,2,4,256]{3,2,1,0:T(4,128)(2,1)}), bf16[32,2,4,256]{3,2,1,0:T(4,128)(2,1)S(1)}, u32[]{:S(2)}, u32[]{:S(2)}) %all-to-all-start) | async-done | bytes 131104 | tf_op jit(solution)/shard_map/all_to_all | solution.py:180
  16.0 1.8 %radial.1.order_ref = bf16[16,2,8,256]{3,2,1,0:T(8,128)(2,1)} custom-call(bf16[16,2,2,4,256]{4,3,2,1,0:T(4,128)(2,1)S(1)} %bitcast.7, f32[31,256]{1,0:T(8,128)S(1)} %copy-done.3), custom_call_target="tpu_custom_call" | custom-call | tf_op jit(solution)/shard_map/radial/pallas_call | solution.py:182
  17.8 4.4 %all-to-all-start.1 = ((bf16[32,8,256]{2,1,0:T(8,128)(2,1)}), bf16[32,8,256]{2,1,0:T(8,128)(2,1)S(1)}, u32[]{:S(2)}, u32[]{:S(2)}) async-start(bf16[32,8,256]{2,1,0:T(8,128)(2,1)} %bitcast.1), calls=%async_computation.1 | async-start | bytes 262144 | tf_op jit(solution)/shard_map/all_to_all | solution.py:206
  22.2 0.0 copy-start
  22.2 0.0 collective-permute-done.1.refs_0_
  22.2 0.0 copy-start.4
  22.2 0.0 copy-start.6
  22.2 0.0 copy-start.7
  22.2 0.0 copy-start.8
  22.2 0.0 copy-start.9
  22.3 2.0 %collective-permute-start.4 = (bf16[2,144,256]{2,1,0:T(8,128)(2,1)S(1)}, bf16[2,144,256]{2,1,0:T(8,128)(2,1)S(1)}, u32[]{:S(2)}, u32[]{:S(2)}) collective-permute-start(bf16[2,144,256]{2,1,0:T(8,128)(2,1)S(1)} %get-tuple-element.11.rest_6_), channel_id=1, source_target_pairs={{0,2},{1,3},{2,0},{3,1},{4,6},{5,7},{6,4},{7,5},{8,10},{9,11},{10,... | collective-permute-start | bytes 442376 | tf_op jit(solution)/shard_map/ppermute | solution.py:158
  24.3 0.1 collective-permute-start
  24.4 1.9 %collective-permute-start.5 = (bf16[1,144,256]{2,1,0:T(8,128)(2,1)S(1)}, bf16[1,144,256]{2,1,0:T(8,128)(2,1)S(1)}, u32[]{:S(2)}, u32[]{:S(2)}) collective-permute-start(bf16[1,144,256]{2,1,0:T(8,128)(2,1)S(1)} %get-tuple-element.12.rest_7_), channel_id=1, source_target_pairs={{0,2},{1,3},{2,0},{3,1},{4,6},{5,7},{6,4},{7,5},{8,10},{9,11},{10,... | collective-permute-start | bytes 221192 | tf_op jit(solution)/shard_map/ppermute | solution.py:158
  26.3 0.5 %collective-permute-start.7 = (bf16[2,144,256]{2,1,0:T(8,128)(2,1)S(1)}, bf16[2,144,256]{2,1,0:T(8,128)(2,1)S(1)}, u32[]{:S(2)}, u32[]{:S(2)}) collective-permute-start(bf16[2,144,256]{2,1,0:T(8,128)(2,1)S(1)} %get-tuple-element.11.rest_6_), channel_id=1, source_target_pairs={{0,1},{1,0},{2,3},{3,2},{4,5},{5,4},{6,7},{7,6},{8,9},{9,8},{10,11... | collective-permute-start | bytes 442376 | tf_op jit(solution)/shard_map/ppermute | solution.py:158
  26.8 5.1 %collective-permute-done.rest_8_ = bf16[1,144,256]{2,1,0:T(8,128)(2,1)S(1)} collective-permute-done((bf16[1,144,256]{2,1,0:T(8,128)(2,1)S(1)}, bf16[1,144,256]{2,1,0:T(8,128)(2,1)S(1)}, u32[]{:S(2)}, u32[]{:S(2)}) %collective-permute-start) | collective-permute-done | bytes 73760 | tf_op jit(solution)/shard_map/ppermute | solution.py:158
  31.9 1.1 %collective-permute-done.5.rest_10_ = bf16[1,144,256]{2,1,0:T(8,128)(2,1)S(1)} collective-permute-done((bf16[1,144,256]{2,1,0:T(8,128)(2,1)S(1)}, bf16[1,144,256]{2,1,0:T(8,128)(2,1)S(1)}, u32[]{:S(2)}, u32[]{:S(2)}) %collective-permute-start.5) | collective-permute-done | bytes 73760 | tf_op jit(solution)/shard_map/ppermute | solution.py:158
  33.0 0.0 collective-permute-done.4.rest_9_
  33.0 0.0 all-to-all-done.1.z_ref
  33.0 0.0 collective-permute-start.10
  33.0 0.5 %collective-permute-start.8 = (bf16[1,144,256]{2,1,0:T(8,128)(2,1)S(1)}, bf16[1,144,256]{2,1,0:T(8,128)(2,1)S(1)}, u32[]{:S(2)}, u32[]{:S(2)}) collective-permute-start(bf16[1,144,256]{2,1,0:T(8,128)(2,1)S(1)} %get-tuple-element.12.rest_7_), channel_id=1, source_target_pairs={{0,1},{1,0},{2,3},{3,2},{4,5},{5,4},{6,7},{7,6},{8,9},{9,8},{10,11... | collective-permute-start | bytes 221192 | tf_op jit(solution)/shard_map/ppermute | solution.py:158
  33.5 0.1 collective-permute-start.9
  33.6 0.4 %collective-permute-start.11 = (bf16[1,144,256]{2,1,0:T(8,128)(2,1)S(1)}, bf16[1,144,256]{2,1,0:T(8,128)(2,1)S(1)}, u32[]{:S(2)}, u32[]{:S(2)}) collective-permute-start(bf16[1,144,256]{2,1,0:T(8,128)(2,1)S(1)} %collective-permute-done.5.rest_10_), channel_id=1, source_target_pairs={{0,1},{1,0},{2,3},{3,2},{4,5},{5,4},{6,7},{7,6},{8,9},{9,8},{10,11... | collective-permute-start | bytes 221192 | tf_op jit(solution)/shard_map/ppermute | solution.py:158
  34.0 0.5 %collective-permute-done.8.rest_13_ = bf16[1,144,256]{2,1,0:T(8,128)(2,1)S(1)} collective-permute-done((bf16[1,144,256]{2,1,0:T(8,128)(2,1)S(1)}, bf16[1,144,256]{2,1,0:T(8,128)(2,1)S(1)}, u32[]{:S(2)}, u32[]{:S(2)}) %collective-permute-start.8) | collective-permute-done | bytes 73760 | tf_op jit(solution)/shard_map/ppermute | solution.py:158
  34.5 0.3 collective-permute-done.9.rest_14_
  34.8 0.2 collective-permute-done.11.rest_16_
  35.0 0.6 %copy-done.5 = f32[256]{0:T(256)S(1)} copy-done((f32[256]{0:T(256)S(1)}, f32[256]{0:T(256)}, u32[]{:S(2)}) %copy-start.5) | copy-done | bytes 1048
  35.6 2.5 %tail.1 = bf16[32,2,4,256]{3,2,1,0:T(4,128)(2,1)} custom-call(bf16[32,8,256]{2,1,0:T(8,128)(2,1)S(1)} %all-to-all-done.1.z_ref, f32[31,256]{1,0:T(8,128)S(1)} %copy-done.4, bf16[32,2,4,256]{3,2,1,0:T(4,128)(2,1)S(1)} %copy-done, f32[1,256]{1,0:T(1,128)S(1)} %bitcast.8, f32[1,256]{1,0:T(1,128)S(1)} %bitcast.9, f32[1,256]{1,0:T(1,128)S(1)} %bitcast.10, ...), custom_call_target="tpu_custom_call" | custom-call | tf_op jit(solution)/shard_map/tail/pallas_call | solution.py:211
  (22 shorter events, 0.1 us)
Async XLA Ops:
  0.0 7.5 %copy-start.2 = (bf16[64,256]{1,0:T(8,128)(2,1)S(1)}, bf16[64,256]{1,0:T(8,128)(2,1)}, u32[]{:S(2)}) copy-start(bf16[64,256]{1,0:T(8,128)(2,1)} %w_out_ref.1) | copy-start | bytes 98308
  0.0 7.6 %copy-start.10 = (bf16[64]{0:T(256)(128)(2,1)S(1)}, bf16[64]{0:T(256)(128)(2,1)}, u32[]{:S(2)}) copy-start(bf16[64]{0:T(256)(128)(2,1)} %b_ref.1) | copy-start | bytes 388
  0.0 7.6 %copy-start.1 = (bf16[64,256]{1,0:T(8,128)(2,1)S(1)}, bf16[64,256]{1,0:T(8,128)(2,1)}, u32[]{:S(2)}) copy-start(bf16[64,256]{1,0:T(8,128)(2,1)} %w_in_ref.1) | copy-start | bytes 98308
  0.0 16.0 %all-to-all-start = ((bf16[32,2,4,256]{3,2,1,0:T(4,128)(2,1)}), bf16[32,2,4,256]{3,2,1,0:T(4,128)(2,1)S(1)}, u32[]{:S(2)}, u32[]{:S(2)}) async-start(bf16[32,2,4,256]{3,2,1,0:T(4,128)(2,1)} %feat_ref.1), calls=%async_computation | async-start | bytes 262144 | tf_op jit(solution)/shard_map/all_to_all | solution.py:180
  7.6 8.4 %copy-start.3 = (f32[31,256]{1,0:T(8,128)S(1)}, f32[31,256]{1,0:T(8,128)}, u32[]{:S(2)}) copy-start(f32[31,256]{1,0:T(8,128)} %taps_ref.2) | copy-start | bytes 95236
  7.8 14.4 %collective-permute-start.3 = (bf16[1,144,256]{2,1,0:T(8,128)(2,1)S(1)}, bf16[1,144,256]{2,1,0:T(8,128)(2,1)S(1)}, u32[]{:S(2)}, u32[]{:S(2)}) collective-permute-start(bf16[1,144,256]{2,1,0:T(8,128)(2,1)S(1)} %pack.1.rest_5_), channel_id=1, source_target_pairs={{0,12},{1,13},{2,14},{3,15},{4,8},{5,9},{6,10},{7,11},{8,4},{9,5},... | collective-permute-start | bytes 221192 | tf_op jit(solution)/shard_map/ppermute | solution.py:158
  11.6 10.6 %collective-permute-start.2 = (bf16[1,144,256]{2,1,0:T(8,128)(2,1)S(1)}, bf16[1,144,256]{2,1,0:T(8,128)(2,1)S(1)}, u32[]{:S(2)}, u32[]{:S(2)}) collective-permute-start(bf16[1,144,256]{2,1,0:T(8,128)(2,1)S(1)} %pack.1.rest_5_), channel_id=1, source_target_pairs={{0,8},{1,9},{2,10},{3,11},{4,12},{5,13},{6,14},{7,15},{8,0},{9,1},... | collective-permute-start | bytes 221192 | tf_op jit(solution)/shard_map/ppermute | solution.py:158
  11.6 10.6 %collective-permute-start.1 = (bf16[1,144,256]{2,1,0:T(8,128)(2,1)S(1)}, bf16[1,144,256]{2,1,0:T(8,128)(2,1)S(1)}, u32[]{:S(2)}, u32[]{:S(2)}) collective-permute-start(bf16[1,144,256]{2,1,0:T(8,128)(2,1)S(1)} %pack.1.rest_5_), channel_id=1, source_target_pairs={{0,4},{1,5},{2,6},{3,7},{4,0},{5,1},{6,2},{7,3},{8,12},{9,13},{10,... | collective-permute-start | bytes 221192 | tf_op jit(solution)/shard_map/ppermute | solution.py:158
  17.8 15.3 %all-to-all-start.1 = ((bf16[32,8,256]{2,1,0:T(8,128)(2,1)}), bf16[32,8,256]{2,1,0:T(8,128)(2,1)S(1)}, u32[]{:S(2)}, u32[]{:S(2)}) async-start(bf16[32,8,256]{2,1,0:T(8,128)(2,1)} %bitcast.1), calls=%async_computation.1 | async-start | bytes 262144 | tf_op jit(solution)/shard_map/all_to_all | solution.py:206
  22.2 12.8 %copy-start = (bf16[32,2,4,256]{3,2,1,0:T(4,128)(2,1)S(1)}, bf16[32,2,4,256]{3,2,1,0:T(4,128)(2,1)}, u32[]{:S(2)}) copy-start(bf16[32,2,4,256]{3,2,1,0:T(4,128)(2,1)} %feat_ref.1) | copy-start | bytes 393220
  22.2 12.8 %copy-start.4 = (f32[31,256]{1,0:T(8,128)S(1)}, f32[31,256]{1,0:T(8,128)}, u32[]{:S(2)}) copy-start(f32[31,256]{1,0:T(8,128)} %taps_ref.3) | copy-start | bytes 95236
  22.2 12.8 %copy-start.6 = (f32[256]{0:T(256)S(1)}, f32[256]{0:T(256)}, u32[]{:S(2)}) copy-start(f32[256]{0:T(256)} %param.15) | copy-start | bytes 3076
  22.2 12.8 %copy-start.7 = (f32[256]{0:T(256)S(1)}, f32[256]{0:T(256)}, u32[]{:S(2)}) copy-start(f32[256]{0:T(256)} %param.16) | copy-start | bytes 3076
  22.2 12.8 %copy-start.8 = (f32[256]{0:T(256)S(1)}, f32[256]{0:T(256)}, u32[]{:S(2)}) copy-start(f32[256]{0:T(256)} %param.20) | copy-start | bytes 3076
  22.2 12.8 %copy-start.9 = (f32[256]{0:T(256)S(1)}, f32[256]{0:T(256)}, u32[]{:S(2)}) copy-start(f32[256]{0:T(256)} %param.21) | copy-start | bytes 3076
  22.3 10.7 %collective-permute-start.4 = (bf16[2,144,256]{2,1,0:T(8,128)(2,1)S(1)}, bf16[2,144,256]{2,1,0:T(8,128)(2,1)S(1)}, u32[]{:S(2)}, u32[]{:S(2)}) collective-permute-start(bf16[2,144,256]{2,1,0:T(8,128)(2,1)S(1)} %get-tuple-element.11.rest_6_), channel_id=1, source_target_pairs={{0,2},{1,3},{2,0},{3,1},{4,6},{5,7},{6,4},{7,5},{8,10},{9,11},{10,... | collective-permute-start | bytes 442376 | tf_op jit(solution)/shard_map/ppermute | solution.py:158
  24.3 7.6 %collective-permute-start = (bf16[1,144,256]{2,1,0:T(8,128)(2,1)S(1)}, bf16[1,144,256]{2,1,0:T(8,128)(2,1)S(1)}, u32[]{:S(2)}, u32[]{:S(2)}) collective-permute-start(bf16[1,144,256]{2,1,0:T(8,128)(2,1)S(1)} %pack.1.rest_5_), channel_id=1, source_target_pairs={{0,2},{1,3},{2,0},{3,1},{4,6},{5,7},{6,4},{7,5},{8,10},{9,11},{10,... | collective-permute-start | bytes 221192 | tf_op jit(solution)/shard_map/ppermute | solution.py:158
  24.4 8.6 %collective-permute-start.5 = (bf16[1,144,256]{2,1,0:T(8,128)(2,1)S(1)}, bf16[1,144,256]{2,1,0:T(8,128)(2,1)S(1)}, u32[]{:S(2)}, u32[]{:S(2)}) collective-permute-start(bf16[1,144,256]{2,1,0:T(8,128)(2,1)S(1)} %get-tuple-element.12.rest_7_), channel_id=1, source_target_pairs={{0,2},{1,3},{2,0},{3,1},{4,6},{5,7},{6,4},{7,5},{8,10},{9,11},{10,... | collective-permute-start | bytes 221192 | tf_op jit(solution)/shard_map/ppermute | solution.py:158
  26.3 7.3 %collective-permute-start.6 = (bf16[1,144,256]{2,1,0:T(8,128)(2,1)S(1)}, bf16[1,144,256]{2,1,0:T(8,128)(2,1)S(1)}, u32[]{:S(2)}, u32[]{:S(2)}) collective-permute-start(bf16[1,144,256]{2,1,0:T(8,128)(2,1)S(1)} %pack.1.rest_5_), channel_id=1, source_target_pairs={{0,1},{1,0},{2,3},{3,2},{4,5},{5,4},{6,7},{7,6},{8,9},{9,8},{10,11... | collective-permute-start | bytes 221192 | tf_op jit(solution)/shard_map/ppermute | solution.py:158
  26.3 8.2 %collective-permute-start.7 = (bf16[2,144,256]{2,1,0:T(8,128)(2,1)S(1)}, bf16[2,144,256]{2,1,0:T(8,128)(2,1)S(1)}, u32[]{:S(2)}, u32[]{:S(2)}) collective-permute-start(bf16[2,144,256]{2,1,0:T(8,128)(2,1)S(1)} %get-tuple-element.11.rest_6_), channel_id=1, source_target_pairs={{0,1},{1,0},{2,3},{3,2},{4,5},{5,4},{6,7},{7,6},{8,9},{9,8},{10,11... | collective-permute-start | bytes 442376 | tf_op jit(solution)/shard_map/ppermute | solution.py:158
  33.0 1.9 %collective-permute-start.10 = (bf16[2,144,256]{2,1,0:T(8,128)(2,1)S(1)}, bf16[2,144,256]{2,1,0:T(8,128)(2,1)S(1)}, u32[]{:S(2)}, u32[]{:S(2)}) collective-permute-start(bf16[2,144,256]{2,1,0:T(8,128)(2,1)S(1)} %collective-permute-done.4.rest_9_), channel_id=1, source_target_pairs={{0,1},{1,0},{2,3},{3,2},{4,5},{5,4},{6,7},{7,6},{8,9},{9,8},{10,11... | collective-permute-start | bytes 442376 | tf_op jit(solution)/shard_map/ppermute | solution.py:158
  33.0 1.5 %collective-permute-start.8 = (bf16[1,144,256]{2,1,0:T(8,128)(2,1)S(1)}, bf16[1,144,256]{2,1,0:T(8,128)(2,1)S(1)}, u32[]{:S(2)}, u32[]{:S(2)}) collective-permute-start(bf16[1,144,256]{2,1,0:T(8,128)(2,1)S(1)} %get-tuple-element.12.rest_7_), channel_id=1, source_target_pairs={{0,1},{1,0},{2,3},{3,2},{4,5},{5,4},{6,7},{7,6},{8,9},{9,8},{10,11... | collective-permute-start | bytes 221192 | tf_op jit(solution)/shard_map/ppermute | solution.py:158
  33.5 1.3 %collective-permute-start.9 = (bf16[1,144,256]{2,1,0:T(8,128)(2,1)S(1)}, bf16[1,144,256]{2,1,0:T(8,128)(2,1)S(1)}, u32[]{:S(2)}, u32[]{:S(2)}) collective-permute-start(bf16[1,144,256]{2,1,0:T(8,128)(2,1)S(1)} %collective-permute-done.rest_8_), channel_id=1, source_target_pairs={{0,1},{1,0},{2,3},{3,2},{4,5},{5,4},{6,7},{7,6},{8,9},{9,8},{10,11... | collective-permute-start | bytes 221192 | tf_op jit(solution)/shard_map/ppermute | solution.py:158
  33.6 1.4 %collective-permute-start.11 = (bf16[1,144,256]{2,1,0:T(8,128)(2,1)S(1)}, bf16[1,144,256]{2,1,0:T(8,128)(2,1)S(1)}, u32[]{:S(2)}, u32[]{:S(2)}) collective-permute-start(bf16[1,144,256]{2,1,0:T(8,128)(2,1)S(1)} %collective-permute-done.5.rest_10_), channel_id=1, source_target_pairs={{0,1},{1,0},{2,3},{3,2},{4,5},{5,4},{6,7},{7,6},{8,9},{9,8},{10,11... | collective-permute-start | bytes 221192 | tf_op jit(solution)/shard_map/ppermute | solution.py:158
  35.0 0.7 %copy-start.5 = (f32[256]{0:T(256)S(1)}, f32[256]{0:T(256)}, u32[]{:S(2)}) copy-start(f32[256]{0:T(256)} %param.14) | copy-start | bytes 3076

commit v10 on v9

v10 whole, which is shorter than its diff:
```python
import math
from functools import partial

import jax
import jax.numpy as jnp
from jax import lax
from jax.experimental import pallas as pl
from jax.experimental.pallas import tpu as pltpu
from jax.sharding import PartitionSpec as P

SLOT = 64
EXTRA = 16


def vmem():
    return pl.BlockSpec(memory_space=pltpu.VMEM)


def pack_kernel(b_ref, w_in_ref, w_out_ref, *rest):
    *vectors, block_ref, consts_ref = rest
    block_ref[0:SLOT, :] = w_in_ref[...]
    block_ref[SLOT : 2 * SLOT, :] = w_out_ref[...]
    bias = b_ref[...].astype(jnp.float32)[None, :]
    c = block_ref.shape[1]
    wide = jnp.concatenate([bias] * (c // SLOT), axis=1)
    block_ref[2 * SLOT :, :] = jnp.broadcast_to(wide, (EXTRA, c)).astype(block_ref.dtype)
    for i, vector in enumerate(vectors):
        consts_ref[i : i + 1, :] = vector[...]


def join_kernel(*refs):
    blocks, out_ref = refs[2:-1], refs[-1]
    c = out_ref.shape[1]
    row = lax.broadcasted_iota(jnp.int32, (EXTRA, c), 0)
    biases = jnp.zeros((EXTRA, c), jnp.float32)
    for i, block in enumerate(blocks):
        out_ref[2 * SLOT * i : 2 * SLOT * (i + 1), :] = block[0 : 2 * SLOT, :]
        biases = jnp.where(row == i, block[2 * SLOT :, :].astype(jnp.float32), biases)
    out_ref[2 * SLOT * len(blocks) :, :] = biases.astype(out_ref.dtype)


def radial_kernel(x_ref, taps_ref, out_ref, even, odd):
    n, a_loc, _, theta, c = x_ref.shape
    taps = taps_ref.shape[0]
    pad = (taps + 1) // 4
    zeros = jnp.zeros((pad, a_loc, 2 * theta, c), jnp.float32)
    even[0:pad] = zeros
    even[pad + n : 2 * pad + n] = zeros
    odd[0:pad] = zeros
    odd[pad + n - 1 : 2 * pad + n - 1] = zeros
    odd[2 * pad + n - 1 :] = zeros[:1]
    first = x_ref[:, :, 0].astype(jnp.float32)
    second = x_ref[:, :, 1].astype(jnp.float32)
    even[pad : pad + n, :, 0:theta] = first
    even[pad : pad + n, :, theta:] = second
    odd[pad : pad + n, :, 0:theta] = second
    odd[pad - 1 : pad + n - 1, :, theta:] = first

    def step(s, carry):
        total = jnp.zeros((a_loc, 2 * theta, c), jnp.float32)
        for k in range(taps):
            shift = k - taps // 2
            source = even if shift % 2 == 0 else odd
            total = total + source[s + (pad + shift // 2)] * taps_ref[k : k + 1, :]
        out_ref[s] = total.astype(out_ref.dtype)
        return carry

    lax.fori_loop(0, n, step, 0)


def tail_kernel(z_ref, taps_ref, consts_ref, feat_ref, *rest):
    *blocks, out_ref, padded, branch, field, sem = rest
    fetch = pltpu.make_async_copy(feat_ref, field, sem)
    fetch.start()
    axial, rows, c = z_ref.shape
    theta = rows // 2
    taps = taps_ref.shape[0]
    half = taps // 2
    zeros = jnp.zeros((half, rows, c), jnp.float32)
    padded[0:half] = zeros
    padded[half + axial :] = zeros
    padded[half : half + axial] = z_ref[...].astype(jnp.float32)
    block = 4

    def conv(i, carry):
        base = i * block
        total = jnp.zeros((block, rows, c), jnp.float32)
        for k in range(taps):
            total = total + padded[pl.ds(base + k, block)] * taps_ref[k : k + 1, :]
        branch[pl.ds(base, block)] = total
        return carry

    lax.fori_loop(0, axial // block, conv, 0)
    fetch.wait()
    slots = [(block, i) for block in blocks for i in range(block.shape[0] // (2 * SLOT))]
    per = c // SLOT
    lane_slot = lax.broadcasted_iota(jnp.int32, (1, c), 1) // SLOT
    planes = 32

    def mlp(i, carry):
        v = (branch[pl.ds(i * planes, planes)] + consts_ref[0 : 1, :]).reshape(planes * rows, c)
        v = v.astype(jnp.bfloat16).astype(jnp.float32)
        mean = jnp.mean(v, axis=-1, keepdims=True)
        centred = v - mean
        var = jnp.mean(centred * centred, axis=-1, keepdims=True)
        normed = (centred * lax.rsqrt(var + 1e-06) * consts_ref[1 : 2, :] + consts_ref[2 : 3, :]).astype(jnp.bfloat16)
        total = jnp.zeros((planes * rows, c), jnp.float32)
        for g in range(len(slots) // per):
            own = slots[g * per : (g + 1) * per]
            w_in = jnp.concatenate([w[2 * SLOT * j : 2 * SLOT * j + SLOT, :] for w, j in own], axis=0)
            w_out = jnp.concatenate([w[2 * SLOT * j + SLOT : 2 * SLOT * (j + 1), :] for w, j in own], axis=0)
            bias = jnp.zeros((1, c), jnp.float32)
            for at, (w, j) in enumerate(own):
                piece = w[w.shape[0] - EXTRA :, :].astype(jnp.float32)[j : j + 1]
                bias = jnp.where(lane_slot == at, piece, bias)
            u = lax.dot_general(normed, w_in, (((1,), (1,)), ((), ())), preferred_element_type=jnp.float32)
            u = u + bias
            hidden = (0.5 * u * (1.0 + jnp.tanh(0.7978845608028654 * (u + 0.044715 * u * u * u)))).astype(jnp.bfloat16)
            total = total + jnp.dot(hidden, w_out, preferred_element_type=jnp.float32)
        result = (consts_ref[4 : 5, :] * (total + consts_ref[3 : 4, :])).astype(jnp.bfloat16).astype(jnp.float32)
        branch[pl.ds(i * planes, planes)] = result.reshape(planes, rows, c)
        return carry

    if axial == planes:
        mlp(0, 0)
    else:
        lax.fori_loop(0, axial // planes, mlp, 0)
    for r in range(2):
        got = branch[:, r * theta : (r + 1) * theta, :]
        out_ref[:, r] = (field[:, r].astype(jnp.float32) + got).astype(out_ref.dtype)


def digits(n):
    chips = n // 2
    inner = 1
    while inner * inner * 4 <= chips:
        inner *= 2
    return chips // inner, inner, 2


def local(n, features, axial_taps, radial_taps, conv_bias, ln_gain, ln_bias, w_in, b_in, w_out, b_out, layer_scale):
    axial, r_loc, theta, c = features.shape
    rows = r_loc * theta
    hid_loc = w_in.shape[0]
    a_loc = axial // n
    outer, inner, _ = digits(n)
    spread = hid_loc == SLOT and n == 4 * outer and 2 < outer <= EXTRA
    small, middle, large = (pltpu.CompilerParams(vmem_limit_bytes=mib * 1024 * 1024) for mib in (2, 12, 24))
    anywhere = pl.BlockSpec(memory_space=pl.ANY)

    def move(piece, digit, by):
        stride = math.prod(digits(n)[digit + 1 :])
        return lax.ppermute(piece, "row", [(i, i ^ (by * stride)) for i in range(n)])

    vectors = [v[None, :] for v in (conv_bias, ln_gain, ln_bias, b_out, layer_scale)]
    if spread:
        own, consts = pl.pallas_call(
            pack_kernel,
            out_shape=[
                jax.ShapeDtypeStruct((2 * SLOT + EXTRA, c), jnp.bfloat16),
                jax.ShapeDtypeStruct((8, c), jnp.float32),
            ],
            in_specs=[vmem()] * 8,
            out_specs=[vmem()] * 2,
            compiler_params=small,
            name="pack",
        )(b_in, w_in, w_out, *vectors)
        line = [move(own, 0, by) for by in range(1, outer)]
        side = move(own, 1, 1)
    else:
        consts = jnp.concatenate(vectors + [jnp.zeros((3, c), jnp.float32)], axis=0)
        w_all = lax.all_gather(w_in, "row", axis=0, tiled=True).reshape(-1, SLOT, c)
        o_all = lax.all_gather(w_out, "row", axis=0, tiled=True).reshape(-1, SLOT, c)
        b_all = jnp.tile(lax.all_gather(b_in, "row", axis=0, tiled=True).reshape(-1, SLOT), (1, c // SLOT))
        w_all = jnp.concatenate([w_all, o_all], axis=1).reshape(-1, c)
        blocks = [jnp.concatenate([w_all, jnp.pad(b_all, ((0, EXTRA - b_all.shape[0]), (0, 0)))], axis=0)]

    got = lax.all_to_all(features, "row", split_axis=0, concat_axis=0, tiled=True)
    pad = (radial_taps.shape[0] + 1) // 4
    mixed = pl.pallas_call(
        radial_kernel,
        out_shape=jax.ShapeDtypeStruct((n, a_loc, rows, c), jnp.bfloat16),
        in_specs=[vmem()] * 2,
        out_specs=vmem(),
        scratch_shapes=[pltpu.VMEM((n + 2 * pad, a_loc, rows, c), jnp.float32)] * 2,
        compiler_params=middle,
        name="radial",
    )(got.reshape(n, a_loc, r_loc, theta, c), radial_taps)
    if spread:
        joined = pl.pallas_call(
            join_kernel,
            out_shape=jax.ShapeDtypeStruct((2 * SLOT * (outer - 1) + EXTRA, c), jnp.bfloat16),
            in_specs=[anywhere] * 2 + [vmem()] * (outer - 1),
            out_specs=vmem(),
            compiler_params=small,
            cost_estimate=pl.CostEstimate(flops=10**10, bytes_accessed=2 * 10**7, transcendentals=0),
            name="join",
        )(mixed, side, *line)
        across = move(joined, 1, 1)
        twin = [move(h, 2, 1) for h in (own, side, joined)]
    back = lax.all_to_all(mixed.reshape(axial, rows, c), "row", split_axis=0, concat_axis=0, tiled=True)
    if spread:
        across, back = lax.optimization_barrier((across, back))
        blocks = [own, joined, side, across] + twin + [move(across, 2, 1)]
    return pl.pallas_call(
        tail_kernel,
        out_shape=jax.ShapeDtypeStruct(features.shape, jnp.bfloat16),
        in_specs=[vmem()] * 3 + [anywhere] + [vmem()] * len(blocks),
        out_specs=vmem(),
        scratch_shapes=[
            pltpu.VMEM((axial + axial_taps.shape[0] - 1, rows, c), jnp.float32),
            pltpu.VMEM((axial, rows, c), jnp.float32),
            pltpu.VMEM(features.shape, jnp.bfloat16),
            pltpu.SemaphoreType.DMA(()),
        ],
        compiler_params=large,
        name="tail",
    )(back, axial_taps, consts, features, *blocks)


def solution(mesh):
    in_specs = (
        P("groups", "row", None, None),
        P(),
        P(),
        P(),
        P(),
        P(),
        P("row", None),
        P("row"),
        P("row", None),
        P(),
        P(),
    )
    out_specs = P("groups", "row", None, None)
    return jax.shard_map(partial(local, mesh.shape["row"]), mesh=mesh, in_specs=in_specs, out_specs=out_specs, check_vma=False)
```

time: 38.5 us -> 35.7 us (0.927)
  waiting for transfers between devices: 10.9 us -> 9.4 us
  starting transfers between devices: 21.9 us -> 20.7 us
    all_to_all x1, waiting for transfers between devices: 3.73 us -> 1.28 us  [local(): lax.all_to_all(features, 'row', split_axis=0, concat_axis=0, tiled=True)]
    ppermute x12 -> x9, starting transfers between devices: 9.99 us -> 8.81 us  [move(): return lax.ppermute(piece, 'row', [(i, i ^ by * stride) for i in range(n)])]
    ppermute x12 -> x9, waiting for transfers between devices: 7.12 us -> 8.12 us  [move(): return lax.ppermute(piece, 'row', [(i, i ^ by * stride) for i in range(n)])]
  transfers between devices with their start and end apart: 14 -> 11, of which waited for: 6 -> 4; matrix products, arithmetic and copies ran while one was open for 0% -> 0% of each run, Pallas kernels for 5% -> 5%
where the time goes in v10:
time: 35.7 us; the launch traced here: 35.4 us
  starting transfers between devices  20.7 us (58%)
  waiting for transfers between devices  9.4 us (26%)
  Pallas kernels  4.37 us (12%)
  local copies, waits for them, and re-layouts  0.7 us (2%)
    ppermute x9, starting transfers between devices, move(): return lax.ppermute(piece, 'row', [(i, i ^ by * stride) for i in range(n)])  8.81 us
    ppermute x9, waiting for transfers between devices, move(): return lax.ppermute(piece, 'row', [(i, i ^ by * stride) for i in range(n)])  8.12 us
    all_to_all x1, starting transfers between devices, local(): lax.all_to_all(features, 'row', split_axis=0, concat_axis=0, tiled=True)  7.52 us
    all_to_all x1, starting transfers between devices, local(): lax.all_to_all(mixed.reshape(axial, rows, c), 'row', split_axis=0, concat...  4.4 us
    pallas_call x1, Pallas kernels, local(): pl.pallas_call(tail_kernel, out_shape=jax.ShapeDtypeStruct(features.shape...  2.5 us
    pallas_call x1, Pallas kernels, local(): pl.pallas_call(radial_kernel, out_shape=jax.ShapeDtypeStruct((n, a_loc, r...  1.77 us
    all_to_all x1, waiting for transfers between devices, local(): lax.all_to_all(features, 'row', split_axis=0, concat_axis=0, tiled=True)  1.28 us
  transfers between devices with their start and end apart: 11, of which 4 were waited for; matrix products, arithmetic and copies ran while one was open for 0% of the time, Pallas kernels for 5%

profile of v10, /device:TPU:0, one launch (start us, length us, event | category | flops | bytes accessed | tf_op | source)
XLA Modules:
  0.0 35.4 jit_solution(17516985324516631561)
XLA Ops:
  0.0 7.5 %all-to-all-start = ((bf16[32,2,4,256]{3,2,1,0:T(4,128)(2,1)}), bf16[32,2,4,256]{3,2,1,0:T(4,128)(2,1)S(1)}, u32[]{:S(2)}, u32[]{:S(2)}) async-start(bf16[32,2,4,256]{3,2,1,0:T(4,128)(2,1)} %feat_ref.1), calls=%async_computation | async-start | bytes 262144 | tf_op jit(solution)/shard_map/all_to_all | solution.py:178
  7.5 0.0 copy-start.6
  7.5 0.0 copy-start.7
  7.6 0.0 copy-start.8
  7.6 0.0 copy-start.9
  7.6 0.0 copy-start.5
  7.6 0.0 copy-start.10
  7.6 0.6 %copy-done.6 = f32[256]{0:T(256)S(1)} copy-done((f32[256]{0:T(256)S(1)}, f32[256]{0:T(256)}, u32[]{:S(2)}) %copy-start.6) | copy-done | bytes 1048
  8.2 0.0 copy-done.7
  8.2 0.0 copy-done.8
  8.2 0.0 copy-done.9
  8.3 0.0 copy-done.5
  8.3 0.1 pack.1
  8.4 3.7 %collective-permute-start.3 = (bf16[144,256]{1,0:T(8,128)(2,1)S(1)}, bf16[144,256]{1,0:T(8,128)(2,1)S(1)}, u32[]{:S(2)}, u32[]{:S(2)}) collective-permute-start(bf16[144,256]{1,0:T(8,128)(2,1)S(1)} %get-tuple-element.9.rest_0_), channel_id=1, source_target_pairs={{0,12},{1,13},{2,14},{3,15},{4,8},{5,9},{6,10},{7,11},{8,4},{9,5},... | collective-permute-start | bytes 221192 | tf_op jit(solution)/shard_map/ppermute | solution.py:153
  12.1 0.7 %collective-permute-start.1 = (bf16[144,256]{1,0:T(8,128)(2,1)S(1)}, bf16[144,256]{1,0:T(8,128)(2,1)S(1)}, u32[]{:S(2)}, u32[]{:S(2)}) collective-permute-start(bf16[144,256]{1,0:T(8,128)(2,1)S(1)} %get-tuple-element.9.rest_0_), channel_id=1, source_target_pairs={{0,4},{1,5},{2,6},{3,7},{4,0},{5,1},{6,2},{7,3},{8,12},{9,13},{10,... | collective-permute-start | bytes 221192 | tf_op jit(solution)/shard_map/ppermute | solution.py:153
  12.7 1.9 %collective-permute-start = (bf16[144,256]{1,0:T(8,128)(2,1)S(1)}, bf16[144,256]{1,0:T(8,128)(2,1)S(1)}, u32[]{:S(2)}, u32[]{:S(2)}) collective-permute-start(bf16[144,256]{1,0:T(8,128)(2,1)S(1)} %get-tuple-element.9.rest_0_), channel_id=1, source_target_pairs={{0,2},{1,3},{2,0},{3,1},{4,6},{5,7},{6,4},{7,5},{8,10},{9,11},{10,... | collective-permute-start | bytes 221192 | tf_op jit(solution)/shard_map/ppermute | solution.py:153
  14.7 1.3 %all-to-all-done = bf16[32,2,4,256]{3,2,1,0:T(4,128)(2,1)S(1)} async-done(((bf16[32,2,4,256]{3,2,1,0:T(4,128)(2,1)}), bf16[32,2,4,256]{3,2,1,0:T(4,128)(2,1)S(1)}, u32[]{:S(2)}, u32[]{:S(2)}) %all-to-all-start) | async-done | bytes 131104 | tf_op jit(solution)/shard_map/all_to_all | solution.py:178
  16.0 1.8 %radial.1.refs_0_ = bf16[16,2,8,256]{3,2,1,0:T(8,128)(2,1)} custom-call(bf16[16,2,2,4,256]{4,3,2,1,0:T(4,128)(2,1)S(1)} %bitcast.7, f32[31,256]{1,0:T(8,128)S(1)} %copy-done.1), custom_call_target="tpu_custom_call" | custom-call | tf_op jit(solution)/shard_map/radial/pallas_call | solution.py:180
  17.7 4.4 %all-to-all-start.1 = ((bf16[32,8,256]{2,1,0:T(8,128)(2,1)}), bf16[32,8,256]{2,1,0:T(8,128)(2,1)S(1)}, u32[]{:S(2)}, u32[]{:S(2)}) async-start(bf16[32,8,256]{2,1,0:T(8,128)(2,1)} %bitcast.6), calls=%async_computation.1 | async-start | bytes 262144 | tf_op jit(solution)/shard_map/all_to_all | solution.py:201
  22.1 0.0 copy-start
  22.1 0.0 copy-start.2
  22.2 0.0 collective-permute-done.3.refs_4_
  22.2 0.0 collective-permute-done.1.refs_2_
  22.2 0.0 collective-permute-done.refs_1_.rest_2_
  22.2 2.0 %collective-permute-start.4 = (bf16[400,256]{1,0:T(8,128)(2,1)S(1)}, bf16[400,256]{1,0:T(8,128)(2,1)S(1)}, u32[]{:S(2)}, u32[]{:S(2)}) collective-permute-start(bf16[400,256]{1,0:T(8,128)(2,1)S(1)} %join.1.rest_1_), channel_id=1, source_target_pairs={{0,2},{1,3},{2,0},{3,1},{4,6},{5,7},{6,4},{7,5},{8,10},{9,11},{10,... | collective-permute-start | bytes 614408 | tf_op jit(solution)/shard_map/ppermute | solution.py:153
  24.2 0.0 collective-permute-start.7
  24.2 6.8 %collective-permute-done.4.rest_3_ = bf16[400,256]{1,0:T(8,128)(2,1)S(1)} collective-permute-done((bf16[400,256]{1,0:T(8,128)(2,1)S(1)}, bf16[400,256]{1,0:T(8,128)(2,1)S(1)}, u32[]{:S(2)}, u32[]{:S(2)}) %collective-permute-start.4) | collective-permute-done | bytes 204832 | tf_op jit(solution)/shard_map/ppermute | solution.py:153
  31.1 0.5 %collective-permute-start.5 = (bf16[144,256]{1,0:T(8,128)(2,1)S(1)}, bf16[144,256]{1,0:T(8,128)(2,1)S(1)}, u32[]{:S(2)}, u32[]{:S(2)}) collective-permute-start(bf16[144,256]{1,0:T(8,128)(2,1)S(1)} %get-tuple-element.9.rest_0_), channel_id=1, source_target_pairs={{0,1},{1,0},{2,3},{3,2},{4,5},{5,4},{6,7},{7,6},{8,9},{9,8},{10,11... | collective-permute-start | bytes 221192 | tf_op jit(solution)/shard_map/ppermute | solution.py:153
  31.6 0.0 collective-permute-start.6
  31.6 1.0 %collective-permute-done.5.rest_4_ = bf16[144,256]{1,0:T(8,128)(2,1)S(1)} collective-permute-done((bf16[144,256]{1,0:T(8,128)(2,1)S(1)}, bf16[144,256]{1,0:T(8,128)(2,1)S(1)}, u32[]{:S(2)}, u32[]{:S(2)}) %collective-permute-start.5) | collective-permute-done | bytes 73760 | tf_op jit(solution)/shard_map/ppermute | solution.py:153
  32.6 0.2 collective-permute-done.6.rest_5_
  32.9 2.5 %tail.1 = bf16[32,2,4,256]{3,2,1,0:T(4,128)(2,1)} custom-call(bf16[32,8,256]{2,1,0:T(8,128)(2,1)S(1)} %all-to-all-done.1.z_ref, f32[31,256]{1,0:T(8,128)S(1)} %copy-done.2, f32[8,256]{1,0:T(8,128)S(1)} %get-tuple-element.11.consts_ref, bf16[32,2,4,256]{3,2,1,0:T(4,128)(2,1)S(1)} %copy-done, bf16[144,256]{1,0:T(8,128)(2,1)S(1)} %get-tuple-element.9.rest_0_, ...), custom_call_target="tpu_custom_call" | custom-call | tf_op jit(solution)/shard_map/tail/pallas_call | solution.py:205
  (16 shorter events, 0.1 us)
Async XLA Ops:
  0.0 7.6 %copy-start.4 = (bf16[64,256]{1,0:T(8,128)(2,1)S(1)}, bf16[64,256]{1,0:T(8,128)(2,1)}, u32[]{:S(2)}) copy-start(bf16[64,256]{1,0:T(8,128)(2,1)} %w_out_ref.1) | copy-start | bytes 98308
  0.0 7.6 %copy-start.3 = (bf16[64,256]{1,0:T(8,128)(2,1)S(1)}, bf16[64,256]{1,0:T(8,128)(2,1)}, u32[]{:S(2)}) copy-start(bf16[64,256]{1,0:T(8,128)(2,1)} %w_in_ref.1) | copy-start | bytes 98308
  0.0 16.0 %all-to-all-start = ((bf16[32,2,4,256]{3,2,1,0:T(4,128)(2,1)}), bf16[32,2,4,256]{3,2,1,0:T(4,128)(2,1)S(1)}, u32[]{:S(2)}, u32[]{:S(2)}) async-start(bf16[32,2,4,256]{3,2,1,0:T(4,128)(2,1)} %feat_ref.1), calls=%async_computation | async-start | bytes 262144 | tf_op jit(solution)/shard_map/all_to_all | solution.py:178
  7.5 0.7 %copy-start.6 = (f32[256]{0:T(256)S(1)}, f32[256]{0:T(256)}, u32[]{:S(2)}) copy-start(f32[256]{0:T(256)} %param.15) | copy-start | bytes 3076
  7.5 0.7 %copy-start.7 = (f32[256]{0:T(256)S(1)}, f32[256]{0:T(256)}, u32[]{:S(2)}) copy-start(f32[256]{0:T(256)} %param.16) | copy-start | bytes 3076
  7.6 0.7 %copy-start.8 = (f32[256]{0:T(256)S(1)}, f32[256]{0:T(256)}, u32[]{:S(2)}) copy-start(f32[256]{0:T(256)} %param.20) | copy-start | bytes 3076
  7.6 0.7 %copy-start.9 = (f32[256]{0:T(256)S(1)}, f32[256]{0:T(256)}, u32[]{:S(2)}) copy-start(f32[256]{0:T(256)} %param.21) | copy-start | bytes 3076
  7.6 0.7 %copy-start.5 = (f32[256]{0:T(256)S(1)}, f32[256]{0:T(256)}, u32[]{:S(2)}) copy-start(f32[256]{0:T(256)} %param.14) | copy-start | bytes 3076
  7.6 0.7 %copy-start.10 = (bf16[64]{0:T(256)(128)(2,1)S(1)}, bf16[64]{0:T(256)(128)(2,1)}, u32[]{:S(2)}) copy-start(bf16[64]{0:T(256)(128)(2,1)} %b_ref.1) | copy-start | bytes 388
  8.3 7.7 %copy-start.1 = (f32[31,256]{1,0:T(8,128)S(1)}, f32[31,256]{1,0:T(8,128)}, u32[]{:S(2)}) copy-start(f32[31,256]{1,0:T(8,128)} %taps_ref.2) | copy-start | bytes 95236
  8.4 13.8 %collective-permute-start.3 = (bf16[144,256]{1,0:T(8,128)(2,1)S(1)}, bf16[144,256]{1,0:T(8,128)(2,1)S(1)}, u32[]{:S(2)}, u32[]{:S(2)}) collective-permute-start(bf16[144,256]{1,0:T(8,128)(2,1)S(1)} %get-tuple-element.9.rest_0_), channel_id=1, source_target_pairs={{0,12},{1,13},{2,14},{3,15},{4,8},{5,9},{6,10},{7,11},{8,4},{9,5},... | collective-permute-start | bytes 221192 | tf_op jit(solution)/shard_map/ppermute | solution.py:153
  12.1 10.1 %collective-permute-start.2 = (bf16[144,256]{1,0:T(8,128)(2,1)S(1)}, bf16[144,256]{1,0:T(8,128)(2,1)S(1)}, u32[]{:S(2)}, u32[]{:S(2)}) collective-permute-start(bf16[144,256]{1,0:T(8,128)(2,1)S(1)} %get-tuple-element.9.rest_0_), channel_id=1, source_target_pairs={{0,8},{1,9},{2,10},{3,11},{4,12},{5,13},{6,14},{7,15},{8,0},{9,1},... | collective-permute-start | bytes 221192 | tf_op jit(solution)/shard_map/ppermute | solution.py:153
  12.1 10.1 %collective-permute-start.1 = (bf16[144,256]{1,0:T(8,128)(2,1)S(1)}, bf16[144,256]{1,0:T(8,128)(2,1)S(1)}, u32[]{:S(2)}, u32[]{:S(2)}) collective-permute-start(bf16[144,256]{1,0:T(8,128)(2,1)S(1)} %get-tuple-element.9.rest_0_), channel_id=1, source_target_pairs={{0,4},{1,5},{2,6},{3,7},{4,0},{5,1},{6,2},{7,3},{8,12},{9,13},{10,... | collective-permute-start | bytes 221192 | tf_op jit(solution)/shard_map/ppermute | solution.py:153
  12.7 9.4 %collective-permute-start = (bf16[144,256]{1,0:T(8,128)(2,1)S(1)}, bf16[144,256]{1,0:T(8,128)(2,1)S(1)}, u32[]{:S(2)}, u32[]{:S(2)}) collective-permute-start(bf16[144,256]{1,0:T(8,128)(2,1)S(1)} %get-tuple-element.9.rest_0_), channel_id=1, source_target_pairs={{0,2},{1,3},{2,0},{3,1},{4,6},{5,7},{6,4},{7,5},{8,10},{9,11},{10,... | collective-permute-start | bytes 221192 | tf_op jit(solution)/shard_map/ppermute | solution.py:153
  17.7 13.3 %all-to-all-start.1 = ((bf16[32,8,256]{2,1,0:T(8,128)(2,1)}), bf16[32,8,256]{2,1,0:T(8,128)(2,1)S(1)}, u32[]{:S(2)}, u32[]{:S(2)}) async-start(bf16[32,8,256]{2,1,0:T(8,128)(2,1)} %bitcast.6), calls=%async_computation.1 | async-start | bytes 262144 | tf_op jit(solution)/shard_map/all_to_all | solution.py:201
  22.1 10.7 %copy-start = (bf16[32,2,4,256]{3,2,1,0:T(4,128)(2,1)S(1)}, bf16[32,2,4,256]{3,2,1,0:T(4,128)(2,1)}, u32[]{:S(2)}) copy-start(bf16[32,2,4,256]{3,2,1,0:T(4,128)(2,1)} %feat_ref.1) | copy-start | bytes 393220
  22.1 10.7 %copy-start.2 = (f32[31,256]{1,0:T(8,128)S(1)}, f32[31,256]{1,0:T(8,128)}, u32[]{:S(2)}) copy-start(f32[31,256]{1,0:T(8,128)} %taps_ref.3) | copy-start | bytes 95236
  22.2 8.8 %collective-permute-start.4 = (bf16[400,256]{1,0:T(8,128)(2,1)S(1)}, bf16[400,256]{1,0:T(8,128)(2,1)S(1)}, u32[]{:S(2)}, u32[]{:S(2)}) collective-permute-start(bf16[400,256]{1,0:T(8,128)(2,1)S(1)} %join.1.rest_1_), channel_id=1, source_target_pairs={{0,2},{1,3},{2,0},{3,1},{4,6},{5,7},{6,4},{7,5},{8,10},{9,11},{10,... | collective-permute-start | bytes 614408 | tf_op jit(solution)/shard_map/ppermute | solution.py:153
  24.2 8.6 %collective-permute-start.7 = (bf16[400,256]{1,0:T(8,128)(2,1)S(1)}, bf16[400,256]{1,0:T(8,128)(2,1)S(1)}, u32[]{:S(2)}, u32[]{:S(2)}) collective-permute-start(bf16[400,256]{1,0:T(8,128)(2,1)S(1)} %join.1.rest_1_), channel_id=1, source_target_pairs={{0,1},{1,0},{2,3},{3,2},{4,5},{5,4},{6,7},{7,6},{8,9},{9,8},{10,11... | collective-permute-start | bytes 614408 | tf_op jit(solution)/shard_map/ppermute | solution.py:153
  31.1 1.8 %collective-permute-start.8 = (bf16[400,256]{1,0:T(8,128)(2,1)S(1)}, bf16[400,256]{1,0:T(8,128)(2,1)S(1)}, u32[]{:S(2)}, u32[]{:S(2)}) collective-permute-start(bf16[400,256]{1,0:T(8,128)(2,1)S(1)} %collective-permute-done.4.rest_3_), channel_id=1, source_target_pairs={{0,1},{1,0},{2,3},{3,2},{4,5},{5,4},{6,7},{7,6},{8,9},{9,8},{10,11... | collective-permute-start | bytes 614408 | tf_op jit(solution)/shard_map/ppermute | solution.py:153
  31.1 1.6 %collective-permute-start.5 = (bf16[144,256]{1,0:T(8,128)(2,1)S(1)}, bf16[144,256]{1,0:T(8,128)(2,1)S(1)}, u32[]{:S(2)}, u32[]{:S(2)}) collective-permute-start(bf16[144,256]{1,0:T(8,128)(2,1)S(1)} %get-tuple-element.9.rest_0_), channel_id=1, source_target_pairs={{0,1},{1,0},{2,3},{3,2},{4,5},{5,4},{6,7},{7,6},{8,9},{9,8},{10,11... | collective-permute-start | bytes 221192 | tf_op jit(solution)/shard_map/ppermute | solution.py:153
  31.6 1.3 %collective-permute-start.6 = (bf16[144,256]{1,0:T(8,128)(2,1)S(1)}, bf16[144,256]{1,0:T(8,128)(2,1)S(1)}, u32[]{:S(2)}, u32[]{:S(2)}) collective-permute-start(bf16[144,256]{1,0:T(8,128)(2,1)S(1)} %collective-permute-done.refs_1_.rest_2_), channel_id=1, source_target_pairs={{0,1},{1,0},{2,3},{3,2},{4,5},{5,4},{6,7},{7,6},{8,9},{9,8},{10,11... | collective-permute-start | bytes 221192 | tf_op jit(solution)/shard_map/ppermute | solution.py:153

commit v11 on v10

--- a/solution.py
+++ b/solution.py
@@ -9,6 +9,7 @@
 from jax.sharding import PartitionSpec as P
 
 SLOT = 64
+PLANES = 32
 EXTRA = 16
 
 
@@ -29,14 +30,16 @@
 
 
 def join_kernel(*refs):
-    blocks, out_ref = refs[2:-1], refs[-1]
-    c = out_ref.shape[1]
+    *blocks, all_ref, line_ref = refs[1:]
+    c = all_ref.shape[1]
     row = lax.broadcasted_iota(jnp.int32, (EXTRA, c), 0)
-    biases = jnp.zeros((EXTRA, c), jnp.float32)
-    for i, block in enumerate(blocks):
-        out_ref[2 * SLOT * i : 2 * SLOT * (i + 1), :] = block[0 : 2 * SLOT, :]
-        biases = jnp.where(row == i, block[2 * SLOT :, :].astype(jnp.float32), biases)
-    out_ref[2 * SLOT * len(blocks) :, :] = biases.astype(out_ref.dtype)
+    for out_ref in (all_ref, line_ref):
+        count = out_ref.shape[0] // (2 * SLOT)
+        biases = jnp.zeros((EXTRA, c), jnp.float32)
+        for i, block in enumerate(blocks[:count]):
+            out_ref[2 * SLOT * i : 2 * SLOT * (i + 1), :] = block[0 : 2 * SLOT, :]
+            biases = jnp.where(row == i, block[2 * SLOT :, :].astype(jnp.float32), biases)
+        out_ref[2 * SLOT * count :, :] = biases.astype(out_ref.dtype)
 
 
 def radial_kernel(x_ref, taps_ref, out_ref, even, odd):
@@ -56,78 +59,90 @@
     odd[pad : pad + n, :, 0:theta] = second
     odd[pad - 1 : pad + n - 1, :, theta:] = first
 
-    def step(s, carry):
-        total = jnp.zeros((a_loc, 2 * theta, c), jnp.float32)
+    block = 4
+
+    def step(i, carry):
+        base = i * block
+        total = jnp.zeros((block, a_loc, 2 * theta, c), jnp.float32)
         for k in range(taps):
             shift = k - taps // 2
             source = even if shift % 2 == 0 else odd
-            total = total + source[s + (pad + shift // 2)] * taps_ref[k : k + 1, :]
-        out_ref[s] = total.astype(out_ref.dtype)
-        return carry
-
-    lax.fori_loop(0, n, step, 0)
-
-
-def tail_kernel(z_ref, taps_ref, consts_ref, feat_ref, *rest):
-    *blocks, out_ref, padded, branch, field, sem = rest
-    fetch = pltpu.make_async_copy(feat_ref, field, sem)
-    fetch.start()
+            total = total + source[pl.ds(base + (pad + shift // 2), block)] * taps_ref[k : k + 1, :]
+        out_ref[pl.ds(base, block)] = total.astype(out_ref.dtype)
+        return carry
+
+    lax.fori_loop(0, n // block, step, 0)
+
+
+def axial_kernel(z_ref, taps_ref, consts_ref, out_ref, padded, summed):
     axial, rows, c = z_ref.shape
-    theta = rows // 2
     taps = taps_ref.shape[0]
     half = taps // 2
     zeros = jnp.zeros((half, rows, c), jnp.float32)
     padded[0:half] = zeros
     padded[half + axial :] = zeros
     padded[half : half + axial] = z_ref[...].astype(jnp.float32)
-    block = 4
+    block = 8
 
     def conv(i, carry):
         base = i * block
         total = jnp.zeros((block, rows, c), jnp.float32)
         for k in range(taps):
             total = total + padded[pl.ds(base + k, block)] * taps_ref[k : k + 1, :]
-        branch[pl.ds(base, block)] = total
+        summed[pl.ds(base, block)] = total
         return carry
 
     lax.fori_loop(0, axial // block, conv, 0)
-    fetch.wait()
-    slots = [(block, i) for block in blocks for i in range(block.shape[0] // (2 * SLOT))]
-    per = c // SLOT
-    lane_slot = lax.broadcasted_iota(jnp.int32, (1, c), 1) // SLOT
-    planes = 32
-
-    def mlp(i, carry):
-        v = (branch[pl.ds(i * planes, planes)] + consts_ref[0 : 1, :]).reshape(planes * rows, c)
+
+    def norm(i, carry):
+        v = (summed[pl.ds(i * PLANES, PLANES)] + consts_ref[0:1, :]).reshape(PLANES * rows, c)
         v = v.astype(jnp.bfloat16).astype(jnp.float32)
         mean = jnp.mean(v, axis=-1, keepdims=True)
         centred = v - mean
         var = jnp.mean(centred * centred, axis=-1, keepdims=True)
-        normed = (centred * lax.rsqrt(var + 1e-06) * consts_ref[1 : 2, :] + consts_ref[2 : 3, :]).astype(jnp.bfloat16)
-        total = jnp.zeros((planes * rows, c), jnp.float32)
+        normed = centred * lax.rsqrt(var + 1e-06) * consts_ref[1:2, :] + consts_ref[2:3, :]
+        at = pl.multiple_of(i * PLANES * rows, PLANES * rows)
+        out_ref[pl.ds(at, PLANES * rows), :] = normed.astype(out_ref.dtype)
+        return carry
+
+    lax.fori_loop(0, axial // PLANES, norm, 0)
+
+
+def mlp_kernel(normed_ref, consts_ref, feat_ref, *rest):
+    *blocks, out_ref, branch = rest
+    axial, _, theta, c = feat_ref.shape
+    rows = 2 * theta
+    slots = [(block, i) for block in blocks for i in range(block.shape[0] // (2 * SLOT))]
+    per = c // SLOT
+    lane_slot = lax.broadcasted_iota(jnp.int32, (1, c), 1) // SLOT
+
+    def mlp(i, carry):
+        at = pl.multiple_of(i * PLANES * rows, PLANES * rows)
+        normed = normed_ref[pl.ds(at, PLANES * rows), :]
+        total = jnp.zeros((PLANES * rows, c), jnp.float32)
         for g in range(len(slots) // per):
             own = slots[g * per : (g + 1) * per]
             w_in = jnp.concatenate([w[2 * SLOT * j : 2 * SLOT * j + SLOT, :] for w, j in own], axis=0)
             w_out = jnp.concatenate([w[2 * SLOT * j + SLOT : 2 * SLOT * (j + 1), :] for w, j in own], axis=0)
             bias = jnp.zeros((1, c), jnp.float32)
-            for at, (w, j) in enumerate(own):
+            for spot, (w, j) in enumerate(own):
                 piece = w[w.shape[0] - EXTRA :, :].astype(jnp.float32)[j : j + 1]
-                bias = jnp.where(lane_slot == at, piece, bias)
+                bias = jnp.where(lane_slot == spot, piece, bias)
             u = lax.dot_general(normed, w_in, (((1,), (1,)), ((), ())), preferred_element_type=jnp.float32)
             u = u + bias
             hidden = (0.5 * u * (1.0 + jnp.tanh(0.7978845608028654 * (u + 0.044715 * u * u * u)))).astype(jnp.bfloat16)
             total = total + jnp.dot(hidden, w_out, preferred_element_type=jnp.float32)
         result = (consts_ref[4 : 5, :] * (total + consts_ref[3 : 4, :])).astype(jnp.bfloat16).astype(jnp.float32)
-        branch[pl.ds(i * planes, planes)] = result.reshape(planes, rows, c)
-        return carry
-
-    if axial == planes:
+        branch[pl.ds(i * PLANES, PLANES)] = result.reshape(PLANES, rows, c)
+        return carry
+
+    if axial == PLANES:
         mlp(0, 0)
     else:
-        lax.fori_loop(0, axial // planes, mlp, 0)
+        lax.fori_loop(0, axial // PLANES, mlp, 0)
     for r in range(2):
         got = branch[:, r * theta : (r + 1) * theta, :]
-        out_ref[:, r] = (field[:, r].astype(jnp.float32) + got).astype(out_ref.dtype)
+        out_ref[:, r] = (feat_ref[:, r].astype(jnp.float32) + got).astype(out_ref.dtype)
 
 
 def digits(n):
@@ -187,35 +202,42 @@
         name="radial",
     )(got.reshape(n, a_loc, r_loc, theta, c), radial_taps)
     if spread:
-        joined = pl.pallas_call(
+        joined, reach = pl.pallas_call(
             join_kernel,
-            out_shape=jax.ShapeDtypeStruct((2 * SLOT * (outer - 1) + EXTRA, c), jnp.bfloat16),
-            in_specs=[anywhere] * 2 + [vmem()] * (outer - 1),
-            out_specs=vmem(),
+            out_shape=[jax.ShapeDtypeStruct((2 * SLOT * size + EXTRA, c), jnp.bfloat16) for size in (outer + 1, outer - 1)],
+            in_specs=[anywhere] + [vmem()] * (outer + 1),
+            out_specs=[vmem()] * 2,
             compiler_params=small,
             cost_estimate=pl.CostEstimate(flops=10**10, bytes_accessed=2 * 10**7, transcendentals=0),
             name="join",
-        )(mixed, side, *line)
-        across = move(joined, 1, 1)
-        twin = [move(h, 2, 1) for h in (own, side, joined)]
+        )(mixed, *line, own, side)
+        across = move(reach, 1, 1)
+        twin = move(joined, 2, 1)
     back = lax.all_to_all(mixed.reshape(axial, rows, c), "row", split_axis=0, concat_axis=0, tiled=True)
-    if spread:
-        across, back = lax.optimization_barrier((across, back))
-        blocks = [own, joined, side, across] + twin + [move(across, 2, 1)]
-    return pl.pallas_call(
-        tail_kernel,
-        out_shape=jax.ShapeDtypeStruct(features.shape, jnp.bfloat16),
-        in_specs=[vmem()] * 3 + [anywhere] + [vmem()] * len(blocks),
+    normed = pl.pallas_call(
+        axial_kernel,
+        out_shape=jax.ShapeDtypeStruct((axial * rows, c), jnp.bfloat16),
+        in_specs=[vmem()] * 3,
         out_specs=vmem(),
         scratch_shapes=[
             pltpu.VMEM((axial + axial_taps.shape[0] - 1, rows, c), jnp.float32),
             pltpu.VMEM((axial, rows, c), jnp.float32),
-            pltpu.VMEM(features.shape, jnp.bfloat16),
-            pltpu.SemaphoreType.DMA(()),
         ],
+        compiler_params=middle,
+        name="axial",
+    )(back, axial_taps, consts)
+    if spread:
+        across, normed = lax.optimization_barrier((across, normed))
+        blocks = [joined, across, twin, move(across, 2, 1)]
+    return pl.pallas_call(
+        mlp_kernel,
+        out_shape=jax.ShapeDtypeStruct(features.shape, jnp.bfloat16),
+        in_specs=[vmem()] * (3 + len(blocks)),
+        out_specs=vmem(),
+        scratch_shapes=[pltpu.VMEM((axial, rows, c), jnp.float32)],
         compiler_params=large,
-        name="tail",
-    )(back, axial_taps, consts, features, *blocks)
+        name="mlp",
+    )(normed, consts, features, *blocks)
 
 
 def solution(mesh):

time: 35.7 us -> 33.7 us (0.944)
  starting transfers between devices: 20.7 us -> 20 us
  waiting for transfers between devices: 9.4 us -> 8.77 us
  Pallas kernels: 4.37 us -> 3.75 us
    ppermute x9 -> x7, waiting for transfers between devices: 8.12 us -> 1.55 us  [move(): return lax.ppermute(piece, 'row', [(i, i ^ by * stride) for i in range(n)])]
    all_to_all x1, waiting for transfers between devices: 0.01 us -> 5.85 us  [local(): lax.all_to_all(mixed.reshape(axial, rows, c), 'row', split_axis=0, concat...]
    ppermute x9 -> x7, starting transfers between devices: 8.81 us -> 8.3 us  [move(): return lax.ppermute(piece, 'row', [(i, i ^ by * stride) for i in range(n)])]
    pallas_call x1, Pallas kernels: 1.77 us -> 1.37 us  [local(): pl.pallas_call(radial_kernel, out_shape=jax.ShapeDtypeStruct((n, a_loc, r...]
    pallas_call x2 -> x3, Pallas kernels: 2.52 us -> 2.3 us  [the longest x1 1.39 us: local(): pl.pallas_call(mlp_kernel, out_shape=jax.ShapeDtypeStruct(features.shape,...]
  transfers between devices with their start and end apart: 11 -> 9, of which waited for: 4 -> 4; matrix products, arithmetic and copies ran while one was open for 0% -> 0% of each run, Pallas kernels for 5% -> 7%
where the time goes in v11:
time: 33.7 us; the launch traced here: 33.4 us
  starting transfers between devices  20 us (59%)
  waiting for transfers between devices  8.77 us (26%)
  Pallas kernels  3.75 us (11%)
  local copies, waits for them, and re-layouts  0.7 us (2%)
    ppermute x7, starting transfers between devices, move(): return lax.ppermute(piece, 'row', [(i, i ^ by * stride) for i in range(n)])  8.3 us
    all_to_all x1, starting transfers between devices, local(): lax.all_to_all(features, 'row', split_axis=0, concat_axis=0, tiled=True)  7.52 us
    all_to_all x1, waiting for transfers between devices, local(): lax.all_to_all(mixed.reshape(axial, rows, c), 'row', split_axis=0, concat...  5.85 us
    all_to_all x1, starting transfers between devices, local(): lax.all_to_all(mixed.reshape(axial, rows, c), 'row', split_axis=0, concat...  4.17 us
    ppermute x7, waiting for transfers between devices, move(): return lax.ppermute(piece, 'row', [(i, i ^ by * stride) for i in range(n)])  1.55 us
    pallas_call x1, Pallas kernels, local(): pl.pallas_call(mlp_kernel, out_shape=jax.ShapeDtypeStruct(features.shape,...  1.39 us
    all_to_all x1, waiting for transfers between devices, local(): lax.all_to_all(features, 'row', split_axis=0, concat_axis=0, tiled=True)  1.37 us
    pallas_call x1, Pallas kernels, local(): pl.pallas_call(radial_kernel, out_shape=jax.ShapeDtypeStruct((n, a_loc, r...  1.37 us
  transfers between devices with their start and end apart: 9, of which 4 were waited for; matrix products, arithmetic and copies ran while one was open for 0% of the time, Pallas kernels for 7%

profile of v11, /device:TPU:0, one launch (start us, length us, event | category | flops | bytes accessed | tf_op | source)
XLA Modules:
  0.0 33.4 jit_solution(15090643333980747854)
XLA Ops:
  0.0 7.5 %all-to-all-start = ((bf16[32,2,4,256]{3,2,1,0:T(4,128)(2,1)}), bf16[32,2,4,256]{3,2,1,0:T(4,128)(2,1)S(1)}, u32[]{:S(2)}, u32[]{:S(2)}) async-start(bf16[32,2,4,256]{3,2,1,0:T(4,128)(2,1)} %feat_ref.1), calls=%async_computation | async-start | bytes 262144 | tf_op jit(solution)/shard_map/all_to_all | solution.py:193
  7.5 0.0 copy-start.6
  7.5 0.0 copy-start.7
  7.6 0.0 copy-start.8
  7.6 0.0 copy-start.9
  7.6 0.0 copy-start.5
  7.6 0.0 copy-start.10
  7.6 0.6 %copy-done.6 = f32[256]{0:T(256)S(1)} copy-done((f32[256]{0:T(256)S(1)}, f32[256]{0:T(256)}, u32[]{:S(2)}) %copy-start.6) | copy-done | bytes 1048
  8.2 0.0 copy-done.7
  8.2 0.0 copy-done.8
  8.2 0.0 copy-done.9
  8.3 0.0 copy-done.5
  8.3 0.1 pack.1
  8.4 1.9 %collective-permute-start.3 = (bf16[144,256]{1,0:T(8,128)(2,1)S(1)}, bf16[144,256]{1,0:T(8,128)(2,1)S(1)}, u32[]{:S(2)}, u32[]{:S(2)}) collective-permute-start(bf16[144,256]{1,0:T(8,128)(2,1)S(1)} %get-tuple-element.11.refs_4_), channel_id=1, source_target_pairs={{0,2},{1,3},{2,0},{3,1},{4,6},{5,7},{6,4},{7,5},{8,10},{9,11},{10,... | collective-permute-start | bytes 221192 | tf_op jit(solution)/shard_map/ppermute | solution.py:168
  10.3 3.3 %collective-permute-start.2 = (bf16[144,256]{1,0:T(8,128)(2,1)S(1)}, bf16[144,256]{1,0:T(8,128)(2,1)S(1)}, u32[]{:S(2)}, u32[]{:S(2)}) collective-permute-start(bf16[144,256]{1,0:T(8,128)(2,1)S(1)} %get-tuple-element.11.refs_4_), channel_id=1, source_target_pairs={{0,12},{1,13},{2,14},{3,15},{4,8},{5,9},{6,10},{7,11},{8,4},{9,5},... | collective-permute-start | bytes 221192 | tf_op jit(solution)/shard_map/ppermute | solution.py:168
  13.5 0.0 collective-permute-start.1
  13.6 1.1 %collective-permute-start = (bf16[144,256]{1,0:T(8,128)(2,1)S(1)}, bf16[144,256]{1,0:T(8,128)(2,1)S(1)}, u32[]{:S(2)}, u32[]{:S(2)}) collective-permute-start(bf16[144,256]{1,0:T(8,128)(2,1)S(1)} %get-tuple-element.11.refs_4_), channel_id=1, source_target_pairs={{0,4},{1,5},{2,6},{3,7},{4,0},{5,1},{6,2},{7,3},{8,12},{9,13},{10,... | collective-permute-start | bytes 221192 | tf_op jit(solution)/shard_map/ppermute | solution.py:168
  14.7 1.4 %all-to-all-done = bf16[32,2,4,256]{3,2,1,0:T(4,128)(2,1)S(1)} async-done(((bf16[32,2,4,256]{3,2,1,0:T(4,128)(2,1)}), bf16[32,2,4,256]{3,2,1,0:T(4,128)(2,1)S(1)}, u32[]{:S(2)}, u32[]{:S(2)}) %all-to-all-start) | async-done | bytes 131104 | tf_op jit(solution)/shard_map/all_to_all | solution.py:193
  16.0 1.4 %radial.1.refs_0_ = bf16[16,2,8,256]{3,2,1,0:T(8,128)(2,1)} custom-call(bf16[16,2,2,4,256]{4,3,2,1,0:T(4,128)(2,1)S(1)} %bitcast.7, f32[31,256]{1,0:T(8,128)S(1)} %copy-done.1), custom_call_target="tpu_custom_call" | custom-call | tf_op jit(solution)/shard_map/radial/pallas_call | solution.py:195
  17.4 4.2 %all-to-all-start.1 = ((bf16[32,8,256]{2,1,0:T(8,128)(2,1)}), bf16[32,8,256]{2,1,0:T(8,128)(2,1)S(1)}, u32[]{:S(2)}, u32[]{:S(2)}) async-start(bf16[32,8,256]{2,1,0:T(8,128)(2,1)} %bitcast.6), calls=%async_computation.1 | async-start | bytes 262144 | tf_op jit(solution)/shard_map/all_to_all | solution.py:216
  21.6 0.0 copy-start.2
  21.6 0.0 collective-permute-done.3.refs_5_
  21.6 0.0 collective-permute-done.2.refs_3_
  21.6 0.0 collective-permute-done.refs_1_
  21.7 2.0 %collective-permute-start.4 = (bf16[400,256]{1,0:T(8,128)(2,1)S(1)}, bf16[400,256]{1,0:T(8,128)(2,1)S(1)}, u32[]{:S(2)}, u32[]{:S(2)}) collective-permute-start(bf16[400,256]{1,0:T(8,128)(2,1)S(1)} %get-tuple-element.12), channel_id=1, source_target_pairs={{0,2},{1,3},{2,0},{3,1},{4,6},{5,7},{6,4},{7,5},{8,10},{9,11},{10,... | collective-permute-start | bytes 614408 | tf_op jit(solution)/shard_map/ppermute | solution.py:168
  23.7 5.9 %all-to-all-done.1.z_ref = bf16[32,8,256]{2,1,0:T(8,128)(2,1)S(1)} async-done(((bf16[32,8,256]{2,1,0:T(8,128)(2,1)}), bf16[32,8,256]{2,1,0:T(8,128)(2,1)S(1)}, u32[]{:S(2)}, u32[]{:S(2)}) %all-to-all-start.1) | async-done | bytes 131104 | tf_op jit(solution)/shard_map/all_to_all | solution.py:216
  29.5 0.9 %axial.1.normed_ref = bf16[256,256]{1,0:T(8,128)(2,1)S(1)} custom-call(bf16[32,8,256]{2,1,0:T(8,128)(2,1)S(1)} %all-to-all-done.1.z_ref, f32[31,256]{1,0:T(8,128)S(1)} %copy-done.2, f32[8,256]{1,0:T(8,128)S(1)} %get-tuple-element.13.consts_ref), custom_call_target="tpu_custom_call" | custom-call | tf_op jit(solution)/shard_map/axial/pallas_call | solution.py:217
  30.4 0.1 collective-permute-done.4.rest_1_
  30.5 0.0 collective-permute-start.6
  30.5 0.0 collective-permute-done.5.rest_2_
  30.5 1.4 %collective-permute-done.6.rest_3_ = bf16[400,256]{1,0:T(8,128)(2,1)S(1)} collective-permute-done((bf16[400,256]{1,0:T(8,128)(2,1)S(1)}, bf16[400,256]{1,0:T(8,128)(2,1)S(1)}, u32[]{:S(2)}, u32[]{:S(2)}) %collective-permute-start.6) | collective-permute-done | bytes 204832 | tf_op jit(solution)/shard_map/ppermute | solution.py:168
  32.0 1.4 %mlp.1 = bf16[32,2,4,256]{3,2,1,0:T(4,128)(2,1)} custom-call(bf16[256,256]{1,0:T(8,128)(2,1)S(1)} %axial.1.normed_ref, f32[8,256]{1,0:T(8,128)S(1)} %get-tuple-element.13.consts_ref, bf16[32,2,4,256]{3,2,1,0:T(4,128)(2,1)S(1)} %copy-done, bf16[656,256]{1,0:T(8,128)(2,1)S(1)} %get-tuple-element.15.rest_0_, ...), custom_call_target="tpu_custom_call" | custom-call | tf_op jit(solution)/shard_map/mlp/pallas_call | solution.py:232
  (13 shorter events, 0.1 us)
Async XLA Ops:
  0.0 7.6 %copy-start.4 = (bf16[64,256]{1,0:T(8,128)(2,1)S(1)}, bf16[64,256]{1,0:T(8,128)(2,1)}, u32[]{:S(2)}) copy-start(bf16[64,256]{1,0:T(8,128)(2,1)} %w_out_ref.1) | copy-start | bytes 98308
  0.0 7.6 %copy-start.3 = (bf16[64,256]{1,0:T(8,128)(2,1)S(1)}, bf16[64,256]{1,0:T(8,128)(2,1)}, u32[]{:S(2)}) copy-start(bf16[64,256]{1,0:T(8,128)(2,1)} %w_in_ref.1) | copy-start | bytes 98308
  0.0 16.0 %all-to-all-start = ((bf16[32,2,4,256]{3,2,1,0:T(4,128)(2,1)}), bf16[32,2,4,256]{3,2,1,0:T(4,128)(2,1)S(1)}, u32[]{:S(2)}, u32[]{:S(2)}) async-start(bf16[32,2,4,256]{3,2,1,0:T(4,128)(2,1)} %feat_ref.1), calls=%async_computation | async-start | bytes 262144 | tf_op jit(solution)/shard_map/all_to_all | solution.py:193
  7.5 0.7 %copy-start.6 = (f32[256]{0:T(256)S(1)}, f32[256]{0:T(256)}, u32[]{:S(2)}) copy-start(f32[256]{0:T(256)} %param.15) | copy-start | bytes 3076
  7.5 0.7 %copy-start.7 = (f32[256]{0:T(256)S(1)}, f32[256]{0:T(256)}, u32[]{:S(2)}) copy-start(f32[256]{0:T(256)} %param.16) | copy-start | bytes 3076
  7.6 0.7 %copy-start.8 = (f32[256]{0:T(256)S(1)}, f32[256]{0:T(256)}, u32[]{:S(2)}) copy-start(f32[256]{0:T(256)} %param.20) | copy-start | bytes 3076
  7.6 0.7 %copy-start.9 = (f32[256]{0:T(256)S(1)}, f32[256]{0:T(256)}, u32[]{:S(2)}) copy-start(f32[256]{0:T(256)} %param.21) | copy-start | bytes 3076
  7.6 0.7 %copy-start.5 = (f32[256]{0:T(256)S(1)}, f32[256]{0:T(256)}, u32[]{:S(2)}) copy-start(f32[256]{0:T(256)} %param.14) | copy-start | bytes 3076
  7.6 0.7 %copy-start.10 = (bf16[64]{0:T(256)(128)(2,1)S(1)}, bf16[64]{0:T(256)(128)(2,1)}, u32[]{:S(2)}) copy-start(bf16[64]{0:T(256)(128)(2,1)} %b_ref.1) | copy-start | bytes 388
  8.3 7.8 %copy-start.1 = (f32[31,256]{1,0:T(8,128)S(1)}, f32[31,256]{1,0:T(8,128)}, u32[]{:S(2)}) copy-start(f32[31,256]{1,0:T(8,128)} %taps_ref.2) | copy-start | bytes 95236
  8.4 13.2 %collective-permute-start.3 = (bf16[144,256]{1,0:T(8,128)(2,1)S(1)}, bf16[144,256]{1,0:T(8,128)(2,1)S(1)}, u32[]{:S(2)}, u32[]{:S(2)}) collective-permute-start(bf16[144,256]{1,0:T(8,128)(2,1)S(1)} %get-tuple-element.11.refs_4_), channel_id=1, source_target_pairs={{0,2},{1,3},{2,0},{3,1},{4,6},{5,7},{6,4},{7,5},{8,10},{9,11},{10,... | collective-permute-start | bytes 221192 | tf_op jit(solution)/shard_map/ppermute | solution.py:168
  10.3 11.3 %collective-permute-start.2 = (bf16[144,256]{1,0:T(8,128)(2,1)S(1)}, bf16[144,256]{1,0:T(8,128)(2,1)S(1)}, u32[]{:S(2)}, u32[]{:S(2)}) collective-permute-start(bf16[144,256]{1,0:T(8,128)(2,1)S(1)} %get-tuple-element.11.refs_4_), channel_id=1, source_target_pairs={{0,12},{1,13},{2,14},{3,15},{4,8},{5,9},{6,10},{7,11},{8,4},{9,5},... | collective-permute-start | bytes 221192 | tf_op jit(solution)/shard_map/ppermute | solution.py:168
  13.5 8.1 %collective-permute-start.1 = (bf16[144,256]{1,0:T(8,128)(2,1)S(1)}, bf16[144,256]{1,0:T(8,128)(2,1)S(1)}, u32[]{:S(2)}, u32[]{:S(2)}) collective-permute-start(bf16[144,256]{1,0:T(8,128)(2,1)S(1)} %get-tuple-element.11.refs_4_), channel_id=1, source_target_pairs={{0,8},{1,9},{2,10},{3,11},{4,12},{5,13},{6,14},{7,15},{8,0},{9,1},... | collective-permute-start | bytes 221192 | tf_op jit(solution)/shard_map/ppermute | solution.py:168
  13.6 8.1 %collective-permute-start = (bf16[144,256]{1,0:T(8,128)(2,1)S(1)}, bf16[144,256]{1,0:T(8,128)(2,1)S(1)}, u32[]{:S(2)}, u32[]{:S(2)}) collective-permute-start(bf16[144,256]{1,0:T(8,128)(2,1)S(1)} %get-tuple-element.11.refs_4_), channel_id=1, source_target_pairs={{0,4},{1,5},{2,6},{3,7},{4,0},{5,1},{6,2},{7,3},{8,12},{9,13},{10,... | collective-permute-start | bytes 221192 | tf_op jit(solution)/shard_map/ppermute | solution.py:168
  17.4 12.1 %all-to-all-start.1 = ((bf16[32,8,256]{2,1,0:T(8,128)(2,1)}), bf16[32,8,256]{2,1,0:T(8,128)(2,1)S(1)}, u32[]{:S(2)}, u32[]{:S(2)}) async-start(bf16[32,8,256]{2,1,0:T(8,128)(2,1)} %bitcast.6), calls=%async_computation.1 | async-start | bytes 262144 | tf_op jit(solution)/shard_map/all_to_all | solution.py:216
  21.6 7.9 %copy-start.2 = (f32[31,256]{1,0:T(8,128)S(1)}, f32[31,256]{1,0:T(8,128)}, u32[]{:S(2)}) copy-start(f32[31,256]{1,0:T(8,128)} %taps_ref.3) | copy-start | bytes 95236
  21.7 8.8 %collective-permute-start.4 = (bf16[400,256]{1,0:T(8,128)(2,1)S(1)}, bf16[400,256]{1,0:T(8,128)(2,1)S(1)}, u32[]{:S(2)}, u32[]{:S(2)}) collective-permute-start(bf16[400,256]{1,0:T(8,128)(2,1)S(1)} %get-tuple-element.12), channel_id=1, source_target_pairs={{0,2},{1,3},{2,0},{3,1},{4,6},{5,7},{6,4},{7,5},{8,10},{9,11},{10,... | collective-permute-start | bytes 614408 | tf_op jit(solution)/shard_map/ppermute | solution.py:168
  23.7 6.8 %collective-permute-start.5 = (bf16[656,256]{1,0:T(8,128)(2,1)S(1)}, bf16[656,256]{1,0:T(8,128)(2,1)S(1)}, u32[]{:S(2)}, u32[]{:S(2)}) collective-permute-start(bf16[656,256]{1,0:T(8,128)(2,1)S(1)} %get-tuple-element.15.rest_0_), channel_id=1, source_target_pairs={{0,1},{1,0},{2,3},{3,2},{4,5},{5,4},{6,7},{7,6},{8,9},{9,8},{10,11... | collective-permute-start | bytes 1007624 | tf_op jit(solution)/shard_map/ppermute | solution.py:168
  29.5 2.4 %copy-start = (bf16[32,2,4,256]{3,2,1,0:T(4,128)(2,1)S(1)}, bf16[32,2,4,256]{3,2,1,0:T(4,128)(2,1)}, u32[]{:S(2)}) copy-start(bf16[32,2,4,256]{3,2,1,0:T(4,128)(2,1)} %feat_ref.1) | copy-start | bytes 393220
  30.5 1.5 %collective-permute-start.6 = (bf16[400,256]{1,0:T(8,128)(2,1)S(1)}, bf16[400,256]{1,0:T(8,128)(2,1)S(1)}, u32[]{:S(2)}, u32[]{:S(2)}) collective-permute-start(bf16[400,256]{1,0:T(8,128)(2,1)S(1)} %collective-permute-done.4.rest_1_), channel_id=1, source_target_pairs={{0,1},{1,0},{2,3},{3,2},{4,5},{5,4},{6,7},{7,6},{8,9},{9,8},{10,11... | collective-permute-start | bytes 614408 | tf_op jit(solution)/shard_map/ppermute | solution.py:168

commit v12 on v11

--- a/solution.py
+++ b/solution.py
@@ -30,16 +30,17 @@
 
 
 def join_kernel(*refs):
-    *blocks, all_ref, line_ref = refs[1:]
+    *blocks, all_ref, most_ref, last_ref = refs[1:]
     c = all_ref.shape[1]
     row = lax.broadcasted_iota(jnp.int32, (EXTRA, c), 0)
-    for out_ref in (all_ref, line_ref):
+    for out_ref in (all_ref, most_ref):
         count = out_ref.shape[0] // (2 * SLOT)
         biases = jnp.zeros((EXTRA, c), jnp.float32)
         for i, block in enumerate(blocks[:count]):
             out_ref[2 * SLOT * i : 2 * SLOT * (i + 1), :] = block[0 : 2 * SLOT, :]
             biases = jnp.where(row == i, block[2 * SLOT :, :].astype(jnp.float32), biases)
         out_ref[2 * SLOT * count :, :] = biases.astype(out_ref.dtype)
+    last_ref[...] = blocks[count][...]
 
 
 def radial_kernel(x_ref, taps_ref, out_ref, even, odd):
@@ -108,38 +109,59 @@
     lax.fori_loop(0, axial // PLANES, norm, 0)
 
 
-def mlp_kernel(normed_ref, consts_ref, feat_ref, *rest):
-    *blocks, out_ref, branch = rest
-    axial, _, theta, c = feat_ref.shape
-    rows = 2 * theta
-    slots = [(block, i) for block in blocks for i in range(block.shape[0] // (2 * SLOT))]
+def hidden_sum(normed, blocks):
+    c = normed.shape[1]
     per = c // SLOT
     lane_slot = lax.broadcasted_iota(jnp.int32, (1, c), 1) // SLOT
-
-    def mlp(i, carry):
-        at = pl.multiple_of(i * PLANES * rows, PLANES * rows)
-        normed = normed_ref[pl.ds(at, PLANES * rows), :]
-        total = jnp.zeros((PLANES * rows, c), jnp.float32)
-        for g in range(len(slots) // per):
-            own = slots[g * per : (g + 1) * per]
-            w_in = jnp.concatenate([w[2 * SLOT * j : 2 * SLOT * j + SLOT, :] for w, j in own], axis=0)
-            w_out = jnp.concatenate([w[2 * SLOT * j + SLOT : 2 * SLOT * (j + 1), :] for w, j in own], axis=0)
-            bias = jnp.zeros((1, c), jnp.float32)
-            for spot, (w, j) in enumerate(own):
-                piece = w[w.shape[0] - EXTRA :, :].astype(jnp.float32)[j : j + 1]
-                bias = jnp.where(lane_slot == spot, piece, bias)
-            u = lax.dot_general(normed, w_in, (((1,), (1,)), ((), ())), preferred_element_type=jnp.float32)
-            u = u + bias
-            hidden = (0.5 * u * (1.0 + jnp.tanh(0.7978845608028654 * (u + 0.044715 * u * u * u)))).astype(jnp.bfloat16)
-            total = total + jnp.dot(hidden, w_out, preferred_element_type=jnp.float32)
-        result = (consts_ref[4 : 5, :] * (total + consts_ref[3 : 4, :])).astype(jnp.bfloat16).astype(jnp.float32)
-        branch[pl.ds(i * PLANES, PLANES)] = result.reshape(PLANES, rows, c)
-        return carry
-
-    if axial == PLANES:
-        mlp(0, 0)
+    slots = [(block, i) for block in blocks for i in range(block.shape[0] // (2 * SLOT))]
+    total = None
+    for g in range(0, len(slots), per):
+        own = slots[g : g + per]
+        w_in = jnp.concatenate([w[2 * SLOT * j : 2 * SLOT * j + SLOT, :] for w, j in own], axis=0)
+        w_out = jnp.concatenate([w[2 * SLOT * j + SLOT : 2 * SLOT * (j + 1), :] for w, j in own], axis=0)
+        bias = jnp.zeros((1, c), jnp.float32)
+        for spot, (w, j) in enumerate(own):
+            piece = w[w.shape[0] - EXTRA :, :].astype(jnp.float32)[j : j + 1]
+            bias = jnp.where(lane_slot == spot, piece, bias)
+        u = lax.dot_general(normed, w_in, (((1,), (1,)), ((), ())), preferred_element_type=jnp.float32)
+        u = u + bias[:, : len(own) * SLOT]
+        hidden = (0.5 * u * (1.0 + jnp.tanh(0.7978845608028654 * (u + 0.044715 * u * u * u)))).astype(jnp.bfloat16)
+        part = jnp.dot(hidden, w_out, preferred_element_type=jnp.float32)
+        total = part if total is None else total + part
+    return total
+
+
+def over_tokens(count, size, body):
+    if count == size:
+        body(0)
     else:
-        lax.fori_loop(0, axial // PLANES, mlp, 0)
+        pl.loop(0, count // size)(lambda i: body(pl.multiple_of(i * size, size)))
+
+
+def first_kernel(normed_ref, *rest):
+    *blocks, out_ref = rest
+    size = PLANES * 8
+
+    def part(at):
+        out_ref[pl.ds(at, size), :] = hidden_sum(normed_ref[pl.ds(at, size), :], blocks)
+
+    over_tokens(normed_ref.shape[0], size, part)
+
+
+def mlp_kernel(partials, normed_ref, consts_ref, feat_ref, *rest):
+    *blocks, out_ref, branch = rest
+    theta, c = feat_ref.shape[2:]
+    rows = 2 * theta
+    size = PLANES * rows
+
+    def mlp(at):
+        total = hidden_sum(normed_ref[pl.ds(at, size), :], blocks[partials:])
+        for partial_ref in blocks[:partials]:
+            total = total + partial_ref[pl.ds(at, size), :]
+        result = (consts_ref[4:5, :] * (total + consts_ref[3:4, :])).astype(jnp.bfloat16).astype(jnp.float32)
+        branch[pl.ds(at // rows, PLANES)] = result.reshape(PLANES, rows, c)
+
+    over_tokens(normed_ref.shape[0], size, mlp)
     for r in range(2):
         got = branch[:, r * theta : (r + 1) * theta, :]
         out_ref[:, r] = (feat_ref[:, r].astype(jnp.float32) + got).astype(out_ref.dtype)
@@ -202,16 +224,16 @@
         name="radial",
     )(got.reshape(n, a_loc, r_loc, theta, c), radial_taps)
     if spread:
-        joined, reach = pl.pallas_call(
+        joined, most, last = pl.pallas_call(
             join_kernel,
-            out_shape=[jax.ShapeDtypeStruct((2 * SLOT * size + EXTRA, c), jnp.bfloat16) for size in (outer + 1, outer - 1)],
+            out_shape=[jax.ShapeDtypeStruct((2 * SLOT * size + EXTRA, c), jnp.bfloat16) for size in (outer + 1, outer - 2, 1)],
             in_specs=[anywhere] + [vmem()] * (outer + 1),
-            out_specs=[vmem()] * 2,
+            out_specs=[vmem()] * 3,
             compiler_params=small,
             cost_estimate=pl.CostEstimate(flops=10**10, bytes_accessed=2 * 10**7, transcendentals=0),
             name="join",
         )(mixed, *line, own, side)
-        across = move(reach, 1, 1)
+        across = [move(most, 1, 1), move(last, 1, 1)]
         twin = move(joined, 2, 1)
     back = lax.all_to_all(mixed.reshape(axial, rows, c), "row", split_axis=0, concat_axis=0, tiled=True)
     normed = pl.pallas_call(
@@ -228,16 +250,29 @@
     )(back, axial_taps, consts)
     if spread:
         across, normed = lax.optimization_barrier((across, normed))
-        blocks = [joined, across, twin, move(across, 2, 1)]
+        blocks = across + [move(h, 2, 1) for h in across]
+        partials = [
+            pl.pallas_call(
+                first_kernel,
+                out_shape=jax.ShapeDtypeStruct((axial * rows, c), jnp.float32),
+                in_specs=[vmem()] * 3,
+                out_specs=vmem(),
+                compiler_params=middle,
+                name="first",
+            )(normed, joined, twin)
+        ]
+    else:
+        partials = []
+    operands = partials + blocks
     return pl.pallas_call(
-        mlp_kernel,
+        partial(mlp_kernel, len(partials)),
         out_shape=jax.ShapeDtypeStruct(features.shape, jnp.bfloat16),
-        in_specs=[vmem()] * (3 + len(blocks)),
+        in_specs=[vmem()] * (3 + len(operands)),
         out_specs=vmem(),
         scratch_shapes=[pltpu.VMEM((axial, rows, c), jnp.float32)],
         compiler_params=large,
         name="mlp",
-    )(normed, consts, features, *blocks)
+    )(normed, consts, features, *operands)
 
 
 def solution(mesh):

time: 33.7 us -> 33.1 us (0.982)
  waiting for transfers between devices: 8.77 us -> 7.24 us
  Pallas kernels: 3.75 us -> 4.39 us
    ppermute x7 -> x9, waiting for transfers between devices: 1.55 us -> 0.49 us  [move(): return lax.ppermute(piece, 'row', [(i, i ^ by * stride) for i in range(n)])]
    ppermute x7 -> x9, starting transfers between devices: 8.3 us -> 9.2 us  [move(): return lax.ppermute(piece, 'row', [(i, i ^ by * stride) for i in range(n)])]
    all_to_all x1, starting transfers between devices: 4.17 us -> 3.51 us  [local(): lax.all_to_all(mixed.reshape(axial, rows, c), 'row', split_axis=0, concat...]
    pallas_call x1 -> x2, Pallas kernels: 1.39 us -> 1.97 us  [the longest x1 1.23 us: local(): pl.pallas_call(partial(mlp_kernel, len(partials)), out_shape=jax.ShapeDty...]
    all_to_all x1, waiting for transfers between devices: 5.85 us -> 5.43 us  [local(): lax.all_to_all(mixed.reshape(axial, rows, c), 'row', split_axis=0, concat...]
  transfers between devices with their start and end apart: 9 -> 11, of which waited for: 4 -> 4; matrix products, arithmetic and copies ran while one was open for 0% -> 0% of each run, Pallas kernels for 7% -> 10%
where the time goes in v12:
time: 33.1 us; the launch traced here: 32.7 us
  starting transfers between devices  20.2 us (61%)
  waiting for transfers between devices  7.24 us (22%)
  Pallas kernels  4.39 us (13%)
  local copies, waits for them, and re-layouts  0.7 us (2%)
    ppermute x9, starting transfers between devices, move(): return lax.ppermute(piece, 'row', [(i, i ^ by * stride) for i in range(n)])  9.2 us
    all_to_all x1, starting transfers between devices, local(): lax.all_to_all(features, 'row', split_axis=0, concat_axis=0, tiled=True)  7.52 us
    all_to_all x1, waiting for transfers between devices, local(): lax.all_to_all(mixed.reshape(axial, rows, c), 'row', split_axis=0, concat...  5.43 us
    all_to_all x1, starting transfers between devices, local(): lax.all_to_all(mixed.reshape(axial, rows, c), 'row', split_axis=0, concat...  3.51 us
    pallas_call x1, Pallas kernels, local(): pl.pallas_call(radial_kernel, out_shape=jax.ShapeDtypeStruct((n, a_loc, r...  1.37 us
    all_to_all x1, waiting for transfers between devices, local(): lax.all_to_all(features, 'row', split_axis=0, concat_axis=0, tiled=True)  1.32 us
    pallas_call x1, Pallas kernels, local(): pl.pallas_call(partial(mlp_kernel, len(partials)), out_shape=jax.ShapeDty...  1.23 us
    pallas_call x1, Pallas kernels, local(): pl.pallas_call(axial_kernel, out_shape=jax.ShapeDtypeStruct((axial * rows...  0.94 us
  transfers between devices with their start and end apart: 11, of which 4 were waited for; matrix products, arithmetic and copies ran while one was open for 0% of the time, Pallas kernels for 10%

profile of v12, /device:TPU:0, one launch (start us, length us, event | category | flops | bytes accessed | tf_op | source)
XLA Modules:
  0.0 32.7 jit_solution(2802467187342316293)
XLA Ops:
  0.0 7.5 %all-to-all-start = ((bf16[32,2,4,256]{3,2,1,0:T(4,128)(2,1)}), bf16[32,2,4,256]{3,2,1,0:T(4,128)(2,1)S(1)}, u32[]{:S(2)}, u32[]{:S(2)}) async-start(bf16[32,2,4,256]{3,2,1,0:T(4,128)(2,1)} %feat_ref.1), calls=%async_computation | async-start | bytes 262144 | tf_op jit(solution)/shard_map/all_to_all | solution.py:215
  7.5 0.0 copy-start.6
  7.5 0.0 copy-start.7
  7.6 0.0 copy-start.8
  7.6 0.0 copy-start.9
  7.6 0.0 copy-start.5
  7.6 0.0 copy-start.10
  7.6 0.6 %copy-done.6 = f32[256]{0:T(256)S(1)} copy-done((f32[256]{0:T(256)S(1)}, f32[256]{0:T(256)}, u32[]{:S(2)}) %copy-start.6) | copy-done | bytes 1048
  8.2 0.0 copy-done.7
  8.2 0.0 copy-done.8
  8.2 0.0 copy-done.9
  8.3 0.0 copy-done.5
  8.3 0.1 pack.1
  8.4 1.9 %collective-permute-start = (bf16[144,256]{1,0:T(8,128)(2,1)S(1)}, bf16[144,256]{1,0:T(8,128)(2,1)S(1)}, u32[]{:S(2)}, u32[]{:S(2)}) collective-permute-start(bf16[144,256]{1,0:T(8,128)(2,1)S(1)} %get-tuple-element.13.refs_4_), channel_id=1, source_target_pairs={{0,4},{1,5},{2,6},{3,7},{4,0},{5,1},{6,2},{7,3},{8,12},{9,13},{10,... | collective-permute-start | bytes 221192 | tf_op jit(solution)/shard_map/ppermute | solution.py:190
  10.3 2.4 %collective-permute-start.1 = (bf16[144,256]{1,0:T(8,128)(2,1)S(1)}, bf16[144,256]{1,0:T(8,128)(2,1)S(1)}, u32[]{:S(2)}, u32[]{:S(2)}) collective-permute-start(bf16[144,256]{1,0:T(8,128)(2,1)S(1)} %get-tuple-element.13.refs_4_), channel_id=1, source_target_pairs={{0,8},{1,9},{2,10},{3,11},{4,12},{5,13},{6,14},{7,15},{8,0},{9,1},... | collective-permute-start | bytes 221192 | tf_op jit(solution)/shard_map/ppermute | solution.py:190
  12.6 0.1 collective-permute-start.2
  12.7 1.9 %collective-permute-start.3 = (bf16[144,256]{1,0:T(8,128)(2,1)S(1)}, bf16[144,256]{1,0:T(8,128)(2,1)S(1)}, u32[]{:S(2)}, u32[]{:S(2)}) collective-permute-start(bf16[144,256]{1,0:T(8,128)(2,1)S(1)} %get-tuple-element.13.refs_4_), channel_id=1, source_target_pairs={{0,2},{1,3},{2,0},{3,1},{4,6},{5,7},{6,4},{7,5},{8,10},{9,11},{10,... | collective-permute-start | bytes 221192 | tf_op jit(solution)/shard_map/ppermute | solution.py:190
  14.7 1.3 %all-to-all-done = bf16[32,2,4,256]{3,2,1,0:T(4,128)(2,1)S(1)} async-done(((bf16[32,2,4,256]{3,2,1,0:T(4,128)(2,1)}), bf16[32,2,4,256]{3,2,1,0:T(4,128)(2,1)S(1)}, u32[]{:S(2)}, u32[]{:S(2)}) %all-to-all-start) | async-done | bytes 131104 | tf_op jit(solution)/shard_map/all_to_all | solution.py:215
  16.0 1.4 %radial.1.refs_0_ = bf16[16,2,8,256]{3,2,1,0:T(8,128)(2,1)} custom-call(bf16[16,2,2,4,256]{4,3,2,1,0:T(4,128)(2,1)S(1)} %bitcast.7, f32[31,256]{1,0:T(8,128)S(1)} %copy-done.1), custom_call_target="tpu_custom_call" | custom-call | tf_op jit(solution)/shard_map/radial/pallas_call | solution.py:217
  17.4 3.5 %all-to-all-start.1 = ((bf16[32,8,256]{2,1,0:T(8,128)(2,1)}), bf16[32,8,256]{2,1,0:T(8,128)(2,1)S(1)}, u32[]{:S(2)}, u32[]{:S(2)}) async-start(bf16[32,8,256]{2,1,0:T(8,128)(2,1)} %bitcast.6), calls=%async_computation.1 | async-start | bytes 262144 | tf_op jit(solution)/shard_map/all_to_all | solution.py:238
  20.9 0.0 copy-start.2
  21.0 0.4 %collective-permute-start.6 = (bf16[656,256]{1,0:T(8,128)(2,1)S(1)}, bf16[656,256]{1,0:T(8,128)(2,1)S(1)}, u32[]{:S(2)}, u32[]{:S(2)}) collective-permute-start(bf16[656,256]{1,0:T(8,128)(2,1)S(1)} %get-tuple-element.18.rest_0_), channel_id=1, source_target_pairs={{0,1},{1,0},{2,3},{3,2},{4,5},{5,4},{6,7},{7,6},{8,9},{9,8},{10,11... | collective-permute-start | bytes 1007624 | tf_op jit(solution)/shard_map/ppermute | solution.py:190
  21.3 1.7 %collective-permute-start.4 = (bf16[272,256]{1,0:T(8,128)(2,1)S(1)}, bf16[272,256]{1,0:T(8,128)(2,1)S(1)}, u32[]{:S(2)}, u32[]{:S(2)}) collective-permute-start(bf16[272,256]{1,0:T(8,128)(2,1)S(1)} %get-tuple-element.14), channel_id=1, source_target_pairs={{0,2},{1,3},{2,0},{3,1},{4,6},{5,7},{6,4},{7,5},{8,10},{9,11},{10,... | collective-permute-start | bytes 417800 | tf_op jit(solution)/shard_map/ppermute | solution.py:190
  23.0 0.3 %collective-permute-start.5 = (bf16[144,256]{1,0:T(8,128)(2,1)S(1)}, bf16[144,256]{1,0:T(8,128)(2,1)S(1)}, u32[]{:S(2)}, u32[]{:S(2)}) collective-permute-start(bf16[144,256]{1,0:T(8,128)(2,1)S(1)} %get-tuple-element.15), channel_id=1, source_target_pairs={{0,2},{1,3},{2,0},{3,1},{4,6},{5,7},{6,4},{7,5},{8,10},{9,11},{10,... | collective-permute-start | bytes 221192 | tf_op jit(solution)/shard_map/ppermute | solution.py:190
  23.4 5.4 %all-to-all-done.1.z_ref = bf16[32,8,256]{2,1,0:T(8,128)(2,1)S(1)} async-done(((bf16[32,8,256]{2,1,0:T(8,128)(2,1)}), bf16[32,8,256]{2,1,0:T(8,128)(2,1)S(1)}, u32[]{:S(2)}, u32[]{:S(2)}) %all-to-all-start.1) | async-done | bytes 131104 | tf_op jit(solution)/shard_map/all_to_all | solution.py:238
  28.8 0.9 %axial.1.normed_ref = bf16[256,256]{1,0:T(8,128)(2,1)S(1)} custom-call(bf16[32,8,256]{2,1,0:T(8,128)(2,1)S(1)} %all-to-all-done.1.z_ref, f32[31,256]{1,0:T(8,128)S(1)} %copy-done.2, f32[8,256]{1,0:T(8,128)S(1)} %get-tuple-element.16.consts_ref), custom_call_target="tpu_custom_call" | custom-call | tf_op jit(solution)/shard_map/axial/pallas_call | solution.py:239
  29.7 0.0 copy-start
  29.8 0.3 collective-permute-done.5.rest_2_
  30.0 0.5 %collective-permute-start.8 = (bf16[144,256]{1,0:T(8,128)(2,1)S(1)}, bf16[144,256]{1,0:T(8,128)(2,1)S(1)}, u32[]{:S(2)}, u32[]{:S(2)}) collective-permute-start(bf16[144,256]{1,0:T(8,128)(2,1)S(1)} %collective-permute-done.5.rest_2_), channel_id=1, source_target_pairs={{0,1},{1,0},{2,3},{3,2},{4,5},{5,4},{6,7},{7,6},{8,9},{9,8},{10,11... | collective-permute-start | bytes 221192 | tf_op jit(solution)/shard_map/ppermute | solution.py:190
  30.5 0.7 %first.1.rest_0_ = f32[256,256]{1,0:T(8,128)S(1)} custom-call(bf16[256,256]{1,0:T(8,128)(2,1)S(1)} %axial.1.normed_ref, bf16[656,256]{1,0:T(8,128)(2,1)S(1)} %get-tuple-element.18.rest_0_, bf16[656,256]{1,0:T(8,128)(2,1)S(1)} %collective-permute-done.6.rest_1_), custom_call_target="tpu_custom_call" | custom-call | tf_op jit(solution)/shard_map/first/pallas_call | solution.py:255
  31.3 0.2 collective-permute-done.8.rest_4_
  31.5 1.2 %mlp.1 = bf16[32,2,4,256]{3,2,1,0:T(4,128)(2,1)} custom-call(bf16[256,256]{1,0:T(8,128)(2,1)S(1)} %axial.1.normed_ref, f32[8,256]{1,0:T(8,128)S(1)} %get-tuple-element.16.consts_ref, bf16[32,2,4,256]{3,2,1,0:T(4,128)(2,1)S(1)} %copy-done, f32[256,256]{1,0:T(8,128)S(1)} %first.1.rest_0_, bf16[272,256]{1,0:T(8,128)(2,1)S(1)} %collective-permute-done.4.rest_1_, ...), custom_call_target="tpu_custom_call" | custom-call | tf_op jit(solution)/shard_map/mlp/pallas_call | solution.py:267
  (18 shorter events, 0.1 us)
Async XLA Ops:
  0.0 7.6 %copy-start.3 = (bf16[64,256]{1,0:T(8,128)(2,1)S(1)}, bf16[64,256]{1,0:T(8,128)(2,1)}, u32[]{:S(2)}) copy-start(bf16[64,256]{1,0:T(8,128)(2,1)} %w_in_ref.1) | copy-start | bytes 98308
  0.0 7.6 %copy-start.4 = (bf16[64,256]{1,0:T(8,128)(2,1)S(1)}, bf16[64,256]{1,0:T(8,128)(2,1)}, u32[]{:S(2)}) copy-start(bf16[64,256]{1,0:T(8,128)(2,1)} %w_out_ref.1) | copy-start | bytes 98308
  0.0 16.0 %all-to-all-start = ((bf16[32,2,4,256]{3,2,1,0:T(4,128)(2,1)}), bf16[32,2,4,256]{3,2,1,0:T(4,128)(2,1)S(1)}, u32[]{:S(2)}, u32[]{:S(2)}) async-start(bf16[32,2,4,256]{3,2,1,0:T(4,128)(2,1)} %feat_ref.1), calls=%async_computation | async-start | bytes 262144 | tf_op jit(solution)/shard_map/all_to_all | solution.py:215
  7.5 0.7 %copy-start.6 = (f32[256]{0:T(256)S(1)}, f32[256]{0:T(256)}, u32[]{:S(2)}) copy-start(f32[256]{0:T(256)} %param.15) | copy-start | bytes 3076
  7.5 0.7 %copy-start.7 = (f32[256]{0:T(256)S(1)}, f32[256]{0:T(256)}, u32[]{:S(2)}) copy-start(f32[256]{0:T(256)} %param.16) | copy-start | bytes 3076
  7.6 0.7 %copy-start.8 = (f32[256]{0:T(256)S(1)}, f32[256]{0:T(256)}, u32[]{:S(2)}) copy-start(f32[256]{0:T(256)} %param.20) | copy-start | bytes 3076
  7.6 0.7 %copy-start.9 = (f32[256]{0:T(256)S(1)}, f32[256]{0:T(256)}, u32[]{:S(2)}) copy-start(f32[256]{0:T(256)} %param.21) | copy-start | bytes 3076
  7.6 0.7 %copy-start.5 = (f32[256]{0:T(256)S(1)}, f32[256]{0:T(256)}, u32[]{:S(2)}) copy-start(f32[256]{0:T(256)} %param.14) | copy-start | bytes 3076
  7.6 0.7 %copy-start.10 = (bf16[64]{0:T(256)(128)(2,1)S(1)}, bf16[64]{0:T(256)(128)(2,1)}, u32[]{:S(2)}) copy-start(bf16[64]{0:T(256)(128)(2,1)} %b_ref.1) | copy-start | bytes 388
  8.3 7.7 %copy-start.1 = (f32[31,256]{1,0:T(8,128)S(1)}, f32[31,256]{1,0:T(8,128)}, u32[]{:S(2)}) copy-start(f32[31,256]{1,0:T(8,128)} %taps_ref.2) | copy-start | bytes 95236
  8.4 12.5 %collective-permute-start = (bf16[144,256]{1,0:T(8,128)(2,1)S(1)}, bf16[144,256]{1,0:T(8,128)(2,1)S(1)}, u32[]{:S(2)}, u32[]{:S(2)}) collective-permute-start(bf16[144,256]{1,0:T(8,128)(2,1)S(1)} %get-tuple-element.13.refs_4_), channel_id=1, source_target_pairs={{0,4},{1,5},{2,6},{3,7},{4,0},{5,1},{6,2},{7,3},{8,12},{9,13},{10,... | collective-permute-start | bytes 221192 | tf_op jit(solution)/shard_map/ppermute | solution.py:190
  10.3 10.6 %collective-permute-start.1 = (bf16[144,256]{1,0:T(8,128)(2,1)S(1)}, bf16[144,256]{1,0:T(8,128)(2,1)S(1)}, u32[]{:S(2)}, u32[]{:S(2)}) collective-permute-start(bf16[144,256]{1,0:T(8,128)(2,1)S(1)} %get-tuple-element.13.refs_4_), channel_id=1, source_target_pairs={{0,8},{1,9},{2,10},{3,11},{4,12},{5,13},{6,14},{7,15},{8,0},{9,1},... | collective-permute-start | bytes 221192 | tf_op jit(solution)/shard_map/ppermute | solution.py:190
  12.6 8.3 %collective-permute-start.2 = (bf16[144,256]{1,0:T(8,128)(2,1)S(1)}, bf16[144,256]{1,0:T(8,128)(2,1)S(1)}, u32[]{:S(2)}, u32[]{:S(2)}) collective-permute-start(bf16[144,256]{1,0:T(8,128)(2,1)S(1)} %get-tuple-element.13.refs_4_), channel_id=1, source_target_pairs={{0,12},{1,13},{2,14},{3,15},{4,8},{5,9},{6,10},{7,11},{8,4},{9,5},... | collective-permute-start | bytes 221192 | tf_op jit(solution)/shard_map/ppermute | solution.py:190
  12.7 8.2 %collective-permute-start.3 = (bf16[144,256]{1,0:T(8,128)(2,1)S(1)}, bf16[144,256]{1,0:T(8,128)(2,1)S(1)}, u32[]{:S(2)}, u32[]{:S(2)}) collective-permute-start(bf16[144,256]{1,0:T(8,128)(2,1)S(1)} %get-tuple-element.13.refs_4_), channel_id=1, source_target_pairs={{0,2},{1,3},{2,0},{3,1},{4,6},{5,7},{6,4},{7,5},{8,10},{9,11},{10,... | collective-permute-start | bytes 221192 | tf_op jit(solution)/shard_map/ppermute | solution.py:190
  17.4 11.4 %all-to-all-start.1 = ((bf16[32,8,256]{2,1,0:T(8,128)(2,1)}), bf16[32,8,256]{2,1,0:T(8,128)(2,1)S(1)}, u32[]{:S(2)}, u32[]{:S(2)}) async-start(bf16[32,8,256]{2,1,0:T(8,128)(2,1)} %bitcast.6), calls=%async_computation.1 | async-start | bytes 262144 | tf_op jit(solution)/shard_map/all_to_all | solution.py:238
  20.9 7.9 %copy-start.2 = (f32[31,256]{1,0:T(8,128)S(1)}, f32[31,256]{1,0:T(8,128)}, u32[]{:S(2)}) copy-start(f32[31,256]{1,0:T(8,128)} %taps_ref.3) | copy-start | bytes 95236
  21.0 9.5 %collective-permute-start.6 = (bf16[656,256]{1,0:T(8,128)(2,1)S(1)}, bf16[656,256]{1,0:T(8,128)(2,1)S(1)}, u32[]{:S(2)}, u32[]{:S(2)}) collective-permute-start(bf16[656,256]{1,0:T(8,128)(2,1)S(1)} %get-tuple-element.18.rest_0_), channel_id=1, source_target_pairs={{0,1},{1,0},{2,3},{3,2},{4,5},{5,4},{6,7},{7,6},{8,9},{9,8},{10,11... | collective-permute-start | bytes 1007624 | tf_op jit(solution)/shard_map/ppermute | solution.py:190
  21.3 8.7 %collective-permute-start.4 = (bf16[272,256]{1,0:T(8,128)(2,1)S(1)}, bf16[272,256]{1,0:T(8,128)(2,1)S(1)}, u32[]{:S(2)}, u32[]{:S(2)}) collective-permute-start(bf16[272,256]{1,0:T(8,128)(2,1)S(1)} %get-tuple-element.14), channel_id=1, source_target_pairs={{0,2},{1,3},{2,0},{3,1},{4,6},{5,7},{6,4},{7,5},{8,10},{9,11},{10,... | collective-permute-start | bytes 417800 | tf_op jit(solution)/shard_map/ppermute | solution.py:190
  23.0 7.0 %collective-permute-start.5 = (bf16[144,256]{1,0:T(8,128)(2,1)S(1)}, bf16[144,256]{1,0:T(8,128)(2,1)S(1)}, u32[]{:S(2)}, u32[]{:S(2)}) collective-permute-start(bf16[144,256]{1,0:T(8,128)(2,1)S(1)} %get-tuple-element.15), channel_id=1, source_target_pairs={{0,2},{1,3},{2,0},{3,1},{4,6},{5,7},{6,4},{7,5},{8,10},{9,11},{10,... | collective-permute-start | bytes 221192 | tf_op jit(solution)/shard_map/ppermute | solution.py:190
  29.7 1.8 %copy-start = (bf16[32,2,4,256]{3,2,1,0:T(4,128)(2,1)S(1)}, bf16[32,2,4,256]{3,2,1,0:T(4,128)(2,1)}, u32[]{:S(2)}) copy-start(bf16[32,2,4,256]{3,2,1,0:T(4,128)(2,1)} %feat_ref.1) | copy-start | bytes 393220
  30.0 1.5 %collective-permute-start.7 = (bf16[272,256]{1,0:T(8,128)(2,1)S(1)}, bf16[272,256]{1,0:T(8,128)(2,1)S(1)}, u32[]{:S(2)}, u32[]{:S(2)}) collective-permute-start(bf16[272,256]{1,0:T(8,128)(2,1)S(1)} %collective-permute-done.4.rest_1_), channel_id=1, source_target_pairs={{0,1},{1,0},{2,3},{3,2},{4,5},{5,4},{6,7},{7,6},{8,9},{9,8},{10,11... | collective-permute-start | bytes 417800 | tf_op jit(solution)/shard_map/ppermute | solution.py:190
  30.0 1.5 %collective-permute-start.8 = (bf16[144,256]{1,0:T(8,128)(2,1)S(1)}, bf16[144,256]{1,0:T(8,128)(2,1)S(1)}, u32[]{:S(2)}, u32[]{:S(2)}) collective-permute-start(bf16[144,256]{1,0:T(8,128)(2,1)S(1)} %collective-permute-done.5.rest_2_), channel_id=1, source_target_pairs={{0,1},{1,0},{2,3},{3,2},{4,5},{5,4},{6,7},{7,6},{8,9},{9,8},{10,11... | collective-permute-start | bytes 221192 | tf_op jit(solution)/shard_map/ppermute | solution.py:190

commit v13 on v12

--- a/solution.py
+++ b/solution.py
@@ -17,16 +17,13 @@
     return pl.BlockSpec(memory_space=pltpu.VMEM)
 
 
-def pack_kernel(b_ref, w_in_ref, w_out_ref, *rest):
-    *vectors, block_ref, consts_ref = rest
+def pack_kernel(b_ref, w_in_ref, w_out_ref, block_ref):
     block_ref[0:SLOT, :] = w_in_ref[...]
     block_ref[SLOT : 2 * SLOT, :] = w_out_ref[...]
     bias = b_ref[...].astype(jnp.float32)[None, :]
     c = block_ref.shape[1]
     wide = jnp.concatenate([bias] * (c // SLOT), axis=1)
     block_ref[2 * SLOT :, :] = jnp.broadcast_to(wide, (EXTRA, c)).astype(block_ref.dtype)
-    for i, vector in enumerate(vectors):
-        consts_ref[i : i + 1, :] = vector[...]
 
 
 def join_kernel(*refs):
@@ -43,7 +40,11 @@
     last_ref[...] = blocks[count][...]
 
 
-def radial_kernel(x_ref, taps_ref, out_ref, even, odd):
+def radial_kernel(x_ref, taps_ref, *rest):
+    vectors = rest[:5]
+    out_ref, consts_ref, even, odd, done, sems = rest[5:]
+    for i, vector in enumerate(vectors):
+        consts_ref[i : i + 1, :] = vector[...]
     n, a_loc, _, theta, c = x_ref.shape
     taps = taps_ref.shape[0]
     pad = (taps + 1) // 4
@@ -62,17 +63,28 @@
 
     block = 4
 
-    def step(i, carry):
-        base = i * block
+    def step(base, wanted):
         total = jnp.zeros((block, a_loc, 2 * theta, c), jnp.float32)
-        for k in range(taps):
-            shift = k - taps // 2
+        for shift in wanted:
+            k = shift + taps // 2
             source = even if shift % 2 == 0 else odd
             total = total + source[pl.ds(base + (pad + shift // 2), block)] * taps_ref[k : k + 1, :]
-        out_ref[pl.ds(base, block)] = total.astype(out_ref.dtype)
-        return carry
-
-    lax.fori_loop(0, n // block, step, 0)
+        done[pl.ds(base, block)] = total.astype(done.dtype)
+
+    every = range(-(taps // 2), taps // 2 + 1)
+    if n <= 8 * block:
+        copies = []
+        for base in range(0, n, block):
+            step(base, [s for s in every if base + block - 1 + s // 2 >= -(s % 2) and base + s // 2 < n])
+            part = pl.ds(base, block)
+            copies.append(pltpu.make_async_copy(done.at[part], out_ref.at[part], sems.at[base // block]))
+            copies[-1].start()
+    else:
+        pl.loop(0, n // block)(lambda i: step(i * block, every))
+        copies = [pltpu.make_async_copy(done, out_ref, sems.at[0])]
+        copies[0].start()
+    for copy in copies:
+        copy.wait()
 
 
 def axial_kernel(z_ref, taps_ref, consts_ref, out_ref, padded, summed):
@@ -85,15 +97,17 @@
     padded[half : half + axial] = z_ref[...].astype(jnp.float32)
     block = 8
 
-    def conv(i, carry):
-        base = i * block
+    def conv(base, wanted):
         total = jnp.zeros((block, rows, c), jnp.float32)
-        for k in range(taps):
+        for k in wanted:
             total = total + padded[pl.ds(base + k, block)] * taps_ref[k : k + 1, :]
         summed[pl.ds(base, block)] = total
-        return carry
-
-    lax.fori_loop(0, axial // block, conv, 0)
+
+    if axial <= 8 * block:
+        for base in range(0, axial, block):
+            conv(base, [k for k in range(taps) if base + block - 1 + k >= half and base + k < half + axial])
+    else:
+        pl.loop(0, axial // block)(lambda i: conv(i * block, range(taps)))
 
     def norm(i, carry):
         v = (summed[pl.ds(i * PLANES, PLANES)] + consts_ref[0:1, :]).reshape(PLANES * rows, c)
@@ -149,22 +163,35 @@
 
 
 def mlp_kernel(partials, normed_ref, consts_ref, feat_ref, *rest):
-    *blocks, out_ref, branch = rest
-    theta, c = feat_ref.shape[2:]
+    *blocks, out_ref, branch, done, sems = rest
+    axial, _, theta, c = feat_ref.shape
     rows = 2 * theta
-    size = PLANES * rows
-
-    def mlp(at):
-        total = hidden_sum(normed_ref[pl.ds(at, size), :], blocks[partials:])
+    planes = PLANES // 2
+
+    def mlp(at, size):
+        tokens = pl.ds(at * rows, size * rows)
+        total = hidden_sum(normed_ref[tokens, :], blocks[partials:])
         for partial_ref in blocks[:partials]:
-            total = total + partial_ref[pl.ds(at, size), :]
+            total = total + partial_ref[tokens, :]
         result = (consts_ref[4:5, :] * (total + consts_ref[3:4, :])).astype(jnp.bfloat16).astype(jnp.float32)
-        branch[pl.ds(at // rows, PLANES)] = result.reshape(PLANES, rows, c)
-
-    over_tokens(normed_ref.shape[0], size, mlp)
-    for r in range(2):
-        got = branch[:, r * theta : (r + 1) * theta, :]
-        out_ref[:, r] = (feat_ref[:, r].astype(jnp.float32) + got).astype(out_ref.dtype)
+        branch[pl.ds(at, size)] = result.reshape(size, rows, c)
+        for r in range(2):
+            got = branch[pl.ds(at, size), r * theta : (r + 1) * theta, :]
+            done[pl.ds(at, size), r] = (feat_ref[pl.ds(at, size), r].astype(jnp.float32) + got).astype(done.dtype)
+
+    copies = []
+    if axial == PLANES:
+        for i in range(2):
+            mlp(i * planes, planes)
+            part = pl.ds(i * planes, planes)
+            copies.append(pltpu.make_async_copy(done.at[part], out_ref.at[part], sems.at[i]))
+            copies[-1].start()
+    else:
+        pl.loop(0, axial // PLANES)(lambda i: mlp(pl.multiple_of(i * PLANES, PLANES), PLANES))
+        copies.append(pltpu.make_async_copy(done, out_ref, sems.at[0]))
+        copies[-1].start()
+    for copy in copies:
+        copy.wait()
 
 
 def digits(n):
@@ -191,21 +218,17 @@
 
     vectors = [v[None, :] for v in (conv_bias, ln_gain, ln_bias, b_out, layer_scale)]
     if spread:
-        own, consts = pl.pallas_call(
+        own = pl.pallas_call(
             pack_kernel,
-            out_shape=[
-                jax.ShapeDtypeStruct((2 * SLOT + EXTRA, c), jnp.bfloat16),
-                jax.ShapeDtypeStruct((8, c), jnp.float32),
-            ],
-            in_specs=[vmem()] * 8,
-            out_specs=[vmem()] * 2,
+            out_shape=jax.ShapeDtypeStruct((2 * SLOT + EXTRA, c), jnp.bfloat16),
+            in_specs=[vmem()] * 3,
+            out_specs=vmem(),
             compiler_params=small,
             name="pack",
-        )(b_in, w_in, w_out, *vectors)
+        )(b_in, w_in, w_out)
         line = [move(own, 0, by) for by in range(1, outer)]
         side = move(own, 1, 1)
     else:
-        consts = jnp.concatenate(vectors + [jnp.zeros((3, c), jnp.float32)], axis=0)
         w_all = lax.all_gather(w_in, "row", axis=0, tiled=True).reshape(-1, SLOT, c)
         o_all = lax.all_gather(w_out, "row", axis=0, tiled=True).reshape(-1, SLOT, c)
         b_all = jnp.tile(lax.all_gather(b_in, "row", axis=0, tiled=True).reshape(-1, SLOT), (1, c // SLOT))
@@ -214,15 +237,19 @@
 
     got = lax.all_to_all(features, "row", split_axis=0, concat_axis=0, tiled=True)
     pad = (radial_taps.shape[0] + 1) // 4
-    mixed = pl.pallas_call(
+    mixed, consts = pl.pallas_call(
         radial_kernel,
-        out_shape=jax.ShapeDtypeStruct((n, a_loc, rows, c), jnp.bfloat16),
-        in_specs=[vmem()] * 2,
-        out_specs=vmem(),
-        scratch_shapes=[pltpu.VMEM((n + 2 * pad, a_loc, rows, c), jnp.float32)] * 2,
+        out_shape=[
+            jax.ShapeDtypeStruct((n, a_loc, rows, c), jnp.bfloat16),
+            jax.ShapeDtypeStruct((8, c), jnp.float32),
+        ],
+        in_specs=[vmem()] * 7,
+        out_specs=[anywhere, vmem()],
+        scratch_shapes=[pltpu.VMEM((n + 2 * pad, a_loc, rows, c), jnp.float32)] * 2
+        + [pltpu.VMEM((n, a_loc, rows, c), jnp.bfloat16), pltpu.SemaphoreType.DMA((8,))],
         compiler_params=middle,
         name="radial",
-    )(got.reshape(n, a_loc, r_loc, theta, c), radial_taps)
+    )(got.reshape(n, a_loc, r_loc, theta, c), radial_taps, *vectors)
     if spread:
         joined, most, last = pl.pallas_call(
             join_kernel,
@@ -268,8 +295,12 @@
         partial(mlp_kernel, len(partials)),
         out_shape=jax.ShapeDtypeStruct(features.shape, jnp.bfloat16),
         in_specs=[vmem()] * (3 + len(operands)),
-        out_specs=vmem(),
-        scratch_shapes=[pltpu.VMEM((axial, rows, c), jnp.float32)],
+        out_specs=anywhere,
+        scratch_shapes=[
+            pltpu.VMEM((axial, rows, c), jnp.float32),
+            pltpu.VMEM(features.shape, jnp.bfloat16),
+            pltpu.SemaphoreType.DMA((2,)),
+        ],
         compiler_params=large,
         name="mlp",
     )(normed, consts, features, *operands)

time: 33.1 us -> 33.6 us (1.015)
  waiting for transfers between devices: 7.24 us -> 8.19 us
  Pallas kernels: 4.39 us -> 3.92 us
    all_to_all x1, waiting for transfers between devices: 1.32 us -> 1.98 us  [local(): lax.all_to_all(features, 'row', split_axis=0, concat_axis=0, tiled=True)]
  transfers between devices with their start and end apart: 11 -> 11, of which waited for: 4 -> 4; matrix products, arithmetic and copies ran while one was open for 0% -> 0% of each run, Pallas kernels for 10% -> 8%
where the time goes in v13:
time: 33.6 us; the launch traced here: 33.3 us
  starting transfers between devices  20.3 us (60%)
  waiting for transfers between devices  8.19 us (24%)
  Pallas kernels  3.92 us (12%)
  local copies, waits for them, and re-layouts  0.75 us (2%)
    ppermute x9, starting transfers between devices, move(): return lax.ppermute(piece, 'row', [(i, i ^ by * stride) for i in range(n)])  9.2 us
    all_to_all x1, starting transfers between devices, local(): lax.all_to_all(features, 'row', split_axis=0, concat_axis=0, tiled=True)  7.53 us
    all_to_all x1, waiting for transfers between devices, local(): lax.all_to_all(mixed.reshape(axial, rows, c), 'row', split_axis=0, concat...  5.43 us
    all_to_all x1, starting transfers between devices, local(): lax.all_to_all(mixed.reshape(axial, rows, c), 'row', split_axis=0, concat...  3.52 us
    all_to_all x1, waiting for transfers between devices, local(): lax.all_to_all(features, 'row', split_axis=0, concat_axis=0, tiled=True)  1.98 us
    pallas_call x1, Pallas kernels, local(): pl.pallas_call(partial(mlp_kernel, len(partials)), out_shape=jax.ShapeDty...  1.24 us
    pallas_call x1, Pallas kernels, local(): pl.pallas_call(radial_kernel, out_shape=[jax.ShapeDtypeStruct((n, a_loc,...  1.19 us
    ppermute x9, waiting for transfers between devices, move(): return lax.ppermute(piece, 'row', [(i, i ^ by * stride) for i in range(n)])  0.79 us
  transfers between devices with their start and end apart: 11, of which 4 were waited for; matrix products, arithmetic and copies ran while one was open for 0% of the time, Pallas kernels for 8%

profile of v13, /device:TPU:0, one launch (start us, length us, event | category | flops | bytes accessed | tf_op | source)
XLA Modules:
  0.0 33.3 jit_solution(8516500916265069364)
XLA Ops:
  0.0 7.5 %all-to-all-start = ((bf16[32,2,4,256]{3,2,1,0:T(4,128)(2,1)}), bf16[32,2,4,256]{3,2,1,0:T(4,128)(2,1)S(1)}, u32[]{:S(2)}, u32[]{:S(2)}) async-start(bf16[32,2,4,256]{3,2,1,0:T(4,128)(2,1)} %feat_ref.1), calls=%async_computation | async-start | bytes 262144 | tf_op jit(solution)/shard_map/all_to_all | solution.py:238
  7.6 0.0 copy-start.4
  7.6 0.1 pack.1.refs_4_
  7.7 1.9 %collective-permute-start = (bf16[144,256]{1,0:T(8,128)(2,1)S(1)}, bf16[144,256]{1,0:T(8,128)(2,1)S(1)}, u32[]{:S(2)}, u32[]{:S(2)}) collective-permute-start(bf16[144,256]{1,0:T(8,128)(2,1)S(1)} %pack.1.refs_4_), channel_id=1, source_target_pairs={{0,4},{1,5},{2,6},{3,7},{4,0},{5,1},{6,2},{7,3},{8,12},{9,13},{10,... | collective-permute-start | bytes 221192 | tf_op jit(solution)/shard_map/ppermute | solution.py:217
  9.6 2.4 %collective-permute-start.1 = (bf16[144,256]{1,0:T(8,128)(2,1)S(1)}, bf16[144,256]{1,0:T(8,128)(2,1)S(1)}, u32[]{:S(2)}, u32[]{:S(2)}) collective-permute-start(bf16[144,256]{1,0:T(8,128)(2,1)S(1)} %pack.1.refs_4_), channel_id=1, source_target_pairs={{0,8},{1,9},{2,10},{3,11},{4,12},{5,13},{6,14},{7,15},{8,0},{9,1},... | collective-permute-start | bytes 221192 | tf_op jit(solution)/shard_map/ppermute | solution.py:217
  12.0 0.1 collective-permute-start.2
  12.1 1.9 %collective-permute-start.3 = (bf16[144,256]{1,0:T(8,128)(2,1)S(1)}, bf16[144,256]{1,0:T(8,128)(2,1)S(1)}, u32[]{:S(2)}, u32[]{:S(2)}) collective-permute-start(bf16[144,256]{1,0:T(8,128)(2,1)S(1)} %pack.1.refs_4_), channel_id=1, source_target_pairs={{0,2},{1,3},{2,0},{3,1},{4,6},{5,7},{6,4},{7,5},{8,10},{9,11},{10,... | collective-permute-start | bytes 221192 | tf_op jit(solution)/shard_map/ppermute | solution.py:217
  14.0 2.0 %all-to-all-done = bf16[32,2,4,256]{3,2,1,0:T(4,128)(2,1)S(1)} async-done(((bf16[32,2,4,256]{3,2,1,0:T(4,128)(2,1)}), bf16[32,2,4,256]{3,2,1,0:T(4,128)(2,1)S(1)}, u32[]{:S(2)}, u32[]{:S(2)}) %all-to-all-start) | async-done | bytes 131104 | tf_op jit(solution)/shard_map/all_to_all | solution.py:238
  16.0 0.0 copy-start.5
  16.0 0.6 %copy-done.6 = f32[256]{0:T(256)S(1)} copy-done((f32[256]{0:T(256)S(1)}, f32[256]{0:T(256)}, u32[]{:S(2)}) %copy-start.6) | copy-done | bytes 1048
  16.6 0.0 copy-done.7
  16.7 0.0 copy-done.8
  16.7 0.0 copy-done.9
  16.7 0.0 copy-done.5
  16.7 1.2 %radial.1 = (bf16[16,2,8,256]{3,2,1,0:T(8,128)(2,1)}, f32[8,256]{1,0:T(8,128)S(1)}) custom-call(bf16[16,2,2,4,256]{4,3,2,1,0:T(4,128)(2,1)S(1)} %bitcast.7, f32[31,256]{1,0:T(8,128)S(1)} %copy-done.4, f32[1,256]{1,0:T(1,128)S(1)} %bitcast.8, f32[1,256]{1,0:T(1,128)S(1)} %bitcast.9, f32[1,256]{1,0:T(1,128)S(1)} %bitcast.10, f32[1,256]{1,0:T(1,128)S(1)} %bitcast.11, ...), custom_call_target="tpu_custom_call" | custom-call | tf_op jit(solution)/shard_map/radial/pallas_call | solution.py:240
  17.9 3.5 %all-to-all-start.1 = ((bf16[32,8,256]{2,1,0:T(8,128)(2,1)}), bf16[32,8,256]{2,1,0:T(8,128)(2,1)S(1)}, u32[]{:S(2)}, u32[]{:S(2)}) async-start(bf16[32,8,256]{2,1,0:T(8,128)(2,1)} %bitcast.6), calls=%async_computation.1 | async-start | bytes 262144 | tf_op jit(solution)/shard_map/all_to_all | solution.py:265
  21.4 0.0 copy-start.3
  21.4 0.0 collective-permute-done.refs_1_
  21.5 0.0 collective-permute-done.1.refs_2_
  21.5 0.0 collective-permute-done.3.refs_5_
  21.5 0.4 %collective-permute-start.6 = (bf16[656,256]{1,0:T(8,128)(2,1)S(1)}, bf16[656,256]{1,0:T(8,128)(2,1)S(1)}, u32[]{:S(2)}, u32[]{:S(2)}) collective-permute-start(bf16[656,256]{1,0:T(8,128)(2,1)S(1)} %get-tuple-element.18.rest_0_), channel_id=1, source_target_pairs={{0,1},{1,0},{2,3},{3,2},{4,5},{5,4},{6,7},{7,6},{8,9},{9,8},{10,11... | collective-permute-start | bytes 1007624 | tf_op jit(solution)/shard_map/ppermute | solution.py:217
  21.9 1.7 %collective-permute-start.4 = (bf16[272,256]{1,0:T(8,128)(2,1)S(1)}, bf16[272,256]{1,0:T(8,128)(2,1)S(1)}, u32[]{:S(2)}, u32[]{:S(2)}) collective-permute-start(bf16[272,256]{1,0:T(8,128)(2,1)S(1)} %get-tuple-element.14), channel_id=1, source_target_pairs={{0,2},{1,3},{2,0},{3,1},{4,6},{5,7},{6,4},{7,5},{8,10},{9,11},{10,... | collective-permute-start | bytes 417800 | tf_op jit(solution)/shard_map/ppermute | solution.py:217
  23.6 0.3 %collective-permute-start.5 = (bf16[144,256]{1,0:T(8,128)(2,1)S(1)}, bf16[144,256]{1,0:T(8,128)(2,1)S(1)}, u32[]{:S(2)}, u32[]{:S(2)}) collective-permute-start(bf16[144,256]{1,0:T(8,128)(2,1)S(1)} %get-tuple-element.15), channel_id=1, source_target_pairs={{0,2},{1,3},{2,0},{3,1},{4,6},{5,7},{6,4},{7,5},{8,10},{9,11},{10,... | collective-permute-start | bytes 221192 | tf_op jit(solution)/shard_map/ppermute | solution.py:217
  23.9 5.4 %all-to-all-done.1.z_ref = bf16[32,8,256]{2,1,0:T(8,128)(2,1)S(1)} async-done(((bf16[32,8,256]{2,1,0:T(8,128)(2,1)}), bf16[32,8,256]{2,1,0:T(8,128)(2,1)S(1)}, u32[]{:S(2)}, u32[]{:S(2)}) %all-to-all-start.1) | async-done | bytes 131104 | tf_op jit(solution)/shard_map/all_to_all | solution.py:265
  29.3 0.6 %axial.1.normed_ref = bf16[256,256]{1,0:T(8,128)(2,1)S(1)} custom-call(bf16[32,8,256]{2,1,0:T(8,128)(2,1)S(1)} %all-to-all-done.1.z_ref, f32[31,256]{1,0:T(8,128)S(1)} %copy-done.3, f32[8,256]{1,0:T(8,128)S(1)} %get-tuple-element.16.consts_ref), custom_call_target="tpu_custom_call" | custom-call | tf_op jit(solution)/shard_map/axial/pallas_call | solution.py:266
  30.0 0.0 copy-start
  30.0 0.6 %collective-permute-done.5.rest_2_ = bf16[144,256]{1,0:T(8,128)(2,1)S(1)} collective-permute-done((bf16[144,256]{1,0:T(8,128)(2,1)S(1)}, bf16[144,256]{1,0:T(8,128)(2,1)S(1)}, u32[]{:S(2)}, u32[]{:S(2)}) %collective-permute-start.5) | collective-permute-done | bytes 73760 | tf_op jit(solution)/shard_map/ppermute | solution.py:217
  30.6 0.5 %collective-permute-start.8 = (bf16[144,256]{1,0:T(8,128)(2,1)S(1)}, bf16[144,256]{1,0:T(8,128)(2,1)S(1)}, u32[]{:S(2)}, u32[]{:S(2)}) collective-permute-start(bf16[144,256]{1,0:T(8,128)(2,1)S(1)} %collective-permute-done.5.rest_2_), channel_id=1, source_target_pairs={{0,1},{1,0},{2,3},{3,2},{4,5},{5,4},{6,7},{7,6},{8,9},{9,8},{10,11... | collective-permute-start | bytes 221192 | tf_op jit(solution)/shard_map/ppermute | solution.py:217
  31.1 0.0 collective-permute-done.6.rest_1_
  31.1 0.7 %first.1.rest_0_ = f32[256,256]{1,0:T(8,128)S(1)} custom-call(bf16[256,256]{1,0:T(8,128)(2,1)S(1)} %axial.1.normed_ref, bf16[656,256]{1,0:T(8,128)(2,1)S(1)} %get-tuple-element.18.rest_0_, bf16[656,256]{1,0:T(8,128)(2,1)S(1)} %collective-permute-done.6.rest_1_), custom_call_target="tpu_custom_call" | custom-call | tf_op jit(solution)/shard_map/first/pallas_call | solution.py:282
  31.8 0.2 collective-permute-done.8.rest_4_
  32.0 1.2 %mlp.1 = bf16[32,2,4,256]{3,2,1,0:T(4,128)(2,1)} custom-call(bf16[256,256]{1,0:T(8,128)(2,1)S(1)} %axial.1.normed_ref, f32[8,256]{1,0:T(8,128)S(1)} %get-tuple-element.16.consts_ref, bf16[32,2,4,256]{3,2,1,0:T(4,128)(2,1)S(1)} %copy-done, f32[256,256]{1,0:T(8,128)S(1)} %first.1.rest_0_, bf16[272,256]{1,0:T(8,128)(2,1)S(1)} %collective-permute-done.4.rest_1_, ...), custom_call_target="tpu_custom_call" | custom-call | tf_op jit(solution)/shard_map/mlp/pallas_call | solution.py:294
  (18 shorter events, 0.1 us)
Async XLA Ops:
  0.0 7.5 %copy-start.1 = (bf16[64,256]{1,0:T(8,128)(2,1)S(1)}, bf16[64,256]{1,0:T(8,128)(2,1)}, u32[]{:S(2)}) copy-start(bf16[64,256]{1,0:T(8,128)(2,1)} %w_in_ref.1) | copy-start | bytes 98308
  0.0 7.6 %copy-start.10 = (bf16[64]{0:T(256)(128)(2,1)S(1)}, bf16[64]{0:T(256)(128)(2,1)}, u32[]{:S(2)}) copy-start(bf16[64]{0:T(256)(128)(2,1)} %b_ref.1) | copy-start | bytes 388
  0.0 7.6 %copy-start.2 = (bf16[64,256]{1,0:T(8,128)(2,1)S(1)}, bf16[64,256]{1,0:T(8,128)(2,1)}, u32[]{:S(2)}) copy-start(bf16[64,256]{1,0:T(8,128)(2,1)} %w_out_ref.1) | copy-start | bytes 98308
  0.0 16.0 %all-to-all-start = ((bf16[32,2,4,256]{3,2,1,0:T(4,128)(2,1)}), bf16[32,2,4,256]{3,2,1,0:T(4,128)(2,1)S(1)}, u32[]{:S(2)}, u32[]{:S(2)}) async-start(bf16[32,2,4,256]{3,2,1,0:T(4,128)(2,1)} %feat_ref.1), calls=%async_computation | async-start | bytes 262144 | tf_op jit(solution)/shard_map/all_to_all | solution.py:238
  7.6 8.4 %copy-start.4 = (f32[31,256]{1,0:T(8,128)S(1)}, f32[31,256]{1,0:T(8,128)}, u32[]{:S(2)}) copy-start(f32[31,256]{1,0:T(8,128)} %taps_ref.2) | copy-start | bytes 95236
  7.7 13.8 %collective-permute-start = (bf16[144,256]{1,0:T(8,128)(2,1)S(1)}, bf16[144,256]{1,0:T(8,128)(2,1)S(1)}, u32[]{:S(2)}, u32[]{:S(2)}) collective-permute-start(bf16[144,256]{1,0:T(8,128)(2,1)S(1)} %pack.1.refs_4_), channel_id=1, source_target_pairs={{0,4},{1,5},{2,6},{3,7},{4,0},{5,1},{6,2},{7,3},{8,12},{9,13},{10,... | collective-permute-start | bytes 221192 | tf_op jit(solution)/shard_map/ppermute | solution.py:217
  9.6 11.9 %collective-permute-start.1 = (bf16[144,256]{1,0:T(8,128)(2,1)S(1)}, bf16[144,256]{1,0:T(8,128)(2,1)S(1)}, u32[]{:S(2)}, u32[]{:S(2)}) collective-permute-start(bf16[144,256]{1,0:T(8,128)(2,1)S(1)} %pack.1.refs_4_), channel_id=1, source_target_pairs={{0,8},{1,9},{2,10},{3,11},{4,12},{5,13},{6,14},{7,15},{8,0},{9,1},... | collective-permute-start | bytes 221192 | tf_op jit(solution)/shard_map/ppermute | solution.py:217
  12.0 9.5 %collective-permute-start.2 = (bf16[144,256]{1,0:T(8,128)(2,1)S(1)}, bf16[144,256]{1,0:T(8,128)(2,1)S(1)}, u32[]{:S(2)}, u32[]{:S(2)}) collective-permute-start(bf16[144,256]{1,0:T(8,128)(2,1)S(1)} %pack.1.refs_4_), channel_id=1, source_target_pairs={{0,12},{1,13},{2,14},{3,15},{4,8},{5,9},{6,10},{7,11},{8,4},{9,5},... | collective-permute-start | bytes 221192 | tf_op jit(solution)/shard_map/ppermute | solution.py:217
  12.1 9.4 %collective-permute-start.3 = (bf16[144,256]{1,0:T(8,128)(2,1)S(1)}, bf16[144,256]{1,0:T(8,128)(2,1)S(1)}, u32[]{:S(2)}, u32[]{:S(2)}) collective-permute-start(bf16[144,256]{1,0:T(8,128)(2,1)S(1)} %pack.1.refs_4_), channel_id=1, source_target_pairs={{0,2},{1,3},{2,0},{3,1},{4,6},{5,7},{6,4},{7,5},{8,10},{9,11},{10,... | collective-permute-start | bytes 221192 | tf_op jit(solution)/shard_map/ppermute | solution.py:217
  16.0 0.7 %copy-start.6 = (f32[256]{0:T(256)S(1)}, f32[256]{0:T(256)}, u32[]{:S(2)}) copy-start(f32[256]{0:T(256)} %param.15) | copy-start | bytes 3076
  16.0 0.7 %copy-start.7 = (f32[256]{0:T(256)S(1)}, f32[256]{0:T(256)}, u32[]{:S(2)}) copy-start(f32[256]{0:T(256)} %param.16) | copy-start | bytes 3076
  16.0 0.7 %copy-start.8 = (f32[256]{0:T(256)S(1)}, f32[256]{0:T(256)}, u32[]{:S(2)}) copy-start(f32[256]{0:T(256)} %param.20) | copy-start | bytes 3076
  16.0 0.7 %copy-start.9 = (f32[256]{0:T(256)S(1)}, f32[256]{0:T(256)}, u32[]{:S(2)}) copy-start(f32[256]{0:T(256)} %param.21) | copy-start | bytes 3076
  16.0 0.7 %copy-start.5 = (f32[256]{0:T(256)S(1)}, f32[256]{0:T(256)}, u32[]{:S(2)}) copy-start(f32[256]{0:T(256)} %param.14) | copy-start | bytes 3076
  17.9 11.4 %all-to-all-start.1 = ((bf16[32,8,256]{2,1,0:T(8,128)(2,1)}), bf16[32,8,256]{2,1,0:T(8,128)(2,1)S(1)}, u32[]{:S(2)}, u32[]{:S(2)}) async-start(bf16[32,8,256]{2,1,0:T(8,128)(2,1)} %bitcast.6), calls=%async_computation.1 | async-start | bytes 262144 | tf_op jit(solution)/shard_map/all_to_all | solution.py:265
  21.4 7.9 %copy-start.3 = (f32[31,256]{1,0:T(8,128)S(1)}, f32[31,256]{1,0:T(8,128)}, u32[]{:S(2)}) copy-start(f32[31,256]{1,0:T(8,128)} %taps_ref.3) | copy-start | bytes 95236
  21.5 9.5 %collective-permute-start.6 = (bf16[656,256]{1,0:T(8,128)(2,1)S(1)}, bf16[656,256]{1,0:T(8,128)(2,1)S(1)}, u32[]{:S(2)}, u32[]{:S(2)}) collective-permute-start(bf16[656,256]{1,0:T(8,128)(2,1)S(1)} %get-tuple-element.18.rest_0_), channel_id=1, source_target_pairs={{0,1},{1,0},{2,3},{3,2},{4,5},{5,4},{6,7},{7,6},{8,9},{9,8},{10,11... | collective-permute-start | bytes 1007624 | tf_op jit(solution)/shard_map/ppermute | solution.py:217
  21.9 8.7 %collective-permute-start.4 = (bf16[272,256]{1,0:T(8,128)(2,1)S(1)}, bf16[272,256]{1,0:T(8,128)(2,1)S(1)}, u32[]{:S(2)}, u32[]{:S(2)}) collective-permute-start(bf16[272,256]{1,0:T(8,128)(2,1)S(1)} %get-tuple-element.14), channel_id=1, source_target_pairs={{0,2},{1,3},{2,0},{3,1},{4,6},{5,7},{6,4},{7,5},{8,10},{9,11},{10,... | collective-permute-start | bytes 417800 | tf_op jit(solution)/shard_map/ppermute | solution.py:217
  23.6 7.0 %collective-permute-start.5 = (bf16[144,256]{1,0:T(8,128)(2,1)S(1)}, bf16[144,256]{1,0:T(8,128)(2,1)S(1)}, u32[]{:S(2)}, u32[]{:S(2)}) collective-permute-start(bf16[144,256]{1,0:T(8,128)(2,1)S(1)} %get-tuple-element.15), channel_id=1, source_target_pairs={{0,2},{1,3},{2,0},{3,1},{4,6},{5,7},{6,4},{7,5},{8,10},{9,11},{10,... | collective-permute-start | bytes 221192 | tf_op jit(solution)/shard_map/ppermute | solution.py:217
  30.0 2.0 %copy-start = (bf16[32,2,4,256]{3,2,1,0:T(4,128)(2,1)S(1)}, bf16[32,2,4,256]{3,2,1,0:T(4,128)(2,1)}, u32[]{:S(2)}) copy-start(bf16[32,2,4,256]{3,2,1,0:T(4,128)(2,1)} %feat_ref.1) | copy-start | bytes 393220
  30.6 1.5 %collective-permute-start.7 = (bf16[272,256]{1,0:T(8,128)(2,1)S(1)}, bf16[272,256]{1,0:T(8,128)(2,1)S(1)}, u32[]{:S(2)}, u32[]{:S(2)}) collective-permute-start(bf16[272,256]{1,0:T(8,128)(2,1)S(1)} %collective-permute-done.4.rest_1_), channel_id=1, source_target_pairs={{0,1},{1,0},{2,3},{3,2},{4,5},{5,4},{6,7},{7,6},{8,9},{9,8},{10,11... | collective-permute-start | bytes 417800 | tf_op jit(solution)/shard_map/ppermute | solution.py:217
  30.6 1.5 %collective-permute-start.8 = (bf16[144,256]{1,0:T(8,128)(2,1)S(1)}, bf16[144,256]{1,0:T(8,128)(2,1)S(1)}, u32[]{:S(2)}, u32[]{:S(2)}) collective-permute-start(bf16[144,256]{1,0:T(8,128)(2,1)S(1)} %collective-permute-done.5.rest_2_), channel_id=1, source_target_pairs={{0,1},{1,0},{2,3},{3,2},{4,5},{5,4},{6,7},{7,6},{8,9},{9,8},{10,11... | collective-permute-start | bytes 221192 | tf_op jit(solution)/shard_map/ppermute | solution.py:217

commit v14 on v13

--- a/solution.py
+++ b/solution.py
@@ -40,11 +40,7 @@
     last_ref[...] = blocks[count][...]
 
 
-def radial_kernel(x_ref, taps_ref, *rest):
-    vectors = rest[:5]
-    out_ref, consts_ref, even, odd, done, sems = rest[5:]
-    for i, vector in enumerate(vectors):
-        consts_ref[i : i + 1, :] = vector[...]
+def radial_kernel(x_ref, taps_ref, out_ref, even, odd, done, sems):
     n, a_loc, _, theta, c = x_ref.shape
     taps = taps_ref.shape[0]
     pad = (taps + 1) // 4
@@ -87,7 +83,7 @@
         copy.wait()
 
 
-def axial_kernel(z_ref, taps_ref, consts_ref, out_ref, padded, summed):
+def axial_kernel(z_ref, taps_ref, conv_b_ref, gain_ref, lnb_ref, out_ref, padded, summed):
     axial, rows, c = z_ref.shape
     taps = taps_ref.shape[0]
     half = taps // 2
@@ -110,12 +106,12 @@
         pl.loop(0, axial // block)(lambda i: conv(i * block, range(taps)))
 
     def norm(i, carry):
-        v = (summed[pl.ds(i * PLANES, PLANES)] + consts_ref[0:1, :]).reshape(PLANES * rows, c)
+        v = (summed[pl.ds(i * PLANES, PLANES)] + conv_b_ref[...]).reshape(PLANES * rows, c)
         v = v.astype(jnp.bfloat16).astype(jnp.float32)
         mean = jnp.mean(v, axis=-1, keepdims=True)
         centred = v - mean
         var = jnp.mean(centred * centred, axis=-1, keepdims=True)
-        normed = centred * lax.rsqrt(var + 1e-06) * consts_ref[1:2, :] + consts_ref[2:3, :]
+        normed = centred * lax.rsqrt(var + 1e-06) * gain_ref[...] + lnb_ref[...]
         at = pl.multiple_of(i * PLANES * rows, PLANES * rows)
         out_ref[pl.ds(at, PLANES * rows), :] = normed.astype(out_ref.dtype)
         return carry
@@ -162,7 +158,7 @@
     over_tokens(normed_ref.shape[0], size, part)
 
 
-def mlp_kernel(partials, normed_ref, consts_ref, feat_ref, *rest):
+def mlp_kernel(partials, normed_ref, b_out_ref, scale_ref, feat_ref, *rest):
     *blocks, out_ref, branch, done, sems = rest
     axial, _, theta, c = feat_ref.shape
     rows = 2 * theta
@@ -173,7 +169,7 @@
         total = hidden_sum(normed_ref[tokens, :], blocks[partials:])
         for partial_ref in blocks[:partials]:
             total = total + partial_ref[tokens, :]
-        result = (consts_ref[4:5, :] * (total + consts_ref[3:4, :])).astype(jnp.bfloat16).astype(jnp.float32)
+        result = (scale_ref[...] * (total + b_out_ref[...])).astype(jnp.bfloat16).astype(jnp.float32)
         branch[pl.ds(at, size)] = result.reshape(size, rows, c)
         for r in range(2):
             got = branch[pl.ds(at, size), r * theta : (r + 1) * theta, :]
@@ -216,7 +212,6 @@
         stride = math.prod(digits(n)[digit + 1 :])
         return lax.ppermute(piece, "row", [(i, i ^ (by * stride)) for i in range(n)])
 
-    vectors = [v[None, :] for v in (conv_bias, ln_gain, ln_bias, b_out, layer_scale)]
     if spread:
         own = pl.pallas_call(
             pack_kernel,
@@ -237,19 +232,16 @@
 
     got = lax.all_to_all(features, "row", split_axis=0, concat_axis=0, tiled=True)
     pad = (radial_taps.shape[0] + 1) // 4
-    mixed, consts = pl.pallas_call(
+    mixed = pl.pallas_call(
         radial_kernel,
-        out_shape=[
-            jax.ShapeDtypeStruct((n, a_loc, rows, c), jnp.bfloat16),
-            jax.ShapeDtypeStruct((8, c), jnp.float32),
-        ],
-        in_specs=[vmem()] * 7,
-        out_specs=[anywhere, vmem()],
+        out_shape=jax.ShapeDtypeStruct((n, a_loc, rows, c), jnp.bfloat16),
+        in_specs=[vmem()] * 2,
+        out_specs=anywhere,
         scratch_shapes=[pltpu.VMEM((n + 2 * pad, a_loc, rows, c), jnp.float32)] * 2
         + [pltpu.VMEM((n, a_loc, rows, c), jnp.bfloat16), pltpu.SemaphoreType.DMA((8,))],
         compiler_params=middle,
         name="radial",
-    )(got.reshape(n, a_loc, r_loc, theta, c), radial_taps, *vectors)
+    )(got.reshape(n, a_loc, r_loc, theta, c), radial_taps)
     if spread:
         joined, most, last = pl.pallas_call(
             join_kernel,
@@ -266,7 +258,7 @@
     normed = pl.pallas_call(
         axial_kernel,
         out_shape=jax.ShapeDtypeStruct((axial * rows, c), jnp.bfloat16),
-        in_specs=[vmem()] * 3,
+        in_specs=[vmem()] * 5,
         out_specs=vmem(),
         scratch_shapes=[
             pltpu.VMEM((axial + axial_taps.shape[0] - 1, rows, c), jnp.float32),
@@ -274,19 +266,19 @@
         ],
         compiler_params=middle,
         name="axial",
-    )(back, axial_taps, consts)
+    )(back, axial_taps, conv_bias[None, :], ln_gain[None, :], ln_bias[None, :])
     if spread:
         across, normed = lax.optimization_barrier((across, normed))
-        blocks = across + [move(h, 2, 1) for h in across]
+        blocks = [move(h, 2, 1) for h in across]
         partials = [
             pl.pallas_call(
                 first_kernel,
                 out_shape=jax.ShapeDtypeStruct((axial * rows, c), jnp.float32),
-                in_specs=[vmem()] * 3,
+                in_specs=[vmem()] * 5,
                 out_specs=vmem(),
                 compiler_params=middle,
                 name="first",
-            )(normed, joined, twin)
+            )(normed, joined, twin, *across)
         ]
     else:
         partials = []
@@ -294,7 +286,7 @@
     return pl.pallas_call(
         partial(mlp_kernel, len(partials)),
         out_shape=jax.ShapeDtypeStruct(features.shape, jnp.bfloat16),
-        in_specs=[vmem()] * (3 + len(operands)),
+        in_specs=[vmem()] * (4 + len(operands)),
         out_specs=anywhere,
         scratch_shapes=[
             pltpu.VMEM((axial, rows, c), jnp.float32),
@@ -303,7 +295,7 @@
         ],
         compiler_params=large,
         name="mlp",
-    )(normed, consts, features, *operands)
+    )(normed, b_out[None, :], layer_scale[None, :], features, *operands)
 
 
 def solution(mesh):

time: 33.6 us -> 33.7 us (level)
  waiting for transfers between devices: 8.19 us -> 7.53 us
  local copies, waits for them, and re-layouts: 0.75 us -> 1.38 us
    ppermute x9, waiting for transfers between devices: 0.79 us -> 0.15 us  [move(): return lax.ppermute(piece, 'row', [(i, i ^ by * stride) for i in range(n)])]
    unnamed x22, local copies, waits for them, and re-layouts: 0.75 us -> 1.38 us
  transfers between devices with their start and end apart: 11 -> 11, of which waited for: 4 -> 3; matrix products, arithmetic and copies ran while one was open for 0% -> 0% of each run, Pallas kernels for 8% -> 8%
where the time goes in v14:
time: 33.7 us; the launch traced here: 33.4 us
  starting transfers between devices  20.3 us (60%)
  waiting for transfers between devices  7.53 us (22%)
  Pallas kernels  3.96 us (12%)
  local copies, waits for them, and re-layouts  1.38 us (4%)
    ppermute x9, starting transfers between devices, move(): return lax.ppermute(piece, 'row', [(i, i ^ by * stride) for i in range(n)])  9.26 us
    all_to_all x1, starting transfers between devices, local(): lax.all_to_all(features, 'row', split_axis=0, concat_axis=0, tiled=True)  7.53 us
    all_to_all x1, waiting for transfers between devices, local(): lax.all_to_all(mixed.reshape(axial, rows, c), 'row', split_axis=0, concat...  5.4 us
    all_to_all x1, starting transfers between devices, local(): lax.all_to_all(mixed.reshape(axial, rows, c), 'row', split_axis=0, concat...  3.52 us
    all_to_all x1, waiting for transfers between devices, local(): lax.all_to_all(features, 'row', split_axis=0, concat_axis=0, tiled=True)  1.98 us
    unnamed x22, local copies, waits for them, and re-layouts  1.38 us
    pallas_call x1, Pallas kernels, local(): pl.pallas_call(partial(mlp_kernel, len(partials)), out_shape=jax.ShapeDty...  1.22 us
    pallas_call x1, Pallas kernels, local(): pl.pallas_call(radial_kernel, out_shape=jax.ShapeDtypeStruct((n, a_loc, r...  1.19 us
  transfers between devices with their start and end apart: 11, of which 3 were waited for; matrix products, arithmetic and copies ran while one was open for 0% of the time, Pallas kernels for 8%

profile of v14, /device:TPU:0, one launch (start us, length us, event | category | flops | bytes accessed | tf_op | source)
XLA Modules:
  0.0 33.4 jit_solution(11978216472189792746)
XLA Ops:
  0.0 7.5 %all-to-all-start = ((bf16[32,2,4,256]{3,2,1,0:T(4,128)(2,1)}), bf16[32,2,4,256]{3,2,1,0:T(4,128)(2,1)S(1)}, u32[]{:S(2)}, u32[]{:S(2)}) async-start(bf16[32,2,4,256]{3,2,1,0:T(4,128)(2,1)} %feat_ref.1), calls=%async_computation | async-start | bytes 262144 | tf_op jit(solution)/shard_map/all_to_all | solution.py:233
  7.6 0.0 copy-start.3
  7.6 0.1 pack.1.refs_4_
  7.7 1.9 %collective-permute-start = (bf16[144,256]{1,0:T(8,128)(2,1)S(1)}, bf16[144,256]{1,0:T(8,128)(2,1)S(1)}, u32[]{:S(2)}, u32[]{:S(2)}) collective-permute-start(bf16[144,256]{1,0:T(8,128)(2,1)S(1)} %pack.1.refs_4_), channel_id=1, source_target_pairs={{0,4},{1,5},{2,6},{3,7},{4,0},{5,1},{6,2},{7,3},{8,12},{9,13},{10,... | collective-permute-start | bytes 221192 | tf_op jit(solution)/shard_map/ppermute | solution.py:213
  9.6 2.4 %collective-permute-start.1 = (bf16[144,256]{1,0:T(8,128)(2,1)S(1)}, bf16[144,256]{1,0:T(8,128)(2,1)S(1)}, u32[]{:S(2)}, u32[]{:S(2)}) collective-permute-start(bf16[144,256]{1,0:T(8,128)(2,1)S(1)} %pack.1.refs_4_), channel_id=1, source_target_pairs={{0,8},{1,9},{2,10},{3,11},{4,12},{5,13},{6,14},{7,15},{8,0},{9,1},... | collective-permute-start | bytes 221192 | tf_op jit(solution)/shard_map/ppermute | solution.py:213
  12.0 0.1 collective-permute-start.2
  12.1 1.9 %collective-permute-start.3 = (bf16[144,256]{1,0:T(8,128)(2,1)S(1)}, bf16[144,256]{1,0:T(8,128)(2,1)S(1)}, u32[]{:S(2)}, u32[]{:S(2)}) collective-permute-start(bf16[144,256]{1,0:T(8,128)(2,1)S(1)} %pack.1.refs_4_), channel_id=1, source_target_pairs={{0,2},{1,3},{2,0},{3,1},{4,6},{5,7},{6,4},{7,5},{8,10},{9,11},{10,... | collective-permute-start | bytes 221192 | tf_op jit(solution)/shard_map/ppermute | solution.py:213
  14.0 2.0 %all-to-all-done = bf16[32,2,4,256]{3,2,1,0:T(4,128)(2,1)S(1)} async-done(((bf16[32,2,4,256]{3,2,1,0:T(4,128)(2,1)}), bf16[32,2,4,256]{3,2,1,0:T(4,128)(2,1)S(1)}, u32[]{:S(2)}, u32[]{:S(2)}) %all-to-all-start) | async-done | bytes 131104 | tf_op jit(solution)/shard_map/all_to_all | solution.py:233
  16.0 1.2 %radial.1.refs_0_ = bf16[16,2,8,256]{3,2,1,0:T(8,128)(2,1)} custom-call(bf16[16,2,2,4,256]{4,3,2,1,0:T(4,128)(2,1)S(1)} %bitcast.7, f32[31,256]{1,0:T(8,128)S(1)} %copy-done.3), custom_call_target="tpu_custom_call" | custom-call | tf_op jit(solution)/shard_map/radial/pallas_call | solution.py:235
  17.2 3.5 %all-to-all-start.1 = ((bf16[32,8,256]{2,1,0:T(8,128)(2,1)}), bf16[32,8,256]{2,1,0:T(8,128)(2,1)S(1)}, u32[]{:S(2)}, u32[]{:S(2)}) async-start(bf16[32,8,256]{2,1,0:T(8,128)(2,1)} %bitcast.1), calls=%async_computation.1 | async-start | bytes 262144 | tf_op jit(solution)/shard_map/all_to_all | solution.py:257
  20.7 0.0 collective-permute-done.1.refs_2_
  20.7 0.0 collective-permute-done.2.refs_3_
  20.7 0.0 copy-start.4
  20.7 0.0 copy-start.6
  20.8 0.0 copy-start.7
  20.8 0.4 %collective-permute-start.6 = (bf16[656,256]{1,0:T(8,128)(2,1)S(1)}, bf16[656,256]{1,0:T(8,128)(2,1)S(1)}, u32[]{:S(2)}, u32[]{:S(2)}) collective-permute-start(bf16[656,256]{1,0:T(8,128)(2,1)S(1)} %get-tuple-element.14.rest_0_), channel_id=1, source_target_pairs={{0,1},{1,0},{2,3},{3,2},{4,5},{5,4},{6,7},{7,6},{8,9},{9,8},{10,11... | collective-permute-start | bytes 1007624 | tf_op jit(solution)/shard_map/ppermute | solution.py:213
  21.2 1.7 %collective-permute-start.4 = (bf16[272,256]{1,0:T(8,128)(2,1)S(1)}, bf16[272,256]{1,0:T(8,128)(2,1)S(1)}, u32[]{:S(2)}, u32[]{:S(2)}) collective-permute-start(bf16[272,256]{1,0:T(8,128)(2,1)S(1)} %get-tuple-element.11), channel_id=1, source_target_pairs={{0,2},{1,3},{2,0},{3,1},{4,6},{5,7},{6,4},{7,5},{8,10},{9,11},{10,... | collective-permute-start | bytes 417800 | tf_op jit(solution)/shard_map/ppermute | solution.py:213
  22.9 0.3 %collective-permute-start.5 = (bf16[144,256]{1,0:T(8,128)(2,1)S(1)}, bf16[144,256]{1,0:T(8,128)(2,1)S(1)}, u32[]{:S(2)}, u32[]{:S(2)}) collective-permute-start(bf16[144,256]{1,0:T(8,128)(2,1)S(1)} %get-tuple-element.12), channel_id=1, source_target_pairs={{0,2},{1,3},{2,0},{3,1},{4,6},{5,7},{6,4},{7,5},{8,10},{9,11},{10,... | collective-permute-start | bytes 221192 | tf_op jit(solution)/shard_map/ppermute | solution.py:213
  23.2 5.4 %all-to-all-done.1.z_ref = bf16[32,8,256]{2,1,0:T(8,128)(2,1)S(1)} async-done(((bf16[32,8,256]{2,1,0:T(8,128)(2,1)}), bf16[32,8,256]{2,1,0:T(8,128)(2,1)S(1)}, u32[]{:S(2)}, u32[]{:S(2)}) %all-to-all-start.1) | async-done | bytes 131104 | tf_op jit(solution)/shard_map/all_to_all | solution.py:257
  28.6 0.7 %copy-done.5 = f32[256]{0:T(256)S(1)} copy-done((f32[256]{0:T(256)S(1)}, f32[256]{0:T(256)}, u32[]{:S(2)}) %copy-start.5) | copy-done | bytes 1048
  29.3 0.6 %axial.1.normed_ref = bf16[256,256]{1,0:T(8,128)(2,1)S(1)} custom-call(bf16[32,8,256]{2,1,0:T(8,128)(2,1)S(1)} %all-to-all-done.1.z_ref, f32[31,256]{1,0:T(8,128)S(1)} %copy-done.4, f32[1,256]{1,0:T(1,128)S(1)} %bitcast.8, f32[1,256]{1,0:T(1,128)S(1)} %bitcast.9, f32[1,256]{1,0:T(1,128)S(1)} %bitcast.10), custom_call_target="tpu_custom_call" | custom-call | tf_op jit(solution)/shard_map/axial/pallas_call | solution.py:258
  29.9 0.0 copy-start
  29.9 0.0 collective-permute-done.5.rest_3_
  29.9 0.0 collective-permute-done.4.rest_2_
  29.9 0.1 collective-permute-start.7
  30.0 0.5 %collective-permute-start.8 = (bf16[144,256]{1,0:T(8,128)(2,1)S(1)}, bf16[144,256]{1,0:T(8,128)(2,1)S(1)}, u32[]{:S(2)}, u32[]{:S(2)}) collective-permute-start(bf16[144,256]{1,0:T(8,128)(2,1)S(1)} %collective-permute-done.5.rest_3_), channel_id=1, source_target_pairs={{0,1},{1,0},{2,3},{3,2},{4,5},{5,4},{6,7},{7,6},{8,9},{9,8},{10,11... | collective-permute-start | bytes 221192 | tf_op jit(solution)/shard_map/ppermute | solution.py:213
  30.5 0.0 collective-permute-done.6.rest_1_
  30.5 0.8 %first.1.rest_0_ = f32[256,256]{1,0:T(8,128)S(1)} custom-call(bf16[256,256]{1,0:T(8,128)(2,1)S(1)} %axial.1.normed_ref, bf16[656,256]{1,0:T(8,128)(2,1)S(1)} %get-tuple-element.14.rest_0_, bf16[656,256]{1,0:T(8,128)(2,1)S(1)} %collective-permute-done.6.rest_1_, bf16[272,256]{1,0:T(8,128)(2,1)S(1)} %collective-permute-done.4.rest_2_, ...), custom_call_target="tpu_custom_call" | custom-call | tf_op jit(solution)/shard_map/first/pallas_call | solution.py:274
  31.3 0.1 collective-permute-done.8.rest_2_
  31.5 0.0 collective-permute-done.7.rest_1_
  31.5 0.7 %copy-done.8 = f32[256]{0:T(256)S(1)} copy-done((f32[256]{0:T(256)S(1)}, f32[256]{0:T(256)}, u32[]{:S(2)}) %copy-start.8) | copy-done | bytes 1048
  32.2 1.2 %mlp.1 = bf16[32,2,4,256]{3,2,1,0:T(4,128)(2,1)} custom-call(bf16[256,256]{1,0:T(8,128)(2,1)S(1)} %axial.1.normed_ref, f32[1,256]{1,0:T(1,128)S(1)} %bitcast.11, f32[1,256]{1,0:T(1,128)S(1)} %bitcast.12, bf16[32,2,4,256]{3,2,1,0:T(4,128)(2,1)S(1)} %copy-done, f32[256,256]{1,0:T(8,128)S(1)} %first.1.rest_0_, ...), custom_call_target="tpu_custom_call" | custom-call | tf_op jit(solution)/shard_map/mlp/pallas_call | solution.py:286
  (18 shorter events, 0.1 us)
Async XLA Ops:
  0.0 7.5 %copy-start.1 = (bf16[64,256]{1,0:T(8,128)(2,1)S(1)}, bf16[64,256]{1,0:T(8,128)(2,1)}, u32[]{:S(2)}) copy-start(bf16[64,256]{1,0:T(8,128)(2,1)} %w_in_ref.1) | copy-start | bytes 98308
  0.0 7.6 %copy-start.10 = (bf16[64]{0:T(256)(128)(2,1)S(1)}, bf16[64]{0:T(256)(128)(2,1)}, u32[]{:S(2)}) copy-start(bf16[64]{0:T(256)(128)(2,1)} %b_ref.1) | copy-start | bytes 388
  0.0 7.6 %copy-start.2 = (bf16[64,256]{1,0:T(8,128)(2,1)S(1)}, bf16[64,256]{1,0:T(8,128)(2,1)}, u32[]{:S(2)}) copy-start(bf16[64,256]{1,0:T(8,128)(2,1)} %w_out_ref.1) | copy-start | bytes 98308
  0.0 16.0 %all-to-all-start = ((bf16[32,2,4,256]{3,2,1,0:T(4,128)(2,1)}), bf16[32,2,4,256]{3,2,1,0:T(4,128)(2,1)S(1)}, u32[]{:S(2)}, u32[]{:S(2)}) async-start(bf16[32,2,4,256]{3,2,1,0:T(4,128)(2,1)} %feat_ref.1), calls=%async_computation | async-start | bytes 262144 | tf_op jit(solution)/shard_map/all_to_all | solution.py:233
  7.6 8.4 %copy-start.3 = (f32[31,256]{1,0:T(8,128)S(1)}, f32[31,256]{1,0:T(8,128)}, u32[]{:S(2)}) copy-start(f32[31,256]{1,0:T(8,128)} %taps_ref.2) | copy-start | bytes 95236
  7.7 13.0 %collective-permute-start = (bf16[144,256]{1,0:T(8,128)(2,1)S(1)}, bf16[144,256]{1,0:T(8,128)(2,1)S(1)}, u32[]{:S(2)}, u32[]{:S(2)}) collective-permute-start(bf16[144,256]{1,0:T(8,128)(2,1)S(1)} %pack.1.refs_4_), channel_id=1, source_target_pairs={{0,4},{1,5},{2,6},{3,7},{4,0},{5,1},{6,2},{7,3},{8,12},{9,13},{10,... | collective-permute-start | bytes 221192 | tf_op jit(solution)/shard_map/ppermute | solution.py:213
  9.6 11.1 %collective-permute-start.1 = (bf16[144,256]{1,0:T(8,128)(2,1)S(1)}, bf16[144,256]{1,0:T(8,128)(2,1)S(1)}, u32[]{:S(2)}, u32[]{:S(2)}) collective-permute-start(bf16[144,256]{1,0:T(8,128)(2,1)S(1)} %pack.1.refs_4_), channel_id=1, source_target_pairs={{0,8},{1,9},{2,10},{3,11},{4,12},{5,13},{6,14},{7,15},{8,0},{9,1},... | collective-permute-start | bytes 221192 | tf_op jit(solution)/shard_map/ppermute | solution.py:213
  12.0 8.8 %collective-permute-start.2 = (bf16[144,256]{1,0:T(8,128)(2,1)S(1)}, bf16[144,256]{1,0:T(8,128)(2,1)S(1)}, u32[]{:S(2)}, u32[]{:S(2)}) collective-permute-start(bf16[144,256]{1,0:T(8,128)(2,1)S(1)} %pack.1.refs_4_), channel_id=1, source_target_pairs={{0,12},{1,13},{2,14},{3,15},{4,8},{5,9},{6,10},{7,11},{8,4},{9,5},... | collective-permute-start | bytes 221192 | tf_op jit(solution)/shard_map/ppermute | solution.py:213
  12.1 8.7 %collective-permute-start.3 = (bf16[144,256]{1,0:T(8,128)(2,1)S(1)}, bf16[144,256]{1,0:T(8,128)(2,1)S(1)}, u32[]{:S(2)}, u32[]{:S(2)}) collective-permute-start(bf16[144,256]{1,0:T(8,128)(2,1)S(1)} %pack.1.refs_4_), channel_id=1, source_target_pairs={{0,2},{1,3},{2,0},{3,1},{4,6},{5,7},{6,4},{7,5},{8,10},{9,11},{10,... | collective-permute-start | bytes 221192 | tf_op jit(solution)/shard_map/ppermute | solution.py:213
  17.2 11.4 %all-to-all-start.1 = ((bf16[32,8,256]{2,1,0:T(8,128)(2,1)}), bf16[32,8,256]{2,1,0:T(8,128)(2,1)S(1)}, u32[]{:S(2)}, u32[]{:S(2)}) async-start(bf16[32,8,256]{2,1,0:T(8,128)(2,1)} %bitcast.1), calls=%async_computation.1 | async-start | bytes 262144 | tf_op jit(solution)/shard_map/all_to_all | solution.py:257
  20.7 7.9 %copy-start.4 = (f32[31,256]{1,0:T(8,128)S(1)}, f32[31,256]{1,0:T(8,128)}, u32[]{:S(2)}) copy-start(f32[31,256]{1,0:T(8,128)} %taps_ref.3) | copy-start | bytes 95236
  20.7 7.9 %copy-start.6 = (f32[256]{0:T(256)S(1)}, f32[256]{0:T(256)}, u32[]{:S(2)}) copy-start(f32[256]{0:T(256)} %param.15) | copy-start | bytes 3076
  20.8 7.9 %copy-start.7 = (f32[256]{0:T(256)S(1)}, f32[256]{0:T(256)}, u32[]{:S(2)}) copy-start(f32[256]{0:T(256)} %param.16) | copy-start | bytes 3076
  20.8 9.7 %collective-permute-start.6 = (bf16[656,256]{1,0:T(8,128)(2,1)S(1)}, bf16[656,256]{1,0:T(8,128)(2,1)S(1)}, u32[]{:S(2)}, u32[]{:S(2)}) collective-permute-start(bf16[656,256]{1,0:T(8,128)(2,1)S(1)} %get-tuple-element.14.rest_0_), channel_id=1, source_target_pairs={{0,1},{1,0},{2,3},{3,2},{4,5},{5,4},{6,7},{7,6},{8,9},{9,8},{10,11... | collective-permute-start | bytes 1007624 | tf_op jit(solution)/shard_map/ppermute | solution.py:213
  21.2 8.8 %collective-permute-start.4 = (bf16[272,256]{1,0:T(8,128)(2,1)S(1)}, bf16[272,256]{1,0:T(8,128)(2,1)S(1)}, u32[]{:S(2)}, u32[]{:S(2)}) collective-permute-start(bf16[272,256]{1,0:T(8,128)(2,1)S(1)} %get-tuple-element.11), channel_id=1, source_target_pairs={{0,2},{1,3},{2,0},{3,1},{4,6},{5,7},{6,4},{7,5},{8,10},{9,11},{10,... | collective-permute-start | bytes 417800 | tf_op jit(solution)/shard_map/ppermute | solution.py:213
  22.9 7.1 %collective-permute-start.5 = (bf16[144,256]{1,0:T(8,128)(2,1)S(1)}, bf16[144,256]{1,0:T(8,128)(2,1)S(1)}, u32[]{:S(2)}, u32[]{:S(2)}) collective-permute-start(bf16[144,256]{1,0:T(8,128)(2,1)S(1)} %get-tuple-element.12), channel_id=1, source_target_pairs={{0,2},{1,3},{2,0},{3,1},{4,6},{5,7},{6,4},{7,5},{8,10},{9,11},{10,... | collective-permute-start | bytes 221192 | tf_op jit(solution)/shard_map/ppermute | solution.py:213
  28.6 0.7 %copy-start.5 = (f32[256]{0:T(256)S(1)}, f32[256]{0:T(256)}, u32[]{:S(2)}) copy-start(f32[256]{0:T(256)} %param.14) | copy-start | bytes 3076
  29.9 1.6 %copy-start = (bf16[32,2,4,256]{3,2,1,0:T(4,128)(2,1)S(1)}, bf16[32,2,4,256]{3,2,1,0:T(4,128)(2,1)}, u32[]{:S(2)}) copy-start(bf16[32,2,4,256]{3,2,1,0:T(4,128)(2,1)} %feat_ref.1) | copy-start | bytes 393220
  29.9 1.5 %collective-permute-start.7 = (bf16[272,256]{1,0:T(8,128)(2,1)S(1)}, bf16[272,256]{1,0:T(8,128)(2,1)S(1)}, u32[]{:S(2)}, u32[]{:S(2)}) collective-permute-start(bf16[272,256]{1,0:T(8,128)(2,1)S(1)} %collective-permute-done.4.rest_2_), channel_id=1, source_target_pairs={{0,1},{1,0},{2,3},{3,2},{4,5},{5,4},{6,7},{7,6},{8,9},{9,8},{10,11... | collective-permute-start | bytes 417800 | tf_op jit(solution)/shard_map/ppermute | solution.py:213
  30.0 1.5 %collective-permute-start.8 = (bf16[144,256]{1,0:T(8,128)(2,1)S(1)}, bf16[144,256]{1,0:T(8,128)(2,1)S(1)}, u32[]{:S(2)}, u32[]{:S(2)}) collective-permute-start(bf16[144,256]{1,0:T(8,128)(2,1)S(1)} %collective-permute-done.5.rest_3_), channel_id=1, source_target_pairs={{0,1},{1,0},{2,3},{3,2},{4,5},{5,4},{6,7},{7,6},{8,9},{9,8},{10,11... | collective-permute-start | bytes 221192 | tf_op jit(solution)/shard_map/ppermute | solution.py:213
  30.5 1.0 %copy-start.9 = (f32[256]{0:T(256)S(1)}, f32[256]{0:T(256)}, u32[]{:S(2)}) copy-start(f32[256]{0:T(256)} %param.21) | copy-start | bytes 3076
  31.5 0.7 %copy-start.8 = (f32[256]{0:T(256)S(1)}, f32[256]{0:T(256)}, u32[]{:S(2)}) copy-start(f32[256]{0:T(256)} %param.20) | copy-start | bytes 3076

commit v15 on v14

--- a/solution.py
+++ b/solution.py
@@ -17,13 +17,16 @@
     return pl.BlockSpec(memory_space=pltpu.VMEM)
 
 
-def pack_kernel(b_ref, w_in_ref, w_out_ref, block_ref):
+def pack_kernel(b_ref, w_in_ref, w_out_ref, *rest):
+    *vectors, block_ref, consts_ref = rest
     block_ref[0:SLOT, :] = w_in_ref[...]
     block_ref[SLOT : 2 * SLOT, :] = w_out_ref[...]
     bias = b_ref[...].astype(jnp.float32)[None, :]
     c = block_ref.shape[1]
     wide = jnp.concatenate([bias] * (c // SLOT), axis=1)
     block_ref[2 * SLOT :, :] = jnp.broadcast_to(wide, (EXTRA, c)).astype(block_ref.dtype)
+    for i, vector in enumerate(vectors):
+        consts_ref[i : i + 1, :] = vector[...]
 
 
 def join_kernel(*refs):
@@ -83,7 +86,7 @@
         copy.wait()
 
 
-def axial_kernel(z_ref, taps_ref, conv_b_ref, gain_ref, lnb_ref, out_ref, padded, summed):
+def axial_kernel(z_ref, taps_ref, consts_ref, out_ref, padded, summed):
     axial, rows, c = z_ref.shape
     taps = taps_ref.shape[0]
     half = taps // 2
@@ -106,12 +109,12 @@
         pl.loop(0, axial // block)(lambda i: conv(i * block, range(taps)))
 
     def norm(i, carry):
-        v = (summed[pl.ds(i * PLANES, PLANES)] + conv_b_ref[...]).reshape(PLANES * rows, c)
+        v = (summed[pl.ds(i * PLANES, PLANES)] + consts_ref[0 : 1, :]).reshape(PLANES * rows, c)
         v = v.astype(jnp.bfloat16).astype(jnp.float32)
         mean = jnp.mean(v, axis=-1, keepdims=True)
         centred = v - mean
         var = jnp.mean(centred * centred, axis=-1, keepdims=True)
-        normed = centred * lax.rsqrt(var + 1e-06) * gain_ref[...] + lnb_ref[...]
+        normed = centred * lax.rsqrt(var + 1e-06) * consts_ref[1 : 2, :] + consts_ref[2 : 3, :]
         at = pl.multiple_of(i * PLANES * rows, PLANES * rows)
         out_ref[pl.ds(at, PLANES * rows), :] = normed.astype(out_ref.dtype)
         return carry
@@ -158,7 +161,7 @@
     over_tokens(normed_ref.shape[0], size, part)
 
 
-def mlp_kernel(partials, normed_ref, b_out_ref, scale_ref, feat_ref, *rest):
+def mlp_kernel(partials, normed_ref, consts_ref, feat_ref, *rest):
     *blocks, out_ref, branch, done, sems = rest
     axial, _, theta, c = feat_ref.shape
     rows = 2 * theta
@@ -169,7 +172,7 @@
         total = hidden_sum(normed_ref[tokens, :], blocks[partials:])
         for partial_ref in blocks[:partials]:
             total = total + partial_ref[tokens, :]
-        result = (scale_ref[...] * (total + b_out_ref[...])).astype(jnp.bfloat16).astype(jnp.float32)
+        result = (consts_ref[4 : 5, :] * (total + consts_ref[3 : 4, :])).astype(jnp.bfloat16).astype(jnp.float32)
         branch[pl.ds(at, size)] = result.reshape(size, rows, c)
         for r in range(2):
             got = branch[pl.ds(at, size), r * theta : (r + 1) * theta, :]
@@ -212,18 +215,23 @@
         stride = math.prod(digits(n)[digit + 1 :])
         return lax.ppermute(piece, "row", [(i, i ^ (by * stride)) for i in range(n)])
 
+    vectors = [v[None, :] for v in (conv_bias, ln_gain, ln_bias, b_out, layer_scale)]
     if spread:
-        own = pl.pallas_call(
+        own, consts = pl.pallas_call(
             pack_kernel,
-            out_shape=jax.ShapeDtypeStruct((2 * SLOT + EXTRA, c), jnp.bfloat16),
-            in_specs=[vmem()] * 3,
-            out_specs=vmem(),
+            out_shape=[
+                jax.ShapeDtypeStruct((2 * SLOT + EXTRA, c), jnp.bfloat16),
+                jax.ShapeDtypeStruct((8, c), jnp.float32),
+            ],
+            in_specs=[vmem()] * 8,
+            out_specs=[vmem()] * 2,
             compiler_params=small,
             name="pack",
-        )(b_in, w_in, w_out)
+        )(b_in, w_in, w_out, *vectors)
         line = [move(own, 0, by) for by in range(1, outer)]
         side = move(own, 1, 1)
     else:
+        consts = jnp.concatenate(vectors + [jnp.zeros((3, c), jnp.float32)], axis=0)
         w_all = lax.all_gather(w_in, "row", axis=0, tiled=True).reshape(-1, SLOT, c)
         o_all = lax.all_gather(w_out, "row", axis=0, tiled=True).reshape(-1, SLOT, c)
         b_all = jnp.tile(lax.all_gather(b_in, "row", axis=0, tiled=True).reshape(-1, SLOT), (1, c // SLOT))
@@ -258,7 +266,7 @@
     normed = pl.pallas_call(
         axial_kernel,
         out_shape=jax.ShapeDtypeStruct((axial * rows, c), jnp.bfloat16),
-        in_specs=[vmem()] * 5,
+        in_specs=[vmem()] * 3,
         out_specs=vmem(),
         scratch_shapes=[
             pltpu.VMEM((axial + axial_taps.shape[0] - 1, rows, c), jnp.float32),
@@ -266,7 +274,7 @@
         ],
         compiler_params=middle,
         name="axial",
-    )(back, axial_taps, conv_bias[None, :], ln_gain[None, :], ln_bias[None, :])
+    )(back, axial_taps, consts)
     if spread:
         across, normed = lax.optimization_barrier((across, normed))
         blocks = [move(h, 2, 1) for h in across]
@@ -286,7 +294,7 @@
     return pl.pallas_call(
         partial(mlp_kernel, len(partials)),
         out_shape=jax.ShapeDtypeStruct(features.shape, jnp.bfloat16),
-        in_specs=[vmem()] * (4 + len(operands)),
+        in_specs=[vmem()] * (3 + len(operands)),
         out_specs=anywhere,
         scratch_shapes=[
             pltpu.VMEM((axial, rows, c), jnp.float32),
@@ -295,7 +303,7 @@
         ],
         compiler_params=large,
         name="mlp",
-    )(normed, b_out[None, :], layer_scale[None, :], features, *operands)
+    )(normed, consts, features, *operands)
 
 
 def solution(mesh):

time: 33.7 us -> 32.9 us (0.976)
  local copies, waits for them, and re-layouts: 1.38 us -> 0.7 us
    unnamed x22, local copies, waits for them, and re-layouts: 1.38 us -> 0.7 us
    all_to_all x1, waiting for transfers between devices: 1.98 us -> 1.32 us  [local(): lax.all_to_all(features, 'row', split_axis=0, concat_axis=0, tiled=True)]
    ppermute x9, waiting for transfers between devices: 0.15 us -> 0.71 us  [move(): return lax.ppermute(piece, 'row', [(i, i ^ by * stride) for i in range(n)])]
  transfers between devices with their start and end apart: 11 -> 11, of which waited for: 3 -> 4; matrix products, arithmetic and copies ran while one was open for 0% -> 0% of each run, Pallas kernels for 8% -> 8%
where the time goes in v15:
time: 32.9 us; the launch traced here: 32.5 us
  starting transfers between devices  20.2 us (61%)
  waiting for transfers between devices  7.46 us (23%)
  Pallas kernels  3.97 us (12%)
  local copies, waits for them, and re-layouts  0.7 us (2%)
    ppermute x9, starting transfers between devices, move(): return lax.ppermute(piece, 'row', [(i, i ^ by * stride) for i in range(n)])  9.2 us
    all_to_all x1, starting transfers between devices, local(): lax.all_to_all(features, 'row', split_axis=0, concat_axis=0, tiled=True)  7.52 us
    all_to_all x1, waiting for transfers between devices, local(): lax.all_to_all(mixed.reshape(axial, rows, c), 'row', split_axis=0, concat...  5.43 us
    all_to_all x1, starting transfers between devices, local(): lax.all_to_all(mixed.reshape(axial, rows, c), 'row', split_axis=0, concat...  3.52 us
    all_to_all x1, waiting for transfers between devices, local(): lax.all_to_all(features, 'row', split_axis=0, concat_axis=0, tiled=True)  1.32 us
    pallas_call x1, Pallas kernels, local(): pl.pallas_call(partial(mlp_kernel, len(partials)), out_shape=jax.ShapeDty...  1.22 us
    pallas_call x1, Pallas kernels, local(): pl.pallas_call(radial_kernel, out_shape=jax.ShapeDtypeStruct((n, a_loc, r...  1.19 us
    pallas_call x1, Pallas kernels, local(): pl.pallas_call(first_kernel, out_shape=jax.ShapeDtypeStruct((axial * rows...  0.81 us
  transfers between devices with their start and end apart: 11, of which 4 were waited for; matrix products, arithmetic and copies ran while one was open for 0% of the time, Pallas kernels for 8%

profile of v15, /device:TPU:0, one launch (start us, length us, event | category | flops | bytes accessed | tf_op | source)
XLA Modules:
  0.0 32.5 jit_solution(9284422147646770042)
XLA Ops:
  0.0 7.5 %all-to-all-start = ((bf16[32,2,4,256]{3,2,1,0:T(4,128)(2,1)}), bf16[32,2,4,256]{3,2,1,0:T(4,128)(2,1)S(1)}, u32[]{:S(2)}, u32[]{:S(2)}) async-start(bf16[32,2,4,256]{3,2,1,0:T(4,128)(2,1)} %feat_ref.1), calls=%async_computation | async-start | bytes 262144 | tf_op jit(solution)/shard_map/all_to_all | solution.py:241
  7.5 0.0 copy-start.6
  7.5 0.0 copy-start.7
  7.6 0.0 copy-start.8
  7.6 0.0 copy-start.9
  7.6 0.0 copy-start.5
  7.6 0.0 copy-start.10
  7.6 0.6 %copy-done.6 = f32[256]{0:T(256)S(1)} copy-done((f32[256]{0:T(256)S(1)}, f32[256]{0:T(256)}, u32[]{:S(2)}) %copy-start.6) | copy-done | bytes 1048
  8.2 0.0 copy-done.7
  8.2 0.0 copy-done.8
  8.2 0.0 copy-done.9
  8.3 0.0 copy-done.5
  8.3 0.1 pack.1
  8.4 1.9 %collective-permute-start = (bf16[144,256]{1,0:T(8,128)(2,1)S(1)}, bf16[144,256]{1,0:T(8,128)(2,1)S(1)}, u32[]{:S(2)}, u32[]{:S(2)}) collective-permute-start(bf16[144,256]{1,0:T(8,128)(2,1)S(1)} %get-tuple-element.13.refs_4_), channel_id=1, source_target_pairs={{0,4},{1,5},{2,6},{3,7},{4,0},{5,1},{6,2},{7,3},{8,12},{9,13},{10,... | collective-permute-start | bytes 221192 | tf_op jit(solution)/shard_map/ppermute | solution.py:216
  10.3 2.4 %collective-permute-start.1 = (bf16[144,256]{1,0:T(8,128)(2,1)S(1)}, bf16[144,256]{1,0:T(8,128)(2,1)S(1)}, u32[]{:S(2)}, u32[]{:S(2)}) collective-permute-start(bf16[144,256]{1,0:T(8,128)(2,1)S(1)} %get-tuple-element.13.refs_4_), channel_id=1, source_target_pairs={{0,8},{1,9},{2,10},{3,11},{4,12},{5,13},{6,14},{7,15},{8,0},{9,1},... | collective-permute-start | bytes 221192 | tf_op jit(solution)/shard_map/ppermute | solution.py:216
  12.6 0.1 collective-permute-start.2
  12.7 1.9 %collective-permute-start.3 = (bf16[144,256]{1,0:T(8,128)(2,1)S(1)}, bf16[144,256]{1,0:T(8,128)(2,1)S(1)}, u32[]{:S(2)}, u32[]{:S(2)}) collective-permute-start(bf16[144,256]{1,0:T(8,128)(2,1)S(1)} %get-tuple-element.13.refs_4_), channel_id=1, source_target_pairs={{0,2},{1,3},{2,0},{3,1},{4,6},{5,7},{6,4},{7,5},{8,10},{9,11},{10,... | collective-permute-start | bytes 221192 | tf_op jit(solution)/shard_map/ppermute | solution.py:216
  14.7 1.3 %all-to-all-done = bf16[32,2,4,256]{3,2,1,0:T(4,128)(2,1)S(1)} async-done(((bf16[32,2,4,256]{3,2,1,0:T(4,128)(2,1)}), bf16[32,2,4,256]{3,2,1,0:T(4,128)(2,1)S(1)}, u32[]{:S(2)}, u32[]{:S(2)}) %all-to-all-start) | async-done | bytes 131104 | tf_op jit(solution)/shard_map/all_to_all | solution.py:241
  16.0 1.2 %radial.1.refs_0_ = bf16[16,2,8,256]{3,2,1,0:T(8,128)(2,1)} custom-call(bf16[16,2,2,4,256]{4,3,2,1,0:T(4,128)(2,1)S(1)} %bitcast.7, f32[31,256]{1,0:T(8,128)S(1)} %copy-done.1), custom_call_target="tpu_custom_call" | custom-call | tf_op jit(solution)/shard_map/radial/pallas_call | solution.py:243
  17.2 3.5 %all-to-all-start.1 = ((bf16[32,8,256]{2,1,0:T(8,128)(2,1)}), bf16[32,8,256]{2,1,0:T(8,128)(2,1)S(1)}, u32[]{:S(2)}, u32[]{:S(2)}) async-start(bf16[32,8,256]{2,1,0:T(8,128)(2,1)} %bitcast.6), calls=%async_computation.1 | async-start | bytes 262144 | tf_op jit(solution)/shard_map/all_to_all | solution.py:265
  20.7 0.0 copy-start.2
  20.8 0.4 %collective-permute-start.6 = (bf16[656,256]{1,0:T(8,128)(2,1)S(1)}, bf16[656,256]{1,0:T(8,128)(2,1)S(1)}, u32[]{:S(2)}, u32[]{:S(2)}) collective-permute-start(bf16[656,256]{1,0:T(8,128)(2,1)S(1)} %get-tuple-element.18.rest_0_), channel_id=1, source_target_pairs={{0,1},{1,0},{2,3},{3,2},{4,5},{5,4},{6,7},{7,6},{8,9},{9,8},{10,11... | collective-permute-start | bytes 1007624 | tf_op jit(solution)/shard_map/ppermute | solution.py:216
  21.2 1.7 %collective-permute-start.4 = (bf16[272,256]{1,0:T(8,128)(2,1)S(1)}, bf16[272,256]{1,0:T(8,128)(2,1)S(1)}, u32[]{:S(2)}, u32[]{:S(2)}) collective-permute-start(bf16[272,256]{1,0:T(8,128)(2,1)S(1)} %get-tuple-element.14), channel_id=1, source_target_pairs={{0,2},{1,3},{2,0},{3,1},{4,6},{5,7},{6,4},{7,5},{8,10},{9,11},{10,... | collective-permute-start | bytes 417800 | tf_op jit(solution)/shard_map/ppermute | solution.py:216
  22.9 0.3 %collective-permute-start.5 = (bf16[144,256]{1,0:T(8,128)(2,1)S(1)}, bf16[144,256]{1,0:T(8,128)(2,1)S(1)}, u32[]{:S(2)}, u32[]{:S(2)}) collective-permute-start(bf16[144,256]{1,0:T(8,128)(2,1)S(1)} %get-tuple-element.15), channel_id=1, source_target_pairs={{0,2},{1,3},{2,0},{3,1},{4,6},{5,7},{6,4},{7,5},{8,10},{9,11},{10,... | collective-permute-start | bytes 221192 | tf_op jit(solution)/shard_map/ppermute | solution.py:216
  23.2 5.4 %all-to-all-done.1.z_ref = bf16[32,8,256]{2,1,0:T(8,128)(2,1)S(1)} async-done(((bf16[32,8,256]{2,1,0:T(8,128)(2,1)}), bf16[32,8,256]{2,1,0:T(8,128)(2,1)S(1)}, u32[]{:S(2)}, u32[]{:S(2)}) %all-to-all-start.1) | async-done | bytes 131104 | tf_op jit(solution)/shard_map/all_to_all | solution.py:265
  28.6 0.6 %axial.1.normed_ref = bf16[256,256]{1,0:T(8,128)(2,1)S(1)} custom-call(bf16[32,8,256]{2,1,0:T(8,128)(2,1)S(1)} %all-to-all-done.1.z_ref, f32[31,256]{1,0:T(8,128)S(1)} %copy-done.2, f32[8,256]{1,0:T(8,128)S(1)} %get-tuple-element.16.consts_ref), custom_call_target="tpu_custom_call" | custom-call | tf_op jit(solution)/shard_map/axial/pallas_call | solution.py:266
  29.3 0.0 copy-start
  29.3 0.6 %collective-permute-done.5.rest_3_ = bf16[144,256]{1,0:T(8,128)(2,1)S(1)} collective-permute-done((bf16[144,256]{1,0:T(8,128)(2,1)S(1)}, bf16[144,256]{1,0:T(8,128)(2,1)S(1)}, u32[]{:S(2)}, u32[]{:S(2)}) %collective-permute-start.5) | collective-permute-done | bytes 73760 | tf_op jit(solution)/shard_map/ppermute | solution.py:216
  29.9 0.5 %collective-permute-start.8 = (bf16[144,256]{1,0:T(8,128)(2,1)S(1)}, bf16[144,256]{1,0:T(8,128)(2,1)S(1)}, u32[]{:S(2)}, u32[]{:S(2)}) collective-permute-start(bf16[144,256]{1,0:T(8,128)(2,1)S(1)} %collective-permute-done.5.rest_3_), channel_id=1, source_target_pairs={{0,1},{1,0},{2,3},{3,2},{4,5},{5,4},{6,7},{7,6},{8,9},{9,8},{10,11... | collective-permute-start | bytes 221192 | tf_op jit(solution)/shard_map/ppermute | solution.py:216
  30.4 0.8 %first.1.rest_0_ = f32[256,256]{1,0:T(8,128)S(1)} custom-call(bf16[256,256]{1,0:T(8,128)(2,1)S(1)} %axial.1.normed_ref, bf16[656,256]{1,0:T(8,128)(2,1)S(1)} %get-tuple-element.18.rest_0_, bf16[656,256]{1,0:T(8,128)(2,1)S(1)} %collective-permute-done.6.rest_1_, bf16[272,256]{1,0:T(8,128)(2,1)S(1)} %collective-permute-done.4.rest_2_, ...), custom_call_target="tpu_custom_call" | custom-call | tf_op jit(solution)/shard_map/first/pallas_call | solution.py:282
  31.2 0.1 collective-permute-done.8.rest_2_
  31.3 1.2 %mlp.1 = bf16[32,2,4,256]{3,2,1,0:T(4,128)(2,1)} custom-call(bf16[256,256]{1,0:T(8,128)(2,1)S(1)} %axial.1.normed_ref, f32[8,256]{1,0:T(8,128)S(1)} %get-tuple-element.16.consts_ref, bf16[32,2,4,256]{3,2,1,0:T(4,128)(2,1)S(1)} %copy-done, f32[256,256]{1,0:T(8,128)S(1)} %first.1.rest_0_, bf16[272,256]{1,0:T(8,128)(2,1)S(1)} %collective-permute-done.7.rest_1_, ...), custom_call_target="tpu_custom_call" | custom-call | tf_op jit(solution)/shard_map/mlp/pallas_call | solution.py:294
  (18 shorter events, 0.1 us)
Async XLA Ops:
  0.0 7.6 %copy-start.3 = (bf16[64,256]{1,0:T(8,128)(2,1)S(1)}, bf16[64,256]{1,0:T(8,128)(2,1)}, u32[]{:S(2)}) copy-start(bf16[64,256]{1,0:T(8,128)(2,1)} %w_in_ref.1) | copy-start | bytes 98308
  0.0 7.6 %copy-start.4 = (bf16[64,256]{1,0:T(8,128)(2,1)S(1)}, bf16[64,256]{1,0:T(8,128)(2,1)}, u32[]{:S(2)}) copy-start(bf16[64,256]{1,0:T(8,128)(2,1)} %w_out_ref.1) | copy-start | bytes 98308
  0.0 16.0 %all-to-all-start = ((bf16[32,2,4,256]{3,2,1,0:T(4,128)(2,1)}), bf16[32,2,4,256]{3,2,1,0:T(4,128)(2,1)S(1)}, u32[]{:S(2)}, u32[]{:S(2)}) async-start(bf16[32,2,4,256]{3,2,1,0:T(4,128)(2,1)} %feat_ref.1), calls=%async_computation | async-start | bytes 262144 | tf_op jit(solution)/shard_map/all_to_all | solution.py:241
  7.5 0.7 %copy-start.6 = (f32[256]{0:T(256)S(1)}, f32[256]{0:T(256)}, u32[]{:S(2)}) copy-start(f32[256]{0:T(256)} %param.15) | copy-start | bytes 3076
  7.5 0.7 %copy-start.7 = (f32[256]{0:T(256)S(1)}, f32[256]{0:T(256)}, u32[]{:S(2)}) copy-start(f32[256]{0:T(256)} %param.16) | copy-start | bytes 3076
  7.6 0.7 %copy-start.8 = (f32[256]{0:T(256)S(1)}, f32[256]{0:T(256)}, u32[]{:S(2)}) copy-start(f32[256]{0:T(256)} %param.20) | copy-start | bytes 3076
  7.6 0.7 %copy-start.9 = (f32[256]{0:T(256)S(1)}, f32[256]{0:T(256)}, u32[]{:S(2)}) copy-start(f32[256]{0:T(256)} %param.21) | copy-start | bytes 3076
  7.6 0.7 %copy-start.5 = (f32[256]{0:T(256)S(1)}, f32[256]{0:T(256)}, u32[]{:S(2)}) copy-start(f32[256]{0:T(256)} %param.14) | copy-start | bytes 3076
  7.6 0.7 %copy-start.10 = (bf16[64]{0:T(256)(128)(2,1)S(1)}, bf16[64]{0:T(256)(128)(2,1)}, u32[]{:S(2)}) copy-start(bf16[64]{0:T(256)(128)(2,1)} %b_ref.1) | copy-start | bytes 388
  8.3 7.7 %copy-start.1 = (f32[31,256]{1,0:T(8,128)S(1)}, f32[31,256]{1,0:T(8,128)}, u32[]{:S(2)}) copy-start(f32[31,256]{1,0:T(8,128)} %taps_ref.2) | copy-start | bytes 95236
  8.4 12.4 %collective-permute-start = (bf16[144,256]{1,0:T(8,128)(2,1)S(1)}, bf16[144,256]{1,0:T(8,128)(2,1)S(1)}, u32[]{:S(2)}, u32[]{:S(2)}) collective-permute-start(bf16[144,256]{1,0:T(8,128)(2,1)S(1)} %get-tuple-element.13.refs_4_), channel_id=1, source_target_pairs={{0,4},{1,5},{2,6},{3,7},{4,0},{5,1},{6,2},{7,3},{8,12},{9,13},{10,... | collective-permute-start | bytes 221192 | tf_op jit(solution)/shard_map/ppermute | solution.py:216
  10.3 10.5 %collective-permute-start.1 = (bf16[144,256]{1,0:T(8,128)(2,1)S(1)}, bf16[144,256]{1,0:T(8,128)(2,1)S(1)}, u32[]{:S(2)}, u32[]{:S(2)}) collective-permute-start(bf16[144,256]{1,0:T(8,128)(2,1)S(1)} %get-tuple-element.13.refs_4_), channel_id=1, source_target_pairs={{0,8},{1,9},{2,10},{3,11},{4,12},{5,13},{6,14},{7,15},{8,0},{9,1},... | collective-permute-start | bytes 221192 | tf_op jit(solution)/shard_map/ppermute | solution.py:216
  12.6 8.1 %collective-permute-start.2 = (bf16[144,256]{1,0:T(8,128)(2,1)S(1)}, bf16[144,256]{1,0:T(8,128)(2,1)S(1)}, u32[]{:S(2)}, u32[]{:S(2)}) collective-permute-start(bf16[144,256]{1,0:T(8,128)(2,1)S(1)} %get-tuple-element.13.refs_4_), channel_id=1, source_target_pairs={{0,12},{1,13},{2,14},{3,15},{4,8},{5,9},{6,10},{7,11},{8,4},{9,5},... | collective-permute-start | bytes 221192 | tf_op jit(solution)/shard_map/ppermute | solution.py:216
  12.7 8.0 %collective-permute-start.3 = (bf16[144,256]{1,0:T(8,128)(2,1)S(1)}, bf16[144,256]{1,0:T(8,128)(2,1)S(1)}, u32[]{:S(2)}, u32[]{:S(2)}) collective-permute-start(bf16[144,256]{1,0:T(8,128)(2,1)S(1)} %get-tuple-element.13.refs_4_), channel_id=1, source_target_pairs={{0,2},{1,3},{2,0},{3,1},{4,6},{5,7},{6,4},{7,5},{8,10},{9,11},{10,... | collective-permute-start | bytes 221192 | tf_op jit(solution)/shard_map/ppermute | solution.py:216
  17.2 11.4 %all-to-all-start.1 = ((bf16[32,8,256]{2,1,0:T(8,128)(2,1)}), bf16[32,8,256]{2,1,0:T(8,128)(2,1)S(1)}, u32[]{:S(2)}, u32[]{:S(2)}) async-start(bf16[32,8,256]{2,1,0:T(8,128)(2,1)} %bitcast.6), calls=%async_computation.1 | async-start | bytes 262144 | tf_op jit(solution)/shard_map/all_to_all | solution.py:265
  20.7 7.9 %copy-start.2 = (f32[31,256]{1,0:T(8,128)S(1)}, f32[31,256]{1,0:T(8,128)}, u32[]{:S(2)}) copy-start(f32[31,256]{1,0:T(8,128)} %taps_ref.3) | copy-start | bytes 95236
  20.8 9.5 %collective-permute-start.6 = (bf16[656,256]{1,0:T(8,128)(2,1)S(1)}, bf16[656,256]{1,0:T(8,128)(2,1)S(1)}, u32[]{:S(2)}, u32[]{:S(2)}) collective-permute-start(bf16[656,256]{1,0:T(8,128)(2,1)S(1)} %get-tuple-element.18.rest_0_), channel_id=1, source_target_pairs={{0,1},{1,0},{2,3},{3,2},{4,5},{5,4},{6,7},{7,6},{8,9},{9,8},{10,11... | collective-permute-start | bytes 1007624 | tf_op jit(solution)/shard_map/ppermute | solution.py:216
  21.2 8.7 %collective-permute-start.4 = (bf16[272,256]{1,0:T(8,128)(2,1)S(1)}, bf16[272,256]{1,0:T(8,128)(2,1)S(1)}, u32[]{:S(2)}, u32[]{:S(2)}) collective-permute-start(bf16[272,256]{1,0:T(8,128)(2,1)S(1)} %get-tuple-element.14), channel_id=1, source_target_pairs={{0,2},{1,3},{2,0},{3,1},{4,6},{5,7},{6,4},{7,5},{8,10},{9,11},{10,... | collective-permute-start | bytes 417800 | tf_op jit(solution)/shard_map/ppermute | solution.py:216
  22.9 7.0 %collective-permute-start.5 = (bf16[144,256]{1,0:T(8,128)(2,1)S(1)}, bf16[144,256]{1,0:T(8,128)(2,1)S(1)}, u32[]{:S(2)}, u32[]{:S(2)}) collective-permute-start(bf16[144,256]{1,0:T(8,128)(2,1)S(1)} %get-tuple-element.15), channel_id=1, source_target_pairs={{0,2},{1,3},{2,0},{3,1},{4,6},{5,7},{6,4},{7,5},{8,10},{9,11},{10,... | collective-permute-start | bytes 221192 | tf_op jit(solution)/shard_map/ppermute | solution.py:216
  29.3 2.0 %copy-start = (bf16[32,2,4,256]{3,2,1,0:T(4,128)(2,1)S(1)}, bf16[32,2,4,256]{3,2,1,0:T(4,128)(2,1)}, u32[]{:S(2)}) copy-start(bf16[32,2,4,256]{3,2,1,0:T(4,128)(2,1)} %feat_ref.1) | copy-start | bytes 393220
  29.9 1.5 %collective-permute-start.7 = (bf16[272,256]{1,0:T(8,128)(2,1)S(1)}, bf16[272,256]{1,0:T(8,128)(2,1)S(1)}, u32[]{:S(2)}, u32[]{:S(2)}) collective-permute-start(bf16[272,256]{1,0:T(8,128)(2,1)S(1)} %collective-permute-done.4.rest_2_), channel_id=1, source_target_pairs={{0,1},{1,0},{2,3},{3,2},{4,5},{5,4},{6,7},{7,6},{8,9},{9,8},{10,11... | collective-permute-start | bytes 417800 | tf_op jit(solution)/shard_map/ppermute | solution.py:216
  29.9 1.5 %collective-permute-start.8 = (bf16[144,256]{1,0:T(8,128)(2,1)S(1)}, bf16[144,256]{1,0:T(8,128)(2,1)S(1)}, u32[]{:S(2)}, u32[]{:S(2)}) collective-permute-start(bf16[144,256]{1,0:T(8,128)(2,1)S(1)} %collective-permute-done.5.rest_3_), channel_id=1, source_target_pairs={{0,1},{1,0},{2,3},{3,2},{4,5},{5,4},{6,7},{7,6},{8,9},{9,8},{10,11... | collective-permute-start | bytes 221192 | tf_op jit(solution)/shard_map/ppermute | solution.py:216

commit v16 on v15

--- a/solution.py
+++ b/solution.py
@@ -30,7 +30,7 @@
 
 
 def join_kernel(*refs):
-    *blocks, all_ref, most_ref, last_ref = refs[1:]
+    *blocks, all_ref, most_ref = refs[1:]
     c = all_ref.shape[1]
     row = lax.broadcasted_iota(jnp.int32, (EXTRA, c), 0)
     for out_ref in (all_ref, most_ref):
@@ -40,7 +40,6 @@
             out_ref[2 * SLOT * i : 2 * SLOT * (i + 1), :] = block[0 : 2 * SLOT, :]
             biases = jnp.where(row == i, block[2 * SLOT :, :].astype(jnp.float32), biases)
         out_ref[2 * SLOT * count :, :] = biases.astype(out_ref.dtype)
-    last_ref[...] = blocks[count][...]
 
 
 def radial_kernel(x_ref, taps_ref, out_ref, even, odd, done, sems):
@@ -251,16 +250,16 @@
         name="radial",
     )(got.reshape(n, a_loc, r_loc, theta, c), radial_taps)
     if spread:
-        joined, most, last = pl.pallas_call(
+        joined, most = pl.pallas_call(
             join_kernel,
-            out_shape=[jax.ShapeDtypeStruct((2 * SLOT * size + EXTRA, c), jnp.bfloat16) for size in (outer + 1, outer - 2, 1)],
+            out_shape=[jax.ShapeDtypeStruct((2 * SLOT * size + EXTRA, c), jnp.bfloat16) for size in (outer + 1, outer - 2)],
             in_specs=[anywhere] + [vmem()] * (outer + 1),
-            out_specs=[vmem()] * 3,
+            out_specs=[vmem()] * 2,
             compiler_params=small,
             cost_estimate=pl.CostEstimate(flops=10**10, bytes_accessed=2 * 10**7, transcendentals=0),
             name="join",
-        )(mixed, *line, own, side)
-        across = [move(most, 1, 1), move(last, 1, 1)]
+        )(mixed, *line[1:], line[0], own, side)
+        across = [move(most, 1, 1), move(side, 0, 1)]
         twin = move(joined, 2, 1)
     back = lax.all_to_all(mixed.reshape(axial, rows, c), "row", split_axis=0, concat_axis=0, tiled=True)
     normed = pl.pallas_call(

time: 32.9 us -> 32.8 us (level)
  waiting for transfers between devices: 7.46 us -> 6.68 us
  starting transfers between devices: 20.2 us -> 20.9 us
    all_to_all x1, waiting for transfers between devices: 5.43 us -> 4.7 us  [local(): lax.all_to_all(mixed.reshape(axial, rows, c), 'row', split_axis=0, concat...]
    ppermute x9, starting transfers between devices: 9.2 us -> 9.9 us  [move(): return lax.ppermute(piece, 'row', [(i, i ^ by * stride) for i in range(n)])]
    ppermute x9, waiting for transfers between devices: 0.71 us -> 0.15 us  [move(): return lax.ppermute(piece, 'row', [(i, i ^ by * stride) for i in range(n)])]
    all_to_all x1, waiting for transfers between devices: 1.32 us -> 1.82 us  [local(): lax.all_to_all(features, 'row', split_axis=0, concat_axis=0, tiled=True)]
  transfers between devices with their start and end apart: 11 -> 11, of which waited for: 4 -> 3; matrix products, arithmetic and copies ran while one was open for 0% -> 0% of each run, Pallas kernels for 8% -> 8%
where the time goes in v16:
time: 32.8 us; the launch traced here: 32.5 us
  starting transfers between devices  20.9 us (64%)
  waiting for transfers between devices  6.68 us (20%)
  Pallas kernels  3.97 us (12%)
  local copies, waits for them, and re-layouts  0.7 us (2%)
    ppermute x9, starting transfers between devices, move(): return lax.ppermute(piece, 'row', [(i, i ^ by * stride) for i in range(n)])  9.9 us
    all_to_all x1, starting transfers between devices, local(): lax.all_to_all(features, 'row', split_axis=0, concat_axis=0, tiled=True)  7.52 us
    all_to_all x1, waiting for transfers between devices, local(): lax.all_to_all(mixed.reshape(axial, rows, c), 'row', split_axis=0, concat...  4.7 us
    all_to_all x1, starting transfers between devices, local(): lax.all_to_all(mixed.reshape(axial, rows, c), 'row', split_axis=0, concat...  3.52 us
    all_to_all x1, waiting for transfers between devices, local(): lax.all_to_all(features, 'row', split_axis=0, concat_axis=0, tiled=True)  1.82 us
    pallas_call x1, Pallas kernels, local(): pl.pallas_call(partial(mlp_kernel, len(partials)), out_shape=jax.ShapeDty...  1.22 us
    pallas_call x1, Pallas kernels, local(): pl.pallas_call(radial_kernel, out_shape=jax.ShapeDtypeStruct((n, a_loc, r...  1.19 us
    pallas_call x1, Pallas kernels, local(): pl.pallas_call(first_kernel, out_shape=jax.ShapeDtypeStruct((axial * rows...  0.81 us
  transfers between devices with their start and end apart: 11, of which 3 were waited for; matrix products, arithmetic and copies ran while one was open for 0% of the time, Pallas kernels for 8%

profile of v16, /device:TPU:0, one launch (start us, length us, event | category | flops | bytes accessed | tf_op | source)
XLA Modules:
  0.0 32.5 jit_solution(14972766355091609748)
XLA Ops:
  0.0 7.5 %all-to-all-start = ((bf16[32,2,4,256]{3,2,1,0:T(4,128)(2,1)}), bf16[32,2,4,256]{3,2,1,0:T(4,128)(2,1)S(1)}, u32[]{:S(2)}, u32[]{:S(2)}) async-start(bf16[32,2,4,256]{3,2,1,0:T(4,128)(2,1)} %feat_ref.1), calls=%async_computation | async-start | bytes 262144 | tf_op jit(solution)/shard_map/all_to_all | solution.py:240
  7.5 0.0 copy-start.6
  7.5 0.0 copy-start.7
  7.6 0.0 copy-start.8
  7.6 0.0 copy-start.9
  7.6 0.0 copy-start.5
  7.6 0.0 copy-start.10
  7.6 0.6 %copy-done.6 = f32[256]{0:T(256)S(1)} copy-done((f32[256]{0:T(256)S(1)}, f32[256]{0:T(256)}, u32[]{:S(2)}) %copy-start.6) | copy-done | bytes 1048
  8.2 0.0 copy-done.7
  8.2 0.0 copy-done.8
  8.2 0.0 copy-done.9
  8.3 0.0 copy-done.5
  8.3 0.1 pack.1
  8.4 1.9 %collective-permute-start.3 = (bf16[144,256]{1,0:T(8,128)(2,1)S(1)}, bf16[144,256]{1,0:T(8,128)(2,1)S(1)}, u32[]{:S(2)}, u32[]{:S(2)}) collective-permute-start(bf16[144,256]{1,0:T(8,128)(2,1)S(1)} %get-tuple-element.12.refs_4_), channel_id=1, source_target_pairs={{0,2},{1,3},{2,0},{3,1},{4,6},{5,7},{6,4},{7,5},{8,10},{9,11},{10,... | collective-permute-start | bytes 221192 | tf_op jit(solution)/shard_map/ppermute | solution.py:215
  10.3 2.4 %collective-permute-start = (bf16[144,256]{1,0:T(8,128)(2,1)S(1)}, bf16[144,256]{1,0:T(8,128)(2,1)S(1)}, u32[]{:S(2)}, u32[]{:S(2)}) collective-permute-start(bf16[144,256]{1,0:T(8,128)(2,1)S(1)} %get-tuple-element.12.refs_4_), channel_id=1, source_target_pairs={{0,8},{1,9},{2,10},{3,11},{4,12},{5,13},{6,14},{7,15},{8,0},{9,1},... | collective-permute-start | bytes 221192 | tf_op jit(solution)/shard_map/ppermute | solution.py:215
  12.6 1.5 %collective-permute-start.1 = (bf16[144,256]{1,0:T(8,128)(2,1)S(1)}, bf16[144,256]{1,0:T(8,128)(2,1)S(1)}, u32[]{:S(2)}, u32[]{:S(2)}) collective-permute-start(bf16[144,256]{1,0:T(8,128)(2,1)S(1)} %get-tuple-element.12.refs_4_), channel_id=1, source_target_pairs={{0,12},{1,13},{2,14},{3,15},{4,8},{5,9},{6,10},{7,11},{8,4},{9,5},... | collective-permute-start | bytes 221192 | tf_op jit(solution)/shard_map/ppermute | solution.py:215
  14.1 0.0 collective-permute-start.2
  14.1 1.8 %all-to-all-done = bf16[32,2,4,256]{3,2,1,0:T(4,128)(2,1)S(1)} async-done(((bf16[32,2,4,256]{3,2,1,0:T(4,128)(2,1)}), bf16[32,2,4,256]{3,2,1,0:T(4,128)(2,1)S(1)}, u32[]{:S(2)}, u32[]{:S(2)}) %all-to-all-start) | async-done | bytes 131104 | tf_op jit(solution)/shard_map/all_to_all | solution.py:240
  15.9 1.2 %radial.1.refs_0_ = bf16[16,2,8,256]{3,2,1,0:T(8,128)(2,1)} custom-call(bf16[16,2,2,4,256]{4,3,2,1,0:T(4,128)(2,1)S(1)} %bitcast.7, f32[31,256]{1,0:T(8,128)S(1)} %copy-done.1), custom_call_target="tpu_custom_call" | custom-call | tf_op jit(solution)/shard_map/radial/pallas_call | solution.py:242
  17.1 3.5 %all-to-all-start.1 = ((bf16[32,8,256]{2,1,0:T(8,128)(2,1)}), bf16[32,8,256]{2,1,0:T(8,128)(2,1)S(1)}, u32[]{:S(2)}, u32[]{:S(2)}) async-start(bf16[32,8,256]{2,1,0:T(8,128)(2,1)} %bitcast.6), calls=%async_computation.1 | async-start | bytes 262144 | tf_op jit(solution)/shard_map/all_to_all | solution.py:264
  20.7 0.0 copy-start.2
  20.8 0.4 %collective-permute-start.6 = (bf16[656,256]{1,0:T(8,128)(2,1)S(1)}, bf16[656,256]{1,0:T(8,128)(2,1)S(1)}, u32[]{:S(2)}, u32[]{:S(2)}) collective-permute-start(bf16[656,256]{1,0:T(8,128)(2,1)S(1)} %get-tuple-element.16.rest_0_), channel_id=1, source_target_pairs={{0,1},{1,0},{2,3},{3,2},{4,5},{5,4},{6,7},{7,6},{8,9},{9,8},{10,11... | collective-permute-start | bytes 1007624 | tf_op jit(solution)/shard_map/ppermute | solution.py:215
  21.2 1.7 %collective-permute-start.4 = (bf16[272,256]{1,0:T(8,128)(2,1)S(1)}, bf16[272,256]{1,0:T(8,128)(2,1)S(1)}, u32[]{:S(2)}, u32[]{:S(2)}) collective-permute-start(bf16[272,256]{1,0:T(8,128)(2,1)S(1)} %get-tuple-element.13), channel_id=1, source_target_pairs={{0,2},{1,3},{2,0},{3,1},{4,6},{5,7},{6,4},{7,5},{8,10},{9,11},{10,... | collective-permute-start | bytes 417800 | tf_op jit(solution)/shard_map/ppermute | solution.py:215
  22.9 1.5 %collective-permute-start.5 = (bf16[144,256]{1,0:T(8,128)(2,1)S(1)}, bf16[144,256]{1,0:T(8,128)(2,1)S(1)}, u32[]{:S(2)}, u32[]{:S(2)}) collective-permute-start(bf16[144,256]{1,0:T(8,128)(2,1)S(1)} %collective-permute-done.3.refs_5_), channel_id=1, source_target_pairs={{0,4},{1,5},{2,6},{3,7},{4,0},{5,1},{6,2},{7,3},{8,12},{9,13},{10,... | collective-permute-start | bytes 221192 | tf_op jit(solution)/shard_map/ppermute | solution.py:215
  24.3 4.7 %all-to-all-done.1.z_ref = bf16[32,8,256]{2,1,0:T(8,128)(2,1)S(1)} async-done(((bf16[32,8,256]{2,1,0:T(8,128)(2,1)}), bf16[32,8,256]{2,1,0:T(8,128)(2,1)S(1)}, u32[]{:S(2)}, u32[]{:S(2)}) %all-to-all-start.1) | async-done | bytes 131104 | tf_op jit(solution)/shard_map/all_to_all | solution.py:264
  29.0 0.6 %axial.1.normed_ref = bf16[256,256]{1,0:T(8,128)(2,1)S(1)} custom-call(bf16[32,8,256]{2,1,0:T(8,128)(2,1)S(1)} %all-to-all-done.1.z_ref, f32[31,256]{1,0:T(8,128)S(1)} %copy-done.2, f32[8,256]{1,0:T(8,128)S(1)} %get-tuple-element.14.consts_ref), custom_call_target="tpu_custom_call" | custom-call | tf_op jit(solution)/shard_map/axial/pallas_call | solution.py:265
  29.7 0.0 copy-start
  29.7 0.1 collective-permute-start.7
  29.8 0.5 %collective-permute-start.8 = (bf16[144,256]{1,0:T(8,128)(2,1)S(1)}, bf16[144,256]{1,0:T(8,128)(2,1)S(1)}, u32[]{:S(2)}, u32[]{:S(2)}) collective-permute-start(bf16[144,256]{1,0:T(8,128)(2,1)S(1)} %collective-permute-done.5.rest_3_), channel_id=1, source_target_pairs={{0,1},{1,0},{2,3},{3,2},{4,5},{5,4},{6,7},{7,6},{8,9},{9,8},{10,11... | collective-permute-start | bytes 221192 | tf_op jit(solution)/shard_map/ppermute | solution.py:215
  30.3 0.8 %first.1.rest_0_ = f32[256,256]{1,0:T(8,128)S(1)} custom-call(bf16[256,256]{1,0:T(8,128)(2,1)S(1)} %axial.1.normed_ref, bf16[656,256]{1,0:T(8,128)(2,1)S(1)} %get-tuple-element.16.rest_0_, bf16[656,256]{1,0:T(8,128)(2,1)S(1)} %collective-permute-done.6.rest_1_, bf16[272,256]{1,0:T(8,128)(2,1)S(1)} %collective-permute-done.4.rest_2_, ...), custom_call_target="tpu_custom_call" | custom-call | tf_op jit(solution)/shard_map/first/pallas_call | solution.py:281
  31.1 0.1 collective-permute-done.8.rest_2_
  31.3 1.2 %mlp.1 = bf16[32,2,4,256]{3,2,1,0:T(4,128)(2,1)} custom-call(bf16[256,256]{1,0:T(8,128)(2,1)S(1)} %axial.1.normed_ref, f32[8,256]{1,0:T(8,128)S(1)} %get-tuple-element.14.consts_ref, bf16[32,2,4,256]{3,2,1,0:T(4,128)(2,1)S(1)} %copy-done, f32[256,256]{1,0:T(8,128)S(1)} %first.1.rest_0_, bf16[272,256]{1,0:T(8,128)(2,1)S(1)} %collective-permute-done.7.rest_1_, ...), custom_call_target="tpu_custom_call" | custom-call | tf_op jit(solution)/shard_map/mlp/pallas_call | solution.py:293
  (18 shorter events, 0.1 us)
Async XLA Ops:
  0.0 7.6 %copy-start.3 = (bf16[64,256]{1,0:T(8,128)(2,1)S(1)}, bf16[64,256]{1,0:T(8,128)(2,1)}, u32[]{:S(2)}) copy-start(bf16[64,256]{1,0:T(8,128)(2,1)} %w_in_ref.1) | copy-start | bytes 98308
  0.0 7.6 %copy-start.4 = (bf16[64,256]{1,0:T(8,128)(2,1)S(1)}, bf16[64,256]{1,0:T(8,128)(2,1)}, u32[]{:S(2)}) copy-start(bf16[64,256]{1,0:T(8,128)(2,1)} %w_out_ref.1) | copy-start | bytes 98308
  0.0 15.9 %all-to-all-start = ((bf16[32,2,4,256]{3,2,1,0:T(4,128)(2,1)}), bf16[32,2,4,256]{3,2,1,0:T(4,128)(2,1)S(1)}, u32[]{:S(2)}, u32[]{:S(2)}) async-start(bf16[32,2,4,256]{3,2,1,0:T(4,128)(2,1)} %feat_ref.1), calls=%async_computation | async-start | bytes 262144 | tf_op jit(solution)/shard_map/all_to_all | solution.py:240
  7.5 0.7 %copy-start.6 = (f32[256]{0:T(256)S(1)}, f32[256]{0:T(256)}, u32[]{:S(2)}) copy-start(f32[256]{0:T(256)} %param.15) | copy-start | bytes 3076
  7.5 0.7 %copy-start.7 = (f32[256]{0:T(256)S(1)}, f32[256]{0:T(256)}, u32[]{:S(2)}) copy-start(f32[256]{0:T(256)} %param.16) | copy-start | bytes 3076
  7.6 0.7 %copy-start.8 = (f32[256]{0:T(256)S(1)}, f32[256]{0:T(256)}, u32[]{:S(2)}) copy-start(f32[256]{0:T(256)} %param.20) | copy-start | bytes 3076
  7.6 0.7 %copy-start.9 = (f32[256]{0:T(256)S(1)}, f32[256]{0:T(256)}, u32[]{:S(2)}) copy-start(f32[256]{0:T(256)} %param.21) | copy-start | bytes 3076
  7.6 0.7 %copy-start.5 = (f32[256]{0:T(256)S(1)}, f32[256]{0:T(256)}, u32[]{:S(2)}) copy-start(f32[256]{0:T(256)} %param.14) | copy-start | bytes 3076
  7.6 0.7 %copy-start.10 = (bf16[64]{0:T(256)(128)(2,1)S(1)}, bf16[64]{0:T(256)(128)(2,1)}, u32[]{:S(2)}) copy-start(bf16[64]{0:T(256)(128)(2,1)} %b_ref.1) | copy-start | bytes 388
  8.3 7.7 %copy-start.1 = (f32[31,256]{1,0:T(8,128)S(1)}, f32[31,256]{1,0:T(8,128)}, u32[]{:S(2)}) copy-start(f32[31,256]{1,0:T(8,128)} %taps_ref.2) | copy-start | bytes 95236
  8.4 12.3 %collective-permute-start.3 = (bf16[144,256]{1,0:T(8,128)(2,1)S(1)}, bf16[144,256]{1,0:T(8,128)(2,1)S(1)}, u32[]{:S(2)}, u32[]{:S(2)}) collective-permute-start(bf16[144,256]{1,0:T(8,128)(2,1)S(1)} %get-tuple-element.12.refs_4_), channel_id=1, source_target_pairs={{0,2},{1,3},{2,0},{3,1},{4,6},{5,7},{6,4},{7,5},{8,10},{9,11},{10,... | collective-permute-start | bytes 221192 | tf_op jit(solution)/shard_map/ppermute | solution.py:215
  10.3 10.4 %collective-permute-start = (bf16[144,256]{1,0:T(8,128)(2,1)S(1)}, bf16[144,256]{1,0:T(8,128)(2,1)S(1)}, u32[]{:S(2)}, u32[]{:S(2)}) collective-permute-start(bf16[144,256]{1,0:T(8,128)(2,1)S(1)} %get-tuple-element.12.refs_4_), channel_id=1, source_target_pairs={{0,8},{1,9},{2,10},{3,11},{4,12},{5,13},{6,14},{7,15},{8,0},{9,1},... | collective-permute-start | bytes 221192 | tf_op jit(solution)/shard_map/ppermute | solution.py:215
  12.6 8.1 %collective-permute-start.1 = (bf16[144,256]{1,0:T(8,128)(2,1)S(1)}, bf16[144,256]{1,0:T(8,128)(2,1)S(1)}, u32[]{:S(2)}, u32[]{:S(2)}) collective-permute-start(bf16[144,256]{1,0:T(8,128)(2,1)S(1)} %get-tuple-element.12.refs_4_), channel_id=1, source_target_pairs={{0,12},{1,13},{2,14},{3,15},{4,8},{5,9},{6,10},{7,11},{8,4},{9,5},... | collective-permute-start | bytes 221192 | tf_op jit(solution)/shard_map/ppermute | solution.py:215
  14.1 6.6 %collective-permute-start.2 = (bf16[144,256]{1,0:T(8,128)(2,1)S(1)}, bf16[144,256]{1,0:T(8,128)(2,1)S(1)}, u32[]{:S(2)}, u32[]{:S(2)}) collective-permute-start(bf16[144,256]{1,0:T(8,128)(2,1)S(1)} %get-tuple-element.12.refs_4_), channel_id=1, source_target_pairs={{0,4},{1,5},{2,6},{3,7},{4,0},{5,1},{6,2},{7,3},{8,12},{9,13},{10,... | collective-permute-start | bytes 221192 | tf_op jit(solution)/shard_map/ppermute | solution.py:215
  17.1 11.9 %all-to-all-start.1 = ((bf16[32,8,256]{2,1,0:T(8,128)(2,1)}), bf16[32,8,256]{2,1,0:T(8,128)(2,1)S(1)}, u32[]{:S(2)}, u32[]{:S(2)}) async-start(bf16[32,8,256]{2,1,0:T(8,128)(2,1)} %bitcast.6), calls=%async_computation.1 | async-start | bytes 262144 | tf_op jit(solution)/shard_map/all_to_all | solution.py:264
  20.7 8.4 %copy-start.2 = (f32[31,256]{1,0:T(8,128)S(1)}, f32[31,256]{1,0:T(8,128)}, u32[]{:S(2)}) copy-start(f32[31,256]{1,0:T(8,128)} %taps_ref.3) | copy-start | bytes 95236
  20.8 9.5 %collective-permute-start.6 = (bf16[656,256]{1,0:T(8,128)(2,1)S(1)}, bf16[656,256]{1,0:T(8,128)(2,1)S(1)}, u32[]{:S(2)}, u32[]{:S(2)}) collective-permute-start(bf16[656,256]{1,0:T(8,128)(2,1)S(1)} %get-tuple-element.16.rest_0_), channel_id=1, source_target_pairs={{0,1},{1,0},{2,3},{3,2},{4,5},{5,4},{6,7},{7,6},{8,9},{9,8},{10,11... | collective-permute-start | bytes 1007624 | tf_op jit(solution)/shard_map/ppermute | solution.py:215
  21.2 8.5 %collective-permute-start.4 = (bf16[272,256]{1,0:T(8,128)(2,1)S(1)}, bf16[272,256]{1,0:T(8,128)(2,1)S(1)}, u32[]{:S(2)}, u32[]{:S(2)}) collective-permute-start(bf16[272,256]{1,0:T(8,128)(2,1)S(1)} %get-tuple-element.13), channel_id=1, source_target_pairs={{0,2},{1,3},{2,0},{3,1},{4,6},{5,7},{6,4},{7,5},{8,10},{9,11},{10,... | collective-permute-start | bytes 417800 | tf_op jit(solution)/shard_map/ppermute | solution.py:215
  22.9 6.8 %collective-permute-start.5 = (bf16[144,256]{1,0:T(8,128)(2,1)S(1)}, bf16[144,256]{1,0:T(8,128)(2,1)S(1)}, u32[]{:S(2)}, u32[]{:S(2)}) collective-permute-start(bf16[144,256]{1,0:T(8,128)(2,1)S(1)} %collective-permute-done.3.refs_5_), channel_id=1, source_target_pairs={{0,4},{1,5},{2,6},{3,7},{4,0},{5,1},{6,2},{7,3},{8,12},{9,13},{10,... | collective-permute-start | bytes 221192 | tf_op jit(solution)/shard_map/ppermute | solution.py:215
  29.7 1.6 %copy-start = (bf16[32,2,4,256]{3,2,1,0:T(4,128)(2,1)S(1)}, bf16[32,2,4,256]{3,2,1,0:T(4,128)(2,1)}, u32[]{:S(2)}) copy-start(bf16[32,2,4,256]{3,2,1,0:T(4,128)(2,1)} %feat_ref.1) | copy-start | bytes 393220
  29.7 1.5 %collective-permute-start.7 = (bf16[272,256]{1,0:T(8,128)(2,1)S(1)}, bf16[272,256]{1,0:T(8,128)(2,1)S(1)}, u32[]{:S(2)}, u32[]{:S(2)}) collective-permute-start(bf16[272,256]{1,0:T(8,128)(2,1)S(1)} %collective-permute-done.4.rest_2_), channel_id=1, source_target_pairs={{0,1},{1,0},{2,3},{3,2},{4,5},{5,4},{6,7},{7,6},{8,9},{9,8},{10,11... | collective-permute-start | bytes 417800 | tf_op jit(solution)/shard_map/ppermute | solution.py:215
  29.8 1.5 %collective-permute-start.8 = (bf16[144,256]{1,0:T(8,128)(2,1)S(1)}, bf16[144,256]{1,0:T(8,128)(2,1)S(1)}, u32[]{:S(2)}, u32[]{:S(2)}) collective-permute-start(bf16[144,256]{1,0:T(8,128)(2,1)S(1)} %collective-permute-done.5.rest_3_), channel_id=1, source_target_pairs={{0,1},{1,0},{2,3},{3,2},{4,5},{5,4},{6,7},{7,6},{8,9},{9,8},{10,11... | collective-permute-start | bytes 221192 | tf_op jit(solution)/shard_map/ppermute | solution.py:215

commit v17 on v16

--- a/solution.py
+++ b/solution.py
@@ -30,10 +30,10 @@
 
 
 def join_kernel(*refs):
-    *blocks, all_ref, most_ref = refs[1:]
+    *blocks, all_ref, line_ref = refs[1:]
     c = all_ref.shape[1]
     row = lax.broadcasted_iota(jnp.int32, (EXTRA, c), 0)
-    for out_ref in (all_ref, most_ref):
+    for out_ref in (all_ref, line_ref):
         count = out_ref.shape[0] // (2 * SLOT)
         biases = jnp.zeros((EXTRA, c), jnp.float32)
         for i, block in enumerate(blocks[:count]):
@@ -250,16 +250,16 @@
         name="radial",
     )(got.reshape(n, a_loc, r_loc, theta, c), radial_taps)
     if spread:
-        joined, most = pl.pallas_call(
+        joined, reach = pl.pallas_call(
             join_kernel,
-            out_shape=[jax.ShapeDtypeStruct((2 * SLOT * size + EXTRA, c), jnp.bfloat16) for size in (outer + 1, outer - 2)],
+            out_shape=[jax.ShapeDtypeStruct((2 * SLOT * size + EXTRA, c), jnp.bfloat16) for size in (outer + 1, outer - 1)],
             in_specs=[anywhere] + [vmem()] * (outer + 1),
             out_specs=[vmem()] * 2,
             compiler_params=small,
             cost_estimate=pl.CostEstimate(flops=10**10, bytes_accessed=2 * 10**7, transcendentals=0),
             name="join",
-        )(mixed, *line[1:], line[0], own, side)
-        across = [move(most, 1, 1), move(side, 0, 1)]
+        )(mixed, *line, own, side)
+        across = [move(reach, 1, 1)]
         twin = move(joined, 2, 1)
     back = lax.all_to_all(mixed.reshape(axial, rows, c), "row", split_axis=0, concat_axis=0, tiled=True)
     normed = pl.pallas_call(
@@ -281,7 +281,7 @@
             pl.pallas_call(
                 first_kernel,
                 out_shape=jax.ShapeDtypeStruct((axial * rows, c), jnp.float32),
-                in_specs=[vmem()] * 5,
+                in_specs=[vmem()] * (3 + len(across)),
                 out_specs=vmem(),
                 compiler_params=middle,
                 name="first",

time: 32.8 us -> 32.5 us (level)
  starting transfers between devices: 20.9 us -> 19.2 us
  waiting for transfers between devices: 6.68 us -> 8.15 us
    ppermute x9 -> x7, starting transfers between devices: 9.9 us -> 8.19 us  [move(): return lax.ppermute(piece, 'row', [(i, i ^ by * stride) for i in range(n)])]
    all_to_all x1, waiting for transfers between devices: 4.7 us -> 5.93 us  [local(): lax.all_to_all(mixed.reshape(axial, rows, c), 'row', split_axis=0, concat...]
    ppermute x9 -> x7, waiting for transfers between devices: 0.15 us -> 0.89 us  [move(): return lax.ppermute(piece, 'row', [(i, i ^ by * stride) for i in range(n)])]
    all_to_all x1, waiting for transfers between devices: 1.82 us -> 1.32 us  [local(): lax.all_to_all(features, 'row', split_axis=0, concat_axis=0, tiled=True)]
  transfers between devices with their start and end apart: 11 -> 9, of which waited for: 3 -> 4; matrix products, arithmetic and copies ran while one was open for 0% -> 0% of each run, Pallas kernels for 8% -> 9%
where the time goes in v17:
time: 32.5 us; the launch traced here: 32.2 us
  starting transfers between devices  19.2 us (59%)
  waiting for transfers between devices  8.15 us (25%)
  Pallas kernels  3.96 us (12%)
  local copies, waits for them, and re-layouts  0.7 us (2%)
    ppermute x7, starting transfers between devices, move(): return lax.ppermute(piece, 'row', [(i, i ^ by * stride) for i in range(n)])  8.19 us
    all_to_all x1, starting transfers between devices, local(): lax.all_to_all(features, 'row', split_axis=0, concat_axis=0, tiled=True)  7.52 us
    all_to_all x1, waiting for transfers between devices, local(): lax.all_to_all(mixed.reshape(axial, rows, c), 'row', split_axis=0, concat...  5.93 us
    all_to_all x1, starting transfers between devices, local(): lax.all_to_all(mixed.reshape(axial, rows, c), 'row', split_axis=0, concat...  3.52 us
    all_to_all x1, waiting for transfers between devices, local(): lax.all_to_all(features, 'row', split_axis=0, concat_axis=0, tiled=True)  1.32 us
    pallas_call x1, Pallas kernels, local(): pl.pallas_call(partial(mlp_kernel, len(partials)), out_shape=jax.ShapeDty...  1.22 us
    pallas_call x1, Pallas kernels, local(): pl.pallas_call(radial_kernel, out_shape=jax.ShapeDtypeStruct((n, a_loc, r...  1.19 us
    ppermute x7, waiting for transfers between devices, move(): return lax.ppermute(piece, 'row', [(i, i ^ by * stride) for i in range(n)])  0.89 us
  transfers between devices with their start and end apart: 9, of which 4 were waited for; matrix products, arithmetic and copies ran while one was open for 0% of the time, Pallas kernels for 9%

profile of v17, /device:TPU:0, one launch (start us, length us, event | category | flops | bytes accessed | tf_op | source)
XLA Modules:
  0.0 32.2 jit_solution(6061175692486565404)
XLA Ops:
  0.0 7.5 %all-to-all-start = ((bf16[32,2,4,256]{3,2,1,0:T(4,128)(2,1)}), bf16[32,2,4,256]{3,2,1,0:T(4,128)(2,1)S(1)}, u32[]{:S(2)}, u32[]{:S(2)}) async-start(bf16[32,2,4,256]{3,2,1,0:T(4,128)(2,1)} %feat_ref.1), calls=%async_computation | async-start | bytes 262144 | tf_op jit(solution)/shard_map/all_to_all | solution.py:240
  7.5 0.0 copy-start.6
  7.5 0.0 copy-start.7
  7.6 0.0 copy-start.8
  7.6 0.0 copy-start.9
  7.6 0.0 copy-start.5
  7.6 0.0 copy-start.10
  7.6 0.6 %copy-done.6 = f32[256]{0:T(256)S(1)} copy-done((f32[256]{0:T(256)S(1)}, f32[256]{0:T(256)}, u32[]{:S(2)}) %copy-start.6) | copy-done | bytes 1048
  8.2 0.0 copy-done.7
  8.2 0.0 copy-done.8
  8.2 0.0 copy-done.9
  8.3 0.0 copy-done.5
  8.3 0.1 pack.1
  8.4 1.9 %collective-permute-start = (bf16[144,256]{1,0:T(8,128)(2,1)S(1)}, bf16[144,256]{1,0:T(8,128)(2,1)S(1)}, u32[]{:S(2)}, u32[]{:S(2)}) collective-permute-start(bf16[144,256]{1,0:T(8,128)(2,1)S(1)} %get-tuple-element.11.refs_4_), channel_id=1, source_target_pairs={{0,4},{1,5},{2,6},{3,7},{4,0},{5,1},{6,2},{7,3},{8,12},{9,13},{10,... | collective-permute-start | bytes 221192 | tf_op jit(solution)/shard_map/ppermute | solution.py:215
  10.3 2.4 %collective-permute-start.1 = (bf16[144,256]{1,0:T(8,128)(2,1)S(1)}, bf16[144,256]{1,0:T(8,128)(2,1)S(1)}, u32[]{:S(2)}, u32[]{:S(2)}) collective-permute-start(bf16[144,256]{1,0:T(8,128)(2,1)S(1)} %get-tuple-element.11.refs_4_), channel_id=1, source_target_pairs={{0,8},{1,9},{2,10},{3,11},{4,12},{5,13},{6,14},{7,15},{8,0},{9,1},... | collective-permute-start | bytes 221192 | tf_op jit(solution)/shard_map/ppermute | solution.py:215
  12.6 0.1 collective-permute-start.2
  12.7 1.9 %collective-permute-start.3 = (bf16[144,256]{1,0:T(8,128)(2,1)S(1)}, bf16[144,256]{1,0:T(8,128)(2,1)S(1)}, u32[]{:S(2)}, u32[]{:S(2)}) collective-permute-start(bf16[144,256]{1,0:T(8,128)(2,1)S(1)} %get-tuple-element.11.refs_4_), channel_id=1, source_target_pairs={{0,2},{1,3},{2,0},{3,1},{4,6},{5,7},{6,4},{7,5},{8,10},{9,11},{10,... | collective-permute-start | bytes 221192 | tf_op jit(solution)/shard_map/ppermute | solution.py:215
  14.7 1.3 %all-to-all-done = bf16[32,2,4,256]{3,2,1,0:T(4,128)(2,1)S(1)} async-done(((bf16[32,2,4,256]{3,2,1,0:T(4,128)(2,1)}), bf16[32,2,4,256]{3,2,1,0:T(4,128)(2,1)S(1)}, u32[]{:S(2)}, u32[]{:S(2)}) %all-to-all-start) | async-done | bytes 131104 | tf_op jit(solution)/shard_map/all_to_all | solution.py:240
  16.0 1.2 %radial.1.refs_0_ = bf16[16,2,8,256]{3,2,1,0:T(8,128)(2,1)} custom-call(bf16[16,2,2,4,256]{4,3,2,1,0:T(4,128)(2,1)S(1)} %bitcast.7, f32[31,256]{1,0:T(8,128)S(1)} %copy-done.1), custom_call_target="tpu_custom_call" | custom-call | tf_op jit(solution)/shard_map/radial/pallas_call | solution.py:242
  17.2 3.5 %all-to-all-start.1 = ((bf16[32,8,256]{2,1,0:T(8,128)(2,1)}), bf16[32,8,256]{2,1,0:T(8,128)(2,1)S(1)}, u32[]{:S(2)}, u32[]{:S(2)}) async-start(bf16[32,8,256]{2,1,0:T(8,128)(2,1)} %bitcast.6), calls=%async_computation.1 | async-start | bytes 262144 | tf_op jit(solution)/shard_map/all_to_all | solution.py:264
  20.7 0.0 copy-start.2
  20.7 0.0 collective-permute-done.1.refs_2_
  20.8 0.0 collective-permute-done.2.refs_3_
  20.8 1.9 %collective-permute-start.4 = (bf16[400,256]{1,0:T(8,128)(2,1)S(1)}, bf16[400,256]{1,0:T(8,128)(2,1)S(1)}, u32[]{:S(2)}, u32[]{:S(2)}) collective-permute-start(bf16[400,256]{1,0:T(8,128)(2,1)S(1)} %get-tuple-element.12), channel_id=1, source_target_pairs={{0,2},{1,3},{2,0},{3,1},{4,6},{5,7},{6,4},{7,5},{8,10},{9,11},{10,... | collective-permute-start | bytes 614408 | tf_op jit(solution)/shard_map/ppermute | solution.py:215
  22.7 0.0 collective-permute-start.5
  22.7 5.9 %all-to-all-done.1.z_ref = bf16[32,8,256]{2,1,0:T(8,128)(2,1)S(1)} async-done(((bf16[32,8,256]{2,1,0:T(8,128)(2,1)}), bf16[32,8,256]{2,1,0:T(8,128)(2,1)S(1)}, u32[]{:S(2)}, u32[]{:S(2)}) %all-to-all-start.1) | async-done | bytes 131104 | tf_op jit(solution)/shard_map/all_to_all | solution.py:264
  28.6 0.6 %axial.1.normed_ref = bf16[256,256]{1,0:T(8,128)(2,1)S(1)} custom-call(bf16[32,8,256]{2,1,0:T(8,128)(2,1)S(1)} %all-to-all-done.1.z_ref, f32[31,256]{1,0:T(8,128)S(1)} %copy-done.2, f32[8,256]{1,0:T(8,128)S(1)} %get-tuple-element.13.consts_ref), custom_call_target="tpu_custom_call" | custom-call | tf_op jit(solution)/shard_map/axial/pallas_call | solution.py:265
  29.3 0.0 copy-start
  29.3 0.2 collective-permute-done.4.rest_2_
  29.5 0.8 %first.1.rest_0_ = f32[256,256]{1,0:T(8,128)S(1)} custom-call(bf16[256,256]{1,0:T(8,128)(2,1)S(1)} %axial.1.normed_ref, bf16[656,256]{1,0:T(8,128)(2,1)S(1)} %get-tuple-element.15.rest_0_, bf16[656,256]{1,0:T(8,128)(2,1)S(1)} %collective-permute-done.5.rest_1_, bf16[400,256]{1,0:T(8,128)(2,1)S(1)} %collective-permute-done.4.rest_2_), custom_call_target="tpu_custom_call" | custom-call | tf_op jit(solution)/shard_map/first/pallas_call | solution.py:281
  30.4 0.6 %collective-permute-done.6.rest_1_ = bf16[400,256]{1,0:T(8,128)(2,1)S(1)} collective-permute-done((bf16[400,256]{1,0:T(8,128)(2,1)S(1)}, bf16[400,256]{1,0:T(8,128)(2,1)S(1)}, u32[]{:S(2)}, u32[]{:S(2)}) %collective-permute-start.6) | collective-permute-done | bytes 204832 | tf_op jit(solution)/shard_map/ppermute | solution.py:215
  31.0 1.2 %mlp.1 = bf16[32,2,4,256]{3,2,1,0:T(4,128)(2,1)} custom-call(bf16[256,256]{1,0:T(8,128)(2,1)S(1)} %axial.1.normed_ref, f32[8,256]{1,0:T(8,128)S(1)} %get-tuple-element.13.consts_ref, bf16[32,2,4,256]{3,2,1,0:T(4,128)(2,1)S(1)} %copy-done, f32[256,256]{1,0:T(8,128)S(1)} %first.1.rest_0_, bf16[400,256]{1,0:T(8,128)(2,1)S(1)} %collective-permute-done.6.rest_1_), custom_call_target="tpu_custom_call" | custom-call | tf_op jit(solution)/shard_map/mlp/pallas_call | solution.py:293
  (14 shorter events, 0.1 us)
Async XLA Ops:
  0.0 7.6 %copy-start.3 = (bf16[64,256]{1,0:T(8,128)(2,1)S(1)}, bf16[64,256]{1,0:T(8,128)(2,1)}, u32[]{:S(2)}) copy-start(bf16[64,256]{1,0:T(8,128)(2,1)} %w_in_ref.1) | copy-start | bytes 98308
  0.0 7.6 %copy-start.4 = (bf16[64,256]{1,0:T(8,128)(2,1)S(1)}, bf16[64,256]{1,0:T(8,128)(2,1)}, u32[]{:S(2)}) copy-start(bf16[64,256]{1,0:T(8,128)(2,1)} %w_out_ref.1) | copy-start | bytes 98308
  0.0 16.0 %all-to-all-start = ((bf16[32,2,4,256]{3,2,1,0:T(4,128)(2,1)}), bf16[32,2,4,256]{3,2,1,0:T(4,128)(2,1)S(1)}, u32[]{:S(2)}, u32[]{:S(2)}) async-start(bf16[32,2,4,256]{3,2,1,0:T(4,128)(2,1)} %feat_ref.1), calls=%async_computation | async-start | bytes 262144 | tf_op jit(solution)/shard_map/all_to_all | solution.py:240
  7.5 0.7 %copy-start.6 = (f32[256]{0:T(256)S(1)}, f32[256]{0:T(256)}, u32[]{:S(2)}) copy-start(f32[256]{0:T(256)} %param.15) | copy-start | bytes 3076
  7.5 0.7 %copy-start.7 = (f32[256]{0:T(256)S(1)}, f32[256]{0:T(256)}, u32[]{:S(2)}) copy-start(f32[256]{0:T(256)} %param.16) | copy-start | bytes 3076
  7.6 0.7 %copy-start.8 = (f32[256]{0:T(256)S(1)}, f32[256]{0:T(256)}, u32[]{:S(2)}) copy-start(f32[256]{0:T(256)} %param.20) | copy-start | bytes 3076
  7.6 0.7 %copy-start.9 = (f32[256]{0:T(256)S(1)}, f32[256]{0:T(256)}, u32[]{:S(2)}) copy-start(f32[256]{0:T(256)} %param.21) | copy-start | bytes 3076
  7.6 0.7 %copy-start.5 = (f32[256]{0:T(256)S(1)}, f32[256]{0:T(256)}, u32[]{:S(2)}) copy-start(f32[256]{0:T(256)} %param.14) | copy-start | bytes 3076
  7.6 0.7 %copy-start.10 = (bf16[64]{0:T(256)(128)(2,1)S(1)}, bf16[64]{0:T(256)(128)(2,1)}, u32[]{:S(2)}) copy-start(bf16[64]{0:T(256)(128)(2,1)} %b_ref.1) | copy-start | bytes 388
  8.3 7.7 %copy-start.1 = (f32[31,256]{1,0:T(8,128)S(1)}, f32[31,256]{1,0:T(8,128)}, u32[]{:S(2)}) copy-start(f32[31,256]{1,0:T(8,128)} %taps_ref.2) | copy-start | bytes 95236
  8.4 12.4 %collective-permute-start = (bf16[144,256]{1,0:T(8,128)(2,1)S(1)}, bf16[144,256]{1,0:T(8,128)(2,1)S(1)}, u32[]{:S(2)}, u32[]{:S(2)}) collective-permute-start(bf16[144,256]{1,0:T(8,128)(2,1)S(1)} %get-tuple-element.11.refs_4_), channel_id=1, source_target_pairs={{0,4},{1,5},{2,6},{3,7},{4,0},{5,1},{6,2},{7,3},{8,12},{9,13},{10,... | collective-permute-start | bytes 221192 | tf_op jit(solution)/shard_map/ppermute | solution.py:215
  10.3 10.5 %collective-permute-start.1 = (bf16[144,256]{1,0:T(8,128)(2,1)S(1)}, bf16[144,256]{1,0:T(8,128)(2,1)S(1)}, u32[]{:S(2)}, u32[]{:S(2)}) collective-permute-start(bf16[144,256]{1,0:T(8,128)(2,1)S(1)} %get-tuple-element.11.refs_4_), channel_id=1, source_target_pairs={{0,8},{1,9},{2,10},{3,11},{4,12},{5,13},{6,14},{7,15},{8,0},{9,1},... | collective-permute-start | bytes 221192 | tf_op jit(solution)/shard_map/ppermute | solution.py:215
  12.6 8.1 %collective-permute-start.2 = (bf16[144,256]{1,0:T(8,128)(2,1)S(1)}, bf16[144,256]{1,0:T(8,128)(2,1)S(1)}, u32[]{:S(2)}, u32[]{:S(2)}) collective-permute-start(bf16[144,256]{1,0:T(8,128)(2,1)S(1)} %get-tuple-element.11.refs_4_), channel_id=1, source_target_pairs={{0,12},{1,13},{2,14},{3,15},{4,8},{5,9},{6,10},{7,11},{8,4},{9,5},... | collective-permute-start | bytes 221192 | tf_op jit(solution)/shard_map/ppermute | solution.py:215
  12.7 8.0 %collective-permute-start.3 = (bf16[144,256]{1,0:T(8,128)(2,1)S(1)}, bf16[144,256]{1,0:T(8,128)(2,1)S(1)}, u32[]{:S(2)}, u32[]{:S(2)}) collective-permute-start(bf16[144,256]{1,0:T(8,128)(2,1)S(1)} %get-tuple-element.11.refs_4_), channel_id=1, source_target_pairs={{0,2},{1,3},{2,0},{3,1},{4,6},{5,7},{6,4},{7,5},{8,10},{9,11},{10,... | collective-permute-start | bytes 221192 | tf_op jit(solution)/shard_map/ppermute | solution.py:215
  17.2 11.4 %all-to-all-start.1 = ((bf16[32,8,256]{2,1,0:T(8,128)(2,1)}), bf16[32,8,256]{2,1,0:T(8,128)(2,1)S(1)}, u32[]{:S(2)}, u32[]{:S(2)}) async-start(bf16[32,8,256]{2,1,0:T(8,128)(2,1)} %bitcast.6), calls=%async_computation.1 | async-start | bytes 262144 | tf_op jit(solution)/shard_map/all_to_all | solution.py:264
  20.7 7.9 %copy-start.2 = (f32[31,256]{1,0:T(8,128)S(1)}, f32[31,256]{1,0:T(8,128)}, u32[]{:S(2)}) copy-start(f32[31,256]{1,0:T(8,128)} %taps_ref.3) | copy-start | bytes 95236
  20.8 8.7 %collective-permute-start.4 = (bf16[400,256]{1,0:T(8,128)(2,1)S(1)}, bf16[400,256]{1,0:T(8,128)(2,1)S(1)}, u32[]{:S(2)}, u32[]{:S(2)}) collective-permute-start(bf16[400,256]{1,0:T(8,128)(2,1)S(1)} %get-tuple-element.12), channel_id=1, source_target_pairs={{0,2},{1,3},{2,0},{3,1},{4,6},{5,7},{6,4},{7,5},{8,10},{9,11},{10,... | collective-permute-start | bytes 614408 | tf_op jit(solution)/shard_map/ppermute | solution.py:215
  22.7 6.8 %collective-permute-start.5 = (bf16[656,256]{1,0:T(8,128)(2,1)S(1)}, bf16[656,256]{1,0:T(8,128)(2,1)S(1)}, u32[]{:S(2)}, u32[]{:S(2)}) collective-permute-start(bf16[656,256]{1,0:T(8,128)(2,1)S(1)} %get-tuple-element.15.rest_0_), channel_id=1, source_target_pairs={{0,1},{1,0},{2,3},{3,2},{4,5},{5,4},{6,7},{7,6},{8,9},{9,8},{10,11... | collective-permute-start | bytes 1007624 | tf_op jit(solution)/shard_map/ppermute | solution.py:215
  29.3 1.7 %copy-start = (bf16[32,2,4,256]{3,2,1,0:T(4,128)(2,1)S(1)}, bf16[32,2,4,256]{3,2,1,0:T(4,128)(2,1)}, u32[]{:S(2)}) copy-start(bf16[32,2,4,256]{3,2,1,0:T(4,128)(2,1)} %feat_ref.1) | copy-start | bytes 393220
  29.5 1.5 %collective-permute-start.6 = (bf16[400,256]{1,0:T(8,128)(2,1)S(1)}, bf16[400,256]{1,0:T(8,128)(2,1)S(1)}, u32[]{:S(2)}, u32[]{:S(2)}) collective-permute-start(bf16[400,256]{1,0:T(8,128)(2,1)S(1)} %collective-permute-done.4.rest_2_), channel_id=1, source_target_pairs={{0,1},{1,0},{2,3},{3,2},{4,5},{5,4},{6,7},{7,6},{8,9},{9,8},{10,11... | collective-permute-start | bytes 614408 | tf_op jit(solution)/shard_map/ppermute | solution.py:215

commit v18 on v17

--- a/solution.py
+++ b/solution.py
@@ -164,29 +164,27 @@
     *blocks, out_ref, branch, done, sems = rest
     axial, _, theta, c = feat_ref.shape
     rows = 2 * theta
-    planes = PLANES // 2
-
-    def mlp(at, size):
-        tokens = pl.ds(at * rows, size * rows)
+    parts = 4
+
+    def product(at):
+        tokens = pl.ds(at * rows, PLANES * rows)
         total = hidden_sum(normed_ref[tokens, :], blocks[partials:])
         for partial_ref in blocks[:partials]:
             total = total + partial_ref[tokens, :]
-        result = (consts_ref[4 : 5, :] * (total + consts_ref[3 : 4, :])).astype(jnp.bfloat16).astype(jnp.float32)
-        branch[pl.ds(at, size)] = result.reshape(size, rows, c)
+        result = (consts_ref[4:5, :] * (total + consts_ref[3:4, :])).astype(jnp.bfloat16).astype(jnp.float32)
+        branch[pl.ds(at, PLANES)] = result.reshape(PLANES, rows, c)
+
+    if axial == PLANES:
+        product(0)
+    else:
+        pl.loop(0, axial // PLANES)(lambda i: product(pl.multiple_of(i * PLANES, PLANES)))
+    copies = []
+    for i in range(parts):
+        part = pl.ds(i * (axial // parts), axial // parts)
         for r in range(2):
-            got = branch[pl.ds(at, size), r * theta : (r + 1) * theta, :]
-            done[pl.ds(at, size), r] = (feat_ref[pl.ds(at, size), r].astype(jnp.float32) + got).astype(done.dtype)
-
-    copies = []
-    if axial == PLANES:
-        for i in range(2):
-            mlp(i * planes, planes)
-            part = pl.ds(i * planes, planes)
-            copies.append(pltpu.make_async_copy(done.at[part], out_ref.at[part], sems.at[i]))
-            copies[-1].start()
-    else:
-        pl.loop(0, axial // PLANES)(lambda i: mlp(pl.multiple_of(i * PLANES, PLANES), PLANES))
-        copies.append(pltpu.make_async_copy(done, out_ref, sems.at[0]))
+            got = branch[part, r * theta : (r + 1) * theta, :]
+            done[part, r] = (feat_ref[part, r].astype(jnp.float32) + got).astype(done.dtype)
+        copies.append(pltpu.make_async_copy(done.at[part], out_ref.at[part], sems.at[i]))
         copies[-1].start()
     for copy in copies:
         copy.wait()
@@ -298,7 +296,7 @@
         scratch_shapes=[
             pltpu.VMEM((axial, rows, c), jnp.float32),
             pltpu.VMEM(features.shape, jnp.bfloat16),
-            pltpu.SemaphoreType.DMA((2,)),
+            pltpu.SemaphoreType.DMA((4,)),
         ],
         compiler_params=large,
         name="mlp",

time: 32.5 us -> 32.4 us (level)
  no operation moved by 1% of the time
where the time goes in v18:
time: 32.4 us; the launch traced here: 32.1 us
  starting transfers between devices  19.2 us (59%)
  waiting for transfers between devices  8.15 us (25%)
  Pallas kernels  3.83 us (12%)
  local copies, waits for them, and re-layouts  0.7 us (2%)
    ppermute x7, starting transfers between devices, move(): return lax.ppermute(piece, 'row', [(i, i ^ by * stride) for i in range(n)])  8.19 us
    all_to_all x1, starting transfers between devices, local(): lax.all_to_all(features, 'row', split_axis=0, concat_axis=0, tiled=True)  7.52 us
    all_to_all x1, waiting for transfers between devices, local(): lax.all_to_all(mixed.reshape(axial, rows, c), 'row', split_axis=0, concat...  5.93 us
    all_to_all x1, starting transfers between devices, local(): lax.all_to_all(mixed.reshape(axial, rows, c), 'row', split_axis=0, concat...  3.52 us
    all_to_all x1, waiting for transfers between devices, local(): lax.all_to_all(features, 'row', split_axis=0, concat_axis=0, tiled=True)  1.32 us
    pallas_call x1, Pallas kernels, local(): pl.pallas_call(radial_kernel, out_shape=jax.ShapeDtypeStruct((n, a_loc, r...  1.19 us
    pallas_call x1, Pallas kernels, local(): pl.pallas_call(partial(mlp_kernel, len(partials)), out_shape=jax.ShapeDty...  1.08 us
    ppermute x7, waiting for transfers between devices, move(): return lax.ppermute(piece, 'row', [(i, i ^ by * stride) for i in range(n)])  0.89 us
  transfers between devices with their start and end apart: 9, of which 4 were waited for; matrix products, arithmetic and copies ran while one was open for 0% of the time, Pallas kernels for 9%

profile of v18, /device:TPU:0, one launch (start us, length us, event | category | flops | bytes accessed | tf_op | source)
XLA Modules:
  0.0 32.1 jit_solution(1847543767899371414)
XLA Ops:
  0.0 7.5 %all-to-all-start = ((bf16[32,2,4,256]{3,2,1,0:T(4,128)(2,1)}), bf16[32,2,4,256]{3,2,1,0:T(4,128)(2,1)S(1)}, u32[]{:S(2)}, u32[]{:S(2)}) async-start(bf16[32,2,4,256]{3,2,1,0:T(4,128)(2,1)} %feat_ref.1), calls=%async_computation | async-start | bytes 262144 | tf_op jit(solution)/shard_map/all_to_all | solution.py:238
  7.5 0.0 copy-start.6
  7.5 0.0 copy-start.7
  7.6 0.0 copy-start.8
  7.6 0.0 copy-start.9
  7.6 0.0 copy-start.5
  7.6 0.0 copy-start.10
  7.6 0.6 %copy-done.6 = f32[256]{0:T(256)S(1)} copy-done((f32[256]{0:T(256)S(1)}, f32[256]{0:T(256)}, u32[]{:S(2)}) %copy-start.6) | copy-done | bytes 1048
  8.2 0.0 copy-done.7
  8.2 0.0 copy-done.8
  8.2 0.0 copy-done.9
  8.3 0.0 copy-done.5
  8.3 0.1 pack.1
  8.4 1.9 %collective-permute-start = (bf16[144,256]{1,0:T(8,128)(2,1)S(1)}, bf16[144,256]{1,0:T(8,128)(2,1)S(1)}, u32[]{:S(2)}, u32[]{:S(2)}) collective-permute-start(bf16[144,256]{1,0:T(8,128)(2,1)S(1)} %get-tuple-element.11.refs_4_), channel_id=1, source_target_pairs={{0,4},{1,5},{2,6},{3,7},{4,0},{5,1},{6,2},{7,3},{8,12},{9,13},{10,... | collective-permute-start | bytes 221192 | tf_op jit(solution)/shard_map/ppermute | solution.py:213
  10.3 2.4 %collective-permute-start.1 = (bf16[144,256]{1,0:T(8,128)(2,1)S(1)}, bf16[144,256]{1,0:T(8,128)(2,1)S(1)}, u32[]{:S(2)}, u32[]{:S(2)}) collective-permute-start(bf16[144,256]{1,0:T(8,128)(2,1)S(1)} %get-tuple-element.11.refs_4_), channel_id=1, source_target_pairs={{0,8},{1,9},{2,10},{3,11},{4,12},{5,13},{6,14},{7,15},{8,0},{9,1},... | collective-permute-start | bytes 221192 | tf_op jit(solution)/shard_map/ppermute | solution.py:213
  12.6 0.1 collective-permute-start.2
  12.7 1.9 %collective-permute-start.3 = (bf16[144,256]{1,0:T(8,128)(2,1)S(1)}, bf16[144,256]{1,0:T(8,128)(2,1)S(1)}, u32[]{:S(2)}, u32[]{:S(2)}) collective-permute-start(bf16[144,256]{1,0:T(8,128)(2,1)S(1)} %get-tuple-element.11.refs_4_), channel_id=1, source_target_pairs={{0,2},{1,3},{2,0},{3,1},{4,6},{5,7},{6,4},{7,5},{8,10},{9,11},{10,... | collective-permute-start | bytes 221192 | tf_op jit(solution)/shard_map/ppermute | solution.py:213
  14.7 1.3 %all-to-all-done = bf16[32,2,4,256]{3,2,1,0:T(4,128)(2,1)S(1)} async-done(((bf16[32,2,4,256]{3,2,1,0:T(4,128)(2,1)}), bf16[32,2,4,256]{3,2,1,0:T(4,128)(2,1)S(1)}, u32[]{:S(2)}, u32[]{:S(2)}) %all-to-all-start) | async-done | bytes 131104 | tf_op jit(solution)/shard_map/all_to_all | solution.py:238
  16.0 1.2 %radial.1.refs_0_ = bf16[16,2,8,256]{3,2,1,0:T(8,128)(2,1)} custom-call(bf16[16,2,2,4,256]{4,3,2,1,0:T(4,128)(2,1)S(1)} %bitcast.7, f32[31,256]{1,0:T(8,128)S(1)} %copy-done.1), custom_call_target="tpu_custom_call" | custom-call | tf_op jit(solution)/shard_map/radial/pallas_call | solution.py:240
  17.2 3.5 %all-to-all-start.1 = ((bf16[32,8,256]{2,1,0:T(8,128)(2,1)}), bf16[32,8,256]{2,1,0:T(8,128)(2,1)S(1)}, u32[]{:S(2)}, u32[]{:S(2)}) async-start(bf16[32,8,256]{2,1,0:T(8,128)(2,1)} %bitcast.6), calls=%async_computation.1 | async-start | bytes 262144 | tf_op jit(solution)/shard_map/all_to_all | solution.py:262
  20.7 0.0 copy-start.2
  20.7 0.0 collective-permute-done.1.refs_2_
  20.8 0.0 collective-permute-done.2.refs_3_
  20.8 1.9 %collective-permute-start.4 = (bf16[400,256]{1,0:T(8,128)(2,1)S(1)}, bf16[400,256]{1,0:T(8,128)(2,1)S(1)}, u32[]{:S(2)}, u32[]{:S(2)}) collective-permute-start(bf16[400,256]{1,0:T(8,128)(2,1)S(1)} %get-tuple-element.12), channel_id=1, source_target_pairs={{0,2},{1,3},{2,0},{3,1},{4,6},{5,7},{6,4},{7,5},{8,10},{9,11},{10,... | collective-permute-start | bytes 614408 | tf_op jit(solution)/shard_map/ppermute | solution.py:213
  22.7 0.0 collective-permute-start.5
  22.7 5.9 %all-to-all-done.1.z_ref = bf16[32,8,256]{2,1,0:T(8,128)(2,1)S(1)} async-done(((bf16[32,8,256]{2,1,0:T(8,128)(2,1)}), bf16[32,8,256]{2,1,0:T(8,128)(2,1)S(1)}, u32[]{:S(2)}, u32[]{:S(2)}) %all-to-all-start.1) | async-done | bytes 131104 | tf_op jit(solution)/shard_map/all_to_all | solution.py:262
  28.6 0.6 %axial.1.normed_ref = bf16[256,256]{1,0:T(8,128)(2,1)S(1)} custom-call(bf16[32,8,256]{2,1,0:T(8,128)(2,1)S(1)} %all-to-all-done.1.z_ref, f32[31,256]{1,0:T(8,128)S(1)} %copy-done.2, f32[8,256]{1,0:T(8,128)S(1)} %get-tuple-element.13.consts_ref), custom_call_target="tpu_custom_call" | custom-call | tf_op jit(solution)/shard_map/axial/pallas_call | solution.py:263
  29.3 0.0 copy-start
  29.3 0.2 collective-permute-done.4.rest_2_
  29.5 0.8 %first.1.rest_0_ = f32[256,256]{1,0:T(8,128)S(1)} custom-call(bf16[256,256]{1,0:T(8,128)(2,1)S(1)} %axial.1.normed_ref, bf16[656,256]{1,0:T(8,128)(2,1)S(1)} %get-tuple-element.15.rest_0_, bf16[656,256]{1,0:T(8,128)(2,1)S(1)} %collective-permute-done.5.rest_1_, bf16[400,256]{1,0:T(8,128)(2,1)S(1)} %collective-permute-done.4.rest_2_), custom_call_target="tpu_custom_call" | custom-call | tf_op jit(solution)/shard_map/first/pallas_call | solution.py:279
  30.4 0.6 %collective-permute-done.6.rest_1_ = bf16[400,256]{1,0:T(8,128)(2,1)S(1)} collective-permute-done((bf16[400,256]{1,0:T(8,128)(2,1)S(1)}, bf16[400,256]{1,0:T(8,128)(2,1)S(1)}, u32[]{:S(2)}, u32[]{:S(2)}) %collective-permute-start.6) | collective-permute-done | bytes 204832 | tf_op jit(solution)/shard_map/ppermute | solution.py:213
  31.0 1.1 %mlp.1 = bf16[32,2,4,256]{3,2,1,0:T(4,128)(2,1)} custom-call(bf16[256,256]{1,0:T(8,128)(2,1)S(1)} %axial.1.normed_ref, f32[8,256]{1,0:T(8,128)S(1)} %get-tuple-element.13.consts_ref, bf16[32,2,4,256]{3,2,1,0:T(4,128)(2,1)S(1)} %copy-done, f32[256,256]{1,0:T(8,128)S(1)} %first.1.rest_0_, bf16[400,256]{1,0:T(8,128)(2,1)S(1)} %collective-permute-done.6.rest_1_), custom_call_target="tpu_custom_call" | custom-call | tf_op jit(solution)/shard_map/mlp/pallas_call | solution.py:291
  (14 shorter events, 0.1 us)
Async XLA Ops:
  0.0 7.6 %copy-start.3 = (bf16[64,256]{1,0:T(8,128)(2,1)S(1)}, bf16[64,256]{1,0:T(8,128)(2,1)}, u32[]{:S(2)}) copy-start(bf16[64,256]{1,0:T(8,128)(2,1)} %w_in_ref.1) | copy-start | bytes 98308
  0.0 7.6 %copy-start.4 = (bf16[64,256]{1,0:T(8,128)(2,1)S(1)}, bf16[64,256]{1,0:T(8,128)(2,1)}, u32[]{:S(2)}) copy-start(bf16[64,256]{1,0:T(8,128)(2,1)} %w_out_ref.1) | copy-start | bytes 98308
  0.0 16.0 %all-to-all-start = ((bf16[32,2,4,256]{3,2,1,0:T(4,128)(2,1)}), bf16[32,2,4,256]{3,2,1,0:T(4,128)(2,1)S(1)}, u32[]{:S(2)}, u32[]{:S(2)}) async-start(bf16[32,2,4,256]{3,2,1,0:T(4,128)(2,1)} %feat_ref.1), calls=%async_computation | async-start | bytes 262144 | tf_op jit(solution)/shard_map/all_to_all | solution.py:238
  7.5 0.7 %copy-start.6 = (f32[256]{0:T(256)S(1)}, f32[256]{0:T(256)}, u32[]{:S(2)}) copy-start(f32[256]{0:T(256)} %param.15) | copy-start | bytes 3076
  7.5 0.7 %copy-start.7 = (f32[256]{0:T(256)S(1)}, f32[256]{0:T(256)}, u32[]{:S(2)}) copy-start(f32[256]{0:T(256)} %param.16) | copy-start | bytes 3076
  7.6 0.7 %copy-start.8 = (f32[256]{0:T(256)S(1)}, f32[256]{0:T(256)}, u32[]{:S(2)}) copy-start(f32[256]{0:T(256)} %param.20) | copy-start | bytes 3076
  7.6 0.7 %copy-start.9 = (f32[256]{0:T(256)S(1)}, f32[256]{0:T(256)}, u32[]{:S(2)}) copy-start(f32[256]{0:T(256)} %param.21) | copy-start | bytes 3076
  7.6 0.7 %copy-start.5 = (f32[256]{0:T(256)S(1)}, f32[256]{0:T(256)}, u32[]{:S(2)}) copy-start(f32[256]{0:T(256)} %param.14) | copy-start | bytes 3076
  7.6 0.7 %copy-start.10 = (bf16[64]{0:T(256)(128)(2,1)S(1)}, bf16[64]{0:T(256)(128)(2,1)}, u32[]{:S(2)}) copy-start(bf16[64]{0:T(256)(128)(2,1)} %b_ref.1) | copy-start | bytes 388
  8.3 7.7 %copy-start.1 = (f32[31,256]{1,0:T(8,128)S(1)}, f32[31,256]{1,0:T(8,128)}, u32[]{:S(2)}) copy-start(f32[31,256]{1,0:T(8,128)} %taps_ref.2) | copy-start | bytes 95236
  8.4 12.4 %collective-permute-start = (bf16[144,256]{1,0:T(8,128)(2,1)S(1)}, bf16[144,256]{1,0:T(8,128)(2,1)S(1)}, u32[]{:S(2)}, u32[]{:S(2)}) collective-permute-start(bf16[144,256]{1,0:T(8,128)(2,1)S(1)} %get-tuple-element.11.refs_4_), channel_id=1, source_target_pairs={{0,4},{1,5},{2,6},{3,7},{4,0},{5,1},{6,2},{7,3},{8,12},{9,13},{10,... | collective-permute-start | bytes 221192 | tf_op jit(solution)/shard_map/ppermute | solution.py:213
  10.3 10.5 %collective-permute-start.1 = (bf16[144,256]{1,0:T(8,128)(2,1)S(1)}, bf16[144,256]{1,0:T(8,128)(2,1)S(1)}, u32[]{:S(2)}, u32[]{:S(2)}) collective-permute-start(bf16[144,256]{1,0:T(8,128)(2,1)S(1)} %get-tuple-element.11.refs_4_), channel_id=1, source_target_pairs={{0,8},{1,9},{2,10},{3,11},{4,12},{5,13},{6,14},{7,15},{8,0},{9,1},... | collective-permute-start | bytes 221192 | tf_op jit(solution)/shard_map/ppermute | solution.py:213
  12.6 8.1 %collective-permute-start.2 = (bf16[144,256]{1,0:T(8,128)(2,1)S(1)}, bf16[144,256]{1,0:T(8,128)(2,1)S(1)}, u32[]{:S(2)}, u32[]{:S(2)}) collective-permute-start(bf16[144,256]{1,0:T(8,128)(2,1)S(1)} %get-tuple-element.11.refs_4_), channel_id=1, source_target_pairs={{0,12},{1,13},{2,14},{3,15},{4,8},{5,9},{6,10},{7,11},{8,4},{9,5},... | collective-permute-start | bytes 221192 | tf_op jit(solution)/shard_map/ppermute | solution.py:213
  12.7 8.0 %collective-permute-start.3 = (bf16[144,256]{1,0:T(8,128)(2,1)S(1)}, bf16[144,256]{1,0:T(8,128)(2,1)S(1)}, u32[]{:S(2)}, u32[]{:S(2)}) collective-permute-start(bf16[144,256]{1,0:T(8,128)(2,1)S(1)} %get-tuple-element.11.refs_4_), channel_id=1, source_target_pairs={{0,2},{1,3},{2,0},{3,1},{4,6},{5,7},{6,4},{7,5},{8,10},{9,11},{10,... | collective-permute-start | bytes 221192 | tf_op jit(solution)/shard_map/ppermute | solution.py:213
  17.2 11.4 %all-to-all-start.1 = ((bf16[32,8,256]{2,1,0:T(8,128)(2,1)}), bf16[32,8,256]{2,1,0:T(8,128)(2,1)S(1)}, u32[]{:S(2)}, u32[]{:S(2)}) async-start(bf16[32,8,256]{2,1,0:T(8,128)(2,1)} %bitcast.6), calls=%async_computation.1 | async-start | bytes 262144 | tf_op jit(solution)/shard_map/all_to_all | solution.py:262
  20.7 7.9 %copy-start.2 = (f32[31,256]{1,0:T(8,128)S(1)}, f32[31,256]{1,0:T(8,128)}, u32[]{:S(2)}) copy-start(f32[31,256]{1,0:T(8,128)} %taps_ref.3) | copy-start | bytes 95236
  20.8 8.7 %collective-permute-start.4 = (bf16[400,256]{1,0:T(8,128)(2,1)S(1)}, bf16[400,256]{1,0:T(8,128)(2,1)S(1)}, u32[]{:S(2)}, u32[]{:S(2)}) collective-permute-start(bf16[400,256]{1,0:T(8,128)(2,1)S(1)} %get-tuple-element.12), channel_id=1, source_target_pairs={{0,2},{1,3},{2,0},{3,1},{4,6},{5,7},{6,4},{7,5},{8,10},{9,11},{10,... | collective-permute-start | bytes 614408 | tf_op jit(solution)/shard_map/ppermute | solution.py:213
  22.7 6.8 %collective-permute-start.5 = (bf16[656,256]{1,0:T(8,128)(2,1)S(1)}, bf16[656,256]{1,0:T(8,128)(2,1)S(1)}, u32[]{:S(2)}, u32[]{:S(2)}) collective-permute-start(bf16[656,256]{1,0:T(8,128)(2,1)S(1)} %get-tuple-element.15.rest_0_), channel_id=1, source_target_pairs={{0,1},{1,0},{2,3},{3,2},{4,5},{5,4},{6,7},{7,6},{8,9},{9,8},{10,11... | collective-permute-start | bytes 1007624 | tf_op jit(solution)/shard_map/ppermute | solution.py:213
  29.3 1.7 %copy-start = (bf16[32,2,4,256]{3,2,1,0:T(4,128)(2,1)S(1)}, bf16[32,2,4,256]{3,2,1,0:T(4,128)(2,1)}, u32[]{:S(2)}) copy-start(bf16[32,2,4,256]{3,2,1,0:T(4,128)(2,1)} %feat_ref.1) | copy-start | bytes 393220
  29.5 1.5 %collective-permute-start.6 = (bf16[400,256]{1,0:T(8,128)(2,1)S(1)}, bf16[400,256]{1,0:T(8,128)(2,1)S(1)}, u32[]{:S(2)}, u32[]{:S(2)}) collective-permute-start(bf16[400,256]{1,0:T(8,128)(2,1)S(1)} %collective-permute-done.4.rest_2_), channel_id=1, source_target_pairs={{0,1},{1,0},{2,3},{3,2},{4,5},{5,4},{6,7},{7,6},{8,9},{9,8},{10,11... | collective-permute-start | bytes 614408 | tf_op jit(solution)/shard_map/ppermute | solution.py:213

commit v19 on v18

--- a/solution.py
+++ b/solution.py
@@ -59,7 +59,7 @@
     odd[pad : pad + n, :, 0:theta] = second
     odd[pad - 1 : pad + n - 1, :, theta:] = first
 
-    block = 4
+    block = 2
 
     def step(base, wanted):
         total = jnp.zeros((block, a_loc, 2 * theta, c), jnp.float32)
@@ -93,7 +93,7 @@
     padded[0:half] = zeros
     padded[half + axial :] = zeros
     padded[half : half + axial] = z_ref[...].astype(jnp.float32)
-    block = 8
+    block = 4
 
     def conv(base, wanted):
         total = jnp.zeros((block, rows, c), jnp.float32)

time: 32.4 us -> 32.4 us (level)
  transfers between devices with their start and end apart: 9 -> 9, of which waited for: 4 -> 4; matrix products, arithmetic and copies ran while one was open for 0% -> 0% of each run, Pallas kernels for 9% -> 8%
where the time goes in v19:
time: 32.4 us; the launch traced here: 32.1 us
  starting transfers between devices  19.2 us (59%)
  waiting for transfers between devices  8.16 us (25%)
  Pallas kernels  3.79 us (12%)
  local copies, waits for them, and re-layouts  0.7 us (2%)
    ppermute x7, starting transfers between devices, move(): return lax.ppermute(piece, 'row', [(i, i ^ by * stride) for i in range(n)])  8.19 us
    all_to_all x1, starting transfers between devices, local(): lax.all_to_all(features, 'row', split_axis=0, concat_axis=0, tiled=True)  7.52 us
    all_to_all x1, waiting for transfers between devices, local(): lax.all_to_all(mixed.reshape(axial, rows, c), 'row', split_axis=0, concat...  5.93 us
    all_to_all x1, starting transfers between devices, local(): lax.all_to_all(mixed.reshape(axial, rows, c), 'row', split_axis=0, concat...  3.52 us
    all_to_all x1, waiting for transfers between devices, local(): lax.all_to_all(features, 'row', split_axis=0, concat_axis=0, tiled=True)  1.32 us
    pallas_call x1, Pallas kernels, local(): pl.pallas_call(radial_kernel, out_shape=jax.ShapeDtypeStruct((n, a_loc, r...  1.16 us
    pallas_call x1, Pallas kernels, local(): pl.pallas_call(partial(mlp_kernel, len(partials)), out_shape=jax.ShapeDty...  1.08 us
    ppermute x7, waiting for transfers between devices, move(): return lax.ppermute(piece, 'row', [(i, i ^ by * stride) for i in range(n)])  0.91 us
  transfers between devices with their start and end apart: 9, of which 4 were waited for; matrix products, arithmetic and copies ran while one was open for 0% of the time, Pallas kernels for 8%

profile of v19, /device:TPU:0, one launch (start us, length us, event | category | flops | bytes accessed | tf_op | source)
XLA Modules:
  0.0 32.1 jit_solution(3827320328234166047)
XLA Ops:
  0.0 7.5 %all-to-all-start = ((bf16[32,2,4,256]{3,2,1,0:T(4,128)(2,1)}), bf16[32,2,4,256]{3,2,1,0:T(4,128)(2,1)S(1)}, u32[]{:S(2)}, u32[]{:S(2)}) async-start(bf16[32,2,4,256]{3,2,1,0:T(4,128)(2,1)} %feat_ref.1), calls=%async_computation | async-start | bytes 262144 | tf_op jit(solution)/shard_map/all_to_all | solution.py:238
  7.5 0.0 copy-start.6
  7.5 0.0 copy-start.7
  7.6 0.0 copy-start.8
  7.6 0.0 copy-start.9
  7.6 0.0 copy-start.5
  7.6 0.0 copy-start.10
  7.6 0.6 %copy-done.6 = f32[256]{0:T(256)S(1)} copy-done((f32[256]{0:T(256)S(1)}, f32[256]{0:T(256)}, u32[]{:S(2)}) %copy-start.6) | copy-done | bytes 1048
  8.2 0.0 copy-done.7
  8.2 0.0 copy-done.8
  8.2 0.0 copy-done.9
  8.3 0.0 copy-done.5
  8.3 0.1 pack.1
  8.4 1.9 %collective-permute-start = (bf16[144,256]{1,0:T(8,128)(2,1)S(1)}, bf16[144,256]{1,0:T(8,128)(2,1)S(1)}, u32[]{:S(2)}, u32[]{:S(2)}) collective-permute-start(bf16[144,256]{1,0:T(8,128)(2,1)S(1)} %get-tuple-element.11.refs_4_), channel_id=1, source_target_pairs={{0,4},{1,5},{2,6},{3,7},{4,0},{5,1},{6,2},{7,3},{8,12},{9,13},{10,... | collective-permute-start | bytes 221192 | tf_op jit(solution)/shard_map/ppermute | solution.py:213
  10.3 2.4 %collective-permute-start.1 = (bf16[144,256]{1,0:T(8,128)(2,1)S(1)}, bf16[144,256]{1,0:T(8,128)(2,1)S(1)}, u32[]{:S(2)}, u32[]{:S(2)}) collective-permute-start(bf16[144,256]{1,0:T(8,128)(2,1)S(1)} %get-tuple-element.11.refs_4_), channel_id=1, source_target_pairs={{0,8},{1,9},{2,10},{3,11},{4,12},{5,13},{6,14},{7,15},{8,0},{9,1},... | collective-permute-start | bytes 221192 | tf_op jit(solution)/shard_map/ppermute | solution.py:213
  12.6 0.1 collective-permute-start.2
  12.7 1.9 %collective-permute-start.3 = (bf16[144,256]{1,0:T(8,128)(2,1)S(1)}, bf16[144,256]{1,0:T(8,128)(2,1)S(1)}, u32[]{:S(2)}, u32[]{:S(2)}) collective-permute-start(bf16[144,256]{1,0:T(8,128)(2,1)S(1)} %get-tuple-element.11.refs_4_), channel_id=1, source_target_pairs={{0,2},{1,3},{2,0},{3,1},{4,6},{5,7},{6,4},{7,5},{8,10},{9,11},{10,... | collective-permute-start | bytes 221192 | tf_op jit(solution)/shard_map/ppermute | solution.py:213
  14.7 1.3 %all-to-all-done = bf16[32,2,4,256]{3,2,1,0:T(4,128)(2,1)S(1)} async-done(((bf16[32,2,4,256]{3,2,1,0:T(4,128)(2,1)}), bf16[32,2,4,256]{3,2,1,0:T(4,128)(2,1)S(1)}, u32[]{:S(2)}, u32[]{:S(2)}) %all-to-all-start) | async-done | bytes 131104 | tf_op jit(solution)/shard_map/all_to_all | solution.py:238
  16.0 1.2 %radial.1.refs_0_ = bf16[16,2,8,256]{3,2,1,0:T(8,128)(2,1)} custom-call(bf16[16,2,2,4,256]{4,3,2,1,0:T(4,128)(2,1)S(1)} %bitcast.7, f32[31,256]{1,0:T(8,128)S(1)} %copy-done.1), custom_call_target="tpu_custom_call" | custom-call | tf_op jit(solution)/shard_map/radial/pallas_call | solution.py:240
  17.2 3.5 %all-to-all-start.1 = ((bf16[32,8,256]{2,1,0:T(8,128)(2,1)}), bf16[32,8,256]{2,1,0:T(8,128)(2,1)S(1)}, u32[]{:S(2)}, u32[]{:S(2)}) async-start(bf16[32,8,256]{2,1,0:T(8,128)(2,1)} %bitcast.6), calls=%async_computation.1 | async-start | bytes 262144 | tf_op jit(solution)/shard_map/all_to_all | solution.py:262
  20.7 0.0 copy-start.2
  20.7 0.0 collective-permute-done.refs_1_
  20.7 0.0 collective-permute-done.2.refs_3_
  20.7 0.0 collective-permute-done.3.refs_5_
  20.8 1.9 %collective-permute-start.4 = (bf16[400,256]{1,0:T(8,128)(2,1)S(1)}, bf16[400,256]{1,0:T(8,128)(2,1)S(1)}, u32[]{:S(2)}, u32[]{:S(2)}) collective-permute-start(bf16[400,256]{1,0:T(8,128)(2,1)S(1)} %get-tuple-element.12), channel_id=1, source_target_pairs={{0,2},{1,3},{2,0},{3,1},{4,6},{5,7},{6,4},{7,5},{8,10},{9,11},{10,... | collective-permute-start | bytes 614408 | tf_op jit(solution)/shard_map/ppermute | solution.py:213
  22.7 5.9 %all-to-all-done.1.z_ref = bf16[32,8,256]{2,1,0:T(8,128)(2,1)S(1)} async-done(((bf16[32,8,256]{2,1,0:T(8,128)(2,1)}), bf16[32,8,256]{2,1,0:T(8,128)(2,1)S(1)}, u32[]{:S(2)}, u32[]{:S(2)}) %all-to-all-start.1) | async-done | bytes 131104 | tf_op jit(solution)/shard_map/all_to_all | solution.py:262
  28.6 0.6 %axial.1.normed_ref = bf16[256,256]{1,0:T(8,128)(2,1)S(1)} custom-call(bf16[32,8,256]{2,1,0:T(8,128)(2,1)S(1)} %all-to-all-done.1.z_ref, f32[31,256]{1,0:T(8,128)S(1)} %copy-done.2, f32[8,256]{1,0:T(8,128)S(1)} %get-tuple-element.13.consts_ref), custom_call_target="tpu_custom_call" | custom-call | tf_op jit(solution)/shard_map/axial/pallas_call | solution.py:263
  29.2 0.0 copy-start
  29.2 0.3 collective-permute-done.4.rest_2_
  29.5 0.8 %first.1.rest_0_ = f32[256,256]{1,0:T(8,128)S(1)} custom-call(bf16[256,256]{1,0:T(8,128)(2,1)S(1)} %axial.1.normed_ref, bf16[656,256]{1,0:T(8,128)(2,1)S(1)} %get-tuple-element.15.rest_0_, bf16[656,256]{1,0:T(8,128)(2,1)S(1)} %collective-permute-done.5.rest_1_, bf16[400,256]{1,0:T(8,128)(2,1)S(1)} %collective-permute-done.4.rest_2_), custom_call_target="tpu_custom_call" | custom-call | tf_op jit(solution)/shard_map/first/pallas_call | solution.py:279
  30.3 0.6 %collective-permute-done.6.rest_1_ = bf16[400,256]{1,0:T(8,128)(2,1)S(1)} collective-permute-done((bf16[400,256]{1,0:T(8,128)(2,1)S(1)}, bf16[400,256]{1,0:T(8,128)(2,1)S(1)}, u32[]{:S(2)}, u32[]{:S(2)}) %collective-permute-start.6) | collective-permute-done | bytes 204832 | tf_op jit(solution)/shard_map/ppermute | solution.py:213
  31.0 1.1 %mlp.1 = bf16[32,2,4,256]{3,2,1,0:T(4,128)(2,1)} custom-call(bf16[256,256]{1,0:T(8,128)(2,1)S(1)} %axial.1.normed_ref, f32[8,256]{1,0:T(8,128)S(1)} %get-tuple-element.13.consts_ref, bf16[32,2,4,256]{3,2,1,0:T(4,128)(2,1)S(1)} %copy-done, f32[256,256]{1,0:T(8,128)S(1)} %first.1.rest_0_, bf16[400,256]{1,0:T(8,128)(2,1)S(1)} %collective-permute-done.6.rest_1_), custom_call_target="tpu_custom_call" | custom-call | tf_op jit(solution)/shard_map/mlp/pallas_call | solution.py:291
  (14 shorter events, 0.1 us)
Async XLA Ops:
  0.0 7.6 %copy-start.3 = (bf16[64,256]{1,0:T(8,128)(2,1)S(1)}, bf16[64,256]{1,0:T(8,128)(2,1)}, u32[]{:S(2)}) copy-start(bf16[64,256]{1,0:T(8,128)(2,1)} %w_in_ref.1) | copy-start | bytes 98308
  0.0 7.6 %copy-start.4 = (bf16[64,256]{1,0:T(8,128)(2,1)S(1)}, bf16[64,256]{1,0:T(8,128)(2,1)}, u32[]{:S(2)}) copy-start(bf16[64,256]{1,0:T(8,128)(2,1)} %w_out_ref.1) | copy-start | bytes 98308
  0.0 16.0 %all-to-all-start = ((bf16[32,2,4,256]{3,2,1,0:T(4,128)(2,1)}), bf16[32,2,4,256]{3,2,1,0:T(4,128)(2,1)S(1)}, u32[]{:S(2)}, u32[]{:S(2)}) async-start(bf16[32,2,4,256]{3,2,1,0:T(4,128)(2,1)} %feat_ref.1), calls=%async_computation | async-start | bytes 262144 | tf_op jit(solution)/shard_map/all_to_all | solution.py:238
  7.5 0.7 %copy-start.6 = (f32[256]{0:T(256)S(1)}, f32[256]{0:T(256)}, u32[]{:S(2)}) copy-start(f32[256]{0:T(256)} %param.15) | copy-start | bytes 3076
  7.5 0.7 %copy-start.7 = (f32[256]{0:T(256)S(1)}, f32[256]{0:T(256)}, u32[]{:S(2)}) copy-start(f32[256]{0:T(256)} %param.16) | copy-start | bytes 3076
  7.6 0.7 %copy-start.8 = (f32[256]{0:T(256)S(1)}, f32[256]{0:T(256)}, u32[]{:S(2)}) copy-start(f32[256]{0:T(256)} %param.20) | copy-start | bytes 3076
  7.6 0.7 %copy-start.9 = (f32[256]{0:T(256)S(1)}, f32[256]{0:T(256)}, u32[]{:S(2)}) copy-start(f32[256]{0:T(256)} %param.21) | copy-start | bytes 3076
  7.6 0.7 %copy-start.5 = (f32[256]{0:T(256)S(1)}, f32[256]{0:T(256)}, u32[]{:S(2)}) copy-start(f32[256]{0:T(256)} %param.14) | copy-start | bytes 3076
  7.6 0.7 %copy-start.10 = (bf16[64]{0:T(256)(128)(2,1)S(1)}, bf16[64]{0:T(256)(128)(2,1)}, u32[]{:S(2)}) copy-start(bf16[64]{0:T(256)(128)(2,1)} %b_ref.1) | copy-start | bytes 388
  8.3 7.7 %copy-start.1 = (f32[31,256]{1,0:T(8,128)S(1)}, f32[31,256]{1,0:T(8,128)}, u32[]{:S(2)}) copy-start(f32[31,256]{1,0:T(8,128)} %taps_ref.2) | copy-start | bytes 95236
  8.4 12.4 %collective-permute-start = (bf16[144,256]{1,0:T(8,128)(2,1)S(1)}, bf16[144,256]{1,0:T(8,128)(2,1)S(1)}, u32[]{:S(2)}, u32[]{:S(2)}) collective-permute-start(bf16[144,256]{1,0:T(8,128)(2,1)S(1)} %get-tuple-element.11.refs_4_), channel_id=1, source_target_pairs={{0,4},{1,5},{2,6},{3,7},{4,0},{5,1},{6,2},{7,3},{8,12},{9,13},{10,... | collective-permute-start | bytes 221192 | tf_op jit(solution)/shard_map/ppermute | solution.py:213
  10.3 10.4 %collective-permute-start.1 = (bf16[144,256]{1,0:T(8,128)(2,1)S(1)}, bf16[144,256]{1,0:T(8,128)(2,1)S(1)}, u32[]{:S(2)}, u32[]{:S(2)}) collective-permute-start(bf16[144,256]{1,0:T(8,128)(2,1)S(1)} %get-tuple-element.11.refs_4_), channel_id=1, source_target_pairs={{0,8},{1,9},{2,10},{3,11},{4,12},{5,13},{6,14},{7,15},{8,0},{9,1},... | collective-permute-start | bytes 221192 | tf_op jit(solution)/shard_map/ppermute | solution.py:213
  12.6 8.1 %collective-permute-start.2 = (bf16[144,256]{1,0:T(8,128)(2,1)S(1)}, bf16[144,256]{1,0:T(8,128)(2,1)S(1)}, u32[]{:S(2)}, u32[]{:S(2)}) collective-permute-start(bf16[144,256]{1,0:T(8,128)(2,1)S(1)} %get-tuple-element.11.refs_4_), channel_id=1, source_target_pairs={{0,12},{1,13},{2,14},{3,15},{4,8},{5,9},{6,10},{7,11},{8,4},{9,5},... | collective-permute-start | bytes 221192 | tf_op jit(solution)/shard_map/ppermute | solution.py:213
  12.7 8.0 %collective-permute-start.3 = (bf16[144,256]{1,0:T(8,128)(2,1)S(1)}, bf16[144,256]{1,0:T(8,128)(2,1)S(1)}, u32[]{:S(2)}, u32[]{:S(2)}) collective-permute-start(bf16[144,256]{1,0:T(8,128)(2,1)S(1)} %get-tuple-element.11.refs_4_), channel_id=1, source_target_pairs={{0,2},{1,3},{2,0},{3,1},{4,6},{5,7},{6,4},{7,5},{8,10},{9,11},{10,... | collective-permute-start | bytes 221192 | tf_op jit(solution)/shard_map/ppermute | solution.py:213
  17.2 11.4 %all-to-all-start.1 = ((bf16[32,8,256]{2,1,0:T(8,128)(2,1)}), bf16[32,8,256]{2,1,0:T(8,128)(2,1)S(1)}, u32[]{:S(2)}, u32[]{:S(2)}) async-start(bf16[32,8,256]{2,1,0:T(8,128)(2,1)} %bitcast.6), calls=%async_computation.1 | async-start | bytes 262144 | tf_op jit(solution)/shard_map/all_to_all | solution.py:262
  20.7 7.9 %copy-start.2 = (f32[31,256]{1,0:T(8,128)S(1)}, f32[31,256]{1,0:T(8,128)}, u32[]{:S(2)}) copy-start(f32[31,256]{1,0:T(8,128)} %taps_ref.3) | copy-start | bytes 95236
  20.8 8.7 %collective-permute-start.4 = (bf16[400,256]{1,0:T(8,128)(2,1)S(1)}, bf16[400,256]{1,0:T(8,128)(2,1)S(1)}, u32[]{:S(2)}, u32[]{:S(2)}) collective-permute-start(bf16[400,256]{1,0:T(8,128)(2,1)S(1)} %get-tuple-element.12), channel_id=1, source_target_pairs={{0,2},{1,3},{2,0},{3,1},{4,6},{5,7},{6,4},{7,5},{8,10},{9,11},{10,... | collective-permute-start | bytes 614408 | tf_op jit(solution)/shard_map/ppermute | solution.py:213
  22.7 6.8 %collective-permute-start.5 = (bf16[656,256]{1,0:T(8,128)(2,1)S(1)}, bf16[656,256]{1,0:T(8,128)(2,1)S(1)}, u32[]{:S(2)}, u32[]{:S(2)}) collective-permute-start(bf16[656,256]{1,0:T(8,128)(2,1)S(1)} %get-tuple-element.15.rest_0_), channel_id=1, source_target_pairs={{0,1},{1,0},{2,3},{3,2},{4,5},{5,4},{6,7},{7,6},{8,9},{9,8},{10,11... | collective-permute-start | bytes 1007624 | tf_op jit(solution)/shard_map/ppermute | solution.py:213
  29.2 1.7 %copy-start = (bf16[32,2,4,256]{3,2,1,0:T(4,128)(2,1)S(1)}, bf16[32,2,4,256]{3,2,1,0:T(4,128)(2,1)}, u32[]{:S(2)}) copy-start(bf16[32,2,4,256]{3,2,1,0:T(4,128)(2,1)} %feat_ref.1) | copy-start | bytes 393220
  29.5 1.5 %collective-permute-start.6 = (bf16[400,256]{1,0:T(8,128)(2,1)S(1)}, bf16[400,256]{1,0:T(8,128)(2,1)S(1)}, u32[]{:S(2)}, u32[]{:S(2)}) collective-permute-start(bf16[400,256]{1,0:T(8,128)(2,1)S(1)} %collective-permute-done.4.rest_2_), channel_id=1, source_target_pairs={{0,1},{1,0},{2,3},{3,2},{4,5},{5,4},{6,7},{7,6},{8,9},{9,8},{10,11... | collective-permute-start | bytes 614408 | tf_op jit(solution)/shard_map/ppermute | solution.py:213
